TPU v7x, 32 devices: a whole 2x2x4 slice. The times are simulated.
32 devices in a mesh: replica: 4 (over y, x), shard: 8 (over z, core).
Axes of the slice: x: 2, y: 2, z: 4, core: 2. Of those that a mesh axis runs over, the one named last changes fastest.
Arguments:
- master_weight: float32 [8, 1024, 4096], P(None, 'replica', 'shard'), may hold values from -0.1875 to 0.1875
- gradient: bfloat16 [8, 1024, 4096], P(None, 'replica', 'shard'), may hold values from -6 to 6
- first_moment: bfloat16 [8, 1024, 4096], P(None, 'replica', 'shard'), may hold values from -1.796875 to 1.796875
- second_moment: bfloat16 [8, 1024, 4096], P(None, 'replica', 'shard'), may hold values from 0.049804688 to 2
- hidden: bfloat16 [4, 8, 384, 1024], P('replica', 'shard'), may hold values from -6 to 6
- owner_of_expert: int32 [8], replicated, may hold values from 0 to 7, each once
- slab_order: int32 [4], replicated, may hold values from 0 to 3, each once
Outputs:
- new_master: float32 [8, 1024, 4096], P(None, 'replica', 'shard')
- new_first: bfloat16 [8, 1024, 4096], P(None, 'replica', 'shard')
- new_second: bfloat16 [8, 1024, 4096], P(None, 'replica', 'shard')
- expert_out: bfloat16 [4, 8, 384, 4096], P('replica', 'shard')
Inputs may be any that keep to these rules, and one draw needn't show every extreme that they name: `owner_of_expert`: a permutation: every owner holds exactly one expert. A permutation: row slab j of the learner's arrays holds hidden units from slab_order[j] * 256 on.
All inputs are finite; a program needn't handle non-finite values.
Results may differ from a plain program's by a relative error of at most 0.0049.
Values may be sent and summed in bfloat16 or wider, within the bound.
No kernel may reach another device: no remote copies, remote signals or barrier semaphores. Data moves between devices by JAX's collectives and lax.ppermute only.
A program may use at most 128 MiB of HBM per device.

v0:
```python
import jax
import jax.numpy as jnp
from jax import lax
from jax.sharding import PartitionSpec as P

D = 4096
QB = 128


beta_one = 0.9
beta_two = 0.95
learn_rate = 0.004
adam_epsilon = 1e-08
step_count = 10.0
quant_limit = 448.0
scale_epsilon = 1e-06


def adam_step(master_weight, gradient, first_moment, second_moment):
    float_gradient = gradient.astype(jnp.float32)
    moment_one = beta_one * first_moment.astype(jnp.float32) + (1.0 - beta_one) * float_gradient
    moment_two = (
        beta_two * second_moment.astype(jnp.float32)
        + (1.0 - beta_two) * float_gradient * float_gradient
    )
    first_fix = 1.0 - beta_one**step_count
    second_fix = 1.0 - beta_two**step_count
    update = moment_one / first_fix / (jnp.sqrt(moment_two / second_fix) + adam_epsilon)
    return (master_weight - learn_rate * update, moment_one, moment_two)


def quantize(weights):
    number, height, breadth = weights.shape
    blocks = weights.reshape(number, height // QB, QB, breadth // QB, QB)
    largest = jnp.max(jnp.abs(blocks), axis=(2, 4))
    block_scale = ((largest + scale_epsilon) / quant_limit).astype(jnp.bfloat16)
    block_scale = lax.optimization_barrier(block_scale)
    divided = blocks / block_scale.astype(jnp.float32)[:, :, None, :, None]
    return (divided.astype(jnp.bfloat16).reshape(number, height, breadth), block_scale)


def scaled_product(summed, left_part, quant_rows, scale_rows):
    token_count = left_part.shape[0]
    breadth = quant_rows.shape[1]
    for row_block in range(scale_rows.shape[0]):
        partial_value = jnp.dot(
            left_part[:, row_block * QB : (row_block + 1) * QB],
            quant_rows[row_block * QB : (row_block + 1) * QB],
            preferred_element_type=jnp.float32,
        )
        factor = scale_rows[row_block].astype(jnp.float32)
        summed = summed + (
            partial_value.reshape(token_count, breadth // QB, QB) * factor[None, :, None]
        ).reshape(token_count, breadth)
    return summed


def body(master_weight, gradient, first_moment, second_moment, hidden, owner_of_expert, slab_order):
    updated, moment_one, moment_two = adam_step(
        master_weight, gradient, first_moment, second_moment
    )
    quantized, block_scale = quantize(updated)
    experts = quantized.shape[0]
    slab_rows = quantized.shape[1]
    places = jnp.arange(experts, dtype=jnp.int32)
    held_expert = jnp.sum(
        jnp.where(owner_of_expert[None, :] == places[:, None], places[None, :], 0), axis=1
    )
    outgoing = jnp.take(quantized, held_expert, axis=0)
    outgoing_scale = jnp.take(block_scale, held_expert, axis=0)
    tokens = hidden.shape[2]
    token_rows = hidden.reshape(tokens, hidden.shape[3])
    replica_count = slab_order.shape[0]
    position = jnp.arange(replica_count, dtype=jnp.int32)
    zero_sum = jnp.zeros((tokens, D), jnp.float32)
    own_quant, own_scale = (
        lax.all_to_all(outgoing, "shard", split_axis=0, concat_axis=2, tiled=True),
        lax.all_to_all(outgoing_scale, "shard", split_axis=0, concat_axis=2, tiled=True),
    )
    quant_piece = lax.all_gather(own_quant, "replica", axis=0, tiled=True)
    scale_piece = lax.all_gather(own_scale, "replica", axis=0, tiled=True)

    def one_slab(offset, current):
        chosen = jnp.sum(jnp.where(position == offset, slab_order, 0))
        left_part = lax.dynamic_slice_in_dim(token_rows, chosen * slab_rows, slab_rows, 1)
        slab_quant = lax.dynamic_index_in_dim(quant_piece, offset, 0, keepdims=False)
        slab_scale = lax.dynamic_index_in_dim(scale_piece, offset, 0, keepdims=False)
        return scaled_product(current, left_part, slab_quant, slab_scale)

    summed = lax.fori_loop(0, quant_piece.shape[0], one_slab, zero_sum)
    expert_out = summed.astype(jnp.bfloat16).reshape(1, 1, tokens, D)
    return (updated, moment_one.astype(jnp.bfloat16), moment_two.astype(jnp.bfloat16), expert_out)


def solution(mesh):
    placed = (
        P(None, "replica", "shard"),
        P(None, "replica", "shard"),
        P(None, "replica", "shard"),
        P(None, "replica", "shard"),
        P("replica", "shard", None, None),
        P(),
        P(),
    )
    return jax.shard_map(
        body,
        mesh=mesh,
        in_specs=placed,
        out_specs=(
            P(None, "replica", "shard"),
            P(None, "replica", "shard"),
            P(None, "replica", "shard"),
            P("replica", "shard", None, None),
        ),
        check_vma=False,
    )
```

profile of v0, /device:TPU:8, one launch (start us, length us, event | category | flops | bytes accessed | tf_op | source)
XLA Modules:
  0.0 282.8 jit_solution(10636099461656864485)
XLA Ops:
  8.0 10.6 %fusion.10 = (f32[8,256,512]{2,1,0:T(8,128)}, f32[8,256,512]{2,1,0:T(8,128)}, bf16[8,256,512]{2,1,0:T(8,128)(2,1)}, bf16[8,256,512]{2,1,0:T(8,128)(2,1)}) fusion(f32[8,256,512]{2,1,0:T(8,128)} %param.9, bf16[8,256,512]{2,1,0:T(8,128)(2,1)} %param.12, bf16[8,256,512]{2,1,0:T(8,128)(2,1)} %param.10, bf16[8,256,512]{2,1,0:T(8,128)(2,1)} %param.11), kind=kLoop, calls=%fused_computation.37 | loop fusion | flops 19922944 | bytes 23068672 | tf_op jit(solution)/shard_map/abs | solution.py:35
  18.6 5.2 %abs.7 = f32[8,2,128,4,128]{4,3,2,1,0:T(4,128)} reshape(f32[8,256,512]{2,1,0:T(8,128)} %get-tuple-element.176) | data formatting | bytes 8388608 | tf_op jit(solution)/shard_map/abs | solution.py:35
  23.9 2.9 %reduce_max.9 = f32[8,2,4]{2,1,0:T(2,128)S(1)} reduce(f32[8,2,128,4,128]{4,3,2,1,0:T(4,128)} %abs.7, f32[]{:T(128)} %constant.93.clone.1), dimensions={2,4}, to_apply=%region_1.2 | reduce | flops 1048512 | bytes 4194564 | tf_op jit(solution)/shard_map/reduce_max | solution.py:35
  26.8 2.5 div.39
  29.3 5.5 %div.40 = f32[8,256,512]{2,1,0:T(8,128)} reshape(f32[8,2,128,4,128]{4,3,2,1,0:T(4,128)} %div.39) | data formatting | bytes 8388608 | tf_op jit(solution)/shard_map/div | solution.py:38
  34.8 4.3 %divide_convert_fusion = bf16[8,256,512]{2,1,0:T(8,128)(2,1)S(1)} fusion(f32[8,256,512]{2,1,0:T(8,128)} %get-tuple-element.177, f32[8,256,512]{2,1,0:T(8,128)} %div.40), kind=kLoop, calls=%fused_computation.22 | loop fusion | flops 2097152 | bytes 10485760 | tf_op jit(solution)/shard_map/convert_element_type | solution.py:39
  43.0 51.8 %all_to_all.36 = bf16[8,256,512]{2,1,0:T(8,128)(2,1)S(1)} all-to-all(bf16[8,256,512]{2,1,0:T(8,128)(2,1)S(1)} %broadcast_select_fusion), channel_id=1, replica_groups=mesh['replica'=4,'shard'=8] {'shard'}, dimensions={0} | all-to-all | bytes 4194304 | tf_op jit(solution)/shard_map/all_to_all | solution.py:77
  94.8 2.4 copy.26
  97.1 4.1 %copy.27 = bf16[1,256,4096]{2,1,0:T(8,128)(2,1)} copy(bf16[1,256,4096]{1,2,0:T(8,128)(2,1)} %bitcast.68) | data formatting | bytes 4194304 | tf_op jit(solution)/shard_map/all_to_all | solution.py:77
  102.5 5.6 %all-to-all-start.1 = ((bf16[8,2,4]{2,1,0:T(2,128)(2,1)}), bf16[8,2,4]{2,1,0:T(2,128)(2,1)S(1)}, u32[]{:S(2)}, u32[]{:S(2)}) async-start(bf16[8,2,4]{2,1,0:T(2,128)(2,1)} %broadcast_select_fusion.1), calls=%async_computation.1 | async-start | bytes 8192 | tf_op jit(solution)/shard_map/all_to_all | solution.py:78
  108.1 4.1 %all-to-all-done.1 = bf16[8,2,4]{2,1,0:T(2,128)(2,1)S(1)} async-done(((bf16[8,2,4]{2,1,0:T(2,128)(2,1)}), bf16[8,2,4]{2,1,0:T(2,128)(2,1)S(1)}, u32[]{:S(2)}, u32[]{:S(2)}) %all-to-all-start.1) | async-done | bytes 160 | tf_op jit(solution)/shard_map/all_to_all | solution.py:78
  112.5 7.9 %all_gather.7 = bf16[4,2,32]{2,1,0:T(2,128)(2,1)S(1)} all-gather(bf16[1,2,32]{2,1,0:T(2,128)(2,1)S(1)} %all_to_all.33), channel_id=1, replica_groups=mesh['replica'=4,'shard'=8] {'replica'}, dimensions={0}, use_global_device_ids=true | all-gather | bytes 640 | tf_op jit(solution)/shard_map/all_gather | solution.py:81
  120.4 69.4 %all-gather.2.cloned.1.call-done = bf16[4,256,4096]{2,1,0:T(8,128)(2,1)} async-done(((bf16[1,256,4096]{2,1,0:T(8,128)(2,1)}), bf16[4,256,4096]{2,1,0:T(8,128)(2,1)}) %all-gather.2.cloned.1.call-update) | async-done | bytes 8388624 | tf_op jit(solution)/shard_map/all_gather | solution.py:80
  189.8 80.8 %while.14 = (s32[]{:T(128)}, f32[384,4096]{0,1:T(8,128)}, s32[4]{0:T(128)S(1)}, bf16[384,1024]{1,0:T(8,128)(2,1)}, bf16[4,256,4096]{2,1,0:T(8,128)(2,1)}, /*inde...) while((s32[]{:T(128)}, f32[384,4096]{0,1:T(8,128)}, ...), condition=%wide.region_4.5_spmd.clone, body=%wide.region_2.4_spmd.clone.sunk | while | flops 813170816 | bytes 52626572 | solution.py:90
  195.4 2.4 broadcast_multiply_fusion.5
  197.8 4.4 %broadcast_multiply_fusion.4 = f32[384,32,128]{0,2,1:T(8,128)} fusion(f32[32]{0:T(128)S(1)} %get-tuple-element.225, bf16[32,128,128]{2,1,0:T(8,128)(2,1)S(1)} %bitcast.65, bf16[384,1024]{1,0:T(8,128)(2,1)} %get-tuple-element.254, s32[]{:T(128)S(6)} %add.133), kind=kOutput, calls=%fused_computation.5.clone.1 | convolution fusion | flops 404226048 | bytes 7438468 | tf_op jit(solution)/shard_map/while/body/eval_jaxpr/dot_general | solution.py:46
  202.3 6.3 %bitcast_add_fusion.3 = f32[384,4096]{0,1:T(8,128)} fusion(f32[384,32,128]{0,2,1:T(8,128)} %broadcast_multiply_fusion.4, f32[384,32,128]{0,2,1:T(8,128)S(1)} %broadcast_multiply_fusion.5, f32[384,4096]{0,1:T(8,128)} %get-tuple-element.241, pred[]{:T(512)S(6)} %compare.3), kind=kLoop, calls=%fused_computation.3.clone.1 | loop fusion | flops 4718592 | bytes 25165824 | tf_op jit(solution)/shard_map/while/body/eval_jaxpr/add | solution.py:52
  216.6 4.5 %broadcast_multiply_fusion.4 = f32[384,32,128]{0,2,1:T(8,128)} fusion(f32[32]{0:T(128)S(1)} %get-tuple-element.225, bf16[32,128,128]{2,1,0:T(8,128)(2,1)S(1)} %bitcast.65, bf16[384,1024]{1,0:T(8,128)(2,1)} %get-tuple-element.254, s32[]{:T(128)S(6)} %add.133), kind=kOutput, calls=%fused_computation.5.clone.1 | convolution fusion | flops 404226048 | bytes 7438468 | tf_op jit(solution)/shard_map/while/body/eval_jaxpr/dot_general | solution.py:46
  221.0 8.2 %bitcast_add_fusion.3 = f32[384,4096]{0,1:T(8,128)} fusion(f32[384,32,128]{0,2,1:T(8,128)} %broadcast_multiply_fusion.4, f32[384,32,128]{0,2,1:T(8,128)S(1)} %broadcast_multiply_fusion.5, f32[384,4096]{0,1:T(8,128)} %get-tuple-element.241, pred[]{:T(512)S(6)} %compare.3), kind=kLoop, calls=%fused_computation.3.clone.1 | loop fusion | flops 4718592 | bytes 25165824 | tf_op jit(solution)/shard_map/while/body/eval_jaxpr/add | solution.py:52
  237.2 4.4 %broadcast_multiply_fusion.4 = f32[384,32,128]{0,2,1:T(8,128)} fusion(f32[32]{0:T(128)S(1)} %get-tuple-element.225, bf16[32,128,128]{2,1,0:T(8,128)(2,1)S(1)} %bitcast.65, bf16[384,1024]{1,0:T(8,128)(2,1)} %get-tuple-element.254, s32[]{:T(128)S(6)} %add.133), kind=kOutput, calls=%fused_computation.5.clone.1 | convolution fusion | flops 404226048 | bytes 7438468 | tf_op jit(solution)/shard_map/while/body/eval_jaxpr/dot_general | solution.py:46
  241.7 8.2 %bitcast_add_fusion.3 = f32[384,4096]{0,1:T(8,128)} fusion(f32[384,32,128]{0,2,1:T(8,128)} %broadcast_multiply_fusion.4, f32[384,32,128]{0,2,1:T(8,128)S(1)} %broadcast_multiply_fusion.5, f32[384,4096]{0,1:T(8,128)} %get-tuple-element.241, pred[]{:T(512)S(6)} %compare.3), kind=kLoop, calls=%fused_computation.3.clone.1 | loop fusion | flops 4718592 | bytes 25165824 | tf_op jit(solution)/shard_map/while/body/eval_jaxpr/add | solution.py:52
  257.9 4.4 %broadcast_multiply_fusion.4 = f32[384,32,128]{0,2,1:T(8,128)} fusion(f32[32]{0:T(128)S(1)} %get-tuple-element.225, bf16[32,128,128]{2,1,0:T(8,128)(2,1)S(1)} %bitcast.65, bf16[384,1024]{1,0:T(8,128)(2,1)} %get-tuple-element.254, s32[]{:T(128)S(6)} %add.133), kind=kOutput, calls=%fused_computation.5.clone.1 | convolution fusion | flops 404226048 | bytes 7438468 | tf_op jit(solution)/shard_map/while/body/eval_jaxpr/dot_general | solution.py:46
  262.4 8.2 %bitcast_add_fusion.3 = f32[384,4096]{0,1:T(8,128)} fusion(f32[384,32,128]{0,2,1:T(8,128)} %broadcast_multiply_fusion.4, f32[384,32,128]{0,2,1:T(8,128)S(1)} %broadcast_multiply_fusion.5, f32[384,4096]{0,1:T(8,128)} %get-tuple-element.241, pred[]{:T(512)S(6)} %compare.3), kind=kLoop, calls=%fused_computation.3.clone.1 | loop fusion | flops 4718592 | bytes 25165824 | tf_op jit(solution)/shard_map/while/body/eval_jaxpr/add | solution.py:52
  270.6 5.4 %copy.31 = bf16[384,4096]{1,0:T(8,128)(2,1)} copy(f32[384,4096]{0,1:T(8,128)} %get-tuple-element.128) | data formatting | bytes 9437184 | tf_op jit(solution)/shard_map/while | solution.py:90
  (52 shorter events, 33.2 us)
Async XLA Ops:
  7.2 182.6 %all-gather.2.cloned.1.call-start = ((), (), s32[]{:S(2)}) async-start(), calls=%async_computation.2 | async-start | bytes 10485760 | tf_op jit(solution)/shard_map/all_gather | solution.py:80
  97.1 92.7 %copy-start.1 = (s32[4]{0:T(128)S(1)}, s32[4]{0:T(128)}, u32[]{:S(2)}) copy-start(s32[4]{0:T(128)} %param.15) | copy-start | bytes 52
  102.5 9.7 %all-to-all-start.1 = ((bf16[8,2,4]{2,1,0:T(2,128)(2,1)}), bf16[8,2,4]{2,1,0:T(2,128)(2,1)S(1)}, u32[]{:S(2)}, u32[]{:S(2)}) async-start(bf16[8,2,4]{2,1,0:T(2,128)(2,1)} %broadcast_select_fusion.1), calls=%async_computation.1 | async-start | bytes 8192 | tf_op jit(solution)/shard_map/all_to_all | solution.py:78
  195.4 2.4 copy-start
  214.2 2.4 copy-start
  234.9 2.3 copy-start
  255.5 2.4 copy-start
Sparse Core Ops, SparseCore 0:
  101.4 88.3 all-gather.1
where the time goes:
time: 285 us; the launch traced here: 283 us
  waiting for transfers between devices  73.5 us (26%)
  blocking collectives  59.7 us (21%)
  other arithmetic  54.6 us (19%)
  local copies, waits for them, and re-layouts  45.3 us (16%)
  matrix products  27.2 us (10%)
  between operations  14.1 us (5%)
  starting transfers between devices  5.65 us (2%)
    all_gather x1, waiting for transfers between devices, body(): quant_piece = lax.all_gather(own_quant, 'replica', axis=0, tiled=True)  69.4 us
    all_to_all x1, blocking collectives, body(): lax.all_to_all(outgoing, 'shard', split_axis=0, concat_axis=2, tiled=True)  51.8 us
    add x4, other arithmetic, scaled_product(): summed + (partial_value.reshape(token_count, breadth // QB, QB) * factor[...  30.9 us
    dot_general x8, matrix products, scaled_product(): jnp.dot(left_part[:, row_block * QB:(row_block + 1) * QB], quant_rows[row...  27.2 us
    abs x1, other arithmetic, quantize(): largest = jnp.max(jnp.abs(blocks), axis=(2, 4))  10.6 us
    while x16, local copies, waits for them, and re-layouts  10.6 us
    div x2, local copies, waits for them, and re-layouts, quantize(): divided = blocks / block_scale.astype(jnp.float32)[:, :, None, :, None]  8.01 us
    all_gather x1, blocking collectives, body(): scale_piece = lax.all_gather(own_scale, 'replica', axis=0, tiled=True)  7.93 us
  transfers between devices with their start and end apart: 2, of which 2 were waited for; matrix products, arithmetic and copies ran while one was open for 1% of the time, Pallas kernels for 0%

commit v1 on v0

v1 whole, which is shorter than its diff:
```python
import functools

import jax
import jax.numpy as jnp
from jax import lax
from jax.experimental import pallas as pl
from jax.experimental.pallas import tpu as pltpu
from jax.sharding import PartitionSpec as P

QB = 128

beta_one = 0.9
beta_two = 0.95
learn_rate = 0.004
adam_epsilon = 1e-08
step_count = 10.0
quant_limit = 448.0
scale_epsilon = 1e-06
first_fix = 1.0 - beta_one**step_count
second_fix = 1.0 - beta_two**step_count


def adam_kernel(experts, owner, master, gradient, first, second, *refs):
    new_master, new_first, new_second, send = refs[-4:]

    def one_expert(expert, carry):
        grad = gradient[expert].astype(jnp.float32)
        moment_one = beta_one * first[expert].astype(jnp.float32) + (1.0 - beta_one) * grad
        moment_two = beta_two * second[expert].astype(jnp.float32) + (1.0 - beta_two) * grad * grad
        scaled = moment_two * (1.0 / second_fix)
        root = scaled * lax.rsqrt(scaled)
        updated = master[expert] - (learn_rate / first_fix) * moment_one / (root + adam_epsilon)
        new_master[expert] = updated
        new_first[expert] = moment_one.astype(jnp.bfloat16)
        new_second[expert] = moment_two.astype(jnp.bfloat16)
        largest = jnp.max(jnp.abs(updated), axis=(0, 1), keepdims=True)
        scale = ((largest + scale_epsilon) * (1.0 / quant_limit)).astype(jnp.bfloat16)
        scale = jnp.broadcast_to(scale.astype(jnp.float32), (1, QB))
        quantized = (updated * (1.0 / scale)).astype(jnp.bfloat16)
        send[owner[expert]] = (quantized.astype(jnp.float32) * scale).astype(jnp.bfloat16)
        return carry

    lax.fori_loop(0, experts, one_expert, 0)


def adam_chunk(chunk, owner, arrays, carried):
    experts, rows, columns = arrays[0].shape
    block = (experts, QB, QB)
    here = pl.BlockSpec(block, lambda i, owner: (0, i, chunk))
    sent = pl.BlockSpec(block, lambda i, owner: (0, i, 0))
    whole = pl.BlockSpec(memory_space=pl.ANY)
    shapes = [
        jax.ShapeDtypeStruct(arrays[0].shape, jnp.float32),
        jax.ShapeDtypeStruct(arrays[0].shape, jnp.bfloat16),
        jax.ShapeDtypeStruct(arrays[0].shape, jnp.bfloat16),
        jax.ShapeDtypeStruct((experts, rows, QB), jnp.bfloat16),
    ]
    count = experts * rows * QB
    return pl.pallas_call(
        functools.partial(adam_kernel, experts),
        grid_spec=pltpu.PrefetchScalarGridSpec(
            num_scalar_prefetch=1,
            grid=(rows // QB,),
            in_specs=[here] * 4 + [whole] * len(carried),
            out_specs=[here] * 3 + [sent],
        ),
        out_shape=shapes,
        input_output_aliases={5 + i: i for i in range(len(carried))},
        compiler_params=pltpu.CompilerParams(vmem_limit_bytes=48 * 1024 * 1024),
        cost_estimate=pl.CostEstimate(flops=30 * count, bytes_accessed=20 * count, transcendentals=2 * count),
        name="adam_quantize",
    )(owner, *arrays, *carried)


def product_kernel(order, left, right, *refs):
    out = refs[-1]
    slabs, _, slab_rows, breadth = right.shape
    total = jnp.zeros(out.shape, jnp.float32)
    for slab in range(slabs):
        place = pl.multiple_of(order[slab] * slab_rows, QB)
        total += jnp.dot(
            left[:, pl.ds(place, slab_rows)], right[slab, 0], preferred_element_type=jnp.float32
        )
    out[...] = total.astype(out.dtype)


def product_chunk(chunk, chunks, order, token_rows, gathered, carried):
    slabs, sources, slab_rows, _ = gathered.shape
    tokens, units = token_rows.shape
    shape = (tokens, sources * chunks * QB)
    return pl.pallas_call(
        product_kernel,
        grid_spec=pltpu.PrefetchScalarGridSpec(
            num_scalar_prefetch=1,
            grid=(sources,),
            in_specs=[
                pl.BlockSpec((tokens, units), lambda s, order: (0, 0)),
                pl.BlockSpec((slabs, 1, slab_rows, QB), lambda s, order: (0, s, 0, 0)),
            ]
            + [pl.BlockSpec(memory_space=pl.ANY)] * len(carried),
            out_specs=pl.BlockSpec((tokens, QB), lambda s, order: (0, s * chunks + chunk)),
        ),
        out_shape=jax.ShapeDtypeStruct(shape, jnp.bfloat16),
        input_output_aliases={3: 0} if carried else {},
        compiler_params=pltpu.CompilerParams(vmem_limit_bytes=48 * 1024 * 1024),
        cost_estimate=pl.CostEstimate(
            flops=2 * tokens * units * sources * QB,
            bytes_accessed=2 * (units * sources * QB + tokens * units + tokens * sources * QB),
            transcendentals=0,
        ),
        name="expert_product",
    )(order, token_rows, gathered, *carried)


def body(master_weight, gradient, first_moment, second_moment, hidden, owner_of_expert, slab_order):
    arrays = (master_weight, gradient, first_moment, second_moment)
    chunks = master_weight.shape[2] // QB
    token_rows = hidden.reshape(hidden.shape[2:])
    carried = ()
    sends = []
    for chunk in range(chunks):
        *carried, send = adam_chunk(chunk, owner_of_expert, arrays, tuple(carried))
        sends.append(send)
    out = ()
    for chunk in range(chunks):
        received = lax.all_to_all(sends[chunk], "shard", split_axis=0, concat_axis=0, tiled=True)
        gathered = lax.all_gather(received, "replica", axis=0)
        out = (product_chunk(chunk, chunks, slab_order, token_rows, gathered, out),)
    return (*carried, out[0].reshape(hidden.shape[:2] + out[0].shape))


def solution(mesh):
    weights = P(None, "replica", "shard")
    tokens = P("replica", "shard", None, None)
    return jax.shard_map(
        body,
        mesh=mesh,
        in_specs=(weights, weights, weights, weights, tokens, P(), P()),
        out_specs=(weights, weights, weights, tokens),
        check_vma=False,
    )
```

time: 285 us -> 198 us (0.69)
  other arithmetic: 54.6 us -> 0 us
  Pallas kernels: 0 us -> 43.7 us
  local copies, waits for them, and re-layouts: 45.3 us -> 15 us
  matrix products: 27.2 us -> 0 us
  waiting for transfers between devices: 73.5 us -> 49.8 us
  blocking collectives: 59.7 us -> 73.6 us
  starting transfers between devices: 5.65 us -> 0.16 us
    pallas_call x0 -> x8, Pallas kernels: none -> 43.7 us  [the longest x4 23.2 us: adam_chunk(): pl.pallas_call(functools.partial(adam_kernel, experts), grid_spec=pltpu.P...]
    add x4 -> x0, other arithmetic: 30.9 us -> none  [scaled_product(): summed + (partial_value.reshape(token_count, breadth // QB, QB) * factor[...]
    dot_general x8 -> x0, matrix products: 27.2 us -> none  [scaled_product(): jnp.dot(left_part[:, row_block * QB:(row_block + 1) * QB], quant_rows[row...]
    all_to_all x1 -> x4, blocking collectives: 51.8 us -> 73.6 us  [body(): lax.all_to_all(sends[chunk], 'shard', split_axis=0, concat_axis=0, tiled=...]
    all_gather x1 -> x4, waiting for transfers between devices: 69.4 us -> 49.8 us  [body(): gathered = lax.all_gather(received, 'replica', axis=0)]
    while x17 -> x0, local copies, waits for them, and re-layouts: 15.9 us -> none
    unnamed x2 -> x28, local copies, waits for them, and re-layouts: 0.01 us -> 15 us
    abs x1 -> x0, other arithmetic: 10.6 us -> none  [quantize(): largest = jnp.max(jnp.abs(blocks), axis=(2, 4))]
  transfers between devices with their start and end apart: 2 -> 4, of which waited for: 2 -> 2; matrix products, arithmetic and copies ran while one was open for 1% -> 0% of each run, Pallas kernels for 0% -> 17%
where the time goes in v1:
time: 198 us; the launch traced here: 196 us
  blocking collectives  73.6 us (37%)
  waiting for transfers between devices  49.8 us (25%)
  Pallas kernels  43.7 us (22%)
  local copies, waits for them, and re-layouts  15 us (8%)
  between operations  13.9 us (7%)
    all_to_all x4, blocking collectives, body(): lax.all_to_all(sends[chunk], 'shard', split_axis=0, concat_axis=0, tiled=...  73.6 us
    all_gather x4, waiting for transfers between devices, body(): gathered = lax.all_gather(received, 'replica', axis=0)  49.8 us
    pallas_call x4, Pallas kernels, adam_chunk(): pl.pallas_call(functools.partial(adam_kernel, experts), grid_spec=pltpu.P...  23.2 us
    pallas_call x4, Pallas kernels, product_chunk(): pl.pallas_call(product_kernel, grid_spec=pltpu.PrefetchScalarGridSpec(num...  20.4 us
    unnamed x28, local copies, waits for them, and re-layouts  15 us
  transfers between devices with their start and end apart: 4, of which 2 were waited for; matrix products, arithmetic and copies ran while one was open for 0% of the time, Pallas kernels for 17%

profile of v1, /device:TPU:8, one launch (start us, length us, event | category | flops | bytes accessed | tf_op | source)
XLA Modules:
  0.0 196.1 jit_solution(13647825750175596507)
XLA Ops:
  7.2 1.6 copy-done
  8.8 1.6 copy-done.2
  10.4 0.7 copy-done.12
  11.1 5.9 %adam_quantize.4 = (f32[8,256,512]{2,1,0:T(8,128)}, bf16[8,256,512]{2,1,0:T(8,128)(2,1)}, bf16[8,256,512]{2,1,0:T(8,128)(2,1)}, bf16[8,256,128]{2,1,0:T(8,128)(2,1)S(1)}) custom-call(s32[8]{0:T(128)S(1)} %copy-done.12, f32[8,256,512]{2,1,0:T(8,128)} %master.7, bf16[8,256,512]{2,1,0:T(8,128)(2,1)S(1)} %copy-done, bf16[8,256,512]{2,1,0:T(8,128)(2,1)S(1)} %copy-done.2, ...), custom_call_target="tpu_custom_call" | custom-call | flops 7864320 | bytes 5242880 | tf_op jit(solution)/shard_map/adam_quantize/pallas_call | solution.py:59
  16.9 18.2 %all_to_all.20 = bf16[8,256,128]{2,1,0:T(8,128)(2,1)} all-to-all(bf16[8,256,128]{2,1,0:T(8,128)(2,1)S(1)} %get-tuple-element.35), channel_id=1, replica_groups=mesh['replica'=4,'shard'=8] {'shard'}, dimensions={0} | all-to-all | bytes 1048576 | tf_op jit(solution)/shard_map/all_to_all | solution.py:126
  35.2 1.6 copy-done.3
  36.8 5.8 %adam_quantize.5 = (f32[8,256,512]{2,1,0:T(8,128)}, bf16[8,256,512]{2,1,0:T(8,128)(2,1)}, bf16[8,256,512]{2,1,0:T(8,128)(2,1)}, bf16[8,256,128]{2,1,0:T(8,128)(2,1)S(1)}) custom-call(s32[8]{0:T(128)S(1)} %copy-done.13, f32[8,256,512]{2,1,0:T(8,128)} %master.7, ...), custom_call_target="tpu_custom_call", output_to_operand_aliasing={{0}: (5, {}), {1}: (6, {}), {2}: (7, {})} | custom-call | flops 7864320 | bytes 5242880 | tf_op jit(solution)/shard_map/adam_quantize/pallas_call | solution.py:59
  42.6 18.4 %all_to_all.21 = bf16[8,256,128]{2,1,0:T(8,128)(2,1)} all-to-all(bf16[8,256,128]{2,1,0:T(8,128)(2,1)S(1)} %get-tuple-element.34), channel_id=1, replica_groups=mesh['replica'=4,'shard'=8] {'shard'}, dimensions={0} | all-to-all | bytes 1048576 | tf_op jit(solution)/shard_map/all_to_all | solution.py:126
  61.1 1.6 copy-done.4
  62.7 5.8 %adam_quantize.6 = (f32[8,256,512]{2,1,0:T(8,128)}, bf16[8,256,512]{2,1,0:T(8,128)(2,1)}, bf16[8,256,512]{2,1,0:T(8,128)(2,1)}, bf16[8,256,128]{2,1,0:T(8,128)(2,1)S(1)}) custom-call(s32[8]{0:T(128)S(1)} %copy-done.13, f32[8,256,512]{2,1,0:T(8,128)} %master.7, ...), custom_call_target="tpu_custom_call", output_to_operand_aliasing={{0}: (5, {}), {1}: (6, {}), {2}: (7, {})} | custom-call | flops 7864320 | bytes 5242880 | tf_op jit(solution)/shard_map/adam_quantize/pallas_call | solution.py:59
  68.5 18.4 %all_to_all.22 = bf16[8,256,128]{2,1,0:T(8,128)(2,1)} all-to-all(bf16[8,256,128]{2,1,0:T(8,128)(2,1)S(1)} %get-tuple-element.33), channel_id=1, replica_groups=mesh['replica'=4,'shard'=8] {'shard'}, dimensions={0} | all-to-all | bytes 1048576 | tf_op jit(solution)/shard_map/all_to_all | solution.py:126
  87.0 1.6 copy-done.5
  88.6 5.8 %adam_quantize.7 = (f32[8,256,512]{2,1,0:T(8,128)}, bf16[8,256,512]{2,1,0:T(8,128)(2,1)}, bf16[8,256,512]{2,1,0:T(8,128)(2,1)}, bf16[8,256,128]{2,1,0:T(8,128)(2,1)S(1)}) custom-call(s32[8]{0:T(128)S(1)} %copy-done.13, f32[8,256,512]{2,1,0:T(8,128)} %master.7, ...), custom_call_target="tpu_custom_call", output_to_operand_aliasing={{0}: (5, {}), {1}: (6, {}), {2}: (7, {})} | custom-call | flops 7864320 | bytes 5242880 | tf_op jit(solution)/shard_map/adam_quantize/pallas_call | solution.py:59
  94.4 18.6 %all_to_all.23 = bf16[8,256,128]{2,1,0:T(8,128)(2,1)} all-to-all(bf16[8,256,128]{2,1,0:T(8,128)(2,1)S(1)} %get-tuple-element.32), channel_id=1, replica_groups=mesh['replica'=4,'shard'=8] {'shard'}, dimensions={0} | all-to-all | bytes 1048576 | tf_op jit(solution)/shard_map/all_to_all | solution.py:126
  113.0 1.6 copy-done.7
  114.6 5.1 %expert_product.4.refs_0_ = bf16[384,4096]{1,0:T(8,128)(2,1)} custom-call(s32[4]{0:T(128)S(1)} %copy-done.11, bf16[384,1024]{1,0:T(8,128)(2,1)S(1)} %bitcast.6, bf16[4,8,256,128]{3,2,1,0:T(8,128)(2,1)S(1)} %bitcast.10), custom_call_target="tpu_custom_call" | custom-call | flops 805306368 | bytes 3670016 | tf_op jit(solution)/shard_map/expert_product/pallas_call | solution.py:91
  119.7 1.6 copy-done.8
  121.3 5.1 %expert_product.5.refs_0_ = bf16[384,4096]{1,0:T(8,128)(2,1)} custom-call(s32[4]{0:T(128)S(1)} %copy-done.11, bf16[384,1024]{1,0:T(8,128)(2,1)S(1)} %bitcast.7, bf16[4,8,256,128]{3,2,1,0:T(8,128)(2,1)S(1)} %bitcast.11, bf16[384,4096]{1,0:T(8,128)(2,1)} %expert_product.4.refs_0_), custom_call_target="tpu_custom_call", output_to_operand_aliasing={{}: (3, {})} | custom-call | flops 805306368 | bytes 3670016 | tf_op jit(solution)/shard_map/expert_product/pallas_call | solution.py:91
  126.4 19.4 %all-gather.11.cloned.1.call-done = bf16[32,256,128]{2,1,0:T(8,128)(2,1)} async-done(((bf16[8,256,128]{2,1,0:T(8,128)(2,1)}), bf16[32,256,128]{2,1,0:T(8,128)(2,1)}) %all-gather.11.cloned.1.call-update) | async-done | bytes 2097168 | tf_op jit(solution)/shard_map/all_gather | solution.py:127
  145.8 1.6 copy-done.9
  147.4 5.1 %expert_product.6.refs_0_ = bf16[384,4096]{1,0:T(8,128)(2,1)} custom-call(s32[4]{0:T(128)S(1)} %copy-done.11, bf16[384,1024]{1,0:T(8,128)(2,1)S(1)} %bitcast.8, bf16[4,8,256,128]{3,2,1,0:T(8,128)(2,1)S(1)} %bitcast.12, bf16[384,4096]{1,0:T(8,128)(2,1)} %expert_product.5.refs_0_), custom_call_target="tpu_custom_call", output_to_operand_aliasing={{}: (3, {})} | custom-call | flops 805306368 | bytes 3670016 | tf_op jit(solution)/shard_map/expert_product/pallas_call | solution.py:91
  152.5 30.3 %all-gather.9.cloned.1.call-done = bf16[32,256,128]{2,1,0:T(8,128)(2,1)} async-done(((bf16[8,256,128]{2,1,0:T(8,128)(2,1)}), bf16[32,256,128]{2,1,0:T(8,128)(2,1)}) %all-gather.9.cloned.1.call-update) | async-done | bytes 2097168 | tf_op jit(solution)/shard_map/all_gather | solution.py:127
  182.8 1.6 copy-done.10
  184.4 5.1 %expert_product.7 = bf16[384,4096]{1,0:T(8,128)(2,1)} custom-call(s32[4]{0:T(128)S(1)} %copy-done.11, bf16[384,1024]{1,0:T(8,128)(2,1)S(1)} %bitcast.9, bf16[4,8,256,128]{3,2,1,0:T(8,128)(2,1)S(1)} %bitcast.13, bf16[384,4096]{1,0:T(8,128)(2,1)} %expert_product.6.refs_0_), custom_call_target="tpu_custom_call", output_to_operand_aliasing={{}: (3, {})} | custom-call | flops 805306368 | bytes 3670016 | tf_op jit(solution)/shard_map/expert_product/pallas_call | solution.py:91
  (28 shorter events, 0.3 us)
Async XLA Ops:
  7.2 105.8 %all-gather.15.cloned.1.call-start = ((), (), s32[]{:S(2)}) async-start(), calls=%async_computation.7 | async-start | bytes 2621440 | tf_op jit(solution)/shard_map/all_gather | solution.py:127
  7.2 1.6 copy-start
  8.8 1.6 copy-start.2
  10.4 0.7 copy-start.12
  11.1 24.1 %copy-start.1 = (bf16[8,256,512]{2,1,0:T(8,128)(2,1)S(1)}, bf16[8,256,512]{2,1,0:T(8,128)(2,1)}, u32[]{:S(2)}) copy-start(bf16[8,256,512]{2,1,0:T(8,128)(2,1)} %gradient.7) | copy-start | bytes 6291460
  11.1 24.1 %copy-start.13 = (s32[8]{0:T(128)S(1)}, s32[8]{0:T(128)}, u32[]{:S(2)}) copy-start(s32[8]{0:T(128)} %owner.7) | copy-start | bytes 100
  35.1 84.6 %all-gather.13.cloned.1.call-start = ((), (), s32[]{:S(2)}) async-start(), calls=%async_computation.6 | async-start | bytes 2621440 | tf_op jit(solution)/shard_map/all_gather | solution.py:127
  35.2 1.6 copy-start.3
  61.0 84.8 %all-gather.11.cloned.1.call-start = ((), (), s32[]{:S(2)}) async-start(), calls=%async_computation.5 | async-start | bytes 2621440 | tf_op jit(solution)/shard_map/all_gather | solution.py:127
  61.1 1.6 copy-start.4
  86.9 95.9 %all-gather.9.cloned.1.call-start = ((), (), s32[]{:S(2)}) async-start(), calls=%async_computation.4 | async-start | bytes 2621440 | tf_op jit(solution)/shard_map/all_gather | solution.py:127
  87.0 1.6 copy-start.5
  88.6 24.4 %copy-start.11 = (s32[4]{0:T(128)S(1)}, s32[4]{0:T(128)}, u32[]{:S(2)}) copy-start(s32[4]{0:T(128)} %order.7) | copy-start | bytes 52
  94.4 18.6 %copy-start.6 = (bf16[1,1,384,1024]{3,2,1,0:T(8,128)(2,1)S(1)}, bf16[1,1,384,1024]{3,2,1,0:T(8,128)(2,1)}, u32[]{:S(2)}) copy-start(bf16[1,1,384,1024]{3,2,1,0:T(8,128)(2,1)} %param.11) | copy-start | bytes 2359300
  113.0 1.6 copy-start.7
  119.7 1.6 copy-start.8
  145.8 1.6 copy-start.9
  182.8 1.6 copy-start.10
Sparse Core Ops, SparseCore 0:
  35.2 36.0 all-gather.14
  73.2 35.3 all-gather.12
  110.4 35.3 all-gather.10
  147.5 35.2 all-gather.8

commit v2 on v1

v2 whole, which is shorter than its diff:
```python
import functools

import jax
import jax.numpy as jnp
from jax import lax
from jax.experimental import pallas as pl
from jax.experimental.pallas import tpu as pltpu
from jax.sharding import PartitionSpec as P

QB = 128
VMEM_LIMIT = 48 * 1024 * 1024

beta_one = 0.9
beta_two = 0.95
learn_rate = 0.004
adam_epsilon = 1e-08
step_count = 10.0
quant_limit = 448.0
scale_epsilon = 1e-06
first_fix = 1.0 - beta_one**step_count
second_fix = 1.0 - beta_two**step_count


def adam_kernel(blocks, expert_of, master, gradient, first, second, *refs):
    new_master, new_first, new_second = refs[-3 - blocks : -blocks]
    sends = refs[-blocks:]
    rows, columns = sends[0].shape
    pieces = [
        (slice(i, i + QB), slice(j, j + QB)) for i in range(0, rows, QB) for j in range(0, columns, QB)
    ]
    scaled_out = []
    for piece in pieces:
        at = (0, *piece)
        grad = gradient[at].astype(jnp.float32)
        moment_one = beta_one * first[at].astype(jnp.float32) + (1.0 - beta_one) * grad
        moment_two = beta_two * second[at].astype(jnp.float32) + (1.0 - beta_two) * grad * grad
        new_first[at] = moment_one.astype(jnp.bfloat16)
        new_second[at] = moment_two.astype(jnp.bfloat16)
        scaled = moment_two * (1.0 / second_fix)
        root = scaled * lax.rsqrt(scaled)
        updated = master[at] - (learn_rate / first_fix) * moment_one / (root + adam_epsilon)
        new_master[at] = updated
        largest = jnp.max(jnp.abs(updated), axis=(0, 1), keepdims=True)
        scale = ((largest + scale_epsilon) * (1.0 / quant_limit)).astype(jnp.bfloat16)
        scale = jnp.broadcast_to(scale.astype(jnp.float32), (1, QB))
        quantized = (updated * (1.0 / scale)).astype(jnp.bfloat16)
        scaled_out.append((piece, (quantized.astype(jnp.float32) * scale).astype(jnp.bfloat16)))
    for number in range(blocks):

        @pl.when(pl.program_id(0) == number)
        def _():
            for piece, value in scaled_out:
                sends[number][piece] = value


def adam_blocks(expert_of, arrays, carried):
    _, rows, columns = arrays[0].shape
    blocks = expert_of.shape[0]
    here = pl.BlockSpec((1, rows, columns), lambda i, expert_of: (expert_of[i], 0, 0))
    sent = pl.BlockSpec((rows, columns), lambda i, expert_of: (0, 0))
    whole = pl.BlockSpec(memory_space=pl.ANY)
    shapes = [
        jax.ShapeDtypeStruct(arrays[0].shape, jnp.float32),
        jax.ShapeDtypeStruct(arrays[0].shape, jnp.bfloat16),
        jax.ShapeDtypeStruct(arrays[0].shape, jnp.bfloat16),
    ] + [jax.ShapeDtypeStruct((rows, columns), jnp.bfloat16)] * blocks
    count = blocks * rows * columns
    results = pl.pallas_call(
        functools.partial(adam_kernel, blocks),
        grid_spec=pltpu.PrefetchScalarGridSpec(
            num_scalar_prefetch=1,
            grid=(blocks,),
            in_specs=[here] * 4 + [whole] * len(carried),
            out_specs=[here] * 3 + [sent] * blocks,
        ),
        out_shape=shapes,
        input_output_aliases={5 + i: i for i in range(len(carried))},
        compiler_params=pltpu.CompilerParams(vmem_limit_bytes=VMEM_LIMIT),
        cost_estimate=pl.CostEstimate(
            flops=30 * count, bytes_accessed=20 * count, transcendentals=2 * count
        ),
        name="adam_quantize",
    )(expert_of, *arrays, *carried)
    return results[:3], results[3:]


def product_kernel(slabs, place, left, *refs):
    out = refs[-1]
    total = jnp.zeros(out.shape, jnp.float32)
    for slab in range(slabs):
        right = refs[slab]
        rows = right.shape[0]
        start = pl.multiple_of(place[1 + slab] * rows, QB)
        total += jnp.dot(
            left[:, pl.ds(start, rows)], right[...], preferred_element_type=jnp.float32
        )
    out[...] = total.astype(out.dtype)


def product(place, token_rows, weights, breadth, carried):
    slabs = len(weights)
    tokens, units = token_rows.shape
    rows, columns = weights[0].shape
    return pl.pallas_call(
        functools.partial(product_kernel, slabs),
        grid_spec=pltpu.PrefetchScalarGridSpec(
            num_scalar_prefetch=1,
            grid=(1,),
            in_specs=[pl.BlockSpec((tokens, units), lambda i, place: (0, 0))]
            + [pl.BlockSpec((rows, columns), lambda i, place: (0, 0))] * slabs
            + [pl.BlockSpec(memory_space=pl.ANY)] * len(carried),
            out_specs=pl.BlockSpec((tokens, columns), lambda i, place: (0, place[0])),
        ),
        out_shape=jax.ShapeDtypeStruct((tokens, breadth), jnp.bfloat16),
        input_output_aliases={2 + slabs: 0} if carried else {},
        compiler_params=pltpu.CompilerParams(vmem_limit_bytes=VMEM_LIMIT),
        cost_estimate=pl.CostEstimate(
            flops=2 * tokens * units * columns,
            bytes_accessed=2 * (units * columns + tokens * units + tokens * columns),
            transcendentals=0,
        ),
        name="expert_product",
    )(place, token_rows, *weights, *carried)


def swap(value, axis, size, mask):
    if not mask:
        return value
    return lax.ppermute(value, axis, [(i, i ^ mask) for i in range(size)])


def body(shards, replicas, *arguments):
    *arrays, hidden, owner_of_expert, slab_order = arguments
    shard, replica = lax.axis_index("shard"), lax.axis_index("replica")
    token_rows = hidden.reshape(hidden.shape[2:])
    columns = arrays[0].shape[2]
    bits = [1 << i for i in range((replicas - 1).bit_length())]
    experts = jnp.arange(shards, dtype=jnp.int32)
    sources = shard.astype(jnp.int32) ^ experts
    expert_of = jnp.sum(
        jnp.where(owner_of_expert[None, :] == sources[:, None], experts[None, :], 0), axis=1
    ).astype(jnp.int32)
    members = replica.astype(jnp.int32) ^ jnp.arange(replicas, dtype=jnp.int32)
    slabs = jnp.sum(
        jnp.where(members[:, None] == jnp.arange(replicas)[None, :], slab_order[None, :], 0), axis=1
    ).astype(jnp.int32)
    carried = ()
    weights = []
    for pair in range(0, shards, 2):
        carried, sends = adam_blocks(expert_of[pair : pair + 2], arrays, tuple(carried))
        weights += [swap(send, "shard", shards, pair + i) for i, send in enumerate(sends)]
    out = ()
    for number, weight in enumerate(weights):
        held = {0: weight}
        for step in range(len(bits)):
            bit = bits[(step + number) % len(bits)]
            held.update({m ^ bit: swap(w, "replica", replicas, bit) for m, w in list(held.items())})
        place = jnp.concatenate([sources[number : number + 1], slabs])
        ordered = [held[m] for m in range(replicas)]
        out = (product(place, token_rows, ordered, columns * shards, out),)
    return (*carried, out[0].reshape(hidden.shape[:2] + out[0].shape))


def solution(mesh):
    weights = P(None, "replica", "shard")
    tokens = P("replica", "shard", None, None)
    return jax.shard_map(
        functools.partial(body, mesh.shape["shard"], mesh.shape["replica"]),
        mesh=mesh,
        in_specs=(weights, weights, weights, weights, tokens, P(), P()),
        out_specs=(weights, weights, weights, tokens),
        check_vma=False,
    )
```

time: 198 us -> 133 us (0.67)
  blocking collectives: 73.6 us -> 0 us
  starting transfers between devices: 0.16 us -> 24.6 us
  between operations: 13.9 us -> 0.73 us
  Pallas kernels: 43.7 us -> 33.6 us
  waiting for transfers between devices: 49.8 us -> 59.5 us
  local copies, waits for them, and re-layouts: 15 us -> 7.89 us
  other arithmetic: 0 us -> 5.95 us
    all_to_all x4 -> x0, blocking collectives: 73.6 us -> none  [body(): lax.all_to_all(sends[chunk], 'shard', split_axis=0, concat_axis=0, tiled=...]
    ppermute x0 -> x31, waiting for transfers between devices: none -> 59.5 us  [swap(): return lax.ppermute(value, axis, [(i, i ^ mask) for i in range(size)])]
    all_gather x4 -> x0, waiting for transfers between devices: 49.8 us -> none  [body(): gathered = lax.all_gather(received, 'replica', axis=0)]
    ppermute x0 -> x31, starting transfers between devices: none -> 24.6 us  [swap(): return lax.ppermute(value, axis, [(i, i ^ mask) for i in range(size)])]
    pallas_call x8 -> x12, Pallas kernels: 43.7 us -> 33.6 us  [the longest x8 17.9 us: product(): pl.pallas_call(functools.partial(product_kernel, slabs), grid_spec=pltpu....]
    unnamed x28 -> x40, local copies, waits for them, and re-layouts: 15 us -> 7.13 us
    concatenate x0 -> x2, other arithmetic: none -> 4.93 us  [body(): place = jnp.concatenate([sources[number:number + 1], slabs])]
  transfers between devices with their start and end apart: 4 -> 31, of which waited for: 2 -> 13; matrix products, arithmetic and copies ran while one was open for 0% -> 4% of each run, Pallas kernels for 17% -> 21%
where the time goes in v2:
time: 133 us; the launch traced here: 132 us
  waiting for transfers between devices  59.5 us (45%)
  Pallas kernels  33.6 us (25%)
  starting transfers between devices  24.6 us (18%)
  local copies, waits for them, and re-layouts  7.89 us (6%)
  other arithmetic  5.95 us (4%)
    ppermute x31, waiting for transfers between devices, swap(): return lax.ppermute(value, axis, [(i, i ^ mask) for i in range(size)])  59.5 us
    ppermute x31, starting transfers between devices, swap(): return lax.ppermute(value, axis, [(i, i ^ mask) for i in range(size)])  24.6 us
    pallas_call x8, Pallas kernels, product(): pl.pallas_call(functools.partial(product_kernel, slabs), grid_spec=pltpu....  17.9 us
    pallas_call x4, Pallas kernels, adam_blocks(): pl.pallas_call(functools.partial(adam_kernel, blocks), grid_spec=pltpu.Pr...  15.7 us
    unnamed x40, local copies, waits for them, and re-layouts  7.13 us
    concatenate x2, other arithmetic, body(): place = jnp.concatenate([sources[number:number + 1], slabs])  4.93 us
  transfers between devices with their start and end apart: 31, of which 13 were waited for; matrix products, arithmetic and copies ran while one was open for 4% of the time, Pallas kernels for 21%

profile of v2, /device:TPU:8, one launch (start us, length us, event | category | flops | bytes accessed | tf_op | source)
XLA Modules:
  0.0 132.3 jit_solution(12627334077644232465)
XLA Ops:
  4.8 4.2 %adam_quantize.4 = (f32[8,256,512]{2,1,0:T(8,128)}, bf16[8,256,512]{2,1,0:T(8,128)(2,1)}, bf16[8,256,512]{2,1,0:T(8,128)(2,1)}, bf16[256,512]{1,0:T(8,128)(2,1)S(1)}, bf16[256,512]{1,0:T(8,128)(2,1)S(1)}) custom-call(s32[2]{0:T(128)S(1)} %get-tuple-element.60.expert_of, f32[8,256,512]{2,1,0:T(8,128)} %master.7, bf16[8,256,512]{2,1,0:T(8,128)(2,1)S(1)} %copy-done.1, ...), custom_call_target="tpu_custom_call" | custom-call | flops 7864320 | bytes 5242880 | tf_op jit(solution)/shard_map/adam_quantize/pallas_call | solution.py:68
  12.0 3.8 %adam_quantize.5 = (f32[8,256,512]{2,1,0:T(8,128)}, bf16[8,256,512]{2,1,0:T(8,128)(2,1)}, bf16[8,256,512]{2,1,0:T(8,128)(2,1)}, bf16[256,512]{1,0:T(8,128)(2,1)S(1)}, bf16[256,512]{1,0:T(8,128)(2,1)S(1)}) custom-call(s32[2]{0:T(128)S(1)} %get-tuple-element.61.expert_of, ...), custom_call_target="tpu_custom_call", output_to_operand_aliasing={{0}: (5, {}), {1}: (6, {}), {2}: (7, {})} | custom-call | flops 7864320 | bytes 5242880 | tf_op jit(solution)/shard_map/adam_quantize/pallas_call | solution.py:68
  17.6 3.8 %adam_quantize.6 = (f32[8,256,512]{2,1,0:T(8,128)}, bf16[8,256,512]{2,1,0:T(8,128)(2,1)}, bf16[8,256,512]{2,1,0:T(8,128)(2,1)}, bf16[256,512]{1,0:T(8,128)(2,1)S(1)}, bf16[256,512]{1,0:T(8,128)(2,1)S(1)}) custom-call(s32[2]{0:T(128)S(1)} %get-tuple-element.62.expert_of, ...), custom_call_target="tpu_custom_call", output_to_operand_aliasing={{0}: (5, {}), {1}: (6, {}), {2}: (7, {})} | custom-call | flops 7864320 | bytes 5242880 | tf_op jit(solution)/shard_map/adam_quantize/pallas_call | solution.py:68
  21.5 2.6 %collective-permute-start.12 = (bf16[256,512]{1,0:T(8,128)(2,1)S(1)}, bf16[256,512]{1,0:T(8,128)(2,1)S(1)}, u32[]{:S(2)}, u32[]{:S(2)}) collective-permute-start(bf16[256,512]{1,0:T(8,128)(2,1)S(1)} %get-tuple-element.39), channel_id=1, source_target_pairs={{0,4},{1,5},{2,6},{3,7},{4,0},{5,1},{6,2},{7,3},{8,12},{9,13},{10,... | collective-permute-start | bytes 786440 | tf_op jit(solution)/shard_map/ppermute | solution.py:129
  24.1 3.8 %adam_quantize.7 = (f32[8,256,512]{2,1,0:T(8,128)}, bf16[8,256,512]{2,1,0:T(8,128)(2,1)}, bf16[8,256,512]{2,1,0:T(8,128)(2,1)}, bf16[256,512]{1,0:T(8,128)(2,1)S(1)}, bf16[256,512]{1,0:T(8,128)(2,1)S(1)}) custom-call(s32[2]{0:T(128)S(1)} %get-tuple-element.63.expert_of, ...), custom_call_target="tpu_custom_call", output_to_operand_aliasing={{0}: (5, {}), {1}: (6, {}), {2}: (7, {})} | custom-call | flops 7864320 | bytes 5242880 | tf_op jit(solution)/shard_map/adam_quantize/pallas_call | solution.py:68
  29.8 4.4 %collective-permute-done.16.refs_0_ = bf16[256,512]{1,0:T(8,128)(2,1)S(1)} collective-permute-done((bf16[256,512]{1,0:T(8,128)(2,1)S(1)}, bf16[256,512]{1,0:T(8,128)(2,1)S(1)}, u32[]{:S(2)}, u32[]{:S(2)}) %collective-permute-start.16) | collective-permute-done | bytes 262176 | tf_op jit(solution)/shard_map/ppermute | solution.py:129
  34.7 18.6 %collective-permute-done.12.refs_0_ = bf16[256,512]{1,0:T(8,128)(2,1)S(1)} collective-permute-done((bf16[256,512]{1,0:T(8,128)(2,1)S(1)}, bf16[256,512]{1,0:T(8,128)(2,1)S(1)}, u32[]{:S(2)}, u32[]{:S(2)}) %collective-permute-start.12) | collective-permute-done | bytes 262176 | tf_op jit(solution)/shard_map/ppermute | solution.py:129
  53.8 5.1 %collective-permute-done.8.refs_0_ = bf16[256,512]{1,0:T(8,128)(2,1)S(1)} collective-permute-done((bf16[256,512]{1,0:T(8,128)(2,1)S(1)}, bf16[256,512]{1,0:T(8,128)(2,1)S(1)}, u32[]{:S(2)}, u32[]{:S(2)}) %collective-permute-start.8) | collective-permute-done | bytes 262176 | tf_op jit(solution)/shard_map/ppermute | solution.py:129
  59.4 5.2 %collective-permute-done.4.refs_0_ = bf16[256,512]{1,0:T(8,128)(2,1)S(1)} collective-permute-done((bf16[256,512]{1,0:T(8,128)(2,1)S(1)}, bf16[256,512]{1,0:T(8,128)(2,1)S(1)}, u32[]{:S(2)}, u32[]{:S(2)}) %collective-permute-start.4) | collective-permute-done | bytes 262176 | tf_op jit(solution)/shard_map/ppermute | solution.py:129
  65.1 4.9 %collective-permute-done.refs_0_ = bf16[256,512]{1,0:T(8,128)(2,1)S(1)} collective-permute-done((bf16[256,512]{1,0:T(8,128)(2,1)S(1)}, bf16[256,512]{1,0:T(8,128)(2,1)S(1)}, u32[]{:S(2)}, u32[]{:S(2)}) %collective-permute-start) | collective-permute-done | bytes 262176 | tf_op jit(solution)/shard_map/ppermute | solution.py:129
  76.0 3.1 %collective-permute-done.22.refs_2_ = bf16[256,512]{1,0:T(8,128)(2,1)S(1)} collective-permute-done((bf16[256,512]{1,0:T(8,128)(2,1)S(1)}, bf16[256,512]{1,0:T(8,128)(2,1)S(1)}, u32[]{:S(2)}, u32[]{:S(2)}) %collective-permute-start.22) | collective-permute-done | bytes 262176 | tf_op jit(solution)/shard_map/ppermute | solution.py:129
  80.4 4.4 %collective-permute-done.18.refs_2_ = bf16[256,512]{1,0:T(8,128)(2,1)S(1)} collective-permute-done((bf16[256,512]{1,0:T(8,128)(2,1)S(1)}, bf16[256,512]{1,0:T(8,128)(2,1)S(1)}, u32[]{:S(2)}, u32[]{:S(2)}) %collective-permute-start.18) | collective-permute-done | bytes 262176 | tf_op jit(solution)/shard_map/ppermute | solution.py:129
  88.0 2.5 %collective-permute-done.14.refs_2_ = bf16[256,512]{1,0:T(8,128)(2,1)} collective-permute-done((bf16[256,512]{1,0:T(8,128)(2,1)S(1)}, bf16[256,512]{1,0:T(8,128)(2,1)}, u32[]{:S(2)}, u32[]{:S(2)}) %collective-permute-start.14) | collective-permute-done | bytes 262176 | tf_op jit(solution)/shard_map/ppermute | solution.py:129
  91.0 5.1 %collective-permute-done.10.refs_2_ = bf16[256,512]{1,0:T(8,128)(2,1)} collective-permute-done((bf16[256,512]{1,0:T(8,128)(2,1)S(1)}, bf16[256,512]{1,0:T(8,128)(2,1)}, u32[]{:S(2)}, u32[]{:S(2)}) %collective-permute-start.10) | collective-permute-done | bytes 262176 | tf_op jit(solution)/shard_map/ppermute | solution.py:129
  97.4 2.3 %collective-permute-done.5.refs_1_ = bf16[256,512]{1,0:T(8,128)(2,1)} collective-permute-done((bf16[256,512]{1,0:T(8,128)(2,1)S(1)}, bf16[256,512]{1,0:T(8,128)(2,1)}, u32[]{:S(2)}, u32[]{:S(2)}) %collective-permute-start.5) | collective-permute-done | bytes 262176 | tf_op jit(solution)/shard_map/ppermute | solution.py:129
  100.9 3.7 %pad_add_fusion.7 = (s32[5]{0:T(128)S(1)}, s32[5]{0:T(128)S(1)}, s32[5]{0:T(128)S(1)}, s32[5]{0:T(128)S(1)}, s32[5]{0:T(128)S(1)}, /*index=5*/s32[5]{0:T(128)S(1)}) fusion(s32[1]{0:T(128)} %get-tuple-element.50, s32[4]{0:T(128)S(1)} %select_reduce_fusion.1, s32[1]{0:T(128)} %get-tuple-element.56, s32[1]{0:T(128)} %get-tuple-element.55, ...), kind=kLoop, calls=%fused_computation.10 | loop fusion | flops 30 | bytes 160 | tf_op jit(solution)/shard_map/concatenate | solution.py:158
  108.9 1.9 %collective-permute-done.19.refs_3_ = bf16[256,512]{1,0:T(8,128)(2,1)S(1)} collective-permute-done((bf16[256,512]{1,0:T(8,128)(2,1)}, bf16[256,512]{1,0:T(8,128)(2,1)S(1)}, u32[]{:S(2)}, u32[]{:S(2)}) %collective-permute-start.19) | collective-permute-done | bytes 262176 | tf_op jit(solution)/shard_map/ppermute | solution.py:129
  114.3 1.9 %expert_product.8.refs_4_ = bf16[384,4096]{1,0:T(8,128)(2,1)} custom-call(s32[5]{0:T(128)S(1)} %get-tuple-element.44.place, bf16[384,1024]{1,0:T(8,128)(2,1)S(1)} %bitcast.2, bf16[256,512]{1,0:T(8,128)(2,1)S(1)} %get-tuple-element.43.refs_0_, bf16[256,512]{1,0:T(8,128)(2,1)S(1)} %collective-permute-done.28.refs_1_, ...), custom_call_target="tpu_custom_call" | custom-call | flops 402653184 | bytes 2228224 | tf_op jit(solution)/shard_map/expert_product/pallas_call | solution.py:104
  116.2 1.9 %expert_product.9.refs_4_ = bf16[384,4096]{1,0:T(8,128)(2,1)} custom-call(s32[5]{0:T(128)S(1)} %get-tuple-element.58.place, bf16[384,1024]{1,0:T(8,128)(2,1)S(1)} %bitcast.3, bf16[256,512]{1,0:T(8,128)(2,1)S(1)} %collective-permute-done.24.refs_0_, bf16[256,512]{1,0:T(8,128)(2,1)S(1)} %copy-done.10, ...), custom_call_target="tpu_custom_call", output_to_operand_aliasing={{}: (6, {})} | custom-call | flops 402653184 | bytes 2228224 | tf_op jit(solution)/shard_map/expert_product/pallas_call | solution.py:104
  118.1 1.9 %expert_product.10.refs_4_ = bf16[384,4096]{1,0:T(8,128)(2,1)} custom-call(s32[5]{0:T(128)S(1)} %get-tuple-element.49.place, bf16[384,1024]{1,0:T(8,128)(2,1)S(1)} %bitcast.4, bf16[256,512]{1,0:T(8,128)(2,1)S(1)} %collective-permute-done.20.refs_0_, bf16[256,512]{1,0:T(8,128)(2,1)S(1)} %copy-done.12, ...), custom_call_target="tpu_custom_call", output_to_operand_aliasing={{}: (6, {})} | custom-call | flops 402653184 | bytes 2228224 | tf_op jit(solution)/shard_map/expert_product/pallas_call | solution.py:104
  120.0 1.9 %expert_product.11.refs_4_ = bf16[384,4096]{1,0:T(8,128)(2,1)} custom-call(s32[5]{0:T(128)S(1)} %get-tuple-element.48.place, bf16[384,1024]{1,0:T(8,128)(2,1)S(1)} %bitcast.5, bf16[256,512]{1,0:T(8,128)(2,1)S(1)} %collective-permute-done.16.refs_0_, bf16[256,512]{1,0:T(8,128)(2,1)S(1)} %copy-done.18, ...), custom_call_target="tpu_custom_call", output_to_operand_aliasing={{}: (6, {})} | custom-call | flops 402653184 | bytes 2228224 | tf_op jit(solution)/shard_map/expert_product/pallas_call | solution.py:104
  121.9 2.9 %expert_product.12.refs_4_ = bf16[384,4096]{1,0:T(8,128)(2,1)} custom-call(s32[5]{0:T(128)S(1)} %get-tuple-element.47.place, bf16[384,1024]{1,0:T(8,128)(2,1)S(1)} %bitcast.6, bf16[256,512]{1,0:T(8,128)(2,1)S(1)} %collective-permute-done.12.refs_0_, bf16[256,512]{1,0:T(8,128)(2,1)} %collective-permute-done.13.refs_1_, ...), custom_call_target="tpu_custom_call", output_to_operand_aliasing={{}: (6, {})} | custom-call | flops 402653184 | bytes 2228224 | tf_op jit(solution)/shard_map/expert_product/pallas_call | solution.py:104
  124.7 2.9 %expert_product.13.refs_4_ = bf16[384,4096]{1,0:T(8,128)(2,1)} custom-call(s32[5]{0:T(128)S(1)} %get-tuple-element.46.place, bf16[384,1024]{1,0:T(8,128)(2,1)S(1)} %bitcast.7, bf16[256,512]{1,0:T(8,128)(2,1)S(1)} %collective-permute-done.8.refs_0_, bf16[256,512]{1,0:T(8,128)(2,1)} %collective-permute-done.9.refs_1_, ...), custom_call_target="tpu_custom_call", output_to_operand_aliasing={{}: (6, {})} | custom-call | flops 402653184 | bytes 2228224 | tf_op jit(solution)/shard_map/expert_product/pallas_call | solution.py:104
  127.6 2.8 %expert_product.14.refs_4_ = bf16[384,4096]{1,0:T(8,128)(2,1)} custom-call(s32[5]{0:T(128)S(1)} %get-tuple-element.45.place, bf16[384,1024]{1,0:T(8,128)(2,1)S(1)} %bitcast.8, bf16[256,512]{1,0:T(8,128)(2,1)S(1)} %collective-permute-done.4.refs_0_, bf16[256,512]{1,0:T(8,128)(2,1)} %collective-permute-done.5.refs_1_, ...), custom_call_target="tpu_custom_call", output_to_operand_aliasing={{}: (6, {})} | custom-call | flops 402653184 | bytes 2228224 | tf_op jit(solution)/shard_map/expert_product/pallas_call | solution.py:104
  (98 shorter events, 36.0 us)
Async XLA Ops:
  10.4 17.5 %collective-permute-start.29 = (bf16[256,512]{1,0:T(8,128)(2,1)S(1)}, bf16[256,512]{1,0:T(8,128)(2,1)S(1)}, u32[]{:S(2)}, u32[]{:S(2)}) collective-permute-start(bf16[256,512]{1,0:T(8,128)(2,1)S(1)} %get-tuple-element.43.refs_0_), channel_id=1, source_target_pairs={{0,16},{8,24},{16,0},{24,8},{1,17},{9,25},{17,1},{25,9},{2,18},{10... | collective-permute-start | bytes 786440 | tf_op jit(solution)/shard_map/ppermute | solution.py:129
  12.0 16.0 %collective-permute-start.24 = (bf16[256,512]{1,0:T(8,128)(2,1)S(1)}, bf16[256,512]{1,0:T(8,128)(2,1)S(1)}, u32[]{:S(2)}, u32[]{:S(2)}) collective-permute-start(bf16[256,512]{1,0:T(8,128)(2,1)S(1)} %get-tuple-element.42), channel_id=1, source_target_pairs={{0,1},{1,0},{2,3},{3,2},{4,5},{5,4},{6,7},{7,6},{8,9},{9,8},{10,11... | collective-permute-start | bytes 786440 | tf_op jit(solution)/shard_map/ppermute | solution.py:129
  15.8 13.7 %collective-permute-start.20 = (bf16[256,512]{1,0:T(8,128)(2,1)S(1)}, bf16[256,512]{1,0:T(8,128)(2,1)S(1)}, u32[]{:S(2)}, u32[]{:S(2)}) collective-permute-start(bf16[256,512]{1,0:T(8,128)(2,1)S(1)} %get-tuple-element.41), channel_id=1, source_target_pairs={{0,2},{1,3},{2,0},{3,1},{4,6},{5,7},{6,4},{7,5},{8,10},{9,11},{10,... | collective-permute-start | bytes 786440 | tf_op jit(solution)/shard_map/ppermute | solution.py:129
  16.3 17.9 %collective-permute-start.16 = (bf16[256,512]{1,0:T(8,128)(2,1)S(1)}, bf16[256,512]{1,0:T(8,128)(2,1)S(1)}, u32[]{:S(2)}, u32[]{:S(2)}) collective-permute-start(bf16[256,512]{1,0:T(8,128)(2,1)S(1)} %get-tuple-element.40), channel_id=1, source_target_pairs={{0,3},{1,2},{2,1},{3,0},{4,7},{5,6},{6,5},{7,4},{8,11},{9,10},{10,... | collective-permute-start | bytes 786440 | tf_op jit(solution)/shard_map/ppermute | solution.py:129
  21.5 31.8 %collective-permute-start.12 = (bf16[256,512]{1,0:T(8,128)(2,1)S(1)}, bf16[256,512]{1,0:T(8,128)(2,1)S(1)}, u32[]{:S(2)}, u32[]{:S(2)}) collective-permute-start(bf16[256,512]{1,0:T(8,128)(2,1)S(1)} %get-tuple-element.39), channel_id=1, source_target_pairs={{0,4},{1,5},{2,6},{3,7},{4,0},{5,1},{6,2},{7,3},{8,12},{9,13},{10,... | collective-permute-start | bytes 786440 | tf_op jit(solution)/shard_map/ppermute | solution.py:129
  27.9 30.9 %collective-permute-start.8 = (bf16[256,512]{1,0:T(8,128)(2,1)S(1)}, bf16[256,512]{1,0:T(8,128)(2,1)S(1)}, u32[]{:S(2)}, u32[]{:S(2)}) collective-permute-start(bf16[256,512]{1,0:T(8,128)(2,1)S(1)} %get-tuple-element.38), channel_id=1, source_target_pairs={{0,5},{1,4},{2,7},{3,6},{4,1},{5,0},{6,3},{7,2},{8,13},{9,12},{10,... | collective-permute-start | bytes 786440 | tf_op jit(solution)/shard_map/ppermute | solution.py:129
  28.0 36.6 %collective-permute-start.4 = (bf16[256,512]{1,0:T(8,128)(2,1)S(1)}, bf16[256,512]{1,0:T(8,128)(2,1)S(1)}, u32[]{:S(2)}, u32[]{:S(2)}) collective-permute-start(bf16[256,512]{1,0:T(8,128)(2,1)S(1)} %get-tuple-element.37), channel_id=1, source_target_pairs={{0,6},{1,7},{2,4},{3,5},{4,2},{5,3},{6,0},{7,1},{8,14},{9,15},{10,... | collective-permute-start | bytes 786440 | tf_op jit(solution)/shard_map/ppermute | solution.py:129
  29.5 40.5 %collective-permute-start = (bf16[256,512]{1,0:T(8,128)(2,1)S(1)}, bf16[256,512]{1,0:T(8,128)(2,1)S(1)}, u32[]{:S(2)}, u32[]{:S(2)}) collective-permute-start(bf16[256,512]{1,0:T(8,128)(2,1)S(1)} %get-tuple-element.36), channel_id=1, source_target_pairs={{0,7},{1,6},{2,5},{3,4},{4,3},{5,2},{6,1},{7,0},{8,15},{9,14},{10,... | collective-permute-start | bytes 786440 | tf_op jit(solution)/shard_map/ppermute | solution.py:129
  34.2 36.3 %collective-permute-start.30 = (bf16[256,512]{1,0:T(8,128)(2,1)S(1)}, bf16[256,512]{1,0:T(8,128)(2,1)S(1)}, u32[]{:S(2)}, u32[]{:S(2)}) collective-permute-start(bf16[256,512]{1,0:T(8,128)(2,1)S(1)} %collective-permute-done.28.refs_1_), channel_id=1, source_target_pairs={{0,16},{8,24},{16,0},{24,8},{1,17},{9,25},{17,1},{25,9},{2,18},{10... | collective-permute-start | bytes 786440 | tf_op jit(solution)/shard_map/ppermute | solution.py:129
  53.3 19.5 %collective-permute-start.26 = (bf16[256,512]{1,0:T(8,128)(2,1)S(1)}, bf16[256,512]{1,0:T(8,128)(2,1)S(1)}, u32[]{:S(2)}, u32[]{:S(2)}) collective-permute-start(bf16[256,512]{1,0:T(8,128)(2,1)S(1)} %collective-permute-done.24.refs_0_), channel_id=1, source_target_pairs={{0,16},{8,24},{16,0},{24,8},{1,17},{9,25},{17,1},{25,9},{2,18},{10... | collective-permute-start | bytes 786440 | tf_op jit(solution)/shard_map/ppermute | solution.py:129
  58.9 14.4 %collective-permute-start.25 = (bf16[256,512]{1,0:T(8,128)(2,1)S(1)}, bf16[256,512]{1,0:T(8,128)(2,1)S(1)}, u32[]{:S(2)}, u32[]{:S(2)}) collective-permute-start(bf16[256,512]{1,0:T(8,128)(2,1)S(1)} %collective-permute-done.24.refs_0_), channel_id=1, source_target_pairs={{0,8},{8,0},{16,24},{24,16},{1,9},{9,1},{17,25},{25,17},{2,10},{10... | collective-permute-start | bytes 786440 | tf_op jit(solution)/shard_map/ppermute | solution.py:129
  71.2 13.5 %collective-permute-start.18 = (bf16[256,512]{1,0:T(8,128)(2,1)S(1)}, bf16[256,512]{1,0:T(8,128)(2,1)S(1)}, u32[]{:S(2)}, u32[]{:S(2)}) collective-permute-start(bf16[256,512]{1,0:T(8,128)(2,1)S(1)} %collective-permute-done.16.refs_0_), channel_id=1, source_target_pairs={{0,16},{8,24},{16,0},{24,8},{1,17},{9,25},{17,1},{25,9},{2,18},{10... | collective-permute-start | bytes 786440 | tf_op jit(solution)/shard_map/ppermute | solution.py:129
  74.0 13.5 %collective-permute-start.13 = (bf16[256,512]{1,0:T(8,128)(2,1)S(1)}, bf16[256,512]{1,0:T(8,128)(2,1)}, u32[]{:S(2)}, u32[]{:S(2)}) collective-permute-start(bf16[256,512]{1,0:T(8,128)(2,1)S(1)} %collective-permute-done.12.refs_0_), channel_id=1, source_target_pairs={{0,8},{8,0},{16,24},{24,16},{1,9},{9,1},{17,25},{25,17},{2,10},{10... | collective-permute-start | bytes 786440 | tf_op jit(solution)/shard_map/ppermute | solution.py:129
  75.5 15.0 %collective-permute-start.14 = (bf16[256,512]{1,0:T(8,128)(2,1)S(1)}, bf16[256,512]{1,0:T(8,128)(2,1)}, u32[]{:S(2)}, u32[]{:S(2)}) collective-permute-start(bf16[256,512]{1,0:T(8,128)(2,1)S(1)} %collective-permute-done.12.refs_0_), channel_id=1, source_target_pairs={{0,16},{8,24},{16,0},{24,8},{1,17},{9,25},{17,1},{25,9},{2,18},{10... | collective-permute-start | bytes 786440 | tf_op jit(solution)/shard_map/ppermute | solution.py:129
  79.9 16.2 %collective-permute-start.10 = (bf16[256,512]{1,0:T(8,128)(2,1)S(1)}, bf16[256,512]{1,0:T(8,128)(2,1)}, u32[]{:S(2)}, u32[]{:S(2)}) collective-permute-start(bf16[256,512]{1,0:T(8,128)(2,1)S(1)} %collective-permute-done.8.refs_0_), channel_id=1, source_target_pairs={{0,16},{8,24},{16,0},{24,8},{1,17},{9,25},{17,1},{25,9},{2,18},{10... | collective-permute-start | bytes 786440 | tf_op jit(solution)/shard_map/ppermute | solution.py:129
  86.2 13.6 %collective-permute-start.5 = (bf16[256,512]{1,0:T(8,128)(2,1)S(1)}, bf16[256,512]{1,0:T(8,128)(2,1)}, u32[]{:S(2)}, u32[]{:S(2)}) collective-permute-start(bf16[256,512]{1,0:T(8,128)(2,1)S(1)} %collective-permute-done.4.refs_0_), channel_id=1, source_target_pairs={{0,8},{8,0},{16,24},{24,16},{1,9},{9,1},{17,25},{25,17},{2,10},{10... | collective-permute-start | bytes 786440 | tf_op jit(solution)/shard_map/ppermute | solution.py:129
  87.5 17.2 %collective-permute-start.2 = (bf16[256,512]{1,0:T(8,128)(2,1)S(1)}, bf16[256,512]{1,0:T(8,128)(2,1)S(1)}, u32[]{:S(2)}, u32[]{:S(2)}) collective-permute-start(bf16[256,512]{1,0:T(8,128)(2,1)S(1)} %collective-permute-done.refs_0_), channel_id=1, source_target_pairs={{0,16},{8,24},{16,0},{24,8},{1,17},{9,25},{17,1},{25,9},{2,18},{10... | collective-permute-start | bytes 786440 | tf_op jit(solution)/shard_map/ppermute | solution.py:129
  90.5 15.7 %collective-permute-start.27 = (bf16[256,512]{1,0:T(8,128)(2,1)}, bf16[256,512]{1,0:T(8,128)(2,1)S(1)}, u32[]{:S(2)}, u32[]{:S(2)}) collective-permute-start(bf16[256,512]{1,0:T(8,128)(2,1)} %copy-done.7), channel_id=1, source_target_pairs={{0,8},{8,0},{16,24},{24,16},{1,9},{9,1},{17,25},{25,17},{2,10},{10... | collective-permute-start | bytes 786440 | tf_op jit(solution)/shard_map/ppermute | solution.py:129
  96.8 14.1 %collective-permute-start.19 = (bf16[256,512]{1,0:T(8,128)(2,1)}, bf16[256,512]{1,0:T(8,128)(2,1)S(1)}, u32[]{:S(2)}, u32[]{:S(2)}) collective-permute-start(bf16[256,512]{1,0:T(8,128)(2,1)} %copy-done.15), channel_id=1, source_target_pairs={{0,8},{8,0},{16,24},{24,16},{1,9},{9,1},{17,25},{25,17},{2,10},{10... | collective-permute-start | bytes 786440 | tf_op jit(solution)/shard_map/ppermute | solution.py:129
  104.7 23.0 %collective-permute-start.6 = (bf16[256,512]{1,0:T(8,128)(2,1)S(1)}, bf16[256,512]{1,0:T(8,128)(2,1)S(1)}, u32[]{:S(2)}, u32[]{:S(2)}) collective-permute-start(bf16[256,512]{1,0:T(8,128)(2,1)S(1)} %collective-permute-done.4.refs_0_), channel_id=1, source_target_pairs={{0,16},{8,24},{16,0},{24,8},{1,17},{9,25},{17,1},{25,9},{2,18},{10... | collective-permute-start | bytes 786440 | tf_op jit(solution)/shard_map/ppermute | solution.py:129
  106.2 18.5 %collective-permute-start.11 = (bf16[256,512]{1,0:T(8,128)(2,1)}, bf16[256,512]{1,0:T(8,128)(2,1)S(1)}, u32[]{:S(2)}, u32[]{:S(2)}) collective-permute-start(bf16[256,512]{1,0:T(8,128)(2,1)} %collective-permute-done.10.refs_2_), channel_id=1, source_target_pairs={{0,8},{8,0},{16,24},{24,16},{1,9},{9,1},{17,25},{25,17},{2,10},{10... | collective-permute-start | bytes 786440 | tf_op jit(solution)/shard_map/ppermute | solution.py:129
  107.2 20.4 %collective-permute-start.7 = (bf16[256,512]{1,0:T(8,128)(2,1)}, bf16[256,512]{1,0:T(8,128)(2,1)S(1)}, u32[]{:S(2)}, u32[]{:S(2)}) collective-permute-start(bf16[256,512]{1,0:T(8,128)(2,1)} %collective-permute-done.5.refs_1_), channel_id=1, source_target_pairs={{0,16},{8,24},{16,0},{24,8},{1,17},{9,25},{17,1},{25,9},{2,18},{10... | collective-permute-start | bytes 786440 | tf_op jit(solution)/shard_map/ppermute | solution.py:129
  110.9 19.6 %collective-permute-start.1 = (bf16[256,512]{1,0:T(8,128)(2,1)S(1)}, bf16[256,512]{1,0:T(8,128)(2,1)S(1)}, u32[]{:S(2)}, u32[]{:S(2)}) collective-permute-start(bf16[256,512]{1,0:T(8,128)(2,1)S(1)} %collective-permute-done.refs_0_), channel_id=1, source_target_pairs={{0,8},{8,0},{16,24},{24,16},{1,9},{9,1},{17,25},{25,17},{2,10},{10... | collective-permute-start | bytes 786440 | tf_op jit(solution)/shard_map/ppermute | solution.py:129
  112.9 17.6 %collective-permute-start.3 = (bf16[256,512]{1,0:T(8,128)(2,1)S(1)}, bf16[256,512]{1,0:T(8,128)(2,1)S(1)}, u32[]{:S(2)}, u32[]{:S(2)}) collective-permute-start(bf16[256,512]{1,0:T(8,128)(2,1)S(1)} %collective-permute-done.2.refs_2_), channel_id=1, source_target_pairs={{0,8},{8,0},{16,24},{24,16},{1,9},{9,1},{17,25},{25,17},{2,10},{10... | collective-permute-start | bytes 786440 | tf_op jit(solution)/shard_map/ppermute | solution.py:129
  (27 other events, 299.0 us)

commit v3 on v2

v3 whole, which is shorter than its diff:
```python
import collections
import functools

import jax
import jax.numpy as jnp
from jax import lax
from jax.experimental import pallas as pl
from jax.experimental.pallas import tpu as pltpu
from jax.sharding import PartitionSpec as P

QB = 128
VMEM_LIMIT = 60 * 1024 * 1024
PRODUCT_LIMIT = 16 * 1024 * 1024

beta_one = 0.9
beta_two = 0.95
learn_rate = 0.004
adam_epsilon = 1e-08
step_count = 10.0
quant_limit = 448.0
scale_epsilon = 1e-06
first_fix = 1.0 - beta_one**step_count
second_fix = 1.0 - beta_two**step_count
second_root = second_fix**0.5
step_size = learn_rate / first_fix * second_root
root_epsilon = adam_epsilon * second_root

TOKEN = (132 * 1024, 128)
WHOLE = pl.BlockSpec(memory_space=pl.ANY)
SMALL_COST = pl.CostEstimate(flops=0, bytes_accessed=65536, transcendentals=0)


def like(array):
    return jax.ShapeDtypeStruct(array.shape, array.dtype)


def fence_kernel(*refs):
    pass


def fence(arrays):
    return pl.pallas_call(
        fence_kernel,
        in_specs=[WHOLE] * len(arrays),
        out_specs=[WHOLE] * len(arrays),
        out_shape=[like(array) for array in arrays],
        input_output_aliases={i: i for i in range(len(arrays))},
        compiler_params=pltpu.CompilerParams(vmem_limit_bytes=1024 * 1024),
        cost_estimate=SMALL_COST,
        name="arrival_order",
    )(*arrays)


def adam_kernel(blocks, passed, expert_of, master, gradient, first, second, *refs):
    new_master, new_first, new_second, *sends = refs[passed : passed + 3 + blocks]
    for number in range(blocks):

        @pl.when(pl.program_id(0) == number)
        def _():
            for start in range(0, master.shape[2], QB):
                at = (0, slice(None), slice(start, start + QB))
                grad = gradient[at].astype(jnp.float32)
                moment_one = beta_one * first[at].astype(jnp.float32) + (1.0 - beta_one) * grad
                moment_two = beta_two * second[at].astype(jnp.float32) + (
                    ((1.0 - beta_two) * grad) * grad
                )
                new_first[at] = moment_one.astype(jnp.bfloat16)
                new_second[at] = moment_two.astype(jnp.bfloat16)
                root = moment_two * lax.rsqrt(moment_two) + root_epsilon
                inverse = pl.reciprocal(root, approx=True)
                inverse = inverse * (2.0 - root * inverse)
                updated = master[at] - (step_size * moment_one) * inverse
                new_master[at] = updated
                largest = jnp.max(jnp.abs(updated), axis=0, keepdims=True)
                largest = jnp.max(largest, axis=1, keepdims=True)
                scale = ((largest + scale_epsilon) * (1.0 / quant_limit)).astype(jnp.bfloat16)
                scale = jnp.broadcast_to(scale.astype(jnp.float32), (1, QB))
                quantized = (updated * (1.0 / scale)).astype(jnp.bfloat16)
                value = quantized.astype(jnp.float32) * scale
                sends[number][:, start : start + QB] = value.astype(jnp.bfloat16)


def adam_blocks(expert_of, arrays, carried, token, fenced):
    _, rows, columns = arrays[0].shape
    blocks = expert_of.shape[0]
    passed = len(carried) + len(token)

    def sent(number):
        def place(e, i, expert_of):
            return jnp.where(e == number, i, jnp.where(e > number, rows // QB - 1, 0)), 0

        return pl.BlockSpec((QB, columns), place)

    here = pl.BlockSpec((1, QB, columns), lambda e, i, expert_of: (expert_of[e], i, 0))
    made = [like(arrays[0]), like(arrays[2]), like(arrays[3])]
    made += [jax.ShapeDtypeStruct((rows, columns), jnp.bfloat16)] * blocks
    aliases = {5 + i: i for i in range(len(carried))}
    if token:
        aliases[5 + len(carried)] = len(made)
    results = pl.pallas_call(
        functools.partial(adam_kernel, blocks, passed),
        grid_spec=pltpu.PrefetchScalarGridSpec(
            num_scalar_prefetch=1,
            grid=(blocks, rows // QB),
            in_specs=[here] * 4 + [WHOLE] * passed,
            out_specs=[here] * 3 + [sent(number) for number in range(blocks)] + [WHOLE] * fenced,
        ),
        out_shape=made + [jax.ShapeDtypeStruct(TOKEN, jnp.float32)] * fenced,
        input_output_aliases=aliases,
        compiler_params=pltpu.CompilerParams(vmem_limit_bytes=VMEM_LIMIT),
        cost_estimate=SMALL_COST,
        name="adam_quantize",
    )(expert_of, *arrays, *carried, *token)
    return results[:3], results[3 : 3 + blocks], tuple(results[3 + blocks :])


def product_kernel(number, slabs, sources, places, left, *refs):
    out = refs[-1]
    total = jnp.zeros(out.shape, jnp.float32)
    for slab in range(slabs):
        right = refs[slab]
        rows = right.shape[0]
        start = pl.multiple_of(places[slab] * rows, QB)
        total += jnp.dot(
            left[:, pl.ds(start, rows)], right[...], preferred_element_type=jnp.float32
        )
    out[...] = total.astype(out.dtype)


def product(number, sources, places, token_rows, weights, breadth, carried, token):
    slabs = len(weights)
    tokens, units = token_rows.shape
    rows, columns = weights[0].shape
    passed = len(token) + len(carried)
    *token, out = pl.pallas_call(
        functools.partial(product_kernel, number, slabs),
        grid_spec=pltpu.PrefetchScalarGridSpec(
            num_scalar_prefetch=2,
            grid=(1,),
            in_specs=[pl.BlockSpec((tokens, units), lambda i, sources, places: (0, 0))]
            + [pl.BlockSpec((rows, columns), lambda i, sources, places: (0, 0))] * slabs
            + [WHOLE] * passed,
            out_specs=[WHOLE] * len(token)
            + [pl.BlockSpec((tokens, columns), lambda i, sources, places: (0, sources[number]))],
        ),
        out_shape=[like(array) for array in token]
            + [jax.ShapeDtypeStruct((tokens, breadth), jnp.bfloat16)],
        input_output_aliases={3 + slabs + i: i for i in range(passed)},
        compiler_params=pltpu.CompilerParams(vmem_limit_bytes=PRODUCT_LIMIT),
        cost_estimate=SMALL_COST,
        name="expert_product",
    )(sources, places, token_rows, *weights, *token, *carried)
    return (out,), tuple(token)


def swap(value, axis, size, mask):
    return lax.ppermute(value, axis, [(i, i ^ mask) for i in range(size)])


def body(shards, replicas, *arguments):
    *arrays, hidden, owner_of_expert, slab_order = arguments
    shard = lax.axis_index("shard").astype(jnp.int32)
    replica = lax.axis_index("replica").astype(jnp.int32)
    token_rows = hidden.reshape(hidden.shape[2:])
    breadth = arrays[0].shape[2] * shards
    bits = [1 << i for i in range((replicas - 1).bit_length())]
    experts = jnp.arange(shards, dtype=jnp.int32)
    members = jnp.arange(replicas, dtype=jnp.int32)
    sources = shard ^ experts
    expert_of = jnp.sum(
        jnp.where(owner_of_expert[None, :] == sources[:, None], experts[None, :], 0), axis=1
    ).astype(jnp.int32)
    places = jnp.sum(
        jnp.where((replica ^ members)[:, None] == members[None, :], slab_order[None, :], 0), axis=1
    ).astype(jnp.int32)

    pairs = shards // 2
    fenced = len(bits) == 2 and pairs > 1
    held = [{} for _ in range(shards)]
    made, due, ready = {}, collections.defaultdict(list), set()
    state = {"adam": (), "token": (), "out": ()}

    def adam(pair):
        picked = expert_of[2 * pair : 2 * pair + 2]
        state["adam"], sends, state["token"] = adam_blocks(
            picked, arrays, tuple(state["adam"]), state["token"], fenced
        )
        made[2 * pair], made[2 * pair + 1] = sends

    def deliver(block):
        held[block][0] = swap(made[block], "shard", shards, block) if block else made[block]

    def send(block, member, bit):
        held[block][member ^ bit] = swap(held[block][member], "replica", replicas, bit)

    def arrived(keys):
        token, *passed = fence([*state["token"], *[held[b][m] for b, m in keys]])
        state["token"] = (token,)
        for (block, member), array in zip(keys, passed):
            held[block][member] = array
        ready.update(keys)

    def multiply(block):
        ordered = [held[block][member] for member in range(replicas)]
        state["out"], state["token"] = product(
            block, sources, places, token_rows, ordered, breadth, state["out"], state["token"]
        )

    waiting = list(range(shards))
    if fenced:
        steps, moves = collections.defaultdict(list), collections.defaultdict(list)
        steps[-1], steps[0], steps[1], steps[2] = (
            [(0, 0, 1), (0, 0, 2)],
            [(1, 0, 1), (1, 0, 2)],
            [(0, 1, 2)],
            [(1, 2, 1)],
        )
        for pair in range(1, pairs):
            even, odd = 2 * pair, 2 * pair + 1
            steps[3 * pair] = [(even, 0, 1), (odd, 0, 2)]
            steps[3 * pair + 1] = [(even, 0, 2), (odd, 0, 1)]
            steps[3 * pair + 2] = [(even, 1, 2), (odd, 2, 1)]
        for block in range(2, shards):
            moves[max(block - 2, min(2 * block - 7, 3 * (block // 2) - 2))].append(block)

        def start(step):
            for block in moves[step]:
                deliver(block)
                due[step + 2].append((block, 0))
            for block, member, bit in steps[step]:
                send(block, member, bit)
                due[step + 2].append((block, member ^ bit))

        adam(0)
        deliver(0)
        deliver(1)
        ready.add((0, 0))
        due[0].append((1, 0))
        start(-1)
        adam(1)
        for step in range(3 * pairs + 2):
            arrived(due[step])
            start(step)
            if step + 2 < pairs:
                adam(step + 2)
            for block in list(waiting):
                if all((block, member) in ready for member in range(replicas)):
                    multiply(block)
                    waiting.remove(block)
    else:
        for pair in range(pairs):
            adam(pair)
        for block in range(shards):
            deliver(block)
            for number in range(len(bits)):
                bit = bits[(number + block) % len(bits)]
                for member in list(held[block]):
                    send(block, member, bit)
            multiply(block)
    out = state["out"][0]
    return (*state["adam"], out.reshape(hidden.shape[:2] + out.shape))


def solution(mesh):
    weights = P(None, "replica", "shard")
    tokens = P("replica", "shard", None, None)
    return jax.shard_map(
        functools.partial(body, mesh.shape["shard"], mesh.shape["replica"]),
        mesh=mesh,
        in_specs=(weights, weights, weights, weights, tokens, P(), P()),
        out_specs=(weights, weights, weights, tokens),
        check_vma=False,
    )
```

time: 133 us -> 117 us (0.88)
  the two profiles are of different devices: /device:TPU:8 before, /device:TPU:0 now
where the time goes in v3:
time: 117 us; the launch traced here: 116 us
  waiting for transfers between devices  40.6 us (35%)
  Pallas kernels  36.3 us (31%)
  starting transfers between devices  33 us (28%)
  local copies, waits for them, and re-layouts  4.79 us (4%)
    ppermute x31, waiting for transfers between devices, swap(): return lax.ppermute(value, axis, [(i, i ^ mask) for i in range(size)])  40.6 us
    ppermute x31, starting transfers between devices, swap(): return lax.ppermute(value, axis, [(i, i ^ mask) for i in range(size)])  33 us
    pallas_call x4, Pallas kernels, adam_blocks(): pl.pallas_call(functools.partial(adam_kernel, blocks, passed), grid_spec=...  21.3 us
    pallas_call x8, Pallas kernels, product(): pl.pallas_call(functools.partial(product_kernel, number, slabs), grid_spe...  15 us
    unnamed x28, local copies, waits for them, and re-layouts  4.13 us
  transfers between devices with their start and end apart: 31, of which 11 were waited for; matrix products, arithmetic and copies ran while one was open for 0% of the time, Pallas kernels for 23%

profile of v3, /device:TPU:0, one launch (start us, length us, event | category | flops | bytes accessed | tf_op | source)
XLA Modules:
  0.0 116.5 jit_solution(8456205951962580327)
XLA Ops:
  2.7 5.3 %adam_quantize.4 = (f32[8,256,512]{2,1,0:T(8,128)}, bf16[8,256,512]{2,1,0:T(8,128)(2,1)}, bf16[8,256,512]{2,1,0:T(8,128)(2,1)}, bf16[256,512]{1,0:T(8,128)(2,1)}...) custom-call(s32[2]{0:T(128)} %get-tuple-element.172.expert_of, f32[8,256,512]{2,1,0:T(8,128)} %master.7, ...), custom_call_target="tpu_custom_call" | custom-call | bytes 65536 | tf_op jit(solution)/shard_map/adam_quantize/pallas_call | solution.py:100
  8.5 2.6 %collective-permute-start.1 = (bf16[256,512]{1,0:T(8,128)(2,1)}, bf16[256,512]{1,0:T(8,128)(2,1)S(1)}, u32[]{:S(2)}, u32[]{:S(2)}) collective-permute-start(bf16[256,512]{1,0:T(8,128)(2,1)} %get-tuple-element.102.refs_0_), channel_id=1, source_target_pairs={{0,8},{8,0},{16,24},{24,16},{1,9},{9,1},{17,25},{25,17},{2,10},{10... | collective-permute-start | bytes 786440 | tf_op jit(solution)/shard_map/ppermute | solution.py:157
  12.6 5.3 %adam_quantize.5 = (f32[8,256,512]{2,1,0:T(8,128)}, bf16[8,256,512]{2,1,0:T(8,128)(2,1)}, bf16[8,256,512]{2,1,0:T(8,128)(2,1)}, bf16[256,512]{1,0:T(8,128)(2,1)}...) custom-call(s32[2]{0:T(128)} %get-tuple-element.173.expert_of, ...), custom_call_target="tpu_custom_call", output_to_operand_aliasing={{0}: (5, {}), {1}: (6, {}), {2}: (7, {}), {5}: (8, {})} | custom-call | bytes 65536 | tf_op jit(solution)/shard_map/adam_quantize/pallas_call | solution.py:100
  20.7 5.3 %adam_quantize.6 = (f32[8,256,512]{2,1,0:T(8,128)}, bf16[8,256,512]{2,1,0:T(8,128)(2,1)}, bf16[8,256,512]{2,1,0:T(8,128)(2,1)}, bf16[256,512]{1,0:T(8,128)(2,1)}...) custom-call(s32[2]{0:T(128)} %get-tuple-element.174.expert_of, ...), custom_call_target="tpu_custom_call", output_to_operand_aliasing={{0}: (5, {}), {1}: (6, {}), {2}: (7, {}), {5}: (8, {})} | custom-call | bytes 65536 | tf_op jit(solution)/shard_map/adam_quantize/pallas_call | solution.py:100
  27.7 5.3 %adam_quantize.7 = (f32[8,256,512]{2,1,0:T(8,128)}, bf16[8,256,512]{2,1,0:T(8,128)(2,1)}, bf16[8,256,512]{2,1,0:T(8,128)(2,1)}, bf16[256,512]{1,0:T(8,128)(2,1)}...) custom-call(s32[2]{0:T(128)} %get-tuple-element.175.expert_of, ...), custom_call_target="tpu_custom_call", output_to_operand_aliasing={{0}: (5, {}), {1}: (6, {}), {2}: (7, {}), {5}: (8, {})} | custom-call | bytes 65536 | tf_op jit(solution)/shard_map/adam_quantize/pallas_call | solution.py:100
  33.1 2.7 %collective-permute-start.8 = (bf16[256,512]{1,0:T(8,128)(2,1)}, bf16[256,512]{1,0:T(8,128)(2,1)S(1)}, u32[]{:S(2)}, u32[]{:S(2)}) collective-permute-start(bf16[256,512]{1,0:T(8,128)(2,1)} %get-tuple-element.120), channel_id=1, source_target_pairs={{0,4},{1,5},{2,6},{3,7},{4,0},{5,1},{6,2},{7,3},{8,12},{9,13},{10,... | collective-permute-start | bytes 786440 | tf_op jit(solution)/shard_map/ppermute | solution.py:157
  42.1 1.9 %expert_product.8 = (f32[135168,128]{1,0:T(8,128)}, bf16[384,4096]{1,0:T(8,128)(2,1)}) custom-call(s32[8]{0:T(128)S(1)} %copy-done.9, s32[4]{0:T(128)S(1)} %select_reduce_fusion.1.places, bf16[384,1024]{1,0:T(8,128)(2,1)S(1)} %bitcast.2, bf16[256,512]{1,0:T(8,128)(2,1)S(1)} %copy-done.7, ...), custom_call_target="tpu_custom_call", output_to_operand_aliasing={{0}: (7, {})} | custom-call | bytes 65536 | tf_op jit(solution)/shard_map/expert_product/pallas_call | solution.py:135
  44.0 10.6 %collective-permute-done.8.refs_1_ = bf16[256,512]{1,0:T(8,128)(2,1)S(1)} collective-permute-done((bf16[256,512]{1,0:T(8,128)(2,1)}, bf16[256,512]{1,0:T(8,128)(2,1)S(1)}, u32[]{:S(2)}, u32[]{:S(2)}) %collective-permute-start.8) | collective-permute-done | bytes 262176 | tf_op jit(solution)/shard_map/ppermute | solution.py:157
  54.6 2.5 %collective-permute-start.15 = (bf16[256,512]{1,0:T(8,128)(2,1)S(1)}, bf16[256,512]{1,0:T(8,128)(2,1)S(1)}, u32[]{:S(2)}, u32[]{:S(2)}) collective-permute-start(bf16[256,512]{1,0:T(8,128)(2,1)S(1)} %copy-done.11), channel_id=1, source_target_pairs={{0,6},{1,7},{2,4},{3,5},{4,2},{5,3},{6,0},{7,1},{8,14},{9,15},{10,... | collective-permute-start | bytes 786440 | tf_op jit(solution)/shard_map/ppermute | solution.py:157
  58.6 1.9 %expert_product.9 = (f32[135168,128]{1,0:T(8,128)}, bf16[384,4096]{1,0:T(8,128)(2,1)}) custom-call(s32[8]{0:T(128)S(1)} %copy-done.9, s32[4]{0:T(128)S(1)} %select_reduce_fusion.1.places, bf16[384,1024]{1,0:T(8,128)(2,1)S(1)} %bitcast.3, bf16[256,512]{1,0:T(8,128)(2,1)S(1)} %copy-done.6, ...), custom_call_target="tpu_custom_call", output_to_operand_aliasing={{0}: (7, {}), {1}: (8, {})} | custom-call | bytes 65536 | tf_op jit(solution)/shard_map/expert_product/pallas_call | solution.py:135
  60.5 4.0 %collective-permute-done.10.refs_1_ = bf16[256,512]{1,0:T(8,128)(2,1)S(1)} collective-permute-done((bf16[256,512]{1,0:T(8,128)(2,1)}, bf16[256,512]{1,0:T(8,128)(2,1)S(1)}, u32[]{:S(2)}, u32[]{:S(2)}) %collective-permute-start.10) | collective-permute-done | bytes 262176 | tf_op jit(solution)/shard_map/ppermute | solution.py:157
  68.9 4.5 %collective-permute-done.13.refs_1_ = bf16[256,512]{1,0:T(8,128)(2,1)S(1)} collective-permute-done((bf16[256,512]{1,0:T(8,128)(2,1)S(1)}, bf16[256,512]{1,0:T(8,128)(2,1)S(1)}, u32[]{:S(2)}, u32[]{:S(2)}) %collective-permute-start.13) | collective-permute-done | bytes 262176 | tf_op jit(solution)/shard_map/ppermute | solution.py:157
  75.1 3.9 %collective-permute-done.16.refs_2_ = bf16[256,512]{1,0:T(8,128)(2,1)S(1)} collective-permute-done((bf16[256,512]{1,0:T(8,128)(2,1)S(1)}, bf16[256,512]{1,0:T(8,128)(2,1)S(1)}, u32[]{:S(2)}, u32[]{:S(2)}) %collective-permute-start.16) | collective-permute-done | bytes 262176 | tf_op jit(solution)/shard_map/ppermute | solution.py:157
  81.0 1.9 %expert_product.10 = (f32[135168,128]{1,0:T(8,128)}, bf16[384,4096]{1,0:T(8,128)(2,1)}) custom-call(s32[8]{0:T(128)S(1)} %copy-done.9, s32[4]{0:T(128)S(1)} %select_reduce_fusion.1.places, bf16[384,1024]{1,0:T(8,128)(2,1)S(1)} %bitcast.4, bf16[256,512]{1,0:T(8,128)(2,1)S(1)} %get-tuple-element.126.refs_0_, ...), custom_call_target="tpu_custom_call", output_to_operand_aliasing={{0}: (7, {}), {1}: (8, {})} | custom-call | bytes 65536 | tf_op jit(solution)/shard_map/expert_product/pallas_call | solution.py:135
  82.9 1.9 %expert_product.11 = (f32[135168,128]{1,0:T(8,128)}, bf16[384,4096]{1,0:T(8,128)(2,1)}) custom-call(s32[8]{0:T(128)S(1)} %copy-done.9, s32[4]{0:T(128)S(1)} %select_reduce_fusion.1.places, bf16[384,1024]{1,0:T(8,128)(2,1)S(1)} %bitcast.5, bf16[256,512]{1,0:T(8,128)(2,1)S(1)} %get-tuple-element.113.refs_0_, ...), custom_call_target="tpu_custom_call", output_to_operand_aliasing={{0}: (7, {}), {1}: (8, {})} | custom-call | bytes 65536 | tf_op jit(solution)/shard_map/expert_product/pallas_call | solution.py:135
  87.8 2.5 %collective-permute-done.21.refs_2_ = bf16[256,512]{1,0:T(8,128)(2,1)S(1)} collective-permute-done((bf16[256,512]{1,0:T(8,128)(2,1)S(1)}, bf16[256,512]{1,0:T(8,128)(2,1)S(1)}, u32[]{:S(2)}, u32[]{:S(2)}) %collective-permute-start.21) | collective-permute-done | bytes 262176 | tf_op jit(solution)/shard_map/ppermute | solution.py:157
  90.6 1.7 %collective-permute-start.25 = (bf16[256,512]{1,0:T(8,128)(2,1)S(1)}, bf16[256,512]{1,0:T(8,128)(2,1)S(1)}, u32[]{:S(2)}, u32[]{:S(2)}) collective-permute-start(bf16[256,512]{1,0:T(8,128)(2,1)S(1)} %get-tuple-element.158.refs_0_), channel_id=1, source_target_pairs={{0,8},{8,0},{16,24},{24,16},{1,9},{9,1},{17,25},{25,17},{2,10},{10... | collective-permute-start | bytes 786440 | tf_op jit(solution)/shard_map/ppermute | solution.py:157
  92.6 3.3 %collective-permute-done.23.refs_1_ = bf16[256,512]{1,0:T(8,128)(2,1)S(1)} collective-permute-done((bf16[256,512]{1,0:T(8,128)(2,1)S(1)}, bf16[256,512]{1,0:T(8,128)(2,1)S(1)}, u32[]{:S(2)}, u32[]{:S(2)}) %collective-permute-start.23) | collective-permute-done | bytes 262176 | tf_op jit(solution)/shard_map/ppermute | solution.py:157
  96.2 1.9 %expert_product.12 = (f32[135168,128]{1,0:T(8,128)}, bf16[384,4096]{1,0:T(8,128)(2,1)}) custom-call(s32[8]{0:T(128)S(1)} %copy-done.9, s32[4]{0:T(128)S(1)} %select_reduce_fusion.1.places, bf16[384,1024]{1,0:T(8,128)(2,1)S(1)} %bitcast.6, bf16[256,512]{1,0:T(8,128)(2,1)S(1)} %get-tuple-element.141.refs_0_, ...), custom_call_target="tpu_custom_call", output_to_operand_aliasing={{0}: (7, {}), {1}: (8, {})} | custom-call | bytes 65536 | tf_op jit(solution)/shard_map/expert_product/pallas_call | solution.py:135
  98.1 1.9 %expert_product.13 = (f32[135168,128]{1,0:T(8,128)}, bf16[384,4096]{1,0:T(8,128)(2,1)}) custom-call(s32[8]{0:T(128)S(1)} %copy-done.9, s32[4]{0:T(128)S(1)} %select_reduce_fusion.1.places, bf16[384,1024]{1,0:T(8,128)(2,1)S(1)} %bitcast.7, bf16[256,512]{1,0:T(8,128)(2,1)S(1)} %get-tuple-element.142.refs_0_, ...), custom_call_target="tpu_custom_call", output_to_operand_aliasing={{0}: (7, {}), {1}: (8, {})} | custom-call | bytes 65536 | tf_op jit(solution)/shard_map/expert_product/pallas_call | solution.py:135
  103.5 2.5 %collective-permute-done.28.refs_2_ = bf16[256,512]{1,0:T(8,128)(2,1)S(1)} collective-permute-done((bf16[256,512]{1,0:T(8,128)(2,1)S(1)}, bf16[256,512]{1,0:T(8,128)(2,1)S(1)}, u32[]{:S(2)}, u32[]{:S(2)}) %collective-permute-start.28) | collective-permute-done | bytes 262176 | tf_op jit(solution)/shard_map/ppermute | solution.py:157
  107.1 5.6 %collective-permute-done.29.refs_1_ = bf16[256,512]{1,0:T(8,128)(2,1)S(1)} collective-permute-done((bf16[256,512]{1,0:T(8,128)(2,1)S(1)}, bf16[256,512]{1,0:T(8,128)(2,1)S(1)}, u32[]{:S(2)}, u32[]{:S(2)}) %collective-permute-start.29) | collective-permute-done | bytes 262176 | tf_op jit(solution)/shard_map/ppermute | solution.py:157
  112.7 1.9 %expert_product.14 = (f32[135168,128]{1,0:T(8,128)}, bf16[384,4096]{1,0:T(8,128)(2,1)}) custom-call(s32[8]{0:T(128)S(1)} %copy-done.9, s32[4]{0:T(128)S(1)} %select_reduce_fusion.1.places, bf16[384,1024]{1,0:T(8,128)(2,1)S(1)} %bitcast.8, bf16[256,512]{1,0:T(8,128)(2,1)S(1)} %get-tuple-element.158.refs_0_, ...), custom_call_target="tpu_custom_call", output_to_operand_aliasing={{0}: (7, {}), {1}: (8, {})} | custom-call | bytes 65536 | tf_op jit(solution)/shard_map/expert_product/pallas_call | solution.py:135
  114.6 1.9 %expert_product.15 = (f32[135168,128]{1,0:T(8,128)}, bf16[384,4096]{1,0:T(8,128)(2,1)}) custom-call(s32[8]{0:T(128)S(1)} %copy-done.9, s32[4]{0:T(128)S(1)} %select_reduce_fusion.1.places, bf16[384,1024]{1,0:T(8,128)(2,1)S(1)} %bitcast.9, bf16[256,512]{1,0:T(8,128)(2,1)S(1)} %get-tuple-element.145.refs_0_, ...), custom_call_target="tpu_custom_call", output_to_operand_aliasing={{0}: (7, {}), {1}: (8, {})} | custom-call | bytes 65536 | tf_op jit(solution)/shard_map/expert_product/pallas_call | solution.py:135
  (97 shorter events, 33.1 us)
Async XLA Ops:
  8.1 11.5 %collective-permute-start = (bf16[256,512]{1,0:T(8,128)(2,1)}, bf16[256,512]{1,0:T(8,128)(2,1)S(1)}, u32[]{:S(2)}, u32[]{:S(2)}) collective-permute-start(bf16[256,512]{1,0:T(8,128)(2,1)} %get-tuple-element.96), channel_id=1, source_target_pairs={{0,1},{1,0},{2,3},{3,2},{4,5},{5,4},{6,7},{7,6},{8,9},{9,8},{10,11... | collective-permute-start | bytes 786440 | tf_op jit(solution)/shard_map/ppermute | solution.py:157
  8.5 17.5 %collective-permute-start.1 = (bf16[256,512]{1,0:T(8,128)(2,1)}, bf16[256,512]{1,0:T(8,128)(2,1)S(1)}, u32[]{:S(2)}, u32[]{:S(2)}) collective-permute-start(bf16[256,512]{1,0:T(8,128)(2,1)} %get-tuple-element.102.refs_0_), channel_id=1, source_target_pairs={{0,8},{8,0},{16,24},{24,16},{1,9},{9,1},{17,25},{25,17},{2,10},{10... | collective-permute-start | bytes 786440 | tf_op jit(solution)/shard_map/ppermute | solution.py:157
  11.1 15.0 %collective-permute-start.2 = (bf16[256,512]{1,0:T(8,128)(2,1)}, bf16[256,512]{1,0:T(8,128)(2,1)S(1)}, u32[]{:S(2)}, u32[]{:S(2)}) collective-permute-start(bf16[256,512]{1,0:T(8,128)(2,1)} %get-tuple-element.102.refs_0_), channel_id=1, source_target_pairs={{0,16},{8,24},{16,0},{24,8},{1,17},{9,25},{17,1},{25,9},{2,18},{10... | collective-permute-start | bytes 786440 | tf_op jit(solution)/shard_map/ppermute | solution.py:157
  17.9 15.1 %collective-permute-start.3 = (bf16[256,512]{1,0:T(8,128)(2,1)}, bf16[256,512]{1,0:T(8,128)(2,1)S(1)}, u32[]{:S(2)}, u32[]{:S(2)}) collective-permute-start(bf16[256,512]{1,0:T(8,128)(2,1)} %get-tuple-element.108), channel_id=1, source_target_pairs={{0,2},{1,3},{2,0},{3,1},{4,6},{5,7},{6,4},{7,5},{8,10},{9,11},{10,... | collective-permute-start | bytes 786440 | tf_op jit(solution)/shard_map/ppermute | solution.py:157
  19.6 16.2 %collective-permute-start.4 = (bf16[256,512]{1,0:T(8,128)(2,1)S(1)}, bf16[256,512]{1,0:T(8,128)(2,1)S(1)}, u32[]{:S(2)}, u32[]{:S(2)}) collective-permute-start(bf16[256,512]{1,0:T(8,128)(2,1)S(1)} %get-tuple-element.109.refs_0_), channel_id=1, source_target_pairs={{0,8},{8,0},{16,24},{24,16},{1,9},{9,1},{17,25},{25,17},{2,10},{10... | collective-permute-start | bytes 786440 | tf_op jit(solution)/shard_map/ppermute | solution.py:157
  20.2 15.6 %collective-permute-start.5 = (bf16[256,512]{1,0:T(8,128)(2,1)S(1)}, bf16[256,512]{1,0:T(8,128)(2,1)S(1)}, u32[]{:S(2)}, u32[]{:S(2)}) collective-permute-start(bf16[256,512]{1,0:T(8,128)(2,1)S(1)} %get-tuple-element.109.refs_0_), channel_id=1, source_target_pairs={{0,16},{8,24},{16,0},{24,8},{1,17},{9,25},{17,1},{25,9},{2,18},{10... | collective-permute-start | bytes 786440 | tf_op jit(solution)/shard_map/ppermute | solution.py:157
  26.0 11.3 %collective-permute-start.6 = (bf16[256,512]{1,0:T(8,128)(2,1)S(1)}, bf16[256,512]{1,0:T(8,128)(2,1)S(1)}, u32[]{:S(2)}, u32[]{:S(2)}) collective-permute-start(bf16[256,512]{1,0:T(8,128)(2,1)S(1)} %copy-done.12), channel_id=1, source_target_pairs={{0,3},{1,2},{2,1},{3,0},{4,7},{5,6},{6,5},{7,4},{8,11},{9,10},{10,... | collective-permute-start | bytes 786440 | tf_op jit(solution)/shard_map/ppermute | solution.py:157
  26.1 11.2 %collective-permute-start.7 = (bf16[256,512]{1,0:T(8,128)(2,1)S(1)}, bf16[256,512]{1,0:T(8,128)(2,1)S(1)}, u32[]{:S(2)}, u32[]{:S(2)}) collective-permute-start(bf16[256,512]{1,0:T(8,128)(2,1)S(1)} %get-tuple-element.112.refs_1_), channel_id=1, source_target_pairs={{0,16},{8,24},{16,0},{24,8},{1,17},{9,25},{17,1},{25,9},{2,18},{10... | collective-permute-start | bytes 786440 | tf_op jit(solution)/shard_map/ppermute | solution.py:157
  33.1 21.5 %collective-permute-start.8 = (bf16[256,512]{1,0:T(8,128)(2,1)}, bf16[256,512]{1,0:T(8,128)(2,1)S(1)}, u32[]{:S(2)}, u32[]{:S(2)}) collective-permute-start(bf16[256,512]{1,0:T(8,128)(2,1)} %get-tuple-element.120), channel_id=1, source_target_pairs={{0,4},{1,5},{2,6},{3,7},{4,0},{5,1},{6,2},{7,3},{8,12},{9,13},{10,... | collective-permute-start | bytes 786440 | tf_op jit(solution)/shard_map/ppermute | solution.py:157
  35.8 21.3 %collective-permute-start.9 = (bf16[256,512]{1,0:T(8,128)(2,1)S(1)}, bf16[256,512]{1,0:T(8,128)(2,1)S(1)}, u32[]{:S(2)}, u32[]{:S(2)}) collective-permute-start(bf16[256,512]{1,0:T(8,128)(2,1)S(1)} %get-tuple-element.115.refs_2_), channel_id=1, source_target_pairs={{0,8},{8,0},{16,24},{24,16},{1,9},{9,1},{17,25},{25,17},{2,10},{10... | collective-permute-start | bytes 786440 | tf_op jit(solution)/shard_map/ppermute | solution.py:157
  37.3 27.1 %collective-permute-start.10 = (bf16[256,512]{1,0:T(8,128)(2,1)}, bf16[256,512]{1,0:T(8,128)(2,1)S(1)}, u32[]{:S(2)}, u32[]{:S(2)}) collective-permute-start(bf16[256,512]{1,0:T(8,128)(2,1)} %get-tuple-element.125), channel_id=1, source_target_pairs={{0,5},{1,4},{2,7},{3,6},{4,1},{5,0},{6,3},{7,2},{8,13},{9,12},{10,... | collective-permute-start | bytes 786440 | tf_op jit(solution)/shard_map/ppermute | solution.py:157
  38.0 26.8 %collective-permute-start.12 = (bf16[256,512]{1,0:T(8,128)(2,1)S(1)}, bf16[256,512]{1,0:T(8,128)(2,1)S(1)}, u32[]{:S(2)}, u32[]{:S(2)}) collective-permute-start(bf16[256,512]{1,0:T(8,128)(2,1)S(1)} %get-tuple-element.113.refs_0_), channel_id=1, source_target_pairs={{0,16},{8,24},{16,0},{24,8},{1,17},{9,25},{17,1},{25,9},{2,18},{10... | collective-permute-start | bytes 786440 | tf_op jit(solution)/shard_map/ppermute | solution.py:157
  38.5 26.3 %collective-permute-start.11 = (bf16[256,512]{1,0:T(8,128)(2,1)S(1)}, bf16[256,512]{1,0:T(8,128)(2,1)S(1)}, u32[]{:S(2)}, u32[]{:S(2)}) collective-permute-start(bf16[256,512]{1,0:T(8,128)(2,1)S(1)} %get-tuple-element.126.refs_0_), channel_id=1, source_target_pairs={{0,8},{8,0},{16,24},{24,16},{1,9},{9,1},{17,25},{25,17},{2,10},{10... | collective-permute-start | bytes 786440 | tf_op jit(solution)/shard_map/ppermute | solution.py:157
  54.6 13.4 %collective-permute-start.15 = (bf16[256,512]{1,0:T(8,128)(2,1)S(1)}, bf16[256,512]{1,0:T(8,128)(2,1)S(1)}, u32[]{:S(2)}, u32[]{:S(2)}) collective-permute-start(bf16[256,512]{1,0:T(8,128)(2,1)S(1)} %copy-done.11), channel_id=1, source_target_pairs={{0,6},{1,7},{2,4},{3,5},{4,2},{5,3},{6,0},{7,1},{8,14},{9,15},{10,... | collective-permute-start | bytes 786440 | tf_op jit(solution)/shard_map/ppermute | solution.py:157
  57.1 11.4 %collective-permute-start.14 = (bf16[256,512]{1,0:T(8,128)(2,1)S(1)}, bf16[256,512]{1,0:T(8,128)(2,1)S(1)}, u32[]{:S(2)}, u32[]{:S(2)}) collective-permute-start(bf16[256,512]{1,0:T(8,128)(2,1)S(1)} %get-tuple-element.113.refs_0_), channel_id=1, source_target_pairs={{0,8},{8,0},{16,24},{24,16},{1,9},{9,1},{17,25},{25,17},{2,10},{10... | collective-permute-start | bytes 786440 | tf_op jit(solution)/shard_map/ppermute | solution.py:157
  64.9 14.2 %collective-permute-start.16 = (bf16[256,512]{1,0:T(8,128)(2,1)S(1)}, bf16[256,512]{1,0:T(8,128)(2,1)S(1)}, u32[]{:S(2)}, u32[]{:S(2)}) collective-permute-start(bf16[256,512]{1,0:T(8,128)(2,1)S(1)} %get-tuple-element.132.refs_1_), channel_id=1, source_target_pairs={{0,16},{8,24},{16,0},{24,8},{1,17},{9,25},{17,1},{25,9},{2,18},{10... | collective-permute-start | bytes 786440 | tf_op jit(solution)/shard_map/ppermute | solution.py:157
  66.5 14.0 %collective-permute-start.17 = (bf16[256,512]{1,0:T(8,128)(2,1)S(1)}, bf16[256,512]{1,0:T(8,128)(2,1)S(1)}, u32[]{:S(2)}, u32[]{:S(2)}) collective-permute-start(bf16[256,512]{1,0:T(8,128)(2,1)S(1)} %get-tuple-element.129.refs_2_), channel_id=1, source_target_pairs={{0,8},{8,0},{16,24},{24,16},{1,9},{9,1},{17,25},{25,17},{2,10},{10... | collective-permute-start | bytes 786440 | tf_op jit(solution)/shard_map/ppermute | solution.py:157
  68.0 16.8 %collective-permute-start.19 = (bf16[256,512]{1,0:T(8,128)(2,1)S(1)}, bf16[256,512]{1,0:T(8,128)(2,1)S(1)}, u32[]{:S(2)}, u32[]{:S(2)}) collective-permute-start(bf16[256,512]{1,0:T(8,128)(2,1)S(1)} %get-tuple-element.142.refs_0_), channel_id=1, source_target_pairs={{0,16},{8,24},{16,0},{24,8},{1,17},{9,25},{17,1},{25,9},{2,18},{10... | collective-permute-start | bytes 786440 | tf_op jit(solution)/shard_map/ppermute | solution.py:157
  68.5 16.3 %collective-permute-start.18 = (bf16[256,512]{1,0:T(8,128)(2,1)S(1)}, bf16[256,512]{1,0:T(8,128)(2,1)S(1)}, u32[]{:S(2)}, u32[]{:S(2)}) collective-permute-start(bf16[256,512]{1,0:T(8,128)(2,1)S(1)} %get-tuple-element.141.refs_0_), channel_id=1, source_target_pairs={{0,8},{8,0},{16,24},{24,16},{1,9},{9,1},{17,25},{25,17},{2,10},{10... | collective-permute-start | bytes 786440 | tf_op jit(solution)/shard_map/ppermute | solution.py:157
  73.4 13.4 %collective-permute-start.20 = (bf16[256,512]{1,0:T(8,128)(2,1)S(1)}, bf16[256,512]{1,0:T(8,128)(2,1)S(1)}, u32[]{:S(2)}, u32[]{:S(2)}) collective-permute-start(bf16[256,512]{1,0:T(8,128)(2,1)S(1)} %copy-done.10), channel_id=1, source_target_pairs={{0,7},{1,6},{2,5},{3,4},{4,3},{5,2},{6,1},{7,0},{8,15},{9,14},{10,... | collective-permute-start | bytes 786440 | tf_op jit(solution)/shard_map/ppermute | solution.py:157
  90.3 11.2 %collective-permute-start.26 = (bf16[256,512]{1,0:T(8,128)(2,1)S(1)}, bf16[256,512]{1,0:T(8,128)(2,1)S(1)}, u32[]{:S(2)}, u32[]{:S(2)}) collective-permute-start(bf16[256,512]{1,0:T(8,128)(2,1)S(1)} %get-tuple-element.145.refs_0_), channel_id=1, source_target_pairs={{0,16},{8,24},{16,0},{24,8},{1,17},{9,25},{17,1},{25,9},{2,18},{10... | collective-permute-start | bytes 786440 | tf_op jit(solution)/shard_map/ppermute | solution.py:157
  92.3 13.7 %collective-permute-start.28 = (bf16[256,512]{1,0:T(8,128)(2,1)S(1)}, bf16[256,512]{1,0:T(8,128)(2,1)S(1)}, u32[]{:S(2)}, u32[]{:S(2)}) collective-permute-start(bf16[256,512]{1,0:T(8,128)(2,1)S(1)} %get-tuple-element.145.refs_0_), channel_id=1, source_target_pairs={{0,8},{8,0},{16,24},{24,16},{1,9},{9,1},{17,25},{25,17},{2,10},{10... | collective-permute-start | bytes 786440 | tf_op jit(solution)/shard_map/ppermute | solution.py:157
  95.9 11.2 %collective-permute-start.27 = (bf16[256,512]{1,0:T(8,128)(2,1)S(1)}, bf16[256,512]{1,0:T(8,128)(2,1)S(1)}, u32[]{:S(2)}, u32[]{:S(2)}) collective-permute-start(bf16[256,512]{1,0:T(8,128)(2,1)S(1)} %get-tuple-element.158.refs_0_), channel_id=1, source_target_pairs={{0,16},{8,24},{16,0},{24,8},{1,17},{9,25},{17,1},{25,9},{2,18},{10... | collective-permute-start | bytes 786440 | tf_op jit(solution)/shard_map/ppermute | solution.py:157
  101.5 11.2 %collective-permute-start.29 = (bf16[256,512]{1,0:T(8,128)(2,1)S(1)}, bf16[256,512]{1,0:T(8,128)(2,1)S(1)}, u32[]{:S(2)}, u32[]{:S(2)}) collective-permute-start(bf16[256,512]{1,0:T(8,128)(2,1)S(1)} %get-tuple-element.163.refs_1_), channel_id=1, source_target_pairs={{0,16},{8,24},{16,0},{24,8},{1,17},{9,25},{17,1},{25,9},{2,18},{10... | collective-permute-start | bytes 786440 | tf_op jit(solution)/shard_map/ppermute | solution.py:157
  (21 other events, 151.3 us)

commit v4 on v3

--- a/solution.py
+++ b/solution.py
@@ -53,45 +53,44 @@
 
 def adam_kernel(blocks, passed, expert_of, master, gradient, first, second, *refs):
     new_master, new_first, new_second, *sends = refs[passed : passed + 3 + blocks]
+    _, rows, columns = master.shape
+    places = [
+        (slice(i, i + QB), slice(j, j + QB)) for i in range(0, rows, QB) for j in range(0, columns, QB)
+    ]
+    peaks = []
+    for place in places:
+        at = (0, *place)
+        grad = gradient[at].astype(jnp.float32)
+        moment_one = beta_one * first[at].astype(jnp.float32) + (1.0 - beta_one) * grad
+        moment_two = beta_two * second[at].astype(jnp.float32) + ((1.0 - beta_two) * grad) * grad
+        new_first[at] = moment_one.astype(jnp.bfloat16)
+        new_second[at] = moment_two.astype(jnp.bfloat16)
+        root = moment_two * lax.rsqrt(moment_two) + root_epsilon
+        inverse = pl.reciprocal(root, approx=True)
+        inverse = inverse * (2.0 - root * inverse)
+        updated = master[at] - (step_size * moment_one) * inverse
+        new_master[at] = updated
+        peaks.append(jnp.max(jnp.abs(updated), axis=0, keepdims=True))
+    largest = jnp.max(jnp.concatenate(peaks, axis=0), axis=1, keepdims=True)
+    scale = ((largest + scale_epsilon) * (1.0 / quant_limit)).astype(jnp.bfloat16)
+    scale = jnp.broadcast_to(scale.astype(jnp.float32), (len(places), QB))
+    inverse_scale = 1.0 / scale
     for number in range(blocks):
 
         @pl.when(pl.program_id(0) == number)
         def _():
-            for start in range(0, master.shape[2], QB):
-                at = (0, slice(None), slice(start, start + QB))
-                grad = gradient[at].astype(jnp.float32)
-                moment_one = beta_one * first[at].astype(jnp.float32) + (1.0 - beta_one) * grad
-                moment_two = beta_two * second[at].astype(jnp.float32) + (
-                    ((1.0 - beta_two) * grad) * grad
-                )
-                new_first[at] = moment_one.astype(jnp.bfloat16)
-                new_second[at] = moment_two.astype(jnp.bfloat16)
-                root = moment_two * lax.rsqrt(moment_two) + root_epsilon
-                inverse = pl.reciprocal(root, approx=True)
-                inverse = inverse * (2.0 - root * inverse)
-                updated = master[at] - (step_size * moment_one) * inverse
-                new_master[at] = updated
-                largest = jnp.max(jnp.abs(updated), axis=0, keepdims=True)
-                largest = jnp.max(largest, axis=1, keepdims=True)
-                scale = ((largest + scale_epsilon) * (1.0 / quant_limit)).astype(jnp.bfloat16)
-                scale = jnp.broadcast_to(scale.astype(jnp.float32), (1, QB))
-                quantized = (updated * (1.0 / scale)).astype(jnp.bfloat16)
-                value = quantized.astype(jnp.float32) * scale
-                sends[number][:, start : start + QB] = value.astype(jnp.bfloat16)
-
-
-def adam_blocks(expert_of, arrays, carried, token, fenced):
+            for row, place in enumerate(places):
+                one = slice(row, row + 1)
+                quantized = (new_master[(0, *place)] * inverse_scale[one]).astype(jnp.bfloat16)
+                value = quantized.astype(jnp.float32) * scale[one]
+                sends[number][place] = value.astype(jnp.bfloat16)
+
+
+def adam_blocks(base, blocks, expert_of, arrays, carried, token, fenced):
     _, rows, columns = arrays[0].shape
-    blocks = expert_of.shape[0]
     passed = len(carried) + len(token)
-
-    def sent(number):
-        def place(e, i, expert_of):
-            return jnp.where(e == number, i, jnp.where(e > number, rows // QB - 1, 0)), 0
-
-        return pl.BlockSpec((QB, columns), place)
-
-    here = pl.BlockSpec((1, QB, columns), lambda e, i, expert_of: (expert_of[e], i, 0))
+    here = pl.BlockSpec((1, rows, columns), lambda i, expert_of: (expert_of[base + i], 0, 0))
+    sent = pl.BlockSpec((rows, columns), lambda i, expert_of: (0, 0))
     made = [like(arrays[0]), like(arrays[2]), like(arrays[3])]
     made += [jax.ShapeDtypeStruct((rows, columns), jnp.bfloat16)] * blocks
     aliases = {5 + i: i for i in range(len(carried))}
@@ -101,9 +100,9 @@
         functools.partial(adam_kernel, blocks, passed),
         grid_spec=pltpu.PrefetchScalarGridSpec(
             num_scalar_prefetch=1,
-            grid=(blocks, rows // QB),
+            grid=(blocks,),
             in_specs=[here] * 4 + [WHOLE] * passed,
-            out_specs=[here] * 3 + [sent(number) for number in range(blocks)] + [WHOLE] * fenced,
+            out_specs=[here] * 3 + [sent] * blocks + [WHOLE] * fenced,
         ),
         out_shape=made + [jax.ShapeDtypeStruct(TOKEN, jnp.float32)] * fenced,
         input_output_aliases=aliases,
@@ -180,12 +179,11 @@
     made, due, ready = {}, collections.defaultdict(list), set()
     state = {"adam": (), "token": (), "out": ()}
 
-    def adam(pair):
-        picked = expert_of[2 * pair : 2 * pair + 2]
+    def adam(first, blocks):
         state["adam"], sends, state["token"] = adam_blocks(
-            picked, arrays, tuple(state["adam"]), state["token"], fenced
-        )
-        made[2 * pair], made[2 * pair + 1] = sends
+            first, blocks, expert_of, arrays, tuple(state["adam"]), state["token"], fenced
+        )
+        made.update(zip(range(first, first + blocks), sends))
 
     def deliver(block):
         held[block][0] = swap(made[block], "shard", shards, block) if block else made[block]
@@ -221,7 +219,7 @@
             steps[3 * pair + 1] = [(even, 0, 2), (odd, 0, 1)]
             steps[3 * pair + 2] = [(even, 1, 2), (odd, 2, 1)]
         for block in range(2, shards):
-            moves[max(block - 2, min(2 * block - 7, 3 * (block // 2) - 2))].append(block)
+            moves[max((block - 1) // 2, min(2 * block - 7, 3 * (block // 2) - 2))].append(block)
 
         def start(step):
             for block in moves[step]:
@@ -231,25 +229,25 @@
                 send(block, member, bit)
                 due[step + 2].append((block, member ^ bit))
 
-        adam(0)
+        adam(0, 2)
         deliver(0)
         deliver(1)
         ready.add((0, 0))
         due[0].append((1, 0))
         start(-1)
-        adam(1)
+        adam(2, 2)
         for step in range(3 * pairs + 2):
             arrived(due[step])
             start(step)
             if step + 2 < pairs:
-                adam(step + 2)
+                adam(2 * step + 4, 2)
             for block in list(waiting):
                 if all((block, member) in ready for member in range(replicas)):
                     multiply(block)
                     waiting.remove(block)
     else:
         for pair in range(pairs):
-            adam(pair)
+            adam(2 * pair, 2)
         for block in range(shards):
             deliver(block)
             for number in range(len(bits)):

time: 117 us -> 109 us (0.932)
  waiting for transfers between devices: 40.6 us -> 34.3 us
  Pallas kernels: 36.3 us -> 32.5 us
  starting transfers between devices: 33 us -> 35.8 us
    ppermute x31, waiting for transfers between devices: 40.6 us -> 34.3 us  [swap(): return lax.ppermute(value, axis, [(i, i ^ mask) for i in range(size)])]
    pallas_call x4, Pallas kernels: 21.3 us -> 17.5 us  [adam_blocks(): pl.pallas_call(functools.partial(adam_kernel, blocks, passed), grid_spec=...]
    ppermute x31, starting transfers between devices: 33 us -> 35.8 us  [swap(): return lax.ppermute(value, axis, [(i, i ^ mask) for i in range(size)])]
  transfers between devices with their start and end apart: 31 -> 31, of which waited for: 11 -> 11; matrix products, arithmetic and copies ran while one was open for 0% -> 0% of each run, Pallas kernels for 23% -> 22%
where the time goes in v4:
time: 109 us
  starting transfers between devices  35.8 us (33%)
  waiting for transfers between devices  34.3 us (31%)
  Pallas kernels  32.5 us (30%)
  local copies, waits for them, and re-layouts  3.82 us (4%)
  other arithmetic  1.56 us (1%)
    ppermute x31, starting transfers between devices, swap(): return lax.ppermute(value, axis, [(i, i ^ mask) for i in range(size)])  35.8 us
    ppermute x31, waiting for transfers between devices, swap(): return lax.ppermute(value, axis, [(i, i ^ mask) for i in range(size)])  34.3 us
    pallas_call x4, Pallas kernels, adam_blocks(): pl.pallas_call(functools.partial(adam_kernel, blocks, passed), grid_spec=...  17.5 us
    pallas_call x8, Pallas kernels, product(): pl.pallas_call(functools.partial(product_kernel, number, slabs), grid_spe...  14.9 us
    unnamed x28, local copies, waits for them, and re-layouts  3.82 us
  transfers between devices with their start and end apart: 31, of which 11 were waited for; matrix products, arithmetic and copies ran while one was open for 0% of the time, Pallas kernels for 22%

profile of v4, /device:TPU:0, one launch (start us, length us, event | category | flops | bytes accessed | tf_op | source)
XLA Modules:
  0.0 108.7 jit_solution(13838676012635618229)
XLA Ops:
  2.5 4.4 %adam_quantize.4 = (f32[8,256,512]{2,1,0:T(8,128)}, bf16[8,256,512]{2,1,0:T(8,128)(2,1)}, bf16[8,256,512]{2,1,0:T(8,128)(2,1)}, bf16[256,512]{1,0:T(8,128)(2,1)}...) custom-call(s32[8]{0:T(128)} %select_reduce_fusion.expert_of, f32[8,256,512]{2,1,0:T(8,128)} %master.7, ...), custom_call_target="tpu_custom_call" | custom-call | bytes 65536 | tf_op jit(solution)/shard_map/adam_quantize/pallas_call | solution.py:99
  7.4 2.6 %collective-permute-start.1 = (bf16[256,512]{1,0:T(8,128)(2,1)}, bf16[256,512]{1,0:T(8,128)(2,1)S(1)}, u32[]{:S(2)}, u32[]{:S(2)}) collective-permute-start(bf16[256,512]{1,0:T(8,128)(2,1)} %get-tuple-element.102.refs_0_), channel_id=1, source_target_pairs={{0,8},{8,0},{16,24},{24,16},{1,9},{9,1},{17,25},{25,17},{2,10},{10... | collective-permute-start | bytes 786440 | tf_op jit(solution)/shard_map/ppermute | solution.py:156
  11.5 4.4 %adam_quantize.5 = (f32[8,256,512]{2,1,0:T(8,128)}, bf16[8,256,512]{2,1,0:T(8,128)(2,1)}, bf16[8,256,512]{2,1,0:T(8,128)(2,1)}, bf16[256,512]{1,0:T(8,128)(2,1)}...) custom-call(s32[8]{0:T(128)} %select_reduce_fusion.expert_of, ...), custom_call_target="tpu_custom_call", output_to_operand_aliasing={{0}: (5, {}), {1}: (6, {}), {2}: (7, {}), {5}: (8, {})} | custom-call | bytes 65536 | tf_op jit(solution)/shard_map/adam_quantize/pallas_call | solution.py:99
  15.9 1.6 %collective-permute-start.3 = (bf16[256,512]{1,0:T(8,128)(2,1)}, bf16[256,512]{1,0:T(8,128)(2,1)S(1)}, u32[]{:S(2)}, u32[]{:S(2)}) collective-permute-start(bf16[256,512]{1,0:T(8,128)(2,1)} %get-tuple-element.108), channel_id=1, source_target_pairs={{0,2},{1,3},{2,0},{3,1},{4,6},{5,7},{6,4},{7,5},{8,10},{9,11},{10,... | collective-permute-start | bytes 786440 | tf_op jit(solution)/shard_map/ppermute | solution.py:156
  18.7 4.4 %adam_quantize.6 = (f32[8,256,512]{2,1,0:T(8,128)}, bf16[8,256,512]{2,1,0:T(8,128)(2,1)}, bf16[8,256,512]{2,1,0:T(8,128)(2,1)}, bf16[256,512]{1,0:T(8,128)(2,1)}...) custom-call(s32[8]{0:T(128)} %select_reduce_fusion.expert_of, ...), custom_call_target="tpu_custom_call", output_to_operand_aliasing={{0}: (5, {}), {1}: (6, {}), {2}: (7, {}), {5}: (8, {})} | custom-call | bytes 65536 | tf_op jit(solution)/shard_map/adam_quantize/pallas_call | solution.py:99
  24.8 2.6 %collective-permute-start.7 = (bf16[256,512]{1,0:T(8,128)(2,1)S(1)}, bf16[256,512]{1,0:T(8,128)(2,1)S(1)}, u32[]{:S(2)}, u32[]{:S(2)}) collective-permute-start(bf16[256,512]{1,0:T(8,128)(2,1)S(1)} %copy-done.12), channel_id=1, source_target_pairs={{0,4},{1,5},{2,6},{3,7},{4,0},{5,1},{6,2},{7,3},{8,12},{9,13},{10,... | collective-permute-start | bytes 786440 | tf_op jit(solution)/shard_map/ppermute | solution.py:156
  27.4 4.4 %adam_quantize.7 = (f32[8,256,512]{2,1,0:T(8,128)}, bf16[8,256,512]{2,1,0:T(8,128)(2,1)}, bf16[8,256,512]{2,1,0:T(8,128)(2,1)}, bf16[256,512]{1,0:T(8,128)(2,1)}...) custom-call(s32[8]{0:T(128)} %select_reduce_fusion.expert_of, ...), custom_call_target="tpu_custom_call", output_to_operand_aliasing={{0}: (5, {}), {1}: (6, {}), {2}: (7, {}), {5}: (8, {})} | custom-call | bytes 65536 | tf_op jit(solution)/shard_map/adam_quantize/pallas_call | solution.py:99
  33.4 2.2 %collective-permute-done.6.refs_1_ = bf16[256,512]{1,0:T(8,128)(2,1)S(1)} collective-permute-done((bf16[256,512]{1,0:T(8,128)(2,1)S(1)}, bf16[256,512]{1,0:T(8,128)(2,1)S(1)}, u32[]{:S(2)}, u32[]{:S(2)}) %collective-permute-start.6) | collective-permute-done | bytes 262176 | tf_op jit(solution)/shard_map/ppermute | solution.py:156
  35.6 10.5 %collective-permute-done.7.refs_2_ = bf16[256,512]{1,0:T(8,128)(2,1)S(1)} collective-permute-done((bf16[256,512]{1,0:T(8,128)(2,1)S(1)}, bf16[256,512]{1,0:T(8,128)(2,1)S(1)}, u32[]{:S(2)}, u32[]{:S(2)}) %collective-permute-start.7) | collective-permute-done | bytes 262176 | tf_op jit(solution)/shard_map/ppermute | solution.py:156
  49.2 3.2 %collective-permute-start.15 = (bf16[256,512]{1,0:T(8,128)(2,1)}, bf16[256,512]{1,0:T(8,128)(2,1)S(1)}, u32[]{:S(2)}, u32[]{:S(2)}) collective-permute-start(bf16[256,512]{1,0:T(8,128)(2,1)} %get-tuple-element.131), channel_id=1, source_target_pairs={{0,6},{1,7},{2,4},{3,5},{4,2},{5,3},{6,0},{7,1},{8,14},{9,15},{10,... | collective-permute-start | bytes 786440 | tf_op jit(solution)/shard_map/ppermute | solution.py:156
  54.3 1.9 %expert_product.8 = (f32[135168,128]{1,0:T(8,128)}, bf16[384,4096]{1,0:T(8,128)(2,1)}) custom-call(s32[8]{0:T(128)S(1)} %copy-done.9, s32[4]{0:T(128)S(1)} %select_reduce_fusion.1.places, bf16[384,1024]{1,0:T(8,128)(2,1)S(1)} %bitcast.2, bf16[256,512]{1,0:T(8,128)(2,1)S(1)} %copy-done.7, ...), custom_call_target="tpu_custom_call", output_to_operand_aliasing={{0}: (7, {})} | custom-call | bytes 65536 | tf_op jit(solution)/shard_map/expert_product/pallas_call | solution.py:134
  57.2 1.9 %expert_product.9 = (f32[135168,128]{1,0:T(8,128)}, bf16[384,4096]{1,0:T(8,128)(2,1)}) custom-call(s32[8]{0:T(128)S(1)} %copy-done.9, s32[4]{0:T(128)S(1)} %select_reduce_fusion.1.places, bf16[384,1024]{1,0:T(8,128)(2,1)S(1)} %bitcast.3, bf16[256,512]{1,0:T(8,128)(2,1)S(1)} %copy-done.6, ...), custom_call_target="tpu_custom_call", output_to_operand_aliasing={{0}: (7, {}), {1}: (8, {})} | custom-call | bytes 65536 | tf_op jit(solution)/shard_map/expert_product/pallas_call | solution.py:134
  63.1 2.3 %collective-permute-done.14.refs_2_ = bf16[256,512]{1,0:T(8,128)(2,1)S(1)} collective-permute-done((bf16[256,512]{1,0:T(8,128)(2,1)S(1)}, bf16[256,512]{1,0:T(8,128)(2,1)S(1)}, u32[]{:S(2)}, u32[]{:S(2)}) %collective-permute-start.14) | collective-permute-done | bytes 262176 | tf_op jit(solution)/shard_map/ppermute | solution.py:156
  68.3 5.6 %collective-permute-done.16.refs_2_ = bf16[256,512]{1,0:T(8,128)(2,1)S(1)} collective-permute-done((bf16[256,512]{1,0:T(8,128)(2,1)S(1)}, bf16[256,512]{1,0:T(8,128)(2,1)S(1)}, u32[]{:S(2)}, u32[]{:S(2)}) %collective-permute-start.16) | collective-permute-done | bytes 262176 | tf_op jit(solution)/shard_map/ppermute | solution.py:156
  76.2 1.9 %expert_product.10 = (f32[135168,128]{1,0:T(8,128)}, bf16[384,4096]{1,0:T(8,128)(2,1)}) custom-call(s32[8]{0:T(128)S(1)} %copy-done.9, s32[4]{0:T(128)S(1)} %select_reduce_fusion.1.places, bf16[384,1024]{1,0:T(8,128)(2,1)S(1)} %bitcast.4, bf16[256,512]{1,0:T(8,128)(2,1)S(1)} %get-tuple-element.126.refs_0_, ...), custom_call_target="tpu_custom_call", output_to_operand_aliasing={{0}: (7, {}), {1}: (8, {})} | custom-call | bytes 65536 | tf_op jit(solution)/shard_map/expert_product/pallas_call | solution.py:134
  78.1 1.9 %expert_product.11 = (f32[135168,128]{1,0:T(8,128)}, bf16[384,4096]{1,0:T(8,128)(2,1)}) custom-call(s32[8]{0:T(128)S(1)} %copy-done.9, s32[4]{0:T(128)S(1)} %select_reduce_fusion.1.places, bf16[384,1024]{1,0:T(8,128)(2,1)S(1)} %bitcast.5, bf16[256,512]{1,0:T(8,128)(2,1)S(1)} %get-tuple-element.114.refs_0_, ...), custom_call_target="tpu_custom_call", output_to_operand_aliasing={{0}: (7, {}), {1}: (8, {})} | custom-call | bytes 65536 | tf_op jit(solution)/shard_map/expert_product/pallas_call | solution.py:134
  81.8 3.3 %collective-permute-done.21.refs_2_ = bf16[256,512]{1,0:T(8,128)(2,1)S(1)} collective-permute-done((bf16[256,512]{1,0:T(8,128)(2,1)S(1)}, bf16[256,512]{1,0:T(8,128)(2,1)S(1)}, u32[]{:S(2)}, u32[]{:S(2)}) %collective-permute-start.21) | collective-permute-done | bytes 262176 | tf_op jit(solution)/shard_map/ppermute | solution.py:156
  88.7 2.1 %collective-permute-done.23.refs_1_ = bf16[256,512]{1,0:T(8,128)(2,1)S(1)} collective-permute-done((bf16[256,512]{1,0:T(8,128)(2,1)S(1)}, bf16[256,512]{1,0:T(8,128)(2,1)S(1)}, u32[]{:S(2)}, u32[]{:S(2)}) %collective-permute-start.23) | collective-permute-done | bytes 262176 | tf_op jit(solution)/shard_map/ppermute | solution.py:156
  92.3 1.9 %expert_product.12 = (f32[135168,128]{1,0:T(8,128)}, bf16[384,4096]{1,0:T(8,128)(2,1)}) custom-call(s32[8]{0:T(128)S(1)} %copy-done.9, s32[4]{0:T(128)S(1)} %select_reduce_fusion.1.places, bf16[384,1024]{1,0:T(8,128)(2,1)S(1)} %bitcast.6, bf16[256,512]{1,0:T(8,128)(2,1)S(1)} %copy-done.4, ...), custom_call_target="tpu_custom_call", output_to_operand_aliasing={{0}: (7, {}), {1}: (8, {})} | custom-call | bytes 65536 | tf_op jit(solution)/shard_map/expert_product/pallas_call | solution.py:134
  94.2 1.9 %expert_product.13 = (f32[135168,128]{1,0:T(8,128)}, bf16[384,4096]{1,0:T(8,128)(2,1)}) custom-call(s32[8]{0:T(128)S(1)} %copy-done.9, s32[4]{0:T(128)S(1)} %select_reduce_fusion.1.places, bf16[384,1024]{1,0:T(8,128)(2,1)S(1)} %bitcast.7, bf16[256,512]{1,0:T(8,128)(2,1)S(1)} %get-tuple-element.142.refs_0_, ...), custom_call_target="tpu_custom_call", output_to_operand_aliasing={{0}: (7, {}), {1}: (8, {})} | custom-call | bytes 65536 | tf_op jit(solution)/shard_map/expert_product/pallas_call | solution.py:134
  98.7 2.4 %collective-permute-done.28.refs_2_ = bf16[256,512]{1,0:T(8,128)(2,1)S(1)} collective-permute-done((bf16[256,512]{1,0:T(8,128)(2,1)S(1)}, bf16[256,512]{1,0:T(8,128)(2,1)S(1)}, u32[]{:S(2)}, u32[]{:S(2)}) %collective-permute-start.28) | collective-permute-done | bytes 262176 | tf_op jit(solution)/shard_map/ppermute | solution.py:156
  102.0 3.0 %collective-permute-done.29.refs_1_ = bf16[256,512]{1,0:T(8,128)(2,1)S(1)} collective-permute-done((bf16[256,512]{1,0:T(8,128)(2,1)S(1)}, bf16[256,512]{1,0:T(8,128)(2,1)S(1)}, u32[]{:S(2)}, u32[]{:S(2)}) %collective-permute-start.29) | collective-permute-done | bytes 262176 | tf_op jit(solution)/shard_map/ppermute | solution.py:156
  105.0 1.9 %expert_product.14 = (f32[135168,128]{1,0:T(8,128)}, bf16[384,4096]{1,0:T(8,128)(2,1)}) custom-call(s32[8]{0:T(128)S(1)} %copy-done.9, s32[4]{0:T(128)S(1)} %select_reduce_fusion.1.places, bf16[384,1024]{1,0:T(8,128)(2,1)S(1)} %bitcast.8, bf16[256,512]{1,0:T(8,128)(2,1)S(1)} %get-tuple-element.158.refs_0_, ...), custom_call_target="tpu_custom_call", output_to_operand_aliasing={{0}: (7, {}), {1}: (8, {})} | custom-call | bytes 65536 | tf_op jit(solution)/shard_map/expert_product/pallas_call | solution.py:134
  106.9 1.9 %expert_product.15 = (f32[135168,128]{1,0:T(8,128)}, bf16[384,4096]{1,0:T(8,128)(2,1)}) custom-call(s32[8]{0:T(128)S(1)} %copy-done.9, s32[4]{0:T(128)S(1)} %select_reduce_fusion.1.places, bf16[384,1024]{1,0:T(8,128)(2,1)S(1)} %bitcast.9, bf16[256,512]{1,0:T(8,128)(2,1)S(1)} %get-tuple-element.145.refs_0_, ...), custom_call_target="tpu_custom_call", output_to_operand_aliasing={{0}: (7, {}), {1}: (8, {})} | custom-call | bytes 65536 | tf_op jit(solution)/shard_map/expert_product/pallas_call | solution.py:134
  (96 shorter events, 34.1 us)
Async XLA Ops:
  6.9 10.6 %collective-permute-start = (bf16[256,512]{1,0:T(8,128)(2,1)}, bf16[256,512]{1,0:T(8,128)(2,1)S(1)}, u32[]{:S(2)}, u32[]{:S(2)}) collective-permute-start(bf16[256,512]{1,0:T(8,128)(2,1)} %get-tuple-element.96), channel_id=1, source_target_pairs={{0,1},{1,0},{2,3},{3,2},{4,5},{5,4},{6,7},{7,6},{8,9},{9,8},{10,11... | collective-permute-start | bytes 786440 | tf_op jit(solution)/shard_map/ppermute | solution.py:156
  7.4 15.6 %collective-permute-start.1 = (bf16[256,512]{1,0:T(8,128)(2,1)}, bf16[256,512]{1,0:T(8,128)(2,1)S(1)}, u32[]{:S(2)}, u32[]{:S(2)}) collective-permute-start(bf16[256,512]{1,0:T(8,128)(2,1)} %get-tuple-element.102.refs_0_), channel_id=1, source_target_pairs={{0,8},{8,0},{16,24},{24,16},{1,9},{9,1},{17,25},{25,17},{2,10},{10... | collective-permute-start | bytes 786440 | tf_op jit(solution)/shard_map/ppermute | solution.py:156
  10.0 13.2 %collective-permute-start.2 = (bf16[256,512]{1,0:T(8,128)(2,1)}, bf16[256,512]{1,0:T(8,128)(2,1)S(1)}, u32[]{:S(2)}, u32[]{:S(2)}) collective-permute-start(bf16[256,512]{1,0:T(8,128)(2,1)} %get-tuple-element.102.refs_0_), channel_id=1, source_target_pairs={{0,16},{8,24},{16,0},{24,8},{1,17},{9,25},{17,1},{25,9},{2,18},{10... | collective-permute-start | bytes 786440 | tf_op jit(solution)/shard_map/ppermute | solution.py:156
  17.6 14.2 %collective-permute-start.4 = (bf16[256,512]{1,0:T(8,128)(2,1)S(1)}, bf16[256,512]{1,0:T(8,128)(2,1)S(1)}, u32[]{:S(2)}, u32[]{:S(2)}) collective-permute-start(bf16[256,512]{1,0:T(8,128)(2,1)S(1)} %get-tuple-element.109.refs_0_), channel_id=1, source_target_pairs={{0,8},{8,0},{16,24},{24,16},{1,9},{9,1},{17,25},{25,17},{2,10},{10... | collective-permute-start | bytes 786440 | tf_op jit(solution)/shard_map/ppermute | solution.py:156
  18.2 13.6 %collective-permute-start.5 = (bf16[256,512]{1,0:T(8,128)(2,1)S(1)}, bf16[256,512]{1,0:T(8,128)(2,1)S(1)}, u32[]{:S(2)}, u32[]{:S(2)}) collective-permute-start(bf16[256,512]{1,0:T(8,128)(2,1)S(1)} %get-tuple-element.109.refs_0_), channel_id=1, source_target_pairs={{0,16},{8,24},{16,0},{24,8},{1,17},{9,25},{17,1},{25,9},{2,18},{10... | collective-permute-start | bytes 786440 | tf_op jit(solution)/shard_map/ppermute | solution.py:156
  23.1 12.5 %collective-permute-start.6 = (bf16[256,512]{1,0:T(8,128)(2,1)S(1)}, bf16[256,512]{1,0:T(8,128)(2,1)S(1)}, u32[]{:S(2)}, u32[]{:S(2)}) collective-permute-start(bf16[256,512]{1,0:T(8,128)(2,1)S(1)} %copy-done.11), channel_id=1, source_target_pairs={{0,3},{1,2},{2,1},{3,0},{4,7},{5,6},{6,5},{7,4},{8,11},{9,10},{10,... | collective-permute-start | bytes 786440 | tf_op jit(solution)/shard_map/ppermute | solution.py:156
  23.2 12.4 %collective-permute-start.8 = (bf16[256,512]{1,0:T(8,128)(2,1)S(1)}, bf16[256,512]{1,0:T(8,128)(2,1)S(1)}, u32[]{:S(2)}, u32[]{:S(2)}) collective-permute-start(bf16[256,512]{1,0:T(8,128)(2,1)S(1)} %get-tuple-element.113.refs_1_), channel_id=1, source_target_pairs={{0,16},{8,24},{16,0},{24,8},{1,17},{9,25},{17,1},{25,9},{2,18},{10... | collective-permute-start | bytes 786440 | tf_op jit(solution)/shard_map/ppermute | solution.py:156
  24.8 21.3 %collective-permute-start.7 = (bf16[256,512]{1,0:T(8,128)(2,1)S(1)}, bf16[256,512]{1,0:T(8,128)(2,1)S(1)}, u32[]{:S(2)}, u32[]{:S(2)}) collective-permute-start(bf16[256,512]{1,0:T(8,128)(2,1)S(1)} %copy-done.12), channel_id=1, source_target_pairs={{0,4},{1,5},{2,6},{3,7},{4,0},{5,1},{6,2},{7,3},{8,12},{9,13},{10,... | collective-permute-start | bytes 786440 | tf_op jit(solution)/shard_map/ppermute | solution.py:156
  31.8 24.3 %collective-permute-start.9 = (bf16[256,512]{1,0:T(8,128)(2,1)S(1)}, bf16[256,512]{1,0:T(8,128)(2,1)S(1)}, u32[]{:S(2)}, u32[]{:S(2)}) collective-permute-start(bf16[256,512]{1,0:T(8,128)(2,1)S(1)} %get-tuple-element.116.refs_2_), channel_id=1, source_target_pairs={{0,8},{8,0},{16,24},{24,16},{1,9},{9,1},{17,25},{25,17},{2,10},{10... | collective-permute-start | bytes 786440 | tf_op jit(solution)/shard_map/ppermute | solution.py:156
  33.4 25.7 %collective-permute-start.10 = (bf16[256,512]{1,0:T(8,128)(2,1)}, bf16[256,512]{1,0:T(8,128)(2,1)S(1)}, u32[]{:S(2)}, u32[]{:S(2)}) collective-permute-start(bf16[256,512]{1,0:T(8,128)(2,1)} %get-tuple-element.125), channel_id=1, source_target_pairs={{0,5},{1,4},{2,7},{3,6},{4,1},{5,0},{6,3},{7,2},{8,13},{9,12},{10,... | collective-permute-start | bytes 786440 | tf_op jit(solution)/shard_map/ppermute | solution.py:156
  47.5 13.1 %collective-permute-start.12 = (bf16[256,512]{1,0:T(8,128)(2,1)S(1)}, bf16[256,512]{1,0:T(8,128)(2,1)S(1)}, u32[]{:S(2)}, u32[]{:S(2)}) collective-permute-start(bf16[256,512]{1,0:T(8,128)(2,1)S(1)} %get-tuple-element.114.refs_0_), channel_id=1, source_target_pairs={{0,16},{8,24},{16,0},{24,8},{1,17},{9,25},{17,1},{25,9},{2,18},{10... | collective-permute-start | bytes 786440 | tf_op jit(solution)/shard_map/ppermute | solution.py:156
  47.5 13.1 %collective-permute-start.11 = (bf16[256,512]{1,0:T(8,128)(2,1)S(1)}, bf16[256,512]{1,0:T(8,128)(2,1)S(1)}, u32[]{:S(2)}, u32[]{:S(2)}) collective-permute-start(bf16[256,512]{1,0:T(8,128)(2,1)S(1)} %get-tuple-element.126.refs_0_), channel_id=1, source_target_pairs={{0,8},{8,0},{16,24},{24,16},{1,9},{9,1},{17,25},{25,17},{2,10},{10... | collective-permute-start | bytes 786440 | tf_op jit(solution)/shard_map/ppermute | solution.py:156
  49.2 12.9 %collective-permute-start.15 = (bf16[256,512]{1,0:T(8,128)(2,1)}, bf16[256,512]{1,0:T(8,128)(2,1)S(1)}, u32[]{:S(2)}, u32[]{:S(2)}) collective-permute-start(bf16[256,512]{1,0:T(8,128)(2,1)} %get-tuple-element.131), channel_id=1, source_target_pairs={{0,6},{1,7},{2,4},{3,5},{4,2},{5,3},{6,0},{7,1},{8,14},{9,15},{10,... | collective-permute-start | bytes 786440 | tf_op jit(solution)/shard_map/ppermute | solution.py:156
  60.6 13.3 %collective-permute-start.16 = (bf16[256,512]{1,0:T(8,128)(2,1)S(1)}, bf16[256,512]{1,0:T(8,128)(2,1)S(1)}, u32[]{:S(2)}, u32[]{:S(2)}) collective-permute-start(bf16[256,512]{1,0:T(8,128)(2,1)S(1)} %get-tuple-element.132.refs_1_), channel_id=1, source_target_pairs={{0,16},{8,24},{16,0},{24,8},{1,17},{9,25},{17,1},{25,9},{2,18},{10... | collective-permute-start | bytes 786440 | tf_op jit(solution)/shard_map/ppermute | solution.py:156
  61.1 14.4 %collective-permute-start.17 = (bf16[256,512]{1,0:T(8,128)(2,1)S(1)}, bf16[256,512]{1,0:T(8,128)(2,1)S(1)}, u32[]{:S(2)}, u32[]{:S(2)}) collective-permute-start(bf16[256,512]{1,0:T(8,128)(2,1)S(1)} %get-tuple-element.129.refs_2_), channel_id=1, source_target_pairs={{0,8},{8,0},{16,24},{24,16},{1,9},{9,1},{17,25},{25,17},{2,10},{10... | collective-permute-start | bytes 786440 | tf_op jit(solution)/shard_map/ppermute | solution.py:156
  62.1 17.9 %collective-permute-start.18 = (bf16[256,512]{1,0:T(8,128)(2,1)S(1)}, bf16[256,512]{1,0:T(8,128)(2,1)S(1)}, u32[]{:S(2)}, u32[]{:S(2)}) collective-permute-start(bf16[256,512]{1,0:T(8,128)(2,1)S(1)} %copy-done.4), channel_id=1, source_target_pairs={{0,8},{8,0},{16,24},{24,16},{1,9},{9,1},{17,25},{25,17},{2,10},{10... | collective-permute-start | bytes 786440 | tf_op jit(solution)/shard_map/ppermute | solution.py:156
  65.4 14.6 %collective-permute-start.19 = (bf16[256,512]{1,0:T(8,128)(2,1)S(1)}, bf16[256,512]{1,0:T(8,128)(2,1)S(1)}, u32[]{:S(2)}, u32[]{:S(2)}) collective-permute-start(bf16[256,512]{1,0:T(8,128)(2,1)S(1)} %get-tuple-element.142.refs_0_), channel_id=1, source_target_pairs={{0,16},{8,24},{16,0},{24,8},{1,17},{9,25},{17,1},{25,9},{2,18},{10... | collective-permute-start | bytes 786440 | tf_op jit(solution)/shard_map/ppermute | solution.py:156
  68.3 13.5 %collective-permute-start.20 = (bf16[256,512]{1,0:T(8,128)(2,1)S(1)}, bf16[256,512]{1,0:T(8,128)(2,1)S(1)}, u32[]{:S(2)}, u32[]{:S(2)}) collective-permute-start(bf16[256,512]{1,0:T(8,128)(2,1)S(1)} %copy-done.10), channel_id=1, source_target_pairs={{0,7},{1,6},{2,5},{3,4},{4,3},{5,2},{6,1},{7,0},{8,15},{9,14},{10,... | collective-permute-start | bytes 786440 | tf_op jit(solution)/shard_map/ppermute | solution.py:156
  73.9 11.2 %collective-permute-start.21 = (bf16[256,512]{1,0:T(8,128)(2,1)S(1)}, bf16[256,512]{1,0:T(8,128)(2,1)S(1)}, u32[]{:S(2)}, u32[]{:S(2)}) collective-permute-start(bf16[256,512]{1,0:T(8,128)(2,1)S(1)} %copy-done.4), channel_id=1, source_target_pairs={{0,16},{8,24},{16,0},{24,8},{1,17},{9,25},{17,1},{25,9},{2,18},{10... | collective-permute-start | bytes 786440 | tf_op jit(solution)/shard_map/ppermute | solution.py:156
  80.0 10.8 %collective-permute-start.23 = (bf16[256,512]{1,0:T(8,128)(2,1)S(1)}, bf16[256,512]{1,0:T(8,128)(2,1)S(1)}, u32[]{:S(2)}, u32[]{:S(2)}) collective-permute-start(bf16[256,512]{1,0:T(8,128)(2,1)S(1)} %get-tuple-element.149.refs_1_), channel_id=1, source_target_pairs={{0,16},{8,24},{16,0},{24,8},{1,17},{9,25},{17,1},{25,9},{2,18},{10... | collective-permute-start | bytes 786440 | tf_op jit(solution)/shard_map/ppermute | solution.py:156
  81.1 11.2 %collective-permute-start.24 = (bf16[256,512]{1,0:T(8,128)(2,1)S(1)}, bf16[256,512]{1,0:T(8,128)(2,1)S(1)}, u32[]{:S(2)}, u32[]{:S(2)}) collective-permute-start(bf16[256,512]{1,0:T(8,128)(2,1)S(1)} %get-tuple-element.147.refs_2_), channel_id=1, source_target_pairs={{0,8},{8,0},{16,24},{24,16},{1,9},{9,1},{17,25},{25,17},{2,10},{10... | collective-permute-start | bytes 786440 | tf_op jit(solution)/shard_map/ppermute | solution.py:156
  85.2 11.2 %collective-permute-start.26 = (bf16[256,512]{1,0:T(8,128)(2,1)S(1)}, bf16[256,512]{1,0:T(8,128)(2,1)S(1)}, u32[]{:S(2)}, u32[]{:S(2)}) collective-permute-start(bf16[256,512]{1,0:T(8,128)(2,1)S(1)} %get-tuple-element.145.refs_0_), channel_id=1, source_target_pairs={{0,16},{8,24},{16,0},{24,8},{1,17},{9,25},{17,1},{25,9},{2,18},{10... | collective-permute-start | bytes 786440 | tf_op jit(solution)/shard_map/ppermute | solution.py:156
  87.5 13.7 %collective-permute-start.28 = (bf16[256,512]{1,0:T(8,128)(2,1)S(1)}, bf16[256,512]{1,0:T(8,128)(2,1)S(1)}, u32[]{:S(2)}, u32[]{:S(2)}) collective-permute-start(bf16[256,512]{1,0:T(8,128)(2,1)S(1)} %get-tuple-element.145.refs_0_), channel_id=1, source_target_pairs={{0,8},{8,0},{16,24},{24,16},{1,9},{9,1},{17,25},{25,17},{2,10},{10... | collective-permute-start | bytes 786440 | tf_op jit(solution)/shard_map/ppermute | solution.py:156
  90.8 11.2 %collective-permute-start.27 = (bf16[256,512]{1,0:T(8,128)(2,1)S(1)}, bf16[256,512]{1,0:T(8,128)(2,1)S(1)}, u32[]{:S(2)}, u32[]{:S(2)}) collective-permute-start(bf16[256,512]{1,0:T(8,128)(2,1)S(1)} %get-tuple-element.158.refs_0_), channel_id=1, source_target_pairs={{0,16},{8,24},{16,0},{24,8},{1,17},{9,25},{17,1},{25,9},{2,18},{10... | collective-permute-start | bytes 786440 | tf_op jit(solution)/shard_map/ppermute | solution.py:156
  (21 other events, 156.4 us)

commit v5 on v4

--- a/solution.py
+++ b/solution.py
@@ -51,65 +51,104 @@
     )(*arrays)
 
 
-def adam_kernel(blocks, passed, expert_of, master, gradient, first, second, *refs):
-    new_master, new_first, new_second, *sends = refs[passed : passed + 3 + blocks]
-    _, rows, columns = master.shape
-    places = [
-        (slice(i, i + QB), slice(j, j + QB)) for i in range(0, rows, QB) for j in range(0, columns, QB)
-    ]
-    peaks = []
-    for place in places:
-        at = (0, *place)
-        grad = gradient[at].astype(jnp.float32)
-        moment_one = beta_one * first[at].astype(jnp.float32) + (1.0 - beta_one) * grad
-        moment_two = beta_two * second[at].astype(jnp.float32) + ((1.0 - beta_two) * grad) * grad
-        new_first[at] = moment_one.astype(jnp.bfloat16)
-        new_second[at] = moment_two.astype(jnp.bfloat16)
-        root = moment_two * lax.rsqrt(moment_two) + root_epsilon
-        inverse = pl.reciprocal(root, approx=True)
-        inverse = inverse * (2.0 - root * inverse)
-        updated = master[at] - (step_size * moment_one) * inverse
-        new_master[at] = updated
-        peaks.append(jnp.max(jnp.abs(updated), axis=0, keepdims=True))
-    largest = jnp.max(jnp.concatenate(peaks, axis=0), axis=1, keepdims=True)
-    scale = ((largest + scale_epsilon) * (1.0 / quant_limit)).astype(jnp.bfloat16)
-    scale = jnp.broadcast_to(scale.astype(jnp.float32), (len(places), QB))
-    inverse_scale = 1.0 / scale
-    for number in range(blocks):
-
-        @pl.when(pl.program_id(0) == number)
-        def _():
-            for row, place in enumerate(places):
-                one = slice(row, row + 1)
-                quantized = (new_master[(0, *place)] * inverse_scale[one]).astype(jnp.bfloat16)
-                value = quantized.astype(jnp.float32) * scale[one]
-                sends[number][place] = value.astype(jnp.bfloat16)
-
-
-def adam_blocks(base, blocks, expert_of, arrays, carried, token, fenced):
+def adam_kernel(numbers, passed, owner, *refs):
+    arrays, outs = refs[:4], refs[4 + passed : 7 + passed]
+    sends = refs[7 + passed : 7 + passed + len(numbers)]
+    *buffers, semaphores = refs[-9:]
+    experts, rows, columns = arrays[0].shape
+    shard = lax.axis_index("shard")
+    chunks = [(n, i) for n in range(len(numbers)) for i in range(rows // QB)]
+    held = []
+    for number in numbers:
+        expert = jnp.int32(0)
+        for candidate in range(experts):
+            expert = jnp.where(owner[candidate] == shard ^ number, candidate, expert)
+        held.append(expert)
+
+    def copies(chunk, inward):
+        n, i = chunk
+        span = pl.ds(i * QB, QB)
+        outer = arrays if inward else (*outs, sends[n])
+        for k, ref in enumerate(outer):
+            far = ref.at[span] if ref is sends[n] else ref.at[held[n], span]
+            near = buffers[k if inward else 4 + k].at[n, span]
+            pair = (far, near) if inward else (near, far)
+            yield pltpu.make_async_copy(*pair, semaphores.at[n, i, k if inward else 4 + k])
+
+    def update(chunk):
+        n, i = chunk
+        master, gradient, first, second, new_master, new_first, new_second, _ = buffers
+        peaks = []
+        for start in range(0, columns, QB):
+            at = (n, slice(i * QB, (i + 1) * QB), slice(start, start + QB))
+            grad = gradient[at].astype(jnp.float32)
+            moment_one = beta_one * first[at].astype(jnp.float32) + (1.0 - beta_one) * grad
+            moment_two = beta_two * second[at].astype(jnp.float32) + (
+                ((1.0 - beta_two) * grad) * grad
+            )
+            new_first[at] = moment_one.astype(jnp.bfloat16)
+            new_second[at] = moment_two.astype(jnp.bfloat16)
+            guess = lax.rsqrt(moment_two)
+            root = moment_two * guess + root_epsilon
+            inverse = guess * (2.0 - root * guess)
+            updated = master[at] - (step_size * moment_one) * inverse
+            new_master[at] = updated
+            peaks.append(jnp.max(jnp.abs(updated), axis=0, keepdims=True))
+        largest = jnp.max(jnp.concatenate(peaks, axis=0), axis=1, keepdims=True)
+        scale = ((largest + scale_epsilon) * (1.0 / quant_limit)).astype(jnp.bfloat16)
+        scale = jnp.broadcast_to(scale.astype(jnp.float32), (len(peaks), QB))
+        return scale, 1.0 / scale
+
+    def quantize(chunk, scale, inverse_scale):
+        n, i = chunk
+        for block, start in enumerate(range(0, columns, QB)):
+            at = (n, slice(i * QB, (i + 1) * QB), slice(start, start + QB))
+            one = slice(block, block + 1)
+            quantized = (buffers[4][at] * inverse_scale[one]).astype(jnp.bfloat16)
+            buffers[7][at] = (quantized.astype(jnp.float32) * scale[one]).astype(jnp.bfloat16)
+        for copy in copies(chunk, False):
+            copy.start()
+
+    for chunk in chunks:
+        for copy in copies(chunk, True):
+            copy.start()
+    pending = None
+    for chunk in chunks:
+        for copy in copies(chunk, True):
+            copy.wait()
+        scales = update(chunk)
+        if pending:
+            quantize(*pending)
+        pending = (chunk, *scales)
+    quantize(*pending)
+    for chunk in chunks:
+        for copy in copies(chunk, False):
+            copy.wait()
+
+
+def adam_blocks(numbers, owner, arrays, carried, token, fenced):
     _, rows, columns = arrays[0].shape
+    blocks = len(numbers)
     passed = len(carried) + len(token)
-    here = pl.BlockSpec((1, rows, columns), lambda i, expert_of: (expert_of[base + i], 0, 0))
-    sent = pl.BlockSpec((rows, columns), lambda i, expert_of: (0, 0))
     made = [like(arrays[0]), like(arrays[2]), like(arrays[3])]
     made += [jax.ShapeDtypeStruct((rows, columns), jnp.bfloat16)] * blocks
     aliases = {5 + i: i for i in range(len(carried))}
     if token:
         aliases[5 + len(carried)] = len(made)
+    made += [jax.ShapeDtypeStruct(TOKEN, jnp.float32)] * fenced
+    kinds = [jnp.float32, jnp.bfloat16, jnp.bfloat16, jnp.bfloat16] * 2
     results = pl.pallas_call(
-        functools.partial(adam_kernel, blocks, passed),
-        grid_spec=pltpu.PrefetchScalarGridSpec(
-            num_scalar_prefetch=1,
-            grid=(blocks,),
-            in_specs=[here] * 4 + [WHOLE] * passed,
-            out_specs=[here] * 3 + [sent] * blocks + [WHOLE] * fenced,
-        ),
-        out_shape=made + [jax.ShapeDtypeStruct(TOKEN, jnp.float32)] * fenced,
+        functools.partial(adam_kernel, numbers, passed),
+        in_specs=[pl.BlockSpec(memory_space=pltpu.SMEM)] + [WHOLE] * (4 + passed),
+        out_specs=[WHOLE] * len(made),
+        out_shape=made,
+        scratch_shapes=[pltpu.VMEM((blocks, rows, columns), kind) for kind in kinds]
+        + [pltpu.SemaphoreType.DMA((blocks, rows // QB, 8))],
         input_output_aliases=aliases,
         compiler_params=pltpu.CompilerParams(vmem_limit_bytes=VMEM_LIMIT),
         cost_estimate=SMALL_COST,
         name="adam_quantize",
-    )(expert_of, *arrays, *carried, *token)
+    )(owner, *arrays, *carried, *token)
     return results[:3], results[3 : 3 + blocks], tuple(results[3 + blocks :])
 
 
@@ -136,9 +175,7 @@
         grid_spec=pltpu.PrefetchScalarGridSpec(
             num_scalar_prefetch=2,
             grid=(1,),
-            in_specs=[pl.BlockSpec((tokens, units), lambda i, sources, places: (0, 0))]
-            + [pl.BlockSpec((rows, columns), lambda i, sources, places: (0, 0))] * slabs
-            + [WHOLE] * passed,
+            in_specs=[pl.BlockSpec(memory_space=pltpu.VMEM)] * (1 + slabs) + [WHOLE] * passed,
             out_specs=[WHOLE] * len(token)
             + [pl.BlockSpec((tokens, columns), lambda i, sources, places: (0, sources[number]))],
         ),
@@ -163,12 +200,8 @@
     token_rows = hidden.reshape(hidden.shape[2:])
     breadth = arrays[0].shape[2] * shards
     bits = [1 << i for i in range((replicas - 1).bit_length())]
-    experts = jnp.arange(shards, dtype=jnp.int32)
     members = jnp.arange(replicas, dtype=jnp.int32)
-    sources = shard ^ experts
-    expert_of = jnp.sum(
-        jnp.where(owner_of_expert[None, :] == sources[:, None], experts[None, :], 0), axis=1
-    ).astype(jnp.int32)
+    sources = shard ^ jnp.arange(shards, dtype=jnp.int32)
     places = jnp.sum(
         jnp.where((replica ^ members)[:, None] == members[None, :], slab_order[None, :], 0), axis=1
     ).astype(jnp.int32)
@@ -179,11 +212,11 @@
     made, due, ready = {}, collections.defaultdict(list), set()
     state = {"adam": (), "token": (), "out": ()}
 
-    def adam(first, blocks):
+    def adam(*numbers):
         state["adam"], sends, state["token"] = adam_blocks(
-            first, blocks, expert_of, arrays, tuple(state["adam"]), state["token"], fenced
+            numbers, owner_of_expert, arrays, tuple(state["adam"]), state["token"], fenced
         )
-        made.update(zip(range(first, first + blocks), sends))
+        made.update(zip(numbers, sends))
 
     def deliver(block):
         held[block][0] = swap(made[block], "shard", shards, block) if block else made[block]
@@ -191,9 +224,11 @@
     def send(block, member, bit):
         held[block][member ^ bit] = swap(held[block][member], "replica", replicas, bit)
 
-    def arrived(keys):
-        token, *passed = fence([*state["token"], *[held[b][m] for b, m in keys]])
+    def arrived(keys, leaving):
+        waiting = [held[b][m] for b, m in keys] + [made[b] for b in leaving]
+        token, *passed = fence([*state["token"], *waiting])
         state["token"] = (token,)
+        made.update(zip(leaving, passed[len(keys) :]))
         for (block, member), array in zip(keys, passed):
             held[block][member] = array
         ready.update(keys)
@@ -229,25 +264,27 @@
                 send(block, member, bit)
                 due[step + 2].append((block, member ^ bit))
 
-        adam(0, 2)
+        half = shards // 2
+        rest = [half, 2, 3, *range(half + 1, shards), *range(4, half)]
+        adam(0, 1)
         deliver(0)
         deliver(1)
         ready.add((0, 0))
         due[0].append((1, 0))
         start(-1)
-        adam(2, 2)
+        adam(*rest[:2])
         for step in range(3 * pairs + 2):
-            arrived(due[step])
+            arrived(due[step], moves[step])
             start(step)
-            if step + 2 < pairs:
-                adam(2 * step + 4, 2)
+            if 2 * step + 2 < len(rest):
+                adam(*rest[2 * step + 2 : 2 * step + 4])
             for block in list(waiting):
                 if all((block, member) in ready for member in range(replicas)):
                     multiply(block)
                     waiting.remove(block)
     else:
         for pair in range(pairs):
-            adam(2 * pair, 2)
+            adam(2 * pair, 2 * pair + 1)
         for block in range(shards):
             deliver(block)
             for number in range(len(bits)):

time: 109 us -> 101 us (0.927)
  the two profiles are of different devices: /device:TPU:0 before, /device:TPU:8 now
where the time goes in v5:
time: 101 us
  waiting for transfers between devices  32.5 us (32%)
  Pallas kernels  31.7 us (31%)
  starting transfers between devices  31.4 us (31%)
  local copies, waits for them, and re-layouts  4.27 us (4%)
    ppermute x31, waiting for transfers between devices, swap(): return lax.ppermute(value, axis, [(i, i ^ mask) for i in range(size)])  32.5 us
    ppermute x31, starting transfers between devices, swap(): return lax.ppermute(value, axis, [(i, i ^ mask) for i in range(size)])  31.4 us
    pallas_call x4, Pallas kernels, adam_blocks(): pl.pallas_call(functools.partial(adam_kernel, numbers, passed), in_specs=...  16.7 us
    pallas_call x8, Pallas kernels, product(): pl.pallas_call(functools.partial(product_kernel, number, slabs), grid_spe...  15 us
    unnamed x24, local copies, waits for them, and re-layouts  4.27 us
  transfers between devices with their start and end apart: 31, of which 11 were waited for; matrix products, arithmetic and copies ran while one was open for 0% of the time, Pallas kernels for 24%

profile of v5, /device:TPU:8, one launch (start us, length us, event | category | flops | bytes accessed | tf_op | source)
XLA Modules:
  0.0 100.9 jit_solution(12992898932846258310)
XLA Ops:
  0.6 4.2 %adam_quantize.4 = (f32[8,256,512]{2,1,0:T(8,128)}, bf16[8,256,512]{2,1,0:T(8,128)(2,1)}, bf16[8,256,512]{2,1,0:T(8,128)(2,1)}, bf16[256,512]{1,0:T(8,128)(2,1)}...) custom-call(s32[8]{0:T(128)} %owner.7, f32[8,256,512]{2,1,0:T(8,128)} %refs_0_.7, bf16[8,256,512]{2,1,0:T(8,128)(2,1)} %refs_1_.7, ...), custom_call_target="tpu_custom_call" | custom-call | bytes 65536 | tf_op jit(solution)/shard_map/adam_quantize/pallas_call | solution.py:140
  4.9 1.6 %collective-permute-start.1 = (bf16[256,512]{1,0:T(8,128)(2,1)}, bf16[256,512]{1,0:T(8,128)(2,1)S(1)}, u32[]{:S(2)}, u32[]{:S(2)}) collective-permute-start(bf16[256,512]{1,0:T(8,128)(2,1)} %get-tuple-element.109.refs_0_), channel_id=1, source_target_pairs={{0,8},{8,0},{16,24},{24,16},{1,9},{9,1},{17,25},{25,17},{2,10},{10... | collective-permute-start | bytes 786440 | tf_op jit(solution)/shard_map/ppermute | solution.py:193
  8.0 4.2 %adam_quantize.5 = (f32[8,256,512]{2,1,0:T(8,128)}, bf16[8,256,512]{2,1,0:T(8,128)(2,1)}, bf16[8,256,512]{2,1,0:T(8,128)(2,1)}, bf16[256,512]{1,0:T(8,128)(2,1)}...) custom-call(s32[8]{0:T(128)} %owner.7, ...), custom_call_target="tpu_custom_call", output_to_operand_aliasing={{0}: (5, {}), {1}: (6, {}), {2}: (7, {}), {5}: (8, {})} | custom-call | bytes 65536 | tf_op jit(solution)/shard_map/adam_quantize/pallas_call | solution.py:140
  13.3 4.2 %adam_quantize.6 = (f32[8,256,512]{2,1,0:T(8,128)}, bf16[8,256,512]{2,1,0:T(8,128)(2,1)}, bf16[8,256,512]{2,1,0:T(8,128)(2,1)}, bf16[256,512]{1,0:T(8,128)(2,1)}...) custom-call(s32[8]{0:T(128)} %owner.7, ...), custom_call_target="tpu_custom_call", output_to_operand_aliasing={{0}: (5, {}), {1}: (6, {}), {2}: (7, {}), {5}: (8, {})} | custom-call | bytes 65536 | tf_op jit(solution)/shard_map/adam_quantize/pallas_call | solution.py:140
  18.9 2.6 %collective-permute-start.7 = (bf16[256,512]{1,0:T(8,128)(2,1)S(1)}, bf16[256,512]{1,0:T(8,128)(2,1)S(1)}, u32[]{:S(2)}, u32[]{:S(2)}) collective-permute-start(bf16[256,512]{1,0:T(8,128)(2,1)S(1)} %get-tuple-element.121), channel_id=1, source_target_pairs={{0,4},{1,5},{2,6},{3,7},{4,0},{5,1},{6,2},{7,3},{8,12},{9,13},{10,... | collective-permute-start | bytes 786440 | tf_op jit(solution)/shard_map/ppermute | solution.py:193
  23.0 4.2 %adam_quantize.7 = (f32[8,256,512]{2,1,0:T(8,128)}, bf16[8,256,512]{2,1,0:T(8,128)(2,1)}, bf16[8,256,512]{2,1,0:T(8,128)(2,1)}, bf16[256,512]{1,0:T(8,128)(2,1)}...) custom-call(s32[8]{0:T(128)} %owner.7, ...), custom_call_target="tpu_custom_call", output_to_operand_aliasing={{0}: (5, {}), {1}: (6, {}), {2}: (7, {}), {5}: (8, {})} | custom-call | bytes 65536 | tf_op jit(solution)/shard_map/adam_quantize/pallas_call | solution.py:140
  28.8 2.0 %collective-permute-done.6.refs_1_ = bf16[256,512]{1,0:T(8,128)(2,1)S(1)} collective-permute-done((bf16[256,512]{1,0:T(8,128)(2,1)}, bf16[256,512]{1,0:T(8,128)(2,1)S(1)}, u32[]{:S(2)}, u32[]{:S(2)}) %collective-permute-start.6) | collective-permute-done | bytes 262176 | tf_op jit(solution)/shard_map/ppermute | solution.py:193
  30.8 2.9 %collective-permute-done.7.refs_2_ = bf16[256,512]{1,0:T(8,128)(2,1)S(1)} collective-permute-done((bf16[256,512]{1,0:T(8,128)(2,1)S(1)}, bf16[256,512]{1,0:T(8,128)(2,1)S(1)}, u32[]{:S(2)}, u32[]{:S(2)}) %collective-permute-start.7) | collective-permute-done | bytes 262176 | tf_op jit(solution)/shard_map/ppermute | solution.py:193
  34.4 2.9 %collective-permute-start.10 = (bf16[256,512]{1,0:T(8,128)(2,1)}, bf16[256,512]{1,0:T(8,128)(2,1)S(1)}, u32[]{:S(2)}, u32[]{:S(2)}) collective-permute-start(bf16[256,512]{1,0:T(8,128)(2,1)} %get-tuple-element.135), channel_id=1, source_target_pairs={{0,5},{1,4},{2,7},{3,6},{4,1},{5,0},{6,3},{7,2},{8,13},{9,12},{10,... | collective-permute-start | bytes 786440 | tf_op jit(solution)/shard_map/ppermute | solution.py:193
  44.0 1.9 %expert_product.8 = (f32[135168,128]{1,0:T(8,128)}, bf16[384,4096]{1,0:T(8,128)(2,1)}) custom-call(s32[8]{0:T(128)S(1)} %iota_xor_fusion.1.sources, s32[4]{0:T(128)S(1)} %select_reduce_fusion.places, bf16[384,1024]{1,0:T(8,128)(2,1)S(1)} %bitcast.2, bf16[256,512]{1,0:T(8,128)(2,1)S(1)} %copy-done.8, ...), custom_call_target="tpu_custom_call", output_to_operand_aliasing={{0}: (7, {})} | custom-call | bytes 65536 | tf_op jit(solution)/shard_map/expert_product/pallas_call | solution.py:173
  46.4 1.9 %expert_product.9 = (f32[135168,128]{1,0:T(8,128)}, bf16[384,4096]{1,0:T(8,128)(2,1)}) custom-call(s32[8]{0:T(128)S(1)} %iota_xor_fusion.1.sources, s32[4]{0:T(128)S(1)} %select_reduce_fusion.places, bf16[384,1024]{1,0:T(8,128)(2,1)S(1)} %bitcast.3, bf16[256,512]{1,0:T(8,128)(2,1)S(1)} %copy-done.6, ...), custom_call_target="tpu_custom_call", output_to_operand_aliasing={{0}: (7, {}), {1}: (8, {})} | custom-call | bytes 65536 | tf_op jit(solution)/shard_map/expert_product/pallas_call | solution.py:173
  48.4 1.6 %collective-permute-start.16 = (bf16[256,512]{1,0:T(8,128)(2,1)S(1)}, bf16[256,512]{1,0:T(8,128)(2,1)S(1)}, u32[]{:S(2)}, u32[]{:S(2)}) collective-permute-start(bf16[256,512]{1,0:T(8,128)(2,1)S(1)} %get-tuple-element.143.refs_1_), channel_id=1, source_target_pairs={{0,16},{8,24},{16,0},{24,8},{1,17},{9,25},{17,1},{25,9},{2,18},{10... | collective-permute-start | bytes 786440 | tf_op jit(solution)/shard_map/ppermute | solution.py:193
  55.3 6.3 %collective-permute-done.15.refs_1_ = bf16[256,512]{1,0:T(8,128)(2,1)S(1)} collective-permute-done((bf16[256,512]{1,0:T(8,128)(2,1)S(1)}, bf16[256,512]{1,0:T(8,128)(2,1)S(1)}, u32[]{:S(2)}, u32[]{:S(2)}) %collective-permute-start.15) | collective-permute-done | bytes 262176 | tf_op jit(solution)/shard_map/ppermute | solution.py:193
  61.6 2.2 %collective-permute-start.21 = (bf16[256,512]{1,0:T(8,128)(2,1)S(1)}, bf16[256,512]{1,0:T(8,128)(2,1)S(1)}, u32[]{:S(2)}, u32[]{:S(2)}) collective-permute-start(bf16[256,512]{1,0:T(8,128)(2,1)S(1)} %get-tuple-element.153.refs_0_), channel_id=1, source_target_pairs={{0,16},{8,24},{16,0},{24,8},{1,17},{9,25},{17,1},{25,9},{2,18},{10... | collective-permute-start | bytes 786440 | tf_op jit(solution)/shard_map/ppermute | solution.py:193
  65.3 1.9 %expert_product.10 = (f32[135168,128]{1,0:T(8,128)}, bf16[384,4096]{1,0:T(8,128)(2,1)}) custom-call(s32[8]{0:T(128)S(1)} %iota_xor_fusion.1.sources, s32[4]{0:T(128)S(1)} %select_reduce_fusion.places, bf16[384,1024]{1,0:T(8,128)(2,1)S(1)} %bitcast.4, bf16[256,512]{1,0:T(8,128)(2,1)S(1)} %get-tuple-element.136.refs_0_, ...), custom_call_target="tpu_custom_call", output_to_operand_aliasing={{0}: (7, {}), {1}: (8, {})} | custom-call | bytes 65536 | tf_op jit(solution)/shard_map/expert_product/pallas_call | solution.py:173
  67.2 1.9 %expert_product.11 = (f32[135168,128]{1,0:T(8,128)}, bf16[384,4096]{1,0:T(8,128)(2,1)}) custom-call(s32[8]{0:T(128)S(1)} %iota_xor_fusion.1.sources, s32[4]{0:T(128)S(1)} %select_reduce_fusion.places, bf16[384,1024]{1,0:T(8,128)(2,1)S(1)} %bitcast.5, bf16[256,512]{1,0:T(8,128)(2,1)S(1)} %get-tuple-element.124.refs_0_, ...), custom_call_target="tpu_custom_call", output_to_operand_aliasing={{0}: (7, {}), {1}: (8, {})} | custom-call | bytes 65536 | tf_op jit(solution)/shard_map/expert_product/pallas_call | solution.py:173
  71.9 5.8 %collective-permute-done.20.refs_1_ = bf16[256,512]{1,0:T(8,128)(2,1)S(1)} collective-permute-done((bf16[256,512]{1,0:T(8,128)(2,1)S(1)}, bf16[256,512]{1,0:T(8,128)(2,1)S(1)}, u32[]{:S(2)}, u32[]{:S(2)}) %collective-permute-start.20) | collective-permute-done | bytes 262176 | tf_op jit(solution)/shard_map/ppermute | solution.py:193
  80.2 1.9 %expert_product.12 = (f32[135168,128]{1,0:T(8,128)}, bf16[384,4096]{1,0:T(8,128)(2,1)}) custom-call(s32[8]{0:T(128)S(1)} %iota_xor_fusion.1.sources, s32[4]{0:T(128)S(1)} %select_reduce_fusion.places, bf16[384,1024]{1,0:T(8,128)(2,1)S(1)} %bitcast.6, bf16[256,512]{1,0:T(8,128)(2,1)S(1)} %get-tuple-element.153.refs_0_, ...), custom_call_target="tpu_custom_call", output_to_operand_aliasing={{0}: (7, {}), {1}: (8, {})} | custom-call | bytes 65536 | tf_op jit(solution)/shard_map/expert_product/pallas_call | solution.py:173
  82.1 1.9 %expert_product.13 = (f32[135168,128]{1,0:T(8,128)}, bf16[384,4096]{1,0:T(8,128)(2,1)}) custom-call(s32[8]{0:T(128)S(1)} %iota_xor_fusion.1.sources, s32[4]{0:T(128)S(1)} %select_reduce_fusion.places, bf16[384,1024]{1,0:T(8,128)(2,1)S(1)} %bitcast.7, bf16[256,512]{1,0:T(8,128)(2,1)S(1)} %get-tuple-element.154.refs_0_, ...), custom_call_target="tpu_custom_call", output_to_operand_aliasing={{0}: (7, {}), {1}: (8, {})} | custom-call | bytes 65536 | tf_op jit(solution)/shard_map/expert_product/pallas_call | solution.py:173
  84.4 2.4 %collective-permute-done.26.refs_2_ = bf16[256,512]{1,0:T(8,128)(2,1)S(1)} collective-permute-done((bf16[256,512]{1,0:T(8,128)(2,1)S(1)}, bf16[256,512]{1,0:T(8,128)(2,1)S(1)}, u32[]{:S(2)}, u32[]{:S(2)}) %collective-permute-start.26) | collective-permute-done | bytes 262176 | tf_op jit(solution)/shard_map/ppermute | solution.py:193
  87.4 5.0 %collective-permute-done.27.refs_1_ = bf16[256,512]{1,0:T(8,128)(2,1)S(1)} collective-permute-done((bf16[256,512]{1,0:T(8,128)(2,1)S(1)}, bf16[256,512]{1,0:T(8,128)(2,1)S(1)}, u32[]{:S(2)}, u32[]{:S(2)}) %collective-permute-start.27) | collective-permute-done | bytes 262176 | tf_op jit(solution)/shard_map/ppermute | solution.py:193
  92.5 4.7 %collective-permute-done.29.refs_1_ = bf16[256,512]{1,0:T(8,128)(2,1)S(1)} collective-permute-done((bf16[256,512]{1,0:T(8,128)(2,1)S(1)}, bf16[256,512]{1,0:T(8,128)(2,1)S(1)}, u32[]{:S(2)}, u32[]{:S(2)}) %collective-permute-start.29) | collective-permute-done | bytes 262176 | tf_op jit(solution)/shard_map/ppermute | solution.py:193
  97.1 1.9 %expert_product.14 = (f32[135168,128]{1,0:T(8,128)}, bf16[384,4096]{1,0:T(8,128)(2,1)}) custom-call(s32[8]{0:T(128)S(1)} %iota_xor_fusion.1.sources, s32[4]{0:T(128)S(1)} %select_reduce_fusion.places, bf16[384,1024]{1,0:T(8,128)(2,1)S(1)} %bitcast.8, bf16[256,512]{1,0:T(8,128)(2,1)S(1)} %get-tuple-element.170.refs_0_, ...), custom_call_target="tpu_custom_call", output_to_operand_aliasing={{0}: (7, {}), {1}: (8, {})} | custom-call | bytes 65536 | tf_op jit(solution)/shard_map/expert_product/pallas_call | solution.py:173
  99.0 1.9 %expert_product.15 = (f32[135168,128]{1,0:T(8,128)}, bf16[384,4096]{1,0:T(8,128)(2,1)}) custom-call(s32[8]{0:T(128)S(1)} %iota_xor_fusion.1.sources, s32[4]{0:T(128)S(1)} %select_reduce_fusion.places, bf16[384,1024]{1,0:T(8,128)(2,1)S(1)} %bitcast.9, bf16[256,512]{1,0:T(8,128)(2,1)S(1)} %get-tuple-element.157.refs_0_, ...), custom_call_target="tpu_custom_call", output_to_operand_aliasing={{0}: (7, {}), {1}: (8, {})} | custom-call | bytes 65536 | tf_op jit(solution)/shard_map/expert_product/pallas_call | solution.py:173
  (91 shorter events, 28.2 us)
Async XLA Ops:
  4.9 12.6 %collective-permute-start.1 = (bf16[256,512]{1,0:T(8,128)(2,1)}, bf16[256,512]{1,0:T(8,128)(2,1)S(1)}, u32[]{:S(2)}, u32[]{:S(2)}) collective-permute-start(bf16[256,512]{1,0:T(8,128)(2,1)} %get-tuple-element.109.refs_0_), channel_id=1, source_target_pairs={{0,8},{8,0},{16,24},{24,16},{1,9},{9,1},{17,25},{25,17},{2,10},{10... | collective-permute-start | bytes 786440 | tf_op jit(solution)/shard_map/ppermute | solution.py:193
  6.4 11.0 %collective-permute-start.2 = (bf16[256,512]{1,0:T(8,128)(2,1)}, bf16[256,512]{1,0:T(8,128)(2,1)S(1)}, u32[]{:S(2)}, u32[]{:S(2)}) collective-permute-start(bf16[256,512]{1,0:T(8,128)(2,1)} %get-tuple-element.109.refs_0_), channel_id=1, source_target_pairs={{0,16},{8,24},{16,0},{24,8},{1,17},{9,25},{17,1},{25,9},{2,18},{10... | collective-permute-start | bytes 786440 | tf_op jit(solution)/shard_map/ppermute | solution.py:193
  12.8 14.4 %collective-permute-start.5 = (bf16[256,512]{1,0:T(8,128)(2,1)S(1)}, bf16[256,512]{1,0:T(8,128)(2,1)S(1)}, u32[]{:S(2)}, u32[]{:S(2)}) collective-permute-start(bf16[256,512]{1,0:T(8,128)(2,1)S(1)} %get-tuple-element.118.refs_0_), channel_id=1, source_target_pairs={{0,16},{8,24},{16,0},{24,8},{1,17},{9,25},{17,1},{25,9},{2,18},{10... | collective-permute-start | bytes 786440 | tf_op jit(solution)/shard_map/ppermute | solution.py:193
  13.3 13.9 %collective-permute-start.3 = (bf16[256,512]{1,0:T(8,128)(2,1)}, bf16[256,512]{1,0:T(8,128)(2,1)S(1)}, u32[]{:S(2)}, u32[]{:S(2)}) collective-permute-start(bf16[256,512]{1,0:T(8,128)(2,1)} %get-tuple-element.117), channel_id=1, source_target_pairs={{0,2},{1,3},{2,0},{3,1},{4,6},{5,7},{6,4},{7,5},{8,10},{9,11},{10,... | collective-permute-start | bytes 786440 | tf_op jit(solution)/shard_map/ppermute | solution.py:193
  18.2 12.6 %collective-permute-start.6 = (bf16[256,512]{1,0:T(8,128)(2,1)}, bf16[256,512]{1,0:T(8,128)(2,1)S(1)}, u32[]{:S(2)}, u32[]{:S(2)}) collective-permute-start(bf16[256,512]{1,0:T(8,128)(2,1)} %get-tuple-element.120), channel_id=1, source_target_pairs={{0,3},{1,2},{2,1},{3,0},{4,7},{5,6},{6,5},{7,4},{8,11},{9,10},{10,... | collective-permute-start | bytes 786440 | tf_op jit(solution)/shard_map/ppermute | solution.py:193
  18.9 14.8 %collective-permute-start.7 = (bf16[256,512]{1,0:T(8,128)(2,1)S(1)}, bf16[256,512]{1,0:T(8,128)(2,1)S(1)}, u32[]{:S(2)}, u32[]{:S(2)}) collective-permute-start(bf16[256,512]{1,0:T(8,128)(2,1)S(1)} %get-tuple-element.121), channel_id=1, source_target_pairs={{0,4},{1,5},{2,6},{3,7},{4,0},{5,1},{6,2},{7,3},{8,12},{9,13},{10,... | collective-permute-start | bytes 786440 | tf_op jit(solution)/shard_map/ppermute | solution.py:193
  21.5 12.2 %collective-permute-start.8 = (bf16[256,512]{1,0:T(8,128)(2,1)S(1)}, bf16[256,512]{1,0:T(8,128)(2,1)S(1)}, u32[]{:S(2)}, u32[]{:S(2)}) collective-permute-start(bf16[256,512]{1,0:T(8,128)(2,1)S(1)} %get-tuple-element.122.refs_1_), channel_id=1, source_target_pairs={{0,16},{8,24},{16,0},{24,8},{1,17},{9,25},{17,1},{25,9},{2,18},{10... | collective-permute-start | bytes 786440 | tf_op jit(solution)/shard_map/ppermute | solution.py:193
  27.2 18.7 %collective-permute-start.9 = (bf16[256,512]{1,0:T(8,128)(2,1)S(1)}, bf16[256,512]{1,0:T(8,128)(2,1)S(1)}, u32[]{:S(2)}, u32[]{:S(2)}) collective-permute-start(bf16[256,512]{1,0:T(8,128)(2,1)S(1)} %get-tuple-element.126.refs_2_), channel_id=1, source_target_pairs={{0,8},{8,0},{16,24},{24,16},{1,9},{9,1},{17,25},{25,17},{2,10},{10... | collective-permute-start | bytes 786440 | tf_op jit(solution)/shard_map/ppermute | solution.py:193
  34.4 13.8 %collective-permute-start.10 = (bf16[256,512]{1,0:T(8,128)(2,1)}, bf16[256,512]{1,0:T(8,128)(2,1)S(1)}, u32[]{:S(2)}, u32[]{:S(2)}) collective-permute-start(bf16[256,512]{1,0:T(8,128)(2,1)} %get-tuple-element.135), channel_id=1, source_target_pairs={{0,5},{1,4},{2,7},{3,6},{4,1},{5,0},{6,3},{7,2},{8,13},{9,12},{10,... | collective-permute-start | bytes 786440 | tf_op jit(solution)/shard_map/ppermute | solution.py:193
  37.3 10.9 %collective-permute-start.12 = (bf16[256,512]{1,0:T(8,128)(2,1)S(1)}, bf16[256,512]{1,0:T(8,128)(2,1)S(1)}, u32[]{:S(2)}, u32[]{:S(2)}) collective-permute-start(bf16[256,512]{1,0:T(8,128)(2,1)S(1)} %get-tuple-element.124.refs_0_), channel_id=1, source_target_pairs={{0,16},{8,24},{16,0},{24,8},{1,17},{9,25},{17,1},{25,9},{2,18},{10... | collective-permute-start | bytes 786440 | tf_op jit(solution)/shard_map/ppermute | solution.py:193
  40.5 12.3 %collective-permute-start.14 = (bf16[256,512]{1,0:T(8,128)(2,1)S(1)}, bf16[256,512]{1,0:T(8,128)(2,1)S(1)}, u32[]{:S(2)}, u32[]{:S(2)}) collective-permute-start(bf16[256,512]{1,0:T(8,128)(2,1)S(1)} %get-tuple-element.124.refs_0_), channel_id=1, source_target_pairs={{0,8},{8,0},{16,24},{24,16},{1,9},{9,1},{17,25},{25,17},{2,10},{10... | collective-permute-start | bytes 786440 | tf_op jit(solution)/shard_map/ppermute | solution.py:193
  48.3 13.3 %collective-permute-start.15 = (bf16[256,512]{1,0:T(8,128)(2,1)S(1)}, bf16[256,512]{1,0:T(8,128)(2,1)S(1)}, u32[]{:S(2)}, u32[]{:S(2)}) collective-permute-start(bf16[256,512]{1,0:T(8,128)(2,1)S(1)} %get-tuple-element.142), channel_id=1, source_target_pairs={{0,6},{1,7},{2,4},{3,5},{4,2},{5,3},{6,0},{7,1},{8,14},{9,15},{10,... | collective-permute-start | bytes 786440 | tf_op jit(solution)/shard_map/ppermute | solution.py:193
  48.4 15.5 %collective-permute-start.16 = (bf16[256,512]{1,0:T(8,128)(2,1)S(1)}, bf16[256,512]{1,0:T(8,128)(2,1)S(1)}, u32[]{:S(2)}, u32[]{:S(2)}) collective-permute-start(bf16[256,512]{1,0:T(8,128)(2,1)S(1)} %get-tuple-element.143.refs_1_), channel_id=1, source_target_pairs={{0,16},{8,24},{16,0},{24,8},{1,17},{9,25},{17,1},{25,9},{2,18},{10... | collective-permute-start | bytes 786440 | tf_op jit(solution)/shard_map/ppermute | solution.py:193
  50.0 15.3 %collective-permute-start.17 = (bf16[256,512]{1,0:T(8,128)(2,1)S(1)}, bf16[256,512]{1,0:T(8,128)(2,1)S(1)}, u32[]{:S(2)}, u32[]{:S(2)}) collective-permute-start(bf16[256,512]{1,0:T(8,128)(2,1)S(1)} %get-tuple-element.140.refs_2_), channel_id=1, source_target_pairs={{0,8},{8,0},{16,24},{24,16},{1,9},{9,1},{17,25},{25,17},{2,10},{10... | collective-permute-start | bytes 786440 | tf_op jit(solution)/shard_map/ppermute | solution.py:193
  52.9 16.2 %collective-permute-start.18 = (bf16[256,512]{1,0:T(8,128)(2,1)S(1)}, bf16[256,512]{1,0:T(8,128)(2,1)S(1)}, u32[]{:S(2)}, u32[]{:S(2)}) collective-permute-start(bf16[256,512]{1,0:T(8,128)(2,1)S(1)} %get-tuple-element.153.refs_0_), channel_id=1, source_target_pairs={{0,8},{8,0},{16,24},{24,16},{1,9},{9,1},{17,25},{25,17},{2,10},{10... | collective-permute-start | bytes 786440 | tf_op jit(solution)/shard_map/ppermute | solution.py:193
  55.1 14.0 %collective-permute-start.19 = (bf16[256,512]{1,0:T(8,128)(2,1)S(1)}, bf16[256,512]{1,0:T(8,128)(2,1)S(1)}, u32[]{:S(2)}, u32[]{:S(2)}) collective-permute-start(bf16[256,512]{1,0:T(8,128)(2,1)S(1)} %get-tuple-element.154.refs_0_), channel_id=1, source_target_pairs={{0,16},{8,24},{16,0},{24,8},{1,17},{9,25},{17,1},{25,9},{2,18},{10... | collective-permute-start | bytes 786440 | tf_op jit(solution)/shard_map/ppermute | solution.py:193
  65.3 12.3 %collective-permute-start.20 = (bf16[256,512]{1,0:T(8,128)(2,1)S(1)}, bf16[256,512]{1,0:T(8,128)(2,1)S(1)}, u32[]{:S(2)}, u32[]{:S(2)}) collective-permute-start(bf16[256,512]{1,0:T(8,128)(2,1)S(1)} %get-tuple-element.156), channel_id=1, source_target_pairs={{0,7},{1,6},{2,5},{3,4},{4,3},{5,2},{6,1},{7,0},{8,15},{9,14},{10,... | collective-permute-start | bytes 786440 | tf_op jit(solution)/shard_map/ppermute | solution.py:193
  69.1 10.6 %collective-permute-start.23 = (bf16[256,512]{1,0:T(8,128)(2,1)S(1)}, bf16[256,512]{1,0:T(8,128)(2,1)S(1)}, u32[]{:S(2)}, u32[]{:S(2)}) collective-permute-start(bf16[256,512]{1,0:T(8,128)(2,1)S(1)} %get-tuple-element.161.refs_1_), channel_id=1, source_target_pairs={{0,16},{8,24},{16,0},{24,8},{1,17},{9,25},{17,1},{25,9},{2,18},{10... | collective-permute-start | bytes 786440 | tf_op jit(solution)/shard_map/ppermute | solution.py:193
  69.6 10.6 %collective-permute-start.24 = (bf16[256,512]{1,0:T(8,128)(2,1)S(1)}, bf16[256,512]{1,0:T(8,128)(2,1)S(1)}, u32[]{:S(2)}, u32[]{:S(2)}) collective-permute-start(bf16[256,512]{1,0:T(8,128)(2,1)S(1)} %get-tuple-element.159.refs_2_), channel_id=1, source_target_pairs={{0,8},{8,0},{16,24},{24,16},{1,9},{9,1},{17,25},{25,17},{2,10},{10... | collective-permute-start | bytes 786440 | tf_op jit(solution)/shard_map/ppermute | solution.py:193
  70.4 14.0 %collective-permute-start.25 = (bf16[256,512]{1,0:T(8,128)(2,1)S(1)}, bf16[256,512]{1,0:T(8,128)(2,1)S(1)}, u32[]{:S(2)}, u32[]{:S(2)}) collective-permute-start(bf16[256,512]{1,0:T(8,128)(2,1)S(1)} %get-tuple-element.170.refs_0_), channel_id=1, source_target_pairs={{0,8},{8,0},{16,24},{24,16},{1,9},{9,1},{17,25},{25,17},{2,10},{10... | collective-permute-start | bytes 786440 | tf_op jit(solution)/shard_map/ppermute | solution.py:193
  78.2 14.3 %collective-permute-start.27 = (bf16[256,512]{1,0:T(8,128)(2,1)S(1)}, bf16[256,512]{1,0:T(8,128)(2,1)S(1)}, u32[]{:S(2)}, u32[]{:S(2)}) collective-permute-start(bf16[256,512]{1,0:T(8,128)(2,1)S(1)} %get-tuple-element.170.refs_0_), channel_id=1, source_target_pairs={{0,16},{8,24},{16,0},{24,8},{1,17},{9,25},{17,1},{25,9},{2,18},{10... | collective-permute-start | bytes 786440 | tf_op jit(solution)/shard_map/ppermute | solution.py:193
  79.7 12.8 %collective-permute-start.28 = (bf16[256,512]{1,0:T(8,128)(2,1)S(1)}, bf16[256,512]{1,0:T(8,128)(2,1)S(1)}, u32[]{:S(2)}, u32[]{:S(2)}) collective-permute-start(bf16[256,512]{1,0:T(8,128)(2,1)S(1)} %get-tuple-element.157.refs_0_), channel_id=1, source_target_pairs={{0,8},{8,0},{16,24},{24,16},{1,9},{9,1},{17,25},{25,17},{2,10},{10... | collective-permute-start | bytes 786440 | tf_op jit(solution)/shard_map/ppermute | solution.py:193
  86.8 10.3 %collective-permute-start.29 = (bf16[256,512]{1,0:T(8,128)(2,1)S(1)}, bf16[256,512]{1,0:T(8,128)(2,1)S(1)}, u32[]{:S(2)}, u32[]{:S(2)}) collective-permute-start(bf16[256,512]{1,0:T(8,128)(2,1)S(1)} %get-tuple-element.175.refs_1_), channel_id=1, source_target_pairs={{0,16},{8,24},{16,0},{24,8},{1,17},{9,25},{17,1},{25,9},{2,18},{10... | collective-permute-start | bytes 786440 | tf_op jit(solution)/shard_map/ppermute | solution.py:193
  87.4 9.8 %collective-permute-start.30 = (bf16[256,512]{1,0:T(8,128)(2,1)S(1)}, bf16[256,512]{1,0:T(8,128)(2,1)S(1)}, u32[]{:S(2)}, u32[]{:S(2)}) collective-permute-start(bf16[256,512]{1,0:T(8,128)(2,1)S(1)} %get-tuple-element.173.refs_2_), channel_id=1, source_target_pairs={{0,8},{8,0},{16,24},{24,16},{1,9},{9,1},{17,25},{25,17},{2,10},{10... | collective-permute-start | bytes 786440 | tf_op jit(solution)/shard_map/ppermute | solution.py:193
  (19 other events, 124.6 us)

commit v6 on v5

--- a/solution.py
+++ b/solution.py
@@ -96,8 +96,8 @@
             peaks.append(jnp.max(jnp.abs(updated), axis=0, keepdims=True))
         largest = jnp.max(jnp.concatenate(peaks, axis=0), axis=1, keepdims=True)
         scale = ((largest + scale_epsilon) * (1.0 / quant_limit)).astype(jnp.bfloat16)
-        scale = jnp.broadcast_to(scale.astype(jnp.float32), (len(peaks), QB))
-        return scale, 1.0 / scale
+        scale = jnp.broadcast_to(scale, (len(peaks), QB))
+        return scale, 1.0 / scale.astype(jnp.float32)
 
     def quantize(chunk, scale, inverse_scale):
         n, i = chunk
@@ -105,7 +105,7 @@
             at = (n, slice(i * QB, (i + 1) * QB), slice(start, start + QB))
             one = slice(block, block + 1)
             quantized = (buffers[4][at] * inverse_scale[one]).astype(jnp.bfloat16)
-            buffers[7][at] = (quantized.astype(jnp.float32) * scale[one]).astype(jnp.bfloat16)
+            buffers[7][at] = quantized * scale[one]
         for copy in copies(chunk, False):
             copy.start()
 
@@ -154,14 +154,13 @@
 
 def product_kernel(number, slabs, sources, places, left, *refs):
     out = refs[-1]
-    total = jnp.zeros(out.shape, jnp.float32)
-    for slab in range(slabs):
-        right = refs[slab]
-        rows = right.shape[0]
-        start = pl.multiple_of(places[slab] * rows, QB)
-        total += jnp.dot(
-            left[:, pl.ds(start, rows)], right[...], preferred_element_type=jnp.float32
-        )
+    rows = refs[0].shape[0]
+    parts = [left[:, pl.ds(pl.multiple_of(places[i] * rows, QB), rows)] for i in range(slabs)]
+    total = jnp.dot(
+        jnp.concatenate(parts, axis=1),
+        jnp.concatenate([right[...] for right in refs[:slabs]], axis=0),
+        preferred_element_type=jnp.float32,
+    )
     out[...] = total.astype(out.dtype)
 
 
@@ -241,43 +240,57 @@
 
     waiting = list(range(shards))
     if fenced:
-        steps, moves = collections.defaultdict(list), collections.defaultdict(list)
-        steps[-1], steps[0], steps[1], steps[2] = (
-            [(0, 0, 1), (0, 0, 2)],
-            [(1, 0, 1), (1, 0, 2)],
-            [(0, 1, 2)],
-            [(1, 2, 1)],
-        )
-        for pair in range(1, pairs):
-            even, odd = 2 * pair, 2 * pair + 1
-            steps[3 * pair] = [(even, 0, 1), (odd, 0, 2)]
-            steps[3 * pair + 1] = [(even, 0, 2), (odd, 0, 1)]
-            steps[3 * pair + 2] = [(even, 1, 2), (odd, 2, 1)]
-        for block in range(2, shards):
-            moves[max((block - 1) // 2, min(2 * block - 7, 3 * (block // 2) - 2))].append(block)
-
-        def start(step):
-            for block in moves[step]:
-                deliver(block)
-                due[step + 2].append((block, 0))
-            for block, member, bit in steps[step]:
-                send(block, member, bit)
-                due[step + 2].append((block, member ^ bit))
-
-        half = shards // 2
-        rest = [half, 2, 3, *range(half + 1, shards), *range(4, half)]
+        fences = collections.defaultdict(lambda: ([], [], []))
+
+        def plan(step, until, *keys):
+            fences[step][1].extend(keys)
+            fences[until][0].extend((block, member ^ bit) for block, member, bit in keys)
+
+        plan(0, 2, (1, 0, 1), (1, 0, 2))
+        plan(1, 3, (0, 1, 2))
+        plan(2, 3, (1, 2, 1))
+        plan(2.5, 4, (2, 0, 1), (3, 0, 2))
+        plan(3, 5, (2, 0, 2), (3, 0, 1))
+        plan(4, 6, (2, 1, 2), (3, 2, 1))
+        for pair in range(2, pairs):
+            even, odd, step = 2 * pair, 2 * pair + 1, 3 * pair
+            if pair + 1 < pairs:
+                plan(step - 1, step + 1, (even, 0, 1), (odd, 0, 2))
+                plan(step, step + 2, (even, 0, 2), (odd, 0, 1))
+                plan(step + 1, step + 3, (even, 1, 2), (odd, 2, 1))
+            else:
+                plan(step - 1, step + 1, (even, 0, 1), (even, 0, 2))
+                plan(step, step + 2, (odd, 0, 1), (odd, 0, 2))
+                plan(step + 1, step + 3, (even, 1, 2))
+                plan(step + 2, step + 4, (odd, 2, 1))
+        for block in range(4, shards):
+            first = min(2 * block - 7, 3 * (block // 2) - 3)
+            fences[first][2].append(block)
+            fences[first + 2][0].append((block, 0))
+        fences[0][0].append((1, 0))
+        fences[1][0].extend([(0, 1), (0, 2)])
+        fences[2.5][0].extend([(2, 0), (3, 0)])
+
         adam(0, 1)
         deliver(0)
         deliver(1)
         ready.add((0, 0))
-        due[0].append((1, 0))
-        start(-1)
-        adam(*rest[:2])
-        for step in range(3 * pairs + 2):
-            arrived(due[step], moves[step])
-            start(step)
-            if 2 * step + 2 < len(rest):
-                adam(*rest[2 * step + 2 : 2 * step + 4])
+        send(0, 0, 1)
+        send(0, 0, 2)
+        adam(2, 3)
+        deliver(2)
+        deliver(3)
+        computed = 4
+        for step in sorted(fences):
+            keys, sending, leaving = fences[step]
+            arrived(keys, leaving)
+            for block in leaving:
+                deliver(block)
+            for key in sending:
+                send(*key)
+            if step not in (1, 2) and computed < shards:
+                adam(computed, computed + 1)
+                computed += 2
             for block in list(waiting):
                 if all((block, member) in ready for member in range(replicas)):
                     multiply(block)

time: 101 us -> 101 us (level)
  local copies, waits for them, and re-layouts: 4.27 us -> 2.89 us
    unnamed x24 -> x30, local copies, waits for them, and re-layouts: 4.27 us -> 2.89 us
  transfers between devices with their start and end apart: 31 -> 31, of which waited for: 11 -> 14; matrix products, arithmetic and copies ran while one was open for 0% -> 0% of each run, Pallas kernels for 24% -> 27%
where the time goes in v6:
time: 101 us; the launch traced here: 100 us
  waiting for transfers between devices  32.8 us (32%)
  Pallas kernels  32.7 us (32%)
  starting transfers between devices  30.8 us (30%)
  local copies, waits for them, and re-layouts  2.89 us (3%)
    ppermute x31, waiting for transfers between devices, swap(): return lax.ppermute(value, axis, [(i, i ^ mask) for i in range(size)])  32.8 us
    ppermute x31, starting transfers between devices, swap(): return lax.ppermute(value, axis, [(i, i ^ mask) for i in range(size)])  30.8 us
    pallas_call x4, Pallas kernels, adam_blocks(): pl.pallas_call(functools.partial(adam_kernel, numbers, passed), in_specs=...  16.8 us
    pallas_call x8, Pallas kernels, product(): pl.pallas_call(functools.partial(product_kernel, number, slabs), grid_spe...  15.9 us
    unnamed x30, local copies, waits for them, and re-layouts  2.89 us
  transfers between devices with their start and end apart: 31, of which 14 were waited for; matrix products, arithmetic and copies ran while one was open for 0% of the time, Pallas kernels for 27%

profile of v6, /device:TPU:8, one launch (start us, length us, event | category | flops | bytes accessed | tf_op | source)
XLA Modules:
  0.0 100.2 jit_solution(4574117317364684921)
XLA Ops:
  0.6 4.2 %adam_quantize.4 = (f32[8,256,512]{2,1,0:T(8,128)}, bf16[8,256,512]{2,1,0:T(8,128)(2,1)}, bf16[8,256,512]{2,1,0:T(8,128)(2,1)}, bf16[256,512]{1,0:T(8,128)(2,1)}...) custom-call(s32[8]{0:T(128)} %owner.7, f32[8,256,512]{2,1,0:T(8,128)} %refs_0_.7, bf16[8,256,512]{2,1,0:T(8,128)(2,1)} %refs_1_.7, ...), custom_call_target="tpu_custom_call" | custom-call | bytes 65536 | tf_op jit(solution)/shard_map/adam_quantize/pallas_call | solution.py:140
  4.9 1.6 %collective-permute-start.1 = (bf16[256,512]{1,0:T(8,128)(2,1)}, bf16[256,512]{1,0:T(8,128)(2,1)S(1)}, u32[]{:S(2)}, u32[]{:S(2)}) collective-permute-start(bf16[256,512]{1,0:T(8,128)(2,1)} %get-tuple-element.107.refs_0_), channel_id=1, source_target_pairs={{0,8},{8,0},{16,24},{24,16},{1,9},{9,1},{17,25},{25,17},{2,10},{10... | collective-permute-start | bytes 786440 | tf_op jit(solution)/shard_map/ppermute | solution.py:192
  6.4 1.5 %collective-permute-start.2 = (bf16[256,512]{1,0:T(8,128)(2,1)}, bf16[256,512]{1,0:T(8,128)(2,1)S(1)}, u32[]{:S(2)}, u32[]{:S(2)}) collective-permute-start(bf16[256,512]{1,0:T(8,128)(2,1)} %get-tuple-element.107.refs_0_), channel_id=1, source_target_pairs={{0,16},{8,24},{16,0},{24,8},{1,17},{9,25},{17,1},{25,9},{2,18},{10... | collective-permute-start | bytes 786440 | tf_op jit(solution)/shard_map/ppermute | solution.py:192
  8.0 4.2 %adam_quantize.5 = (f32[8,256,512]{2,1,0:T(8,128)}, bf16[8,256,512]{2,1,0:T(8,128)(2,1)}, bf16[8,256,512]{2,1,0:T(8,128)(2,1)}, bf16[256,512]{1,0:T(8,128)(2,1)}...) custom-call(s32[8]{0:T(128)} %owner.7, ...), custom_call_target="tpu_custom_call", output_to_operand_aliasing={{0}: (5, {}), {1}: (6, {}), {2}: (7, {}), {5}: (8, {})} | custom-call | bytes 65536 | tf_op jit(solution)/shard_map/adam_quantize/pallas_call | solution.py:140
  14.4 4.2 %adam_quantize.6 = (f32[8,256,512]{2,1,0:T(8,128)}, bf16[8,256,512]{2,1,0:T(8,128)(2,1)}, bf16[8,256,512]{2,1,0:T(8,128)(2,1)}, bf16[256,512]{1,0:T(8,128)(2,1)}...) custom-call(s32[8]{0:T(128)} %owner.7, ...), custom_call_target="tpu_custom_call", output_to_operand_aliasing={{0}: (5, {}), {1}: (6, {}), {2}: (7, {}), {5}: (8, {})} | custom-call | bytes 65536 | tf_op jit(solution)/shard_map/adam_quantize/pallas_call | solution.py:140
  20.3 2.6 %collective-permute-start.9 = (bf16[256,512]{1,0:T(8,128)(2,1)}, bf16[256,512]{1,0:T(8,128)(2,1)S(1)}, u32[]{:S(2)}, u32[]{:S(2)}) collective-permute-start(bf16[256,512]{1,0:T(8,128)(2,1)} %get-tuple-element.123), channel_id=1, source_target_pairs={{0,4},{1,5},{2,6},{3,7},{4,0},{5,1},{6,2},{7,3},{8,12},{9,13},{10,... | collective-permute-start | bytes 786440 | tf_op jit(solution)/shard_map/ppermute | solution.py:192
  24.2 4.8 %collective-permute-done.6.refs_2_ = bf16[256,512]{1,0:T(8,128)(2,1)S(1)} collective-permute-done((bf16[256,512]{1,0:T(8,128)(2,1)S(1)}, bf16[256,512]{1,0:T(8,128)(2,1)S(1)}, u32[]{:S(2)}, u32[]{:S(2)}) %collective-permute-start.6) | collective-permute-done | bytes 262176 | tf_op jit(solution)/shard_map/ppermute | solution.py:192
  29.0 3.0 %collective-permute-start.12 = (bf16[256,512]{1,0:T(8,128)(2,1)S(1)}, bf16[256,512]{1,0:T(8,128)(2,1)S(1)}, u32[]{:S(2)}, u32[]{:S(2)}) collective-permute-start(bf16[256,512]{1,0:T(8,128)(2,1)S(1)} %get-tuple-element.132.refs_0_), channel_id=1, source_target_pairs={{0,16},{8,24},{16,0},{24,8},{1,17},{9,25},{17,1},{25,9},{2,18},{10... | collective-permute-start | bytes 786440 | tf_op jit(solution)/shard_map/ppermute | solution.py:192
  31.9 4.3 %adam_quantize.7 = (f32[8,256,512]{2,1,0:T(8,128)}, bf16[8,256,512]{2,1,0:T(8,128)(2,1)}, bf16[8,256,512]{2,1,0:T(8,128)(2,1)}, bf16[256,512]{1,0:T(8,128)(2,1)}...) custom-call(s32[8]{0:T(128)} %owner.7, ...), custom_call_target="tpu_custom_call", output_to_operand_aliasing={{0}: (5, {}), {1}: (6, {}), {2}: (7, {}), {5}: (8, {})} | custom-call | bytes 65536 | tf_op jit(solution)/shard_map/adam_quantize/pallas_call | solution.py:140
  37.4 1.9 %collective-permute-start.14 = (bf16[256,512]{1,0:T(8,128)(2,1)}, bf16[256,512]{1,0:T(8,128)(2,1)S(1)}, u32[]{:S(2)}, u32[]{:S(2)}) collective-permute-start(bf16[256,512]{1,0:T(8,128)(2,1)} %get-tuple-element.134), channel_id=1, source_target_pairs={{0,5},{1,4},{2,7},{3,6},{4,1},{5,0},{6,3},{7,2},{8,13},{9,12},{10,... | collective-permute-start | bytes 786440 | tf_op jit(solution)/shard_map/ppermute | solution.py:192
  42.4 1.9 %expert_product.8 = (f32[135168,128]{1,0:T(8,128)}, bf16[384,4096]{1,0:T(8,128)(2,1)}) custom-call(s32[8]{0:T(128)S(1)} %iota_xor_fusion.1.sources, s32[4]{0:T(128)S(1)} %select_reduce_fusion.places, bf16[384,1024]{1,0:T(8,128)(2,1)S(1)} %bitcast.2, bf16[256,512]{1,0:T(8,128)(2,1)S(1)} %copy-done.9, ...), custom_call_target="tpu_custom_call", output_to_operand_aliasing={{0}: (7, {})} | custom-call | bytes 65536 | tf_op jit(solution)/shard_map/expert_product/pallas_call | solution.py:172
  44.3 2.8 %expert_product.9 = (f32[135168,128]{1,0:T(8,128)}, bf16[384,4096]{1,0:T(8,128)(2,1)}) custom-call(s32[8]{0:T(128)S(1)} %iota_xor_fusion.1.sources, s32[4]{0:T(128)S(1)} %select_reduce_fusion.places, bf16[384,1024]{1,0:T(8,128)(2,1)S(1)} %bitcast.3, bf16[256,512]{1,0:T(8,128)(2,1)S(1)} %copy-done.8, ...), custom_call_target="tpu_custom_call", output_to_operand_aliasing={{0}: (7, {}), {1}: (8, {})} | custom-call | bytes 65536 | tf_op jit(solution)/shard_map/expert_product/pallas_call | solution.py:172
  48.1 1.5 %collective-permute-start.16 = (bf16[256,512]{1,0:T(8,128)(2,1)S(1)}, bf16[256,512]{1,0:T(8,128)(2,1)S(1)}, u32[]{:S(2)}, u32[]{:S(2)}) collective-permute-start(bf16[256,512]{1,0:T(8,128)(2,1)S(1)} %get-tuple-element.137.refs_2_), channel_id=1, source_target_pairs={{0,8},{8,0},{16,24},{24,16},{1,9},{9,1},{17,25},{25,17},{2,10},{10... | collective-permute-start | bytes 786440 | tf_op jit(solution)/shard_map/ppermute | solution.py:192
  52.6 3.7 %collective-permute-done.15.refs_1_ = bf16[256,512]{1,0:T(8,128)(2,1)S(1)} collective-permute-done((bf16[256,512]{1,0:T(8,128)(2,1)S(1)}, bf16[256,512]{1,0:T(8,128)(2,1)S(1)}, u32[]{:S(2)}, u32[]{:S(2)}) %collective-permute-start.15) | collective-permute-done | bytes 262176 | tf_op jit(solution)/shard_map/ppermute | solution.py:192
  57.3 1.9 %expert_product.10 = (f32[135168,128]{1,0:T(8,128)}, bf16[384,4096]{1,0:T(8,128)(2,1)}) custom-call(s32[8]{0:T(128)S(1)} %iota_xor_fusion.1.sources, s32[4]{0:T(128)S(1)} %select_reduce_fusion.places, bf16[384,1024]{1,0:T(8,128)(2,1)S(1)} %bitcast.4, bf16[256,512]{1,0:T(8,128)(2,1)S(1)} %get-tuple-element.132.refs_0_, ...), custom_call_target="tpu_custom_call", output_to_operand_aliasing={{0}: (7, {}), {1}: (8, {})} | custom-call | bytes 65536 | tf_op jit(solution)/shard_map/expert_product/pallas_call | solution.py:172
  59.2 1.9 %expert_product.11 = (f32[135168,128]{1,0:T(8,128)}, bf16[384,4096]{1,0:T(8,128)(2,1)}) custom-call(s32[8]{0:T(128)S(1)} %iota_xor_fusion.1.sources, s32[4]{0:T(128)S(1)} %select_reduce_fusion.places, bf16[384,1024]{1,0:T(8,128)(2,1)S(1)} %bitcast.5, bf16[256,512]{1,0:T(8,128)(2,1)S(1)} %get-tuple-element.118.refs_0_, ...), custom_call_target="tpu_custom_call", output_to_operand_aliasing={{0}: (7, {}), {1}: (8, {})} | custom-call | bytes 65536 | tf_op jit(solution)/shard_map/expert_product/pallas_call | solution.py:172
  62.6 9.7 %collective-permute-done.19.refs_3_ = bf16[256,512]{1,0:T(8,128)(2,1)S(1)} collective-permute-done((bf16[256,512]{1,0:T(8,128)(2,1)S(1)}, bf16[256,512]{1,0:T(8,128)(2,1)S(1)}, u32[]{:S(2)}, u32[]{:S(2)}) %collective-permute-start.19) | collective-permute-done | bytes 262176 | tf_op jit(solution)/shard_map/ppermute | solution.py:192
  79.3 2.9 %collective-permute-done.24.refs_2_ = bf16[256,512]{1,0:T(8,128)(2,1)S(1)} collective-permute-done((bf16[256,512]{1,0:T(8,128)(2,1)S(1)}, bf16[256,512]{1,0:T(8,128)(2,1)S(1)}, u32[]{:S(2)}, u32[]{:S(2)}) %collective-permute-start.24) | collective-permute-done | bytes 262176 | tf_op jit(solution)/shard_map/ppermute | solution.py:192
  82.2 1.9 %expert_product.12 = (f32[135168,128]{1,0:T(8,128)}, bf16[384,4096]{1,0:T(8,128)(2,1)}) custom-call(s32[8]{0:T(128)S(1)} %iota_xor_fusion.1.sources, s32[4]{0:T(128)S(1)} %select_reduce_fusion.places, bf16[384,1024]{1,0:T(8,128)(2,1)S(1)} %bitcast.6, bf16[256,512]{1,0:T(8,128)(2,1)S(1)} %get-tuple-element.149.refs_0_, ...), custom_call_target="tpu_custom_call", output_to_operand_aliasing={{0}: (7, {}), {1}: (8, {})} | custom-call | bytes 65536 | tf_op jit(solution)/shard_map/expert_product/pallas_call | solution.py:172
  84.1 1.9 %expert_product.13 = (f32[135168,128]{1,0:T(8,128)}, bf16[384,4096]{1,0:T(8,128)(2,1)}) custom-call(s32[8]{0:T(128)S(1)} %iota_xor_fusion.1.sources, s32[4]{0:T(128)S(1)} %select_reduce_fusion.places, bf16[384,1024]{1,0:T(8,128)(2,1)S(1)} %bitcast.7, bf16[256,512]{1,0:T(8,128)(2,1)S(1)} %get-tuple-element.150.refs_0_, ...), custom_call_target="tpu_custom_call", output_to_operand_aliasing={{0}: (7, {}), {1}: (8, {})} | custom-call | bytes 65536 | tf_op jit(solution)/shard_map/expert_product/pallas_call | solution.py:172
  88.4 1.5 %collective-permute-done.27.refs_1_ = bf16[256,512]{1,0:T(8,128)(2,1)S(1)} collective-permute-done((bf16[256,512]{1,0:T(8,128)(2,1)S(1)}, bf16[256,512]{1,0:T(8,128)(2,1)S(1)}, u32[]{:S(2)}, u32[]{:S(2)}) %collective-permute-start.27) | collective-permute-done | bytes 262176 | tf_op jit(solution)/shard_map/ppermute | solution.py:192
  91.2 4.7 %collective-permute-done.29.refs_1_ = bf16[256,512]{1,0:T(8,128)(2,1)S(1)} collective-permute-done((bf16[256,512]{1,0:T(8,128)(2,1)S(1)}, bf16[256,512]{1,0:T(8,128)(2,1)S(1)}, u32[]{:S(2)}, u32[]{:S(2)}) %collective-permute-start.29) | collective-permute-done | bytes 262176 | tf_op jit(solution)/shard_map/ppermute | solution.py:192
  95.9 1.9 %expert_product.14 = (f32[135168,128]{1,0:T(8,128)}, bf16[384,4096]{1,0:T(8,128)(2,1)}) custom-call(s32[8]{0:T(128)S(1)} %iota_xor_fusion.1.sources, s32[4]{0:T(128)S(1)} %select_reduce_fusion.places, bf16[384,1024]{1,0:T(8,128)(2,1)S(1)} %bitcast.8, bf16[256,512]{1,0:T(8,128)(2,1)S(1)} %get-tuple-element.167.refs_0_, ...), custom_call_target="tpu_custom_call", output_to_operand_aliasing={{0}: (7, {}), {1}: (8, {})} | custom-call | bytes 65536 | tf_op jit(solution)/shard_map/expert_product/pallas_call | solution.py:172
  98.4 1.9 %expert_product.15 = (f32[135168,128]{1,0:T(8,128)}, bf16[384,4096]{1,0:T(8,128)(2,1)}) custom-call(s32[8]{0:T(128)S(1)} %iota_xor_fusion.1.sources, s32[4]{0:T(128)S(1)} %select_reduce_fusion.places, bf16[384,1024]{1,0:T(8,128)(2,1)S(1)} %bitcast.9, bf16[256,512]{1,0:T(8,128)(2,1)S(1)} %get-tuple-element.154.refs_0_, ...), custom_call_target="tpu_custom_call", output_to_operand_aliasing={{0}: (7, {}), {1}: (8, {})} | custom-call | bytes 65536 | tf_op jit(solution)/shard_map/expert_product/pallas_call | solution.py:172
  (98 shorter events, 27.4 us)
Async XLA Ops:
  6.4 12.1 %collective-permute-start.2 = (bf16[256,512]{1,0:T(8,128)(2,1)}, bf16[256,512]{1,0:T(8,128)(2,1)S(1)}, u32[]{:S(2)}, u32[]{:S(2)}) collective-permute-start(bf16[256,512]{1,0:T(8,128)(2,1)} %get-tuple-element.107.refs_0_), channel_id=1, source_target_pairs={{0,16},{8,24},{16,0},{24,8},{1,17},{9,25},{17,1},{25,9},{2,18},{10... | collective-permute-start | bytes 786440 | tf_op jit(solution)/shard_map/ppermute | solution.py:192
  12.8 10.2 %collective-permute-start.4 = (bf16[256,512]{1,0:T(8,128)(2,1)S(1)}, bf16[256,512]{1,0:T(8,128)(2,1)}, u32[]{:S(2)}, u32[]{:S(2)}) collective-permute-start(bf16[256,512]{1,0:T(8,128)(2,1)S(1)} %get-tuple-element.110.refs_0_), channel_id=1, source_target_pairs={{0,16},{8,24},{16,0},{24,8},{1,17},{9,25},{17,1},{25,9},{2,18},{10... | collective-permute-start | bytes 786440 | tf_op jit(solution)/shard_map/ppermute | solution.py:192
  13.3 10.9 %collective-permute-start.5 = (bf16[256,512]{1,0:T(8,128)(2,1)S(1)}, bf16[256,512]{1,0:T(8,128)(2,1)S(1)}, u32[]{:S(2)}, u32[]{:S(2)}) collective-permute-start(bf16[256,512]{1,0:T(8,128)(2,1)S(1)} %copy-done.13), channel_id=1, source_target_pairs={{0,2},{1,3},{2,0},{3,1},{4,6},{5,7},{6,4},{7,5},{8,10},{9,11},{10,... | collective-permute-start | bytes 786440 | tf_op jit(solution)/shard_map/ppermute | solution.py:192
  13.8 15.1 %collective-permute-start.6 = (bf16[256,512]{1,0:T(8,128)(2,1)S(1)}, bf16[256,512]{1,0:T(8,128)(2,1)S(1)}, u32[]{:S(2)}, u32[]{:S(2)}) collective-permute-start(bf16[256,512]{1,0:T(8,128)(2,1)S(1)} %copy-done.12), channel_id=1, source_target_pairs={{0,3},{1,2},{2,1},{3,0},{4,7},{5,6},{6,5},{7,4},{8,11},{9,10},{10,... | collective-permute-start | bytes 786440 | tf_op jit(solution)/shard_map/ppermute | solution.py:192
  18.6 17.7 %collective-permute-start.7 = (bf16[256,512]{1,0:T(8,128)(2,1)S(1)}, bf16[256,512]{1,0:T(8,128)(2,1)S(1)}, u32[]{:S(2)}, u32[]{:S(2)}) collective-permute-start(bf16[256,512]{1,0:T(8,128)(2,1)S(1)} %get-tuple-element.122.refs_1_), channel_id=1, source_target_pairs={{0,16},{8,24},{16,0},{24,8},{1,17},{9,25},{17,1},{25,9},{2,18},{10... | collective-permute-start | bytes 786440 | tf_op jit(solution)/shard_map/ppermute | solution.py:192
  20.3 16.0 %collective-permute-start.9 = (bf16[256,512]{1,0:T(8,128)(2,1)}, bf16[256,512]{1,0:T(8,128)(2,1)S(1)}, u32[]{:S(2)}, u32[]{:S(2)}) collective-permute-start(bf16[256,512]{1,0:T(8,128)(2,1)} %get-tuple-element.123), channel_id=1, source_target_pairs={{0,4},{1,5},{2,6},{3,7},{4,0},{5,1},{6,2},{7,3},{8,12},{9,13},{10,... | collective-permute-start | bytes 786440 | tf_op jit(solution)/shard_map/ppermute | solution.py:192
  22.9 14.5 %collective-permute-start.8 = (bf16[256,512]{1,0:T(8,128)(2,1)}, bf16[256,512]{1,0:T(8,128)(2,1)S(1)}, u32[]{:S(2)}, u32[]{:S(2)}) collective-permute-start(bf16[256,512]{1,0:T(8,128)(2,1)} %get-tuple-element.120.refs_2_), channel_id=1, source_target_pairs={{0,8},{8,0},{16,24},{24,16},{1,9},{9,1},{17,25},{25,17},{2,10},{10... | collective-permute-start | bytes 786440 | tf_op jit(solution)/shard_map/ppermute | solution.py:192
  29.0 18.1 %collective-permute-start.10 = (bf16[256,512]{1,0:T(8,128)(2,1)S(1)}, bf16[256,512]{1,0:T(8,128)(2,1)S(1)}, u32[]{:S(2)}, u32[]{:S(2)}) collective-permute-start(bf16[256,512]{1,0:T(8,128)(2,1)S(1)} %get-tuple-element.132.refs_0_), channel_id=1, source_target_pairs={{0,8},{8,0},{16,24},{24,16},{1,9},{9,1},{17,25},{25,17},{2,10},{10... | collective-permute-start | bytes 786440 | tf_op jit(solution)/shard_map/ppermute | solution.py:192
  29.0 20.6 %collective-permute-start.12 = (bf16[256,512]{1,0:T(8,128)(2,1)S(1)}, bf16[256,512]{1,0:T(8,128)(2,1)S(1)}, u32[]{:S(2)}, u32[]{:S(2)}) collective-permute-start(bf16[256,512]{1,0:T(8,128)(2,1)S(1)} %get-tuple-element.132.refs_0_), channel_id=1, source_target_pairs={{0,16},{8,24},{16,0},{24,8},{1,17},{9,25},{17,1},{25,9},{2,18},{10... | collective-permute-start | bytes 786440 | tf_op jit(solution)/shard_map/ppermute | solution.py:192
  36.2 10.8 %collective-permute-start.11 = (bf16[256,512]{1,0:T(8,128)(2,1)S(1)}, bf16[256,512]{1,0:T(8,128)(2,1)S(1)}, u32[]{:S(2)}, u32[]{:S(2)}) collective-permute-start(bf16[256,512]{1,0:T(8,128)(2,1)S(1)} %get-tuple-element.118.refs_0_), channel_id=1, source_target_pairs={{0,16},{8,24},{16,0},{24,8},{1,17},{9,25},{17,1},{25,9},{2,18},{10... | collective-permute-start | bytes 786440 | tf_op jit(solution)/shard_map/ppermute | solution.py:192
  36.3 13.8 %collective-permute-start.13 = (bf16[256,512]{1,0:T(8,128)(2,1)S(1)}, bf16[256,512]{1,0:T(8,128)(2,1)S(1)}, u32[]{:S(2)}, u32[]{:S(2)}) collective-permute-start(bf16[256,512]{1,0:T(8,128)(2,1)S(1)} %get-tuple-element.118.refs_0_), channel_id=1, source_target_pairs={{0,8},{8,0},{16,24},{24,16},{1,9},{9,1},{17,25},{25,17},{2,10},{10... | collective-permute-start | bytes 786440 | tf_op jit(solution)/shard_map/ppermute | solution.py:192
  37.4 13.1 %collective-permute-start.14 = (bf16[256,512]{1,0:T(8,128)(2,1)}, bf16[256,512]{1,0:T(8,128)(2,1)S(1)}, u32[]{:S(2)}, u32[]{:S(2)}) collective-permute-start(bf16[256,512]{1,0:T(8,128)(2,1)} %get-tuple-element.134), channel_id=1, source_target_pairs={{0,5},{1,4},{2,7},{3,6},{4,1},{5,0},{6,3},{7,2},{8,13},{9,12},{10,... | collective-permute-start | bytes 786440 | tf_op jit(solution)/shard_map/ppermute | solution.py:192
  47.1 9.2 %collective-permute-start.15 = (bf16[256,512]{1,0:T(8,128)(2,1)S(1)}, bf16[256,512]{1,0:T(8,128)(2,1)S(1)}, u32[]{:S(2)}, u32[]{:S(2)}) collective-permute-start(bf16[256,512]{1,0:T(8,128)(2,1)S(1)} %get-tuple-element.139.refs_1_), channel_id=1, source_target_pairs={{0,16},{8,24},{16,0},{24,8},{1,17},{9,25},{17,1},{25,9},{2,18},{10... | collective-permute-start | bytes 786440 | tf_op jit(solution)/shard_map/ppermute | solution.py:192
  49.6 12.4 %collective-permute-start.17 = (bf16[256,512]{1,0:T(8,128)(2,1)S(1)}, bf16[256,512]{1,0:T(8,128)(2,1)S(1)}, u32[]{:S(2)}, u32[]{:S(2)}) collective-permute-start(bf16[256,512]{1,0:T(8,128)(2,1)S(1)} %get-tuple-element.149.refs_0_), channel_id=1, source_target_pairs={{0,8},{8,0},{16,24},{24,16},{1,9},{9,1},{17,25},{25,17},{2,10},{10... | collective-permute-start | bytes 786440 | tf_op jit(solution)/shard_map/ppermute | solution.py:192
  50.5 12.1 %collective-permute-start.18 = (bf16[256,512]{1,0:T(8,128)(2,1)S(1)}, bf16[256,512]{1,0:T(8,128)(2,1)S(1)}, u32[]{:S(2)}, u32[]{:S(2)}) collective-permute-start(bf16[256,512]{1,0:T(8,128)(2,1)S(1)} %get-tuple-element.150.refs_0_), channel_id=1, source_target_pairs={{0,16},{8,24},{16,0},{24,8},{1,17},{9,25},{17,1},{25,9},{2,18},{10... | collective-permute-start | bytes 786440 | tf_op jit(solution)/shard_map/ppermute | solution.py:192
  51.8 20.4 %collective-permute-start.19 = (bf16[256,512]{1,0:T(8,128)(2,1)S(1)}, bf16[256,512]{1,0:T(8,128)(2,1)S(1)}, u32[]{:S(2)}, u32[]{:S(2)}) collective-permute-start(bf16[256,512]{1,0:T(8,128)(2,1)S(1)} %get-tuple-element.151), channel_id=1, source_target_pairs={{0,6},{1,7},{2,4},{3,5},{4,2},{5,3},{6,0},{7,1},{8,14},{9,15},{10,... | collective-permute-start | bytes 786440 | tf_op jit(solution)/shard_map/ppermute | solution.py:192
  56.3 17.9 %collective-permute-start.20 = (bf16[256,512]{1,0:T(8,128)(2,1)S(1)}, bf16[256,512]{1,0:T(8,128)(2,1)S(1)}, u32[]{:S(2)}, u32[]{:S(2)}) collective-permute-start(bf16[256,512]{1,0:T(8,128)(2,1)S(1)} %get-tuple-element.149.refs_0_), channel_id=1, source_target_pairs={{0,16},{8,24},{16,0},{24,8},{1,17},{9,25},{17,1},{25,9},{2,18},{10... | collective-permute-start | bytes 786440 | tf_op jit(solution)/shard_map/ppermute | solution.py:192
  57.3 18.2 %collective-permute-start.22 = (bf16[256,512]{1,0:T(8,128)(2,1)S(1)}, bf16[256,512]{1,0:T(8,128)(2,1)S(1)}, u32[]{:S(2)}, u32[]{:S(2)}) collective-permute-start(bf16[256,512]{1,0:T(8,128)(2,1)S(1)} %get-tuple-element.153), channel_id=1, source_target_pairs={{0,7},{1,6},{2,5},{3,4},{4,3},{5,2},{6,1},{7,0},{8,15},{9,14},{10,... | collective-permute-start | bytes 786440 | tf_op jit(solution)/shard_map/ppermute | solution.py:192
  62.0 14.3 %collective-permute-start.21 = (bf16[256,512]{1,0:T(8,128)(2,1)S(1)}, bf16[256,512]{1,0:T(8,128)(2,1)S(1)}, u32[]{:S(2)}, u32[]{:S(2)}) collective-permute-start(bf16[256,512]{1,0:T(8,128)(2,1)S(1)} %get-tuple-element.150.refs_0_), channel_id=1, source_target_pairs={{0,8},{8,0},{16,24},{24,16},{1,9},{9,1},{17,25},{25,17},{2,10},{10... | collective-permute-start | bytes 786440 | tf_op jit(solution)/shard_map/ppermute | solution.py:192
  72.9 9.2 %collective-permute-start.24 = (bf16[256,512]{1,0:T(8,128)(2,1)S(1)}, bf16[256,512]{1,0:T(8,128)(2,1)S(1)}, u32[]{:S(2)}, u32[]{:S(2)}) collective-permute-start(bf16[256,512]{1,0:T(8,128)(2,1)S(1)} %get-tuple-element.156.refs_2_), channel_id=1, source_target_pairs={{0,8},{8,0},{16,24},{24,16},{1,9},{9,1},{17,25},{25,17},{2,10},{10... | collective-permute-start | bytes 786440 | tf_op jit(solution)/shard_map/ppermute | solution.py:192
  74.3 12.9 %collective-permute-start.25 = (bf16[256,512]{1,0:T(8,128)(2,1)S(1)}, bf16[256,512]{1,0:T(8,128)(2,1)S(1)}, u32[]{:S(2)}, u32[]{:S(2)}) collective-permute-start(bf16[256,512]{1,0:T(8,128)(2,1)S(1)} %get-tuple-element.167.refs_0_), channel_id=1, source_target_pairs={{0,8},{8,0},{16,24},{24,16},{1,9},{9,1},{17,25},{25,17},{2,10},{10... | collective-permute-start | bytes 786440 | tf_op jit(solution)/shard_map/ppermute | solution.py:192
  75.5 11.6 %collective-permute-start.26 = (bf16[256,512]{1,0:T(8,128)(2,1)S(1)}, bf16[256,512]{1,0:T(8,128)(2,1)S(1)}, u32[]{:S(2)}, u32[]{:S(2)}) collective-permute-start(bf16[256,512]{1,0:T(8,128)(2,1)S(1)} %get-tuple-element.167.refs_0_), channel_id=1, source_target_pairs={{0,16},{8,24},{16,0},{24,8},{1,17},{9,25},{17,1},{25,9},{2,18},{10... | collective-permute-start | bytes 786440 | tf_op jit(solution)/shard_map/ppermute | solution.py:192
  76.3 13.6 %collective-permute-start.27 = (bf16[256,512]{1,0:T(8,128)(2,1)S(1)}, bf16[256,512]{1,0:T(8,128)(2,1)S(1)}, u32[]{:S(2)}, u32[]{:S(2)}) collective-permute-start(bf16[256,512]{1,0:T(8,128)(2,1)S(1)} %get-tuple-element.154.refs_0_), channel_id=1, source_target_pairs={{0,8},{8,0},{16,24},{24,16},{1,9},{9,1},{17,25},{25,17},{2,10},{10... | collective-permute-start | bytes 786440 | tf_op jit(solution)/shard_map/ppermute | solution.py:192
  78.7 11.3 %collective-permute-start.28 = (bf16[256,512]{1,0:T(8,128)(2,1)S(1)}, bf16[256,512]{1,0:T(8,128)(2,1)S(1)}, u32[]{:S(2)}, u32[]{:S(2)}) collective-permute-start(bf16[256,512]{1,0:T(8,128)(2,1)S(1)} %get-tuple-element.154.refs_0_), channel_id=1, source_target_pairs={{0,16},{8,24},{16,0},{24,8},{1,17},{9,25},{17,1},{25,9},{2,18},{10... | collective-permute-start | bytes 786440 | tf_op jit(solution)/shard_map/ppermute | solution.py:192
  (22 other events, 138.5 us)

commit v7 on v6

--- a/solution.py
+++ b/solution.py
@@ -1,5 +1,6 @@
 import collections
 import functools
+import math
 
 import jax
 import jax.numpy as jnp
@@ -9,6 +10,7 @@
 from jax.sharding import PartitionSpec as P
 
 QB = 128
+GROUP = 32
 VMEM_LIMIT = 60 * 1024 * 1024
 PRODUCT_LIMIT = 16 * 1024 * 1024
 
@@ -51,84 +53,105 @@
     )(*arrays)
 
 
-def adam_kernel(numbers, passed, owner, *refs):
+def adam_kernel(base, blocks, passed, owner, *refs):
     arrays, outs = refs[:4], refs[4 + passed : 7 + passed]
-    sends = refs[7 + passed : 7 + passed + len(numbers)]
+    sends = refs[7 + passed : 7 + passed + blocks]
     *buffers, semaphores = refs[-9:]
+    master, gradient, first, second, new_master, new_first, new_second, sent = buffers
     experts, rows, columns = arrays[0].shape
     shard = lax.axis_index("shard")
-    chunks = [(n, i) for n in range(len(numbers)) for i in range(rows // QB)]
-    held = []
-    for number in numbers:
+    bands = rows // QB
+    starts = range(0, columns, QB)
+
+    def copies(chunk, inward):
+        n, i = chunk // bands, chunk % bands
         expert = jnp.int32(0)
         for candidate in range(experts):
-            expert = jnp.where(owner[candidate] == shard ^ number, candidate, expert)
-        held.append(expert)
-
-    def copies(chunk, inward):
-        n, i = chunk
-        span = pl.ds(i * QB, QB)
-        outer = arrays if inward else (*outs, sends[n])
-        for k, ref in enumerate(outer):
-            far = ref.at[span] if ref is sends[n] else ref.at[held[n], span]
-            near = buffers[k if inward else 4 + k].at[n, span]
+            expert = jnp.where(owner[candidate] == shard ^ (base + n), candidate, expert)
+        span = pl.ds(pl.multiple_of(i * QB, QB), QB)
+        for k, ref in enumerate(arrays if inward else outs):
+            far, near = ref.at[expert, span], buffers[k if inward else 4 + k].at[n, span]
             pair = (far, near) if inward else (near, far)
-            yield pltpu.make_async_copy(*pair, semaphores.at[n, i, k if inward else 4 + k])
-
-    def update(chunk):
-        n, i = chunk
-        master, gradient, first, second, new_master, new_first, new_second, _ = buffers
-        peaks = []
-        for start in range(0, columns, QB):
-            at = (n, slice(i * QB, (i + 1) * QB), slice(start, start + QB))
-            grad = gradient[at].astype(jnp.float32)
-            moment_one = beta_one * first[at].astype(jnp.float32) + (1.0 - beta_one) * grad
-            moment_two = beta_two * second[at].astype(jnp.float32) + (
-                ((1.0 - beta_two) * grad) * grad
-            )
-            new_first[at] = moment_one.astype(jnp.bfloat16)
-            new_second[at] = moment_two.astype(jnp.bfloat16)
-            guess = lax.rsqrt(moment_two)
-            root = moment_two * guess + root_epsilon
-            inverse = guess * (2.0 - root * guess)
-            updated = master[at] - (step_size * moment_one) * inverse
-            new_master[at] = updated
-            peaks.append(jnp.max(jnp.abs(updated), axis=0, keepdims=True))
+            yield pltpu.make_async_copy(*pair, semaphores.at[chunk, k if inward else 4 + k])
+
+    def send_copy(chunk, block):
+        span = pl.ds(pl.multiple_of(chunk % bands * QB, QB), QB)
+        return pltpu.make_async_copy(
+            sent.at[block, span], sends[block].at[span], semaphores.at[chunk, 7]
+        )
+
+    def begin(chunk, carry):
+        for copy in copies(chunk, True):
+            copy.start()
+        return carry
+
+    def work(chunk, carry):
+        for copy in copies(chunk, True):
+            copy.wait()
+        n, i = chunk // bands, chunk % bands
+
+        def span(group):
+            return pl.ds(pl.multiple_of(i * QB + group * GROUP, GROUP), GROUP)
+
+        def update(group, peaks):
+            found = []
+            for start, peak in zip(starts, peaks):
+                at = (n, span(group), slice(start, start + QB))
+                grad = gradient[at].astype(jnp.float32)
+                moment_one = beta_one * first[at].astype(jnp.float32) + (1.0 - beta_one) * grad
+                moment_two = beta_two * second[at].astype(jnp.float32) + (
+                    ((1.0 - beta_two) * grad) * grad
+                )
+                new_first[at] = moment_one.astype(jnp.bfloat16)
+                new_second[at] = moment_two.astype(jnp.bfloat16)
+                guess = lax.rsqrt(moment_two)
+                root = moment_two * guess + root_epsilon
+                inverse = guess * (2.0 - root * guess)
+                updated = master[at] - (step_size * moment_one) * inverse
+                new_master[at] = updated
+                sizes = jnp.abs(updated).reshape(GROUP // 8, 8, QB)
+                found.append(jnp.maximum(peak, jnp.max(sizes, axis=0)))
+            return tuple(found)
+
+        empty = tuple(jnp.zeros((8, QB), jnp.float32) for _ in starts)
+        peaks = lax.fori_loop(0, QB // GROUP, update, empty)
+        peaks = [jnp.max(peak, axis=0, keepdims=True) for peak in peaks]
         largest = jnp.max(jnp.concatenate(peaks, axis=0), axis=1, keepdims=True)
         scale = ((largest + scale_epsilon) * (1.0 / quant_limit)).astype(jnp.bfloat16)
         scale = jnp.broadcast_to(scale, (len(peaks), QB))
-        return scale, 1.0 / scale.astype(jnp.float32)
-
-    def quantize(chunk, scale, inverse_scale):
-        n, i = chunk
-        for block, start in enumerate(range(0, columns, QB)):
-            at = (n, slice(i * QB, (i + 1) * QB), slice(start, start + QB))
-            one = slice(block, block + 1)
-            quantized = (buffers[4][at] * inverse_scale[one]).astype(jnp.bfloat16)
-            buffers[7][at] = quantized * scale[one]
+        inverse_scale = 1.0 / scale.astype(jnp.float32)
+
+        def quantize(group, carry):
+            for block, start in enumerate(starts):
+                at = (n, span(group), slice(start, start + QB))
+                one = slice(block, block + 1)
+                quantized = (new_master[at] * inverse_scale[one]).astype(jnp.bfloat16)
+                sent[at] = quantized * scale[one]
+            return carry
+
+        lax.fori_loop(0, QB // GROUP, quantize, 0)
         for copy in copies(chunk, False):
             copy.start()
-
-    for chunk in chunks:
-        for copy in copies(chunk, True):
-            copy.start()
-    pending = None
-    for chunk in chunks:
-        for copy in copies(chunk, True):
-            copy.wait()
-        scales = update(chunk)
-        if pending:
-            quantize(*pending)
-        pending = (chunk, *scales)
-    quantize(*pending)
-    for chunk in chunks:
+        for block in range(blocks):
+
+            @pl.when(n == block)
+            def _():
+                send_copy(chunk, block).start()
+
+        return carry
+
+    def finish(chunk, carry):
         for copy in copies(chunk, False):
             copy.wait()
-
-
-def adam_blocks(numbers, owner, arrays, carried, token, fenced):
+        send_copy(chunk, 0).wait()
+        return carry
+
+    for part in (begin, work, finish):
+        lax.fori_loop(0, blocks * bands, part, 0)
+
+
+def adam_blocks(base, blocks, owner, arrays, carried, token, fenced):
     _, rows, columns = arrays[0].shape
-    blocks = len(numbers)
     passed = len(carried) + len(token)
     made = [like(arrays[0]), like(arrays[2]), like(arrays[3])]
     made += [jax.ShapeDtypeStruct((rows, columns), jnp.bfloat16)] * blocks
@@ -138,12 +161,12 @@
     made += [jax.ShapeDtypeStruct(TOKEN, jnp.float32)] * fenced
     kinds = [jnp.float32, jnp.bfloat16, jnp.bfloat16, jnp.bfloat16] * 2
     results = pl.pallas_call(
-        functools.partial(adam_kernel, numbers, passed),
+        functools.partial(adam_kernel, base, blocks, passed),
         in_specs=[pl.BlockSpec(memory_space=pltpu.SMEM)] + [WHOLE] * (4 + passed),
         out_specs=[WHOLE] * len(made),
         out_shape=made,
         scratch_shapes=[pltpu.VMEM((blocks, rows, columns), kind) for kind in kinds]
-        + [pltpu.SemaphoreType.DMA((blocks, rows // QB, 8))],
+        + [pltpu.SemaphoreType.DMA((blocks * (rows // QB), 8))],
         input_output_aliases=aliases,
         compiler_params=pltpu.CompilerParams(vmem_limit_bytes=VMEM_LIMIT),
         cost_estimate=SMALL_COST,
@@ -152,13 +175,14 @@
     return results[:3], results[3 : 3 + blocks], tuple(results[3 + blocks :])
 
 
-def product_kernel(number, slabs, sources, places, left, *refs):
+def product_kernel(slabs, sources, places, left, *refs):
     out = refs[-1]
-    rows = refs[0].shape[0]
+    rows, breadth = refs[0].shape[0], out.shape[1]
     parts = [left[:, pl.ds(pl.multiple_of(places[i] * rows, QB), rows)] for i in range(slabs)]
+    span = pl.ds(pl.multiple_of(pl.program_id(0) * breadth, QB), breadth)
     total = jnp.dot(
         jnp.concatenate(parts, axis=1),
-        jnp.concatenate([right[...] for right in refs[:slabs]], axis=0),
+        jnp.concatenate([right[:, span] for right in refs[:slabs]], axis=0),
         preferred_element_type=jnp.float32,
     )
     out[...] = total.astype(out.dtype)
@@ -169,14 +193,19 @@
     tokens, units = token_rows.shape
     rows, columns = weights[0].shape
     passed = len(token) + len(carried)
+    tile = math.gcd(columns, 2 * QB)
+
+    def place(i, sources, places):
+        return 0, sources[number] * (columns // tile) + i
+
     *token, out = pl.pallas_call(
-        functools.partial(product_kernel, number, slabs),
+        functools.partial(product_kernel, slabs),
         grid_spec=pltpu.PrefetchScalarGridSpec(
             num_scalar_prefetch=2,
-            grid=(1,),
+            grid=(columns // tile,),
             in_specs=[pl.BlockSpec(memory_space=pltpu.VMEM)] * (1 + slabs) + [WHOLE] * passed,
             out_specs=[WHOLE] * len(token)
-            + [pl.BlockSpec((tokens, columns), lambda i, sources, places: (0, sources[number]))],
+            + [pl.BlockSpec((tokens, tile), place)],
         ),
         out_shape=[like(array) for array in token]
             + [jax.ShapeDtypeStruct((tokens, breadth), jnp.bfloat16)],
@@ -211,11 +240,11 @@
     made, due, ready = {}, collections.defaultdict(list), set()
     state = {"adam": (), "token": (), "out": ()}
 
-    def adam(*numbers):
+    def adam(base, blocks):
         state["adam"], sends, state["token"] = adam_blocks(
-            numbers, owner_of_expert, arrays, tuple(state["adam"]), state["token"], fenced
+            base, blocks, owner_of_expert, arrays, tuple(state["adam"]), state["token"], fenced
         )
-        made.update(zip(numbers, sends))
+        made.update(zip(range(base, base + blocks), sends))
 
     def deliver(block):
         held[block][0] = swap(made[block], "shard", shards, block) if block else made[block]
@@ -247,9 +276,9 @@
             fences[until][0].extend((block, member ^ bit) for block, member, bit in keys)
 
         plan(0, 2, (1, 0, 1), (1, 0, 2))
-        plan(1, 3, (0, 1, 2))
+        plan(0, 3, (0, 1, 2))
         plan(2, 3, (1, 2, 1))
-        plan(2.5, 4, (2, 0, 1), (3, 0, 2))
+        plan(2.5, 4, (3, 0, 2), (2, 0, 1))
         plan(3, 5, (2, 0, 2), (3, 0, 1))
         plan(4, 6, (2, 1, 2), (3, 2, 1))
         for pair in range(2, pairs):
@@ -265,19 +294,19 @@
                 plan(step + 2, step + 4, (odd, 2, 1))
         for block in range(4, shards):
             first = min(2 * block - 7, 3 * (block // 2) - 3)
-            fences[first][2].append(block)
+            if first > 1:
+                fences[first][2].append(block)
             fences[first + 2][0].append((block, 0))
-        fences[0][0].append((1, 0))
-        fences[1][0].extend([(0, 1), (0, 2)])
+        fences[0][0].extend([(1, 0), (0, 1), (0, 2)])
         fences[2.5][0].extend([(2, 0), (3, 0)])
 
-        adam(0, 1)
+        adam(0, 2)
         deliver(0)
         deliver(1)
         ready.add((0, 0))
         send(0, 0, 1)
         send(0, 0, 2)
-        adam(2, 3)
+        adam(2, 2)
         deliver(2)
         deliver(3)
         computed = 4
@@ -288,8 +317,10 @@
                 deliver(block)
             for key in sending:
                 send(*key)
-            if step not in (1, 2) and computed < shards:
-                adam(computed, computed + 1)
+            if computed < shards:
+                adam(computed, 2)
+                if not step:
+                    deliver(computed)
                 computed += 2
             for block in list(waiting):
                 if all((block, member) in ready for member in range(replicas)):
@@ -297,7 +328,7 @@
                     waiting.remove(block)
     else:
         for pair in range(pairs):
-            adam(2 * pair, 2 * pair + 1)
+            adam(2 * pair, 2)
         for block in range(shards):
             deliver(block)
             for number in range(len(bits)):

time: 101 us -> 103 us (1.020)
  Pallas kernels: 32.7 us -> 34.2 us
  starting transfers between devices: 30.8 us -> 32.1 us
    pallas_call x12, Pallas kernels: 32.7 us -> 34.2 us  [the longest x4 18.1 us: adam_blocks(): pl.pallas_call(functools.partial(adam_kernel, base, blocks, passed), in_s...]
    ppermute x31, starting transfers between devices: 30.8 us -> 32.1 us  [swap(): return lax.ppermute(value, axis, [(i, i ^ mask) for i in range(size)])]
    unnamed x30 -> x34, local copies, waits for them, and re-layouts: 2.89 us -> 2.9 us
  transfers between devices with their start and end apart: 31 -> 31, of which waited for: 14 -> 15; matrix products, arithmetic and copies ran while one was open for 0% -> 0% of each run, Pallas kernels for 27% -> 27%
where the time goes in v7:
time: 103 us
  Pallas kernels  34.2 us (33%)
  waiting for transfers between devices  32.4 us (31%)
  starting transfers between devices  32.1 us (31%)
  local copies, waits for them, and re-layouts  2.9 us (3%)
    ppermute x31, waiting for transfers between devices, swap(): return lax.ppermute(value, axis, [(i, i ^ mask) for i in range(size)])  32.4 us
    ppermute x31, starting transfers between devices, swap(): return lax.ppermute(value, axis, [(i, i ^ mask) for i in range(size)])  32.1 us
    pallas_call x4, Pallas kernels, adam_blocks(): pl.pallas_call(functools.partial(adam_kernel, base, blocks, passed), in_s...  18.1 us
    pallas_call x8, Pallas kernels, product(): pl.pallas_call(functools.partial(product_kernel, slabs), grid_spec=pltpu....  16 us
    unnamed x34, local copies, waits for them, and re-layouts  2.9 us
  transfers between devices with their start and end apart: 31, of which 15 were waited for; matrix products, arithmetic and copies ran while one was open for 0% of the time, Pallas kernels for 27%

profile of v7, /device:TPU:8, one launch (start us, length us, event | category | flops | bytes accessed | tf_op | source)
XLA Modules:
  0.0 102.6 jit_solution(10278922788406842967)
XLA Ops:
  0.6 4.5 %adam_quantize.4 = (f32[8,256,512]{2,1,0:T(8,128)}, bf16[8,256,512]{2,1,0:T(8,128)(2,1)}, bf16[8,256,512]{2,1,0:T(8,128)(2,1)}, bf16[256,512]{1,0:T(8,128)(2,1)}...) custom-call(s32[8]{0:T(128)} %owner.7, f32[8,256,512]{2,1,0:T(8,128)} %refs_0_.7, bf16[8,256,512]{2,1,0:T(8,128)(2,1)} %refs_1_.7, ...), custom_call_target="tpu_custom_call" | custom-call | bytes 65536 | tf_op jit(solution)/shard_map/adam_quantize/pallas_call | solution.py:163
  5.2 1.6 %collective-permute-start.1 = (bf16[256,512]{1,0:T(8,128)(2,1)}, bf16[256,512]{1,0:T(8,128)(2,1)S(1)}, u32[]{:S(2)}, u32[]{:S(2)}) collective-permute-start(bf16[256,512]{1,0:T(8,128)(2,1)} %get-tuple-element.100.refs_0_), channel_id=1, source_target_pairs={{0,8},{8,0},{16,24},{24,16},{1,9},{9,1},{17,25},{25,17},{2,10},{10... | collective-permute-start | bytes 786440 | tf_op jit(solution)/shard_map/ppermute | solution.py:221
  8.3 4.5 %adam_quantize.5 = (f32[8,256,512]{2,1,0:T(8,128)}, bf16[8,256,512]{2,1,0:T(8,128)(2,1)}, bf16[8,256,512]{2,1,0:T(8,128)(2,1)}, bf16[256,512]{1,0:T(8,128)(2,1)}...) custom-call(s32[8]{0:T(128)} %owner.7, ...), custom_call_target="tpu_custom_call", output_to_operand_aliasing={{0}: (5, {}), {1}: (6, {}), {2}: (7, {}), {5}: (8, {})} | custom-call | bytes 65536 | tf_op jit(solution)/shard_map/adam_quantize/pallas_call | solution.py:163
  17.3 4.5 %adam_quantize.6 = (f32[8,256,512]{2,1,0:T(8,128)}, bf16[8,256,512]{2,1,0:T(8,128)(2,1)}, bf16[8,256,512]{2,1,0:T(8,128)(2,1)}, bf16[256,512]{1,0:T(8,128)(2,1)}...) custom-call(s32[8]{0:T(128)} %owner.7, ...), custom_call_target="tpu_custom_call", output_to_operand_aliasing={{0}: (5, {}), {1}: (6, {}), {2}: (7, {}), {5}: (8, {})} | custom-call | bytes 65536 | tf_op jit(solution)/shard_map/adam_quantize/pallas_call | solution.py:163
  21.9 2.7 %collective-permute-start.9 = (bf16[256,512]{1,0:T(8,128)(2,1)}, bf16[256,512]{1,0:T(8,128)(2,1)S(1)}, u32[]{:S(2)}, u32[]{:S(2)}) collective-permute-start(bf16[256,512]{1,0:T(8,128)(2,1)} %get-tuple-element.119), channel_id=1, source_target_pairs={{0,4},{1,5},{2,6},{3,7},{4,0},{5,1},{6,2},{7,3},{8,12},{9,13},{10,... | collective-permute-start | bytes 786440 | tf_op jit(solution)/shard_map/ppermute | solution.py:221
  25.1 1.6 %collective-permute-start.8 = (bf16[256,512]{1,0:T(8,128)(2,1)S(1)}, bf16[256,512]{1,0:T(8,128)(2,1)S(1)}, u32[]{:S(2)}, u32[]{:S(2)}) collective-permute-start(bf16[256,512]{1,0:T(8,128)(2,1)S(1)} %get-tuple-element.116.refs_2_), channel_id=1, source_target_pairs={{0,8},{8,0},{16,24},{24,16},{1,9},{9,1},{17,25},{25,17},{2,10},{10... | collective-permute-start | bytes 786440 | tf_op jit(solution)/shard_map/ppermute | solution.py:221
  26.6 4.5 %adam_quantize.7 = (f32[8,256,512]{2,1,0:T(8,128)}, bf16[8,256,512]{2,1,0:T(8,128)(2,1)}, bf16[8,256,512]{2,1,0:T(8,128)(2,1)}, bf16[256,512]{1,0:T(8,128)(2,1)}...) custom-call(s32[8]{0:T(128)} %owner.7, ...), custom_call_target="tpu_custom_call", output_to_operand_aliasing={{0}: (5, {}), {1}: (6, {}), {2}: (7, {}), {5}: (8, {})} | custom-call | bytes 65536 | tf_op jit(solution)/shard_map/adam_quantize/pallas_call | solution.py:163
  33.3 3.1 %collective-permute-done.9.refs_3_ = bf16[256,512]{1,0:T(8,128)(2,1)S(1)} collective-permute-done((bf16[256,512]{1,0:T(8,128)(2,1)}, bf16[256,512]{1,0:T(8,128)(2,1)S(1)}, u32[]{:S(2)}, u32[]{:S(2)}) %collective-permute-start.9) | collective-permute-done | bytes 262176 | tf_op jit(solution)/shard_map/ppermute | solution.py:221
  38.5 2.8 %collective-permute-start.14 = (bf16[256,512]{1,0:T(8,128)(2,1)}, bf16[256,512]{1,0:T(8,128)(2,1)S(1)}, u32[]{:S(2)}, u32[]{:S(2)}) collective-permute-start(bf16[256,512]{1,0:T(8,128)(2,1)} %get-tuple-element.130), channel_id=1, source_target_pairs={{0,5},{1,4},{2,7},{3,6},{4,1},{5,0},{6,3},{7,2},{8,13},{9,12},{10,... | collective-permute-start | bytes 786440 | tf_op jit(solution)/shard_map/ppermute | solution.py:221
  44.4 2.0 %expert_product.8 = (f32[135168,128]{1,0:T(8,128)}, bf16[384,4096]{1,0:T(8,128)(2,1)}) custom-call(s32[8]{0:T(128)S(1)} %iota_xor_fusion.1.sources, s32[4]{0:T(128)S(1)} %select_reduce_fusion.places, bf16[384,1024]{1,0:T(8,128)(2,1)S(1)} %bitcast.2, bf16[256,512]{1,0:T(8,128)(2,1)S(1)} %copy-done.11, ...), custom_call_target="tpu_custom_call", output_to_operand_aliasing={{0}: (7, {})} | custom-call | bytes 65536 | tf_op jit(solution)/shard_map/expert_product/pallas_call | solution.py:201
  46.4 2.0 %expert_product.9 = (f32[135168,128]{1,0:T(8,128)}, bf16[384,4096]{1,0:T(8,128)(2,1)}) custom-call(s32[8]{0:T(128)S(1)} %iota_xor_fusion.1.sources, s32[4]{0:T(128)S(1)} %select_reduce_fusion.places, bf16[384,1024]{1,0:T(8,128)(2,1)S(1)} %bitcast.3, bf16[256,512]{1,0:T(8,128)(2,1)S(1)} %copy-done.10, ...), custom_call_target="tpu_custom_call", output_to_operand_aliasing={{0}: (7, {}), {1}: (8, {})} | custom-call | bytes 65536 | tf_op jit(solution)/shard_map/expert_product/pallas_call | solution.py:201
  48.4 1.6 %collective-permute-start.15 = (bf16[256,512]{1,0:T(8,128)(2,1)S(1)}, bf16[256,512]{1,0:T(8,128)(2,1)S(1)}, u32[]{:S(2)}, u32[]{:S(2)}) collective-permute-start(bf16[256,512]{1,0:T(8,128)(2,1)S(1)} %get-tuple-element.135.refs_1_), channel_id=1, source_target_pairs={{0,16},{8,24},{16,0},{24,8},{1,17},{9,25},{17,1},{25,9},{2,18},{10... | collective-permute-start | bytes 786440 | tf_op jit(solution)/shard_map/ppermute | solution.py:221
  55.1 2.5 %collective-permute-done.15.refs_1_ = bf16[256,512]{1,0:T(8,128)(2,1)S(1)} collective-permute-done((bf16[256,512]{1,0:T(8,128)(2,1)S(1)}, bf16[256,512]{1,0:T(8,128)(2,1)S(1)}, u32[]{:S(2)}, u32[]{:S(2)}) %collective-permute-start.15) | collective-permute-done | bytes 262176 | tf_op jit(solution)/shard_map/ppermute | solution.py:221
  59.1 2.0 %expert_product.10 = (f32[135168,128]{1,0:T(8,128)}, bf16[384,4096]{1,0:T(8,128)(2,1)}) custom-call(s32[8]{0:T(128)S(1)} %iota_xor_fusion.1.sources, s32[4]{0:T(128)S(1)} %select_reduce_fusion.places, bf16[384,1024]{1,0:T(8,128)(2,1)S(1)} %bitcast.4, bf16[256,512]{1,0:T(8,128)(2,1)S(1)} %get-tuple-element.128.refs_0_, ...), custom_call_target="tpu_custom_call", output_to_operand_aliasing={{0}: (7, {}), {1}: (8, {})} | custom-call | bytes 65536 | tf_op jit(solution)/shard_map/expert_product/pallas_call | solution.py:201
  61.1 2.0 %expert_product.11 = (f32[135168,128]{1,0:T(8,128)}, bf16[384,4096]{1,0:T(8,128)(2,1)}) custom-call(s32[8]{0:T(128)S(1)} %iota_xor_fusion.1.sources, s32[4]{0:T(128)S(1)} %select_reduce_fusion.places, bf16[384,1024]{1,0:T(8,128)(2,1)S(1)} %bitcast.5, bf16[256,512]{1,0:T(8,128)(2,1)S(1)} %get-tuple-element.114.refs_0_, ...), custom_call_target="tpu_custom_call", output_to_operand_aliasing={{0}: (7, {}), {1}: (8, {})} | custom-call | bytes 65536 | tf_op jit(solution)/shard_map/expert_product/pallas_call | solution.py:201
  64.7 9.5 %collective-permute-done.19.refs_3_ = bf16[256,512]{1,0:T(8,128)(2,1)S(1)} collective-permute-done((bf16[256,512]{1,0:T(8,128)(2,1)S(1)}, bf16[256,512]{1,0:T(8,128)(2,1)S(1)}, u32[]{:S(2)}, u32[]{:S(2)}) %collective-permute-start.19) | collective-permute-done | bytes 262176 | tf_op jit(solution)/shard_map/ppermute | solution.py:221
  75.1 1.5 %collective-permute-start.25 = (bf16[256,512]{1,0:T(8,128)(2,1)S(1)}, bf16[256,512]{1,0:T(8,128)(2,1)S(1)}, u32[]{:S(2)}, u32[]{:S(2)}) collective-permute-start(bf16[256,512]{1,0:T(8,128)(2,1)S(1)} %get-tuple-element.163.refs_0_), channel_id=1, source_target_pairs={{0,8},{8,0},{16,24},{24,16},{1,9},{9,1},{17,25},{25,17},{2,10},{10... | collective-permute-start | bytes 786440 | tf_op jit(solution)/shard_map/ppermute | solution.py:221
  78.8 1.8 %collective-permute-done.23.refs_1_ = bf16[256,512]{1,0:T(8,128)(2,1)S(1)} collective-permute-done((bf16[256,512]{1,0:T(8,128)(2,1)S(1)}, bf16[256,512]{1,0:T(8,128)(2,1)S(1)}, u32[]{:S(2)}, u32[]{:S(2)}) %collective-permute-start.23) | collective-permute-done | bytes 262176 | tf_op jit(solution)/shard_map/ppermute | solution.py:221
  81.0 2.9 %collective-permute-done.24.refs_2_ = bf16[256,512]{1,0:T(8,128)(2,1)S(1)} collective-permute-done((bf16[256,512]{1,0:T(8,128)(2,1)S(1)}, bf16[256,512]{1,0:T(8,128)(2,1)S(1)}, u32[]{:S(2)}, u32[]{:S(2)}) %collective-permute-start.24) | collective-permute-done | bytes 262176 | tf_op jit(solution)/shard_map/ppermute | solution.py:221
  83.9 2.0 %expert_product.12 = (f32[135168,128]{1,0:T(8,128)}, bf16[384,4096]{1,0:T(8,128)(2,1)}) custom-call(s32[8]{0:T(128)S(1)} %iota_xor_fusion.1.sources, s32[4]{0:T(128)S(1)} %select_reduce_fusion.places, bf16[384,1024]{1,0:T(8,128)(2,1)S(1)} %bitcast.6, bf16[256,512]{1,0:T(8,128)(2,1)S(1)} %get-tuple-element.145.refs_0_, ...), custom_call_target="tpu_custom_call", output_to_operand_aliasing={{0}: (7, {}), {1}: (8, {})} | custom-call | bytes 65536 | tf_op jit(solution)/shard_map/expert_product/pallas_call | solution.py:201
  85.9 2.0 %expert_product.13 = (f32[135168,128]{1,0:T(8,128)}, bf16[384,4096]{1,0:T(8,128)(2,1)}) custom-call(s32[8]{0:T(128)S(1)} %iota_xor_fusion.1.sources, s32[4]{0:T(128)S(1)} %select_reduce_fusion.places, bf16[384,1024]{1,0:T(8,128)(2,1)S(1)} %bitcast.7, bf16[256,512]{1,0:T(8,128)(2,1)S(1)} %get-tuple-element.146.refs_0_, ...), custom_call_target="tpu_custom_call", output_to_operand_aliasing={{0}: (7, {}), {1}: (8, {})} | custom-call | bytes 65536 | tf_op jit(solution)/shard_map/expert_product/pallas_call | solution.py:201
  92.8 5.2 %collective-permute-done.29.refs_1_ = bf16[256,512]{1,0:T(8,128)(2,1)S(1)} collective-permute-done((bf16[256,512]{1,0:T(8,128)(2,1)S(1)}, bf16[256,512]{1,0:T(8,128)(2,1)S(1)}, u32[]{:S(2)}, u32[]{:S(2)}) %collective-permute-start.29) | collective-permute-done | bytes 262176 | tf_op jit(solution)/shard_map/ppermute | solution.py:221
  98.0 2.0 %expert_product.14 = (f32[135168,128]{1,0:T(8,128)}, bf16[384,4096]{1,0:T(8,128)(2,1)}) custom-call(s32[8]{0:T(128)S(1)} %iota_xor_fusion.1.sources, s32[4]{0:T(128)S(1)} %select_reduce_fusion.places, bf16[384,1024]{1,0:T(8,128)(2,1)S(1)} %bitcast.8, bf16[256,512]{1,0:T(8,128)(2,1)S(1)} %get-tuple-element.163.refs_0_, ...), custom_call_target="tpu_custom_call", output_to_operand_aliasing={{0}: (7, {}), {1}: (8, {})} | custom-call | bytes 65536 | tf_op jit(solution)/shard_map/expert_product/pallas_call | solution.py:201
  100.6 2.0 %expert_product.15 = (f32[135168,128]{1,0:T(8,128)}, bf16[384,4096]{1,0:T(8,128)(2,1)}) custom-call(s32[8]{0:T(128)S(1)} %iota_xor_fusion.1.sources, s32[4]{0:T(128)S(1)} %select_reduce_fusion.places, bf16[384,1024]{1,0:T(8,128)(2,1)S(1)} %bitcast.9, bf16[256,512]{1,0:T(8,128)(2,1)S(1)} %get-tuple-element.150.refs_0_, ...), custom_call_target="tpu_custom_call", output_to_operand_aliasing={{0}: (7, {}), {1}: (8, {})} | custom-call | bytes 65536 | tf_op jit(solution)/shard_map/expert_product/pallas_call | solution.py:201
  (101 shorter events, 31.0 us)
Async XLA Ops:
  14.7 9.8 %collective-permute-start.3 = (bf16[256,512]{1,0:T(8,128)(2,1)S(1)}, bf16[256,512]{1,0:T(8,128)(2,1)S(1)}, u32[]{:S(2)}, u32[]{:S(2)}) collective-permute-start(bf16[256,512]{1,0:T(8,128)(2,1)S(1)} %get-tuple-element.106.refs_0_), channel_id=1, source_target_pairs={{0,8},{8,0},{16,24},{24,16},{1,9},{9,1},{17,25},{25,17},{2,10},{10... | collective-permute-start | bytes 786440 | tf_op jit(solution)/shard_map/ppermute | solution.py:221
  15.3 9.7 %collective-permute-start.4 = (bf16[256,512]{1,0:T(8,128)(2,1)S(1)}, bf16[256,512]{1,0:T(8,128)(2,1)S(1)}, u32[]{:S(2)}, u32[]{:S(2)}) collective-permute-start(bf16[256,512]{1,0:T(8,128)(2,1)S(1)} %get-tuple-element.106.refs_0_), channel_id=1, source_target_pairs={{0,16},{8,24},{16,0},{24,8},{1,17},{9,25},{17,1},{25,9},{2,18},{10... | collective-permute-start | bytes 786440 | tf_op jit(solution)/shard_map/ppermute | solution.py:221
  16.9 14.3 %collective-permute-start.5 = (bf16[256,512]{1,0:T(8,128)(2,1)S(1)}, bf16[256,512]{1,0:T(8,128)(2,1)S(1)}, u32[]{:S(2)}, u32[]{:S(2)}) collective-permute-start(bf16[256,512]{1,0:T(8,128)(2,1)S(1)} %copy-done.15), channel_id=1, source_target_pairs={{0,2},{1,3},{2,0},{3,1},{4,6},{5,7},{6,4},{7,5},{8,10},{9,11},{10,... | collective-permute-start | bytes 786440 | tf_op jit(solution)/shard_map/ppermute | solution.py:221
  17.3 13.9 %collective-permute-start.6 = (bf16[256,512]{1,0:T(8,128)(2,1)S(1)}, bf16[256,512]{1,0:T(8,128)(2,1)S(1)}, u32[]{:S(2)}, u32[]{:S(2)}) collective-permute-start(bf16[256,512]{1,0:T(8,128)(2,1)S(1)} %copy-done.14), channel_id=1, source_target_pairs={{0,3},{1,2},{2,1},{3,0},{4,7},{5,6},{6,5},{7,4},{8,11},{9,10},{10,... | collective-permute-start | bytes 786440 | tf_op jit(solution)/shard_map/ppermute | solution.py:221
  21.9 14.6 %collective-permute-start.9 = (bf16[256,512]{1,0:T(8,128)(2,1)}, bf16[256,512]{1,0:T(8,128)(2,1)S(1)}, u32[]{:S(2)}, u32[]{:S(2)}) collective-permute-start(bf16[256,512]{1,0:T(8,128)(2,1)} %get-tuple-element.119), channel_id=1, source_target_pairs={{0,4},{1,5},{2,6},{3,7},{4,0},{5,1},{6,2},{7,3},{8,12},{9,13},{10,... | collective-permute-start | bytes 786440 | tf_op jit(solution)/shard_map/ppermute | solution.py:221
  24.5 12.5 %collective-permute-start.7 = (bf16[256,512]{1,0:T(8,128)(2,1)S(1)}, bf16[256,512]{1,0:T(8,128)(2,1)S(1)}, u32[]{:S(2)}, u32[]{:S(2)}) collective-permute-start(bf16[256,512]{1,0:T(8,128)(2,1)S(1)} %get-tuple-element.118.refs_1_), channel_id=1, source_target_pairs={{0,16},{8,24},{16,0},{24,8},{1,17},{9,25},{17,1},{25,9},{2,18},{10... | collective-permute-start | bytes 786440 | tf_op jit(solution)/shard_map/ppermute | solution.py:221
  25.1 13.4 %collective-permute-start.8 = (bf16[256,512]{1,0:T(8,128)(2,1)S(1)}, bf16[256,512]{1,0:T(8,128)(2,1)S(1)}, u32[]{:S(2)}, u32[]{:S(2)}) collective-permute-start(bf16[256,512]{1,0:T(8,128)(2,1)S(1)} %get-tuple-element.116.refs_2_), channel_id=1, source_target_pairs={{0,8},{8,0},{16,24},{24,16},{1,9},{9,1},{17,25},{25,17},{2,10},{10... | collective-permute-start | bytes 786440 | tf_op jit(solution)/shard_map/ppermute | solution.py:221
  31.2 17.2 %collective-permute-start.11 = (bf16[256,512]{1,0:T(8,128)(2,1)S(1)}, bf16[256,512]{1,0:T(8,128)(2,1)S(1)}, u32[]{:S(2)}, u32[]{:S(2)}) collective-permute-start(bf16[256,512]{1,0:T(8,128)(2,1)S(1)} %get-tuple-element.128.refs_0_), channel_id=1, source_target_pairs={{0,8},{8,0},{16,24},{24,16},{1,9},{9,1},{17,25},{25,17},{2,10},{10... | collective-permute-start | bytes 786440 | tf_op jit(solution)/shard_map/ppermute | solution.py:221
  31.8 18.7 %collective-permute-start.12 = (bf16[256,512]{1,0:T(8,128)(2,1)S(1)}, bf16[256,512]{1,0:T(8,128)(2,1)S(1)}, u32[]{:S(2)}, u32[]{:S(2)}) collective-permute-start(bf16[256,512]{1,0:T(8,128)(2,1)S(1)} %get-tuple-element.128.refs_0_), channel_id=1, source_target_pairs={{0,16},{8,24},{16,0},{24,8},{1,17},{9,25},{17,1},{25,9},{2,18},{10... | collective-permute-start | bytes 786440 | tf_op jit(solution)/shard_map/ppermute | solution.py:221
  36.5 11.9 %collective-permute-start.10 = (bf16[256,512]{1,0:T(8,128)(2,1)S(1)}, bf16[256,512]{1,0:T(8,128)(2,1)S(1)}, u32[]{:S(2)}, u32[]{:S(2)}) collective-permute-start(bf16[256,512]{1,0:T(8,128)(2,1)S(1)} %get-tuple-element.114.refs_0_), channel_id=1, source_target_pairs={{0,16},{8,24},{16,0},{24,8},{1,17},{9,25},{17,1},{25,9},{2,18},{10... | collective-permute-start | bytes 786440 | tf_op jit(solution)/shard_map/ppermute | solution.py:221
  37.0 15.0 %collective-permute-start.13 = (bf16[256,512]{1,0:T(8,128)(2,1)S(1)}, bf16[256,512]{1,0:T(8,128)(2,1)S(1)}, u32[]{:S(2)}, u32[]{:S(2)}) collective-permute-start(bf16[256,512]{1,0:T(8,128)(2,1)S(1)} %get-tuple-element.114.refs_0_), channel_id=1, source_target_pairs={{0,8},{8,0},{16,24},{24,16},{1,9},{9,1},{17,25},{25,17},{2,10},{10... | collective-permute-start | bytes 786440 | tf_op jit(solution)/shard_map/ppermute | solution.py:221
  38.5 13.7 %collective-permute-start.14 = (bf16[256,512]{1,0:T(8,128)(2,1)}, bf16[256,512]{1,0:T(8,128)(2,1)S(1)}, u32[]{:S(2)}, u32[]{:S(2)}) collective-permute-start(bf16[256,512]{1,0:T(8,128)(2,1)} %get-tuple-element.130), channel_id=1, source_target_pairs={{0,5},{1,4},{2,7},{3,6},{4,1},{5,0},{6,3},{7,2},{8,13},{9,12},{10,... | collective-permute-start | bytes 786440 | tf_op jit(solution)/shard_map/ppermute | solution.py:221
  50.5 13.6 %collective-permute-start.17 = (bf16[256,512]{1,0:T(8,128)(2,1)S(1)}, bf16[256,512]{1,0:T(8,128)(2,1)S(1)}, u32[]{:S(2)}, u32[]{:S(2)}) collective-permute-start(bf16[256,512]{1,0:T(8,128)(2,1)S(1)} %get-tuple-element.145.refs_0_), channel_id=1, source_target_pairs={{0,8},{8,0},{16,24},{24,16},{1,9},{9,1},{17,25},{25,17},{2,10},{10... | collective-permute-start | bytes 786440 | tf_op jit(solution)/shard_map/ppermute | solution.py:221
  52.2 12.5 %collective-permute-start.18 = (bf16[256,512]{1,0:T(8,128)(2,1)S(1)}, bf16[256,512]{1,0:T(8,128)(2,1)S(1)}, u32[]{:S(2)}, u32[]{:S(2)}) collective-permute-start(bf16[256,512]{1,0:T(8,128)(2,1)S(1)} %get-tuple-element.146.refs_0_), channel_id=1, source_target_pairs={{0,16},{8,24},{16,0},{24,8},{1,17},{9,25},{17,1},{25,9},{2,18},{10... | collective-permute-start | bytes 786440 | tf_op jit(solution)/shard_map/ppermute | solution.py:221
  53.7 20.4 %collective-permute-start.19 = (bf16[256,512]{1,0:T(8,128)(2,1)S(1)}, bf16[256,512]{1,0:T(8,128)(2,1)S(1)}, u32[]{:S(2)}, u32[]{:S(2)}) collective-permute-start(bf16[256,512]{1,0:T(8,128)(2,1)S(1)} %get-tuple-element.147), channel_id=1, source_target_pairs={{0,6},{1,7},{2,4},{3,5},{4,2},{5,3},{6,0},{7,1},{8,14},{9,15},{10,... | collective-permute-start | bytes 786440 | tf_op jit(solution)/shard_map/ppermute | solution.py:221
  57.6 17.6 %collective-permute-start.20 = (bf16[256,512]{1,0:T(8,128)(2,1)S(1)}, bf16[256,512]{1,0:T(8,128)(2,1)S(1)}, u32[]{:S(2)}, u32[]{:S(2)}) collective-permute-start(bf16[256,512]{1,0:T(8,128)(2,1)S(1)} %get-tuple-element.145.refs_0_), channel_id=1, source_target_pairs={{0,16},{8,24},{16,0},{24,8},{1,17},{9,25},{17,1},{25,9},{2,18},{10... | collective-permute-start | bytes 786440 | tf_op jit(solution)/shard_map/ppermute | solution.py:221
  59.1 18.5 %collective-permute-start.22 = (bf16[256,512]{1,0:T(8,128)(2,1)S(1)}, bf16[256,512]{1,0:T(8,128)(2,1)S(1)}, u32[]{:S(2)}, u32[]{:S(2)}) collective-permute-start(bf16[256,512]{1,0:T(8,128)(2,1)S(1)} %get-tuple-element.149), channel_id=1, source_target_pairs={{0,7},{1,6},{2,5},{3,4},{4,3},{5,2},{6,1},{7,0},{8,15},{9,14},{10,... | collective-permute-start | bytes 786440 | tf_op jit(solution)/shard_map/ppermute | solution.py:221
  64.1 14.1 %collective-permute-start.21 = (bf16[256,512]{1,0:T(8,128)(2,1)S(1)}, bf16[256,512]{1,0:T(8,128)(2,1)S(1)}, u32[]{:S(2)}, u32[]{:S(2)}) collective-permute-start(bf16[256,512]{1,0:T(8,128)(2,1)S(1)} %get-tuple-element.146.refs_0_), channel_id=1, source_target_pairs={{0,8},{8,0},{16,24},{24,16},{1,9},{9,1},{17,25},{25,17},{2,10},{10... | collective-permute-start | bytes 786440 | tf_op jit(solution)/shard_map/ppermute | solution.py:221
  74.7 9.2 %collective-permute-start.24 = (bf16[256,512]{1,0:T(8,128)(2,1)S(1)}, bf16[256,512]{1,0:T(8,128)(2,1)S(1)}, u32[]{:S(2)}, u32[]{:S(2)}) collective-permute-start(bf16[256,512]{1,0:T(8,128)(2,1)S(1)} %get-tuple-element.152.refs_2_), channel_id=1, source_target_pairs={{0,8},{8,0},{16,24},{24,16},{1,9},{9,1},{17,25},{25,17},{2,10},{10... | collective-permute-start | bytes 786440 | tf_op jit(solution)/shard_map/ppermute | solution.py:221
  75.1 13.7 %collective-permute-start.25 = (bf16[256,512]{1,0:T(8,128)(2,1)S(1)}, bf16[256,512]{1,0:T(8,128)(2,1)S(1)}, u32[]{:S(2)}, u32[]{:S(2)}) collective-permute-start(bf16[256,512]{1,0:T(8,128)(2,1)S(1)} %get-tuple-element.163.refs_0_), channel_id=1, source_target_pairs={{0,8},{8,0},{16,24},{24,16},{1,9},{9,1},{17,25},{25,17},{2,10},{10... | collective-permute-start | bytes 786440 | tf_op jit(solution)/shard_map/ppermute | solution.py:221
  77.6 11.2 %collective-permute-start.26 = (bf16[256,512]{1,0:T(8,128)(2,1)S(1)}, bf16[256,512]{1,0:T(8,128)(2,1)S(1)}, u32[]{:S(2)}, u32[]{:S(2)}) collective-permute-start(bf16[256,512]{1,0:T(8,128)(2,1)S(1)} %get-tuple-element.163.refs_0_), channel_id=1, source_target_pairs={{0,16},{8,24},{16,0},{24,8},{1,17},{9,25},{17,1},{25,9},{2,18},{10... | collective-permute-start | bytes 786440 | tf_op jit(solution)/shard_map/ppermute | solution.py:221
  78.2 13.4 %collective-permute-start.27 = (bf16[256,512]{1,0:T(8,128)(2,1)S(1)}, bf16[256,512]{1,0:T(8,128)(2,1)S(1)}, u32[]{:S(2)}, u32[]{:S(2)}) collective-permute-start(bf16[256,512]{1,0:T(8,128)(2,1)S(1)} %get-tuple-element.150.refs_0_), channel_id=1, source_target_pairs={{0,8},{8,0},{16,24},{24,16},{1,9},{9,1},{17,25},{25,17},{2,10},{10... | collective-permute-start | bytes 786440 | tf_op jit(solution)/shard_map/ppermute | solution.py:221
  80.5 11.8 %collective-permute-start.28 = (bf16[256,512]{1,0:T(8,128)(2,1)S(1)}, bf16[256,512]{1,0:T(8,128)(2,1)S(1)}, u32[]{:S(2)}, u32[]{:S(2)}) collective-permute-start(bf16[256,512]{1,0:T(8,128)(2,1)S(1)} %get-tuple-element.150.refs_0_), channel_id=1, source_target_pairs={{0,16},{8,24},{16,0},{24,8},{1,17},{9,25},{17,1},{25,9},{2,18},{10... | collective-permute-start | bytes 786440 | tf_op jit(solution)/shard_map/ppermute | solution.py:221
  88.8 9.2 %collective-permute-start.29 = (bf16[256,512]{1,0:T(8,128)(2,1)S(1)}, bf16[256,512]{1,0:T(8,128)(2,1)S(1)}, u32[]{:S(2)}, u32[]{:S(2)}) collective-permute-start(bf16[256,512]{1,0:T(8,128)(2,1)S(1)} %get-tuple-element.167.refs_1_), channel_id=1, source_target_pairs={{0,16},{8,24},{16,0},{24,8},{1,17},{9,25},{17,1},{25,9},{2,18},{10... | collective-permute-start | bytes 786440 | tf_op jit(solution)/shard_map/ppermute | solution.py:221
  (24 other events, 159.5 us)

commit v8 on v7

--- a/solution.py
+++ b/solution.py
@@ -12,6 +12,7 @@
 QB = 128
 GROUP = 32
 VMEM_LIMIT = 60 * 1024 * 1024
+LATER_LIMIT = 54 * 1024 * 1024
 PRODUCT_LIMIT = 16 * 1024 * 1024
 
 beta_one = 0.9
@@ -28,6 +29,7 @@
 root_epsilon = adam_epsilon * second_root
 
 TOKEN = (132 * 1024, 128)
+PLANNED = (4, 8)
 WHOLE = pl.BlockSpec(memory_space=pl.ANY)
 SMALL_COST = pl.CostEstimate(flops=0, bytes_accessed=65536, transcendentals=0)
 
@@ -150,7 +152,7 @@
         lax.fori_loop(0, blocks * bands, part, 0)
 
 
-def adam_blocks(base, blocks, owner, arrays, carried, token, fenced):
+def adam_blocks(base, blocks, owner, arrays, carried, token, fenced, limit):
     _, rows, columns = arrays[0].shape
     passed = len(carried) + len(token)
     made = [like(arrays[0]), like(arrays[2]), like(arrays[3])]
@@ -168,7 +170,7 @@
         scratch_shapes=[pltpu.VMEM((blocks, rows, columns), kind) for kind in kinds]
         + [pltpu.SemaphoreType.DMA((blocks * (rows // QB), 8))],
         input_output_aliases=aliases,
-        compiler_params=pltpu.CompilerParams(vmem_limit_bytes=VMEM_LIMIT),
+        compiler_params=pltpu.CompilerParams(vmem_limit_bytes=limit),
         cost_estimate=SMALL_COST,
         name="adam_quantize",
     )(owner, *arrays, *carried, *token)
@@ -235,14 +237,14 @@
     ).astype(jnp.int32)
 
     pairs = shards // 2
-    fenced = len(bits) == 2 and pairs > 1
+    fenced = (replicas, shards) == PLANNED
     held = [{} for _ in range(shards)]
     made, due, ready = {}, collections.defaultdict(list), set()
     state = {"adam": (), "token": (), "out": ()}
 
-    def adam(base, blocks):
+    def adam(base, blocks, limit):
         state["adam"], sends, state["token"] = adam_blocks(
-            base, blocks, owner_of_expert, arrays, tuple(state["adam"]), state["token"], fenced
+            base, blocks, owner_of_expert, arrays, tuple(state["adam"]), state["token"], fenced, limit
         )
         made.update(zip(range(base, base + blocks), sends))
 
@@ -269,66 +271,47 @@
 
     waiting = list(range(shards))
     if fenced:
-        fences = collections.defaultdict(lambda: ([], [], []))
-
-        def plan(step, until, *keys):
-            fences[step][1].extend(keys)
-            fences[until][0].extend((block, member ^ bit) for block, member, bit in keys)
-
-        plan(0, 2, (1, 0, 1), (1, 0, 2))
-        plan(0, 3, (0, 1, 2))
-        plan(2, 3, (1, 2, 1))
-        plan(2.5, 4, (3, 0, 2), (2, 0, 1))
-        plan(3, 5, (2, 0, 2), (3, 0, 1))
-        plan(4, 6, (2, 1, 2), (3, 2, 1))
-        for pair in range(2, pairs):
-            even, odd, step = 2 * pair, 2 * pair + 1, 3 * pair
-            if pair + 1 < pairs:
-                plan(step - 1, step + 1, (even, 0, 1), (odd, 0, 2))
-                plan(step, step + 2, (even, 0, 2), (odd, 0, 1))
-                plan(step + 1, step + 3, (even, 1, 2), (odd, 2, 1))
-            else:
-                plan(step - 1, step + 1, (even, 0, 1), (even, 0, 2))
-                plan(step, step + 2, (odd, 0, 1), (odd, 0, 2))
-                plan(step + 1, step + 3, (even, 1, 2))
-                plan(step + 2, step + 4, (odd, 2, 1))
-        for block in range(4, shards):
-            first = min(2 * block - 7, 3 * (block // 2) - 3)
-            if first > 1:
-                fences[first][2].append(block)
-            fences[first + 2][0].append((block, 0))
-        fences[0][0].extend([(1, 0), (0, 1), (0, 2)])
-        fences[2.5][0].extend([(2, 0), (3, 0)])
-
-        adam(0, 2)
+        plan = [
+            ([(1, 0), (0, 1), (0, 2)], [(1, 0, 1), (1, 0, 2)], []),
+            ([(1, 1), (1, 2)], [(0, 1, 2), (1, 2, 1)], []),
+            ([(2, 0), (3, 0), (4, 0)], [(3, 0, 2), (2, 0, 1)], []),
+            ([(0, 3), (1, 3)], [(2, 0, 2), (3, 0, 1)], [5]),
+            ([(2, 1), (3, 2)], [(2, 1, 2), (3, 2, 1)], []),
+            ([(2, 2), (3, 1), (5, 0)], [(4, 0, 1), (4, 0, 2)], [6]),
+            ([(2, 3), (3, 3)], [(5, 0, 1), (5, 0, 2)], []),
+            ([(4, 1), (4, 2)], [(4, 1, 2)], []),
+            ([(6, 0), (5, 1), (5, 2)], [(6, 0, 1), (6, 0, 2), (5, 2, 1)], [7]),
+            ([(4, 3), (5, 3)], [], []),
+            ([(6, 1), (6, 2)], [(6, 1, 2)], []),
+            ([(7, 0)], [(7, 0, 1), (7, 0, 2)], []),
+            ([(6, 3)], [], []),
+            ([(7, 1), (7, 2)], [(7, 2, 1)], []),
+            ([(7, 3)], [], []),
+        ]
+        adam(0, 2, VMEM_LIMIT)
         deliver(0)
         deliver(1)
         ready.add((0, 0))
         send(0, 0, 1)
         send(0, 0, 2)
-        adam(2, 2)
-        deliver(2)
-        deliver(3)
-        computed = 4
-        for step in sorted(fences):
-            keys, sending, leaving = fences[step]
+        adam(2, 4, VMEM_LIMIT)
+        for block in (4, 2, 3):
+            deliver(block)
+        for step, (keys, sending, leaving) in enumerate(plan):
             arrived(keys, leaving)
             for block in leaving:
                 deliver(block)
             for key in sending:
                 send(*key)
-            if computed < shards:
-                adam(computed, 2)
-                if not step:
-                    deliver(computed)
-                computed += 2
+            if not step:
+                adam(6, 2, LATER_LIMIT)
             for block in list(waiting):
                 if all((block, member) in ready for member in range(replicas)):
                     multiply(block)
                     waiting.remove(block)
     else:
         for pair in range(pairs):
-            adam(2 * pair, 2)
+            adam(2 * pair, 2, VMEM_LIMIT)
         for block in range(shards):
             deliver(block)
             for number in range(len(bits)):

time: 103 us -> 105 us (1.019)
  waiting for transfers between devices: 32.4 us -> 40 us
  Pallas kernels: 34.2 us -> 31.6 us
  local copies, waits for them, and re-layouts: 2.9 us -> 0.72 us
  starting transfers between devices: 32.1 us -> 30.9 us
    ppermute x31, waiting for transfers between devices: 32.4 us -> 40 us  [swap(): return lax.ppermute(value, axis, [(i, i ^ mask) for i in range(size)])]
    pallas_call x4 -> x3, Pallas kernels: 18.1 us -> 15.6 us  [adam_blocks(): pl.pallas_call(functools.partial(adam_kernel, base, blocks, passed), in_s...]
    unnamed x34 -> x24, local copies, waits for them, and re-layouts: 2.9 us -> 0.72 us
    ppermute x31, starting transfers between devices: 32.1 us -> 30.9 us  [swap(): return lax.ppermute(value, axis, [(i, i ^ mask) for i in range(size)])]
  transfers between devices with their start and end apart: 31 -> 31, of which waited for: 15 -> 15; matrix products, arithmetic and copies ran while one was open for 0% -> 0% of each run, Pallas kernels for 27% -> 24%
where the time goes in v8:
time: 105 us; the launch traced here: 104 us
  waiting for transfers between devices  40 us (38%)
  Pallas kernels  31.6 us (30%)
  starting transfers between devices  30.9 us (29%)
    ppermute x31, waiting for transfers between devices, swap(): return lax.ppermute(value, axis, [(i, i ^ mask) for i in range(size)])  40 us
    ppermute x31, starting transfers between devices, swap(): return lax.ppermute(value, axis, [(i, i ^ mask) for i in range(size)])  30.9 us
    pallas_call x8, Pallas kernels, product(): pl.pallas_call(functools.partial(product_kernel, slabs), grid_spec=pltpu....  16 us
    pallas_call x3, Pallas kernels, adam_blocks(): pl.pallas_call(functools.partial(adam_kernel, base, blocks, passed), in_s...  15.6 us
  transfers between devices with their start and end apart: 31, of which 15 were waited for; matrix products, arithmetic and copies ran while one was open for 0% of the time, Pallas kernels for 24%

profile of v8, /device:TPU:8, one launch (start us, length us, event | category | flops | bytes accessed | tf_op | source)
XLA Modules:
  0.0 104.3 jit_solution(11912683763711660550)
XLA Ops:
  0.6 4.5 %adam_quantize.3 = (f32[8,256,512]{2,1,0:T(8,128)}, bf16[8,256,512]{2,1,0:T(8,128)(2,1)}, bf16[8,256,512]{2,1,0:T(8,128)(2,1)}, bf16[256,512]{1,0:T(8,128)(2,1)}...) custom-call(s32[8]{0:T(128)} %owner.5, f32[8,256,512]{2,1,0:T(8,128)} %refs_0_.5, bf16[8,256,512]{2,1,0:T(8,128)(2,1)} %refs_1_.5, ...), custom_call_target="tpu_custom_call" | custom-call | bytes 65536 | tf_op jit(solution)/shard_map/adam_quantize/pallas_call | solution.py:165
  8.3 6.5 %adam_quantize.4 = (f32[8,256,512]{2,1,0:T(8,128)}, bf16[8,256,512]{2,1,0:T(8,128)(2,1)}, bf16[8,256,512]{2,1,0:T(8,128)(2,1)}, bf16[256,512]{1,0:T(8,128)(2,1)}...) custom-call(s32[8]{0:T(128)} %owner.5, ...), custom_call_target="tpu_custom_call", output_to_operand_aliasing={{0}: (5, {}), {1}: (6, {}), {2}: (7, {}), {7}: (8, {})} | custom-call | bytes 65536 | tf_op jit(solution)/shard_map/adam_quantize/pallas_call | solution.py:165
  17.9 2.7 %collective-permute-start.7 = (bf16[256,512]{1,0:T(8,128)(2,1)S(1)}, bf16[256,512]{1,0:T(8,128)(2,1)S(1)}, u32[]{:S(2)}, u32[]{:S(2)}) collective-permute-start(bf16[256,512]{1,0:T(8,128)(2,1)S(1)} %copy-done.8), channel_id=1, source_target_pairs={{0,4},{1,5},{2,6},{3,7},{4,0},{5,1},{6,2},{7,3},{8,12},{9,13},{10,... | collective-permute-start | bytes 786440 | tf_op jit(solution)/shard_map/ppermute | solution.py:223
  20.6 4.5 %adam_quantize.5 = (f32[8,256,512]{2,1,0:T(8,128)}, bf16[8,256,512]{2,1,0:T(8,128)(2,1)}, bf16[8,256,512]{2,1,0:T(8,128)(2,1)}, bf16[256,512]{1,0:T(8,128)(2,1)}...) custom-call(s32[8]{0:T(128)} %owner.5, ...), custom_call_target="tpu_custom_call", output_to_operand_aliasing={{0}: (5, {}), {1}: (6, {}), {2}: (7, {}), {5}: (8, {})} | custom-call | bytes 65536 | tf_op jit(solution)/shard_map/adam_quantize/pallas_call | solution.py:165
  28.2 2.1 %collective-permute-done.5.refs_1_ = bf16[256,512]{1,0:T(8,128)(2,1)S(1)} collective-permute-done((bf16[256,512]{1,0:T(8,128)(2,1)S(1)}, bf16[256,512]{1,0:T(8,128)(2,1)S(1)}, u32[]{:S(2)}, u32[]{:S(2)}) %collective-permute-start.5) | collective-permute-done | bytes 262176 | tf_op jit(solution)/shard_map/ppermute | solution.py:223
  30.3 3.5 %collective-permute-done.6.refs_2_ = bf16[256,512]{1,0:T(8,128)(2,1)S(1)} collective-permute-done((bf16[256,512]{1,0:T(8,128)(2,1)S(1)}, bf16[256,512]{1,0:T(8,128)(2,1)S(1)}, u32[]{:S(2)}, u32[]{:S(2)}) %collective-permute-start.6) | collective-permute-done | bytes 262176 | tf_op jit(solution)/shard_map/ppermute | solution.py:223
  33.8 3.2 %collective-permute-done.7.refs_3_ = bf16[256,512]{1,0:T(8,128)(2,1)S(1)} collective-permute-done((bf16[256,512]{1,0:T(8,128)(2,1)S(1)}, bf16[256,512]{1,0:T(8,128)(2,1)S(1)}, u32[]{:S(2)}, u32[]{:S(2)}) %collective-permute-start.7) | collective-permute-done | bytes 262176 | tf_op jit(solution)/shard_map/ppermute | solution.py:223
  41.3 2.0 %expert_product.8 = (f32[135168,128]{1,0:T(8,128)}, bf16[384,4096]{1,0:T(8,128)(2,1)}) custom-call(s32[8]{0:T(128)S(1)} %iota_xor_fusion.1.sources, s32[4]{0:T(128)S(1)} %select_reduce_fusion.places, bf16[384,1024]{1,0:T(8,128)(2,1)S(1)} %bitcast.2, bf16[256,512]{1,0:T(8,128)(2,1)S(1)} %copy-done.6, ...), custom_call_target="tpu_custom_call", output_to_operand_aliasing={{0}: (7, {})} | custom-call | bytes 65536 | tf_op jit(solution)/shard_map/expert_product/pallas_call | solution.py:203
  43.4 2.0 %expert_product.9 = (f32[135168,128]{1,0:T(8,128)}, bf16[384,4096]{1,0:T(8,128)(2,1)}) custom-call(s32[8]{0:T(128)S(1)} %iota_xor_fusion.1.sources, s32[4]{0:T(128)S(1)} %select_reduce_fusion.places, bf16[384,1024]{1,0:T(8,128)(2,1)S(1)} %bitcast.3, bf16[256,512]{1,0:T(8,128)(2,1)S(1)} %copy-done.4, ...), custom_call_target="tpu_custom_call", output_to_operand_aliasing={{0}: (7, {}), {1}: (8, {})} | custom-call | bytes 65536 | tf_op jit(solution)/shard_map/expert_product/pallas_call | solution.py:203
  45.4 2.3 %collective-permute-done.11.refs_2_ = bf16[256,512]{1,0:T(8,128)(2,1)S(1)} collective-permute-done((bf16[256,512]{1,0:T(8,128)(2,1)S(1)}, bf16[256,512]{1,0:T(8,128)(2,1)S(1)}, u32[]{:S(2)}, u32[]{:S(2)}) %collective-permute-start.11) | collective-permute-done | bytes 262176 | tf_op jit(solution)/shard_map/ppermute | solution.py:223
  49.8 3.5 %collective-permute-done.12.refs_1_ = bf16[256,512]{1,0:T(8,128)(2,1)S(1)} collective-permute-done((bf16[256,512]{1,0:T(8,128)(2,1)S(1)}, bf16[256,512]{1,0:T(8,128)(2,1)S(1)}, u32[]{:S(2)}, u32[]{:S(2)}) %collective-permute-start.12) | collective-permute-done | bytes 262176 | tf_op jit(solution)/shard_map/ppermute | solution.py:223
  55.8 3.0 %collective-permute-done.15.refs_1_ = bf16[256,512]{1,0:T(8,128)(2,1)S(1)} collective-permute-done((bf16[256,512]{1,0:T(8,128)(2,1)S(1)}, bf16[256,512]{1,0:T(8,128)(2,1)S(1)}, u32[]{:S(2)}, u32[]{:S(2)}) %collective-permute-start.15) | collective-permute-done | bytes 262176 | tf_op jit(solution)/shard_map/ppermute | solution.py:223
  60.5 2.0 %expert_product.10 = (f32[135168,128]{1,0:T(8,128)}, bf16[384,4096]{1,0:T(8,128)(2,1)}) custom-call(s32[8]{0:T(128)S(1)} %iota_xor_fusion.1.sources, s32[4]{0:T(128)S(1)} %select_reduce_fusion.places, bf16[384,1024]{1,0:T(8,128)(2,1)S(1)} %bitcast.4, bf16[256,512]{1,0:T(8,128)(2,1)S(1)} %get-tuple-element.120.refs_0_, ...), custom_call_target="tpu_custom_call", output_to_operand_aliasing={{0}: (7, {}), {1}: (8, {})} | custom-call | bytes 65536 | tf_op jit(solution)/shard_map/expert_product/pallas_call | solution.py:203
  62.5 2.0 %expert_product.11 = (f32[135168,128]{1,0:T(8,128)}, bf16[384,4096]{1,0:T(8,128)(2,1)}) custom-call(s32[8]{0:T(128)S(1)} %iota_xor_fusion.1.sources, s32[4]{0:T(128)S(1)} %select_reduce_fusion.places, bf16[384,1024]{1,0:T(8,128)(2,1)S(1)} %bitcast.5, bf16[256,512]{1,0:T(8,128)(2,1)S(1)} %get-tuple-element.121.refs_0_, ...), custom_call_target="tpu_custom_call", output_to_operand_aliasing={{0}: (7, {}), {1}: (8, {})} | custom-call | bytes 65536 | tf_op jit(solution)/shard_map/expert_product/pallas_call | solution.py:203
  66.8 3.4 %collective-permute-done.21.refs_3_ = bf16[256,512]{1,0:T(8,128)(2,1)S(1)} collective-permute-done((bf16[256,512]{1,0:T(8,128)(2,1)S(1)}, bf16[256,512]{1,0:T(8,128)(2,1)S(1)}, u32[]{:S(2)}, u32[]{:S(2)}) %collective-permute-start.21) | collective-permute-done | bytes 262176 | tf_op jit(solution)/shard_map/ppermute | solution.py:223
  70.2 2.0 %collective-permute-start.24 = (bf16[256,512]{1,0:T(8,128)(2,1)S(1)}, bf16[256,512]{1,0:T(8,128)(2,1)S(1)}, u32[]{:S(2)}, u32[]{:S(2)}) collective-permute-start(bf16[256,512]{1,0:T(8,128)(2,1)S(1)} %get-tuple-element.154.refs_0_), channel_id=1, source_target_pairs={{0,8},{8,0},{16,24},{24,16},{1,9},{9,1},{17,25},{25,17},{2,10},{10... | collective-permute-start | bytes 786440 | tf_op jit(solution)/shard_map/ppermute | solution.py:223
  73.7 2.0 %collective-permute-done.22.refs_1_ = bf16[256,512]{1,0:T(8,128)(2,1)S(1)} collective-permute-done((bf16[256,512]{1,0:T(8,128)(2,1)S(1)}, bf16[256,512]{1,0:T(8,128)(2,1)S(1)}, u32[]{:S(2)}, u32[]{:S(2)}) %collective-permute-start.22) | collective-permute-done | bytes 262176 | tf_op jit(solution)/shard_map/ppermute | solution.py:223
  76.5 2.0 %expert_product.12 = (f32[135168,128]{1,0:T(8,128)}, bf16[384,4096]{1,0:T(8,128)(2,1)}) custom-call(s32[8]{0:T(128)S(1)} %iota_xor_fusion.1.sources, s32[4]{0:T(128)S(1)} %select_reduce_fusion.places, bf16[384,1024]{1,0:T(8,128)(2,1)S(1)} %bitcast.6, bf16[256,512]{1,0:T(8,128)(2,1)S(1)} %get-tuple-element.138.refs_0_, ...), custom_call_target="tpu_custom_call", output_to_operand_aliasing={{0}: (7, {}), {1}: (8, {})} | custom-call | bytes 65536 | tf_op jit(solution)/shard_map/expert_product/pallas_call | solution.py:203
  78.5 2.0 %expert_product.13 = (f32[135168,128]{1,0:T(8,128)}, bf16[384,4096]{1,0:T(8,128)(2,1)}) custom-call(s32[8]{0:T(128)S(1)} %iota_xor_fusion.1.sources, s32[4]{0:T(128)S(1)} %select_reduce_fusion.places, bf16[384,1024]{1,0:T(8,128)(2,1)S(1)} %bitcast.7, bf16[256,512]{1,0:T(8,128)(2,1)S(1)} %get-tuple-element.125.refs_0_, ...), custom_call_target="tpu_custom_call", output_to_operand_aliasing={{0}: (7, {}), {1}: (8, {})} | custom-call | bytes 65536 | tf_op jit(solution)/shard_map/expert_product/pallas_call | solution.py:203
  82.5 4.2 %collective-permute-done.26.refs_1_ = bf16[256,512]{1,0:T(8,128)(2,1)S(1)} collective-permute-done((bf16[256,512]{1,0:T(8,128)(2,1)S(1)}, bf16[256,512]{1,0:T(8,128)(2,1)S(1)}, u32[]{:S(2)}, u32[]{:S(2)}) %collective-permute-start.26) | collective-permute-done | bytes 262176 | tf_op jit(solution)/shard_map/ppermute | solution.py:223
  87.3 2.0 %expert_product.14 = (f32[135168,128]{1,0:T(8,128)}, bf16[384,4096]{1,0:T(8,128)(2,1)}) custom-call(s32[8]{0:T(128)S(1)} %iota_xor_fusion.1.sources, s32[4]{0:T(128)S(1)} %select_reduce_fusion.places, bf16[384,1024]{1,0:T(8,128)(2,1)S(1)} %bitcast.8, bf16[256,512]{1,0:T(8,128)(2,1)S(1)} %get-tuple-element.154.refs_0_, ...), custom_call_target="tpu_custom_call", output_to_operand_aliasing={{0}: (7, {}), {1}: (8, {})} | custom-call | bytes 65536 | tf_op jit(solution)/shard_map/expert_product/pallas_call | solution.py:203
  89.3 5.6 %collective-permute-done.28.refs_1_ = bf16[256,512]{1,0:T(8,128)(2,1)S(1)} collective-permute-done((bf16[256,512]{1,0:T(8,128)(2,1)S(1)}, bf16[256,512]{1,0:T(8,128)(2,1)S(1)}, u32[]{:S(2)}, u32[]{:S(2)}) %collective-permute-start.28) | collective-permute-done | bytes 262176 | tf_op jit(solution)/shard_map/ppermute | solution.py:223
  96.7 5.6 %collective-permute-done.30.refs_1_ = bf16[256,512]{1,0:T(8,128)(2,1)S(1)} collective-permute-done((bf16[256,512]{1,0:T(8,128)(2,1)S(1)}, bf16[256,512]{1,0:T(8,128)(2,1)S(1)}, u32[]{:S(2)}, u32[]{:S(2)}) %collective-permute-start.30) | collective-permute-done | bytes 262176 | tf_op jit(solution)/shard_map/ppermute | solution.py:223
  102.3 2.0 %expert_product.15 = (f32[135168,128]{1,0:T(8,128)}, bf16[384,4096]{1,0:T(8,128)(2,1)}) custom-call(s32[8]{0:T(128)S(1)} %iota_xor_fusion.1.sources, s32[4]{0:T(128)S(1)} %select_reduce_fusion.places, bf16[384,1024]{1,0:T(8,128)(2,1)S(1)} %bitcast.9, bf16[256,512]{1,0:T(8,128)(2,1)S(1)} %get-tuple-element.157.refs_0_, ...), custom_call_target="tpu_custom_call", output_to_operand_aliasing={{0}: (7, {}), {1}: (8, {})} | custom-call | bytes 65536 | tf_op jit(solution)/shard_map/expert_product/pallas_call | solution.py:203
  (91 shorter events, 28.8 us)
Async XLA Ops:
  5.2 9.6 %collective-permute-start.1 = (bf16[256,512]{1,0:T(8,128)(2,1)}, bf16[256,512]{1,0:T(8,128)(2,1)S(1)}, u32[]{:S(2)}, u32[]{:S(2)}) collective-permute-start(bf16[256,512]{1,0:T(8,128)(2,1)} %get-tuple-element.97.refs_0_), channel_id=1, source_target_pairs={{0,8},{8,0},{16,24},{24,16},{1,9},{9,1},{17,25},{25,17},{2,10},{10... | collective-permute-start | bytes 786440 | tf_op jit(solution)/shard_map/ppermute | solution.py:223
  15.5 9.6 %collective-permute-start.3 = (bf16[256,512]{1,0:T(8,128)(2,1)S(1)}, bf16[256,512]{1,0:T(8,128)(2,1)S(1)}, u32[]{:S(2)}, u32[]{:S(2)}) collective-permute-start(bf16[256,512]{1,0:T(8,128)(2,1)S(1)} %get-tuple-element.102.refs_0_), channel_id=1, source_target_pairs={{0,8},{8,0},{16,24},{24,16},{1,9},{9,1},{17,25},{25,17},{2,10},{10... | collective-permute-start | bytes 786440 | tf_op jit(solution)/shard_map/ppermute | solution.py:223
  16.1 10.5 %collective-permute-start.4 = (bf16[256,512]{1,0:T(8,128)(2,1)S(1)}, bf16[256,512]{1,0:T(8,128)(2,1)S(1)}, u32[]{:S(2)}, u32[]{:S(2)}) collective-permute-start(bf16[256,512]{1,0:T(8,128)(2,1)S(1)} %get-tuple-element.102.refs_0_), channel_id=1, source_target_pairs={{0,16},{8,24},{16,0},{24,8},{1,17},{9,25},{17,1},{25,9},{2,18},{10... | collective-permute-start | bytes 786440 | tf_op jit(solution)/shard_map/ppermute | solution.py:223
  17.5 12.8 %collective-permute-start.5 = (bf16[256,512]{1,0:T(8,128)(2,1)S(1)}, bf16[256,512]{1,0:T(8,128)(2,1)S(1)}, u32[]{:S(2)}, u32[]{:S(2)}) collective-permute-start(bf16[256,512]{1,0:T(8,128)(2,1)S(1)} %copy-done.10), channel_id=1, source_target_pairs={{0,2},{1,3},{2,0},{3,1},{4,6},{5,7},{6,4},{7,5},{8,10},{9,11},{10,... | collective-permute-start | bytes 786440 | tf_op jit(solution)/shard_map/ppermute | solution.py:223
  17.9 15.9 %collective-permute-start.6 = (bf16[256,512]{1,0:T(8,128)(2,1)S(1)}, bf16[256,512]{1,0:T(8,128)(2,1)S(1)}, u32[]{:S(2)}, u32[]{:S(2)}) collective-permute-start(bf16[256,512]{1,0:T(8,128)(2,1)S(1)} %copy-done.9), channel_id=1, source_target_pairs={{0,3},{1,2},{2,1},{3,0},{4,7},{5,6},{6,5},{7,4},{8,11},{9,10},{10,... | collective-permute-start | bytes 786440 | tf_op jit(solution)/shard_map/ppermute | solution.py:223
  17.9 19.1 %collective-permute-start.7 = (bf16[256,512]{1,0:T(8,128)(2,1)S(1)}, bf16[256,512]{1,0:T(8,128)(2,1)S(1)}, u32[]{:S(2)}, u32[]{:S(2)}) collective-permute-start(bf16[256,512]{1,0:T(8,128)(2,1)S(1)} %copy-done.8), channel_id=1, source_target_pairs={{0,4},{1,5},{2,6},{3,7},{4,0},{5,1},{6,2},{7,3},{8,12},{9,13},{10,... | collective-permute-start | bytes 786440 | tf_op jit(solution)/shard_map/ppermute | solution.py:223
  25.1 15.6 %collective-permute-start.8 = (bf16[256,512]{1,0:T(8,128)(2,1)S(1)}, bf16[256,512]{1,0:T(8,128)(2,1)S(1)}, u32[]{:S(2)}, u32[]{:S(2)}) collective-permute-start(bf16[256,512]{1,0:T(8,128)(2,1)S(1)} %get-tuple-element.111.refs_1_), channel_id=1, source_target_pairs={{0,16},{8,24},{16,0},{24,8},{1,17},{9,25},{17,1},{25,9},{2,18},{10... | collective-permute-start | bytes 786440 | tf_op jit(solution)/shard_map/ppermute | solution.py:223
  26.6 14.7 %collective-permute-start.9 = (bf16[256,512]{1,0:T(8,128)(2,1)S(1)}, bf16[256,512]{1,0:T(8,128)(2,1)S(1)}, u32[]{:S(2)}, u32[]{:S(2)}) collective-permute-start(bf16[256,512]{1,0:T(8,128)(2,1)S(1)} %get-tuple-element.105.refs_2_), channel_id=1, source_target_pairs={{0,8},{8,0},{16,24},{24,16},{1,9},{9,1},{17,25},{25,17},{2,10},{10... | collective-permute-start | bytes 786440 | tf_op jit(solution)/shard_map/ppermute | solution.py:223
  37.0 8.4 %collective-permute-start.10 = (bf16[256,512]{1,0:T(8,128)(2,1)S(1)}, bf16[256,512]{1,0:T(8,128)(2,1)S(1)}, u32[]{:S(2)}, u32[]{:S(2)}) collective-permute-start(bf16[256,512]{1,0:T(8,128)(2,1)S(1)} %get-tuple-element.120.refs_0_), channel_id=1, source_target_pairs={{0,8},{8,0},{16,24},{24,16},{1,9},{9,1},{17,25},{25,17},{2,10},{10... | collective-permute-start | bytes 786440 | tf_op jit(solution)/shard_map/ppermute | solution.py:223
  38.5 9.2 %collective-permute-start.11 = (bf16[256,512]{1,0:T(8,128)(2,1)S(1)}, bf16[256,512]{1,0:T(8,128)(2,1)S(1)}, u32[]{:S(2)}, u32[]{:S(2)}) collective-permute-start(bf16[256,512]{1,0:T(8,128)(2,1)S(1)} %get-tuple-element.121.refs_0_), channel_id=1, source_target_pairs={{0,16},{8,24},{16,0},{24,8},{1,17},{9,25},{17,1},{25,9},{2,18},{10... | collective-permute-start | bytes 786440 | tf_op jit(solution)/shard_map/ppermute | solution.py:223
  40.2 13.1 %collective-permute-start.12 = (bf16[256,512]{1,0:T(8,128)(2,1)S(1)}, bf16[256,512]{1,0:T(8,128)(2,1)S(1)}, u32[]{:S(2)}, u32[]{:S(2)}) collective-permute-start(bf16[256,512]{1,0:T(8,128)(2,1)S(1)} %get-tuple-element.120.refs_0_), channel_id=1, source_target_pairs={{0,16},{8,24},{16,0},{24,8},{1,17},{9,25},{17,1},{25,9},{2,18},{10... | collective-permute-start | bytes 786440 | tf_op jit(solution)/shard_map/ppermute | solution.py:223
  40.8 12.5 %collective-permute-start.13 = (bf16[256,512]{1,0:T(8,128)(2,1)S(1)}, bf16[256,512]{1,0:T(8,128)(2,1)S(1)}, u32[]{:S(2)}, u32[]{:S(2)}) collective-permute-start(bf16[256,512]{1,0:T(8,128)(2,1)S(1)} %get-tuple-element.121.refs_0_), channel_id=1, source_target_pairs={{0,8},{8,0},{16,24},{24,16},{1,9},{9,1},{17,25},{25,17},{2,10},{10... | collective-permute-start | bytes 786440 | tf_op jit(solution)/shard_map/ppermute | solution.py:223
  41.3 13.6 %collective-permute-start.14 = (bf16[256,512]{1,0:T(8,128)(2,1)}, bf16[256,512]{1,0:T(8,128)(2,1)S(1)}, u32[]{:S(2)}, u32[]{:S(2)}) collective-permute-start(bf16[256,512]{1,0:T(8,128)(2,1)} %get-tuple-element.123), channel_id=1, source_target_pairs={{0,5},{1,4},{2,7},{3,6},{4,1},{5,0},{6,3},{7,2},{8,13},{9,12},{10,... | collective-permute-start | bytes 786440 | tf_op jit(solution)/shard_map/ppermute | solution.py:223
  47.7 11.2 %collective-permute-start.15 = (bf16[256,512]{1,0:T(8,128)(2,1)S(1)}, bf16[256,512]{1,0:T(8,128)(2,1)S(1)}, u32[]{:S(2)}, u32[]{:S(2)}) collective-permute-start(bf16[256,512]{1,0:T(8,128)(2,1)S(1)} %get-tuple-element.129.refs_1_), channel_id=1, source_target_pairs={{0,16},{8,24},{16,0},{24,8},{1,17},{9,25},{17,1},{25,9},{2,18},{10... | collective-permute-start | bytes 786440 | tf_op jit(solution)/shard_map/ppermute | solution.py:223
  49.2 9.7 %collective-permute-start.16 = (bf16[256,512]{1,0:T(8,128)(2,1)S(1)}, bf16[256,512]{1,0:T(8,128)(2,1)S(1)}, u32[]{:S(2)}, u32[]{:S(2)}) collective-permute-start(bf16[256,512]{1,0:T(8,128)(2,1)S(1)} %get-tuple-element.127.refs_2_), channel_id=1, source_target_pairs={{0,8},{8,0},{16,24},{24,16},{1,9},{9,1},{17,25},{25,17},{2,10},{10... | collective-permute-start | bytes 786440 | tf_op jit(solution)/shard_map/ppermute | solution.py:223
  53.3 11.2 %collective-permute-start.17 = (bf16[256,512]{1,0:T(8,128)(2,1)S(1)}, bf16[256,512]{1,0:T(8,128)(2,1)S(1)}, u32[]{:S(2)}, u32[]{:S(2)}) collective-permute-start(bf16[256,512]{1,0:T(8,128)(2,1)S(1)} %get-tuple-element.138.refs_0_), channel_id=1, source_target_pairs={{0,8},{8,0},{16,24},{24,16},{1,9},{9,1},{17,25},{25,17},{2,10},{10... | collective-permute-start | bytes 786440 | tf_op jit(solution)/shard_map/ppermute | solution.py:223
  53.3 11.2 %collective-permute-start.18 = (bf16[256,512]{1,0:T(8,128)(2,1)S(1)}, bf16[256,512]{1,0:T(8,128)(2,1)S(1)}, u32[]{:S(2)}, u32[]{:S(2)}) collective-permute-start(bf16[256,512]{1,0:T(8,128)(2,1)S(1)} %get-tuple-element.138.refs_0_), channel_id=1, source_target_pairs={{0,16},{8,24},{16,0},{24,8},{1,17},{9,25},{17,1},{25,9},{2,18},{10... | collective-permute-start | bytes 786440 | tf_op jit(solution)/shard_map/ppermute | solution.py:223
  54.9 11.8 %collective-permute-start.19 = (bf16[256,512]{1,0:T(8,128)(2,1)S(1)}, bf16[256,512]{1,0:T(8,128)(2,1)S(1)}, u32[]{:S(2)}, u32[]{:S(2)}) collective-permute-start(bf16[256,512]{1,0:T(8,128)(2,1)S(1)} %get-tuple-element.140), channel_id=1, source_target_pairs={{0,6},{1,7},{2,4},{3,5},{4,2},{5,3},{6,0},{7,1},{8,14},{9,15},{10,... | collective-permute-start | bytes 786440 | tf_op jit(solution)/shard_map/ppermute | solution.py:223
  58.9 11.2 %collective-permute-start.21 = (bf16[256,512]{1,0:T(8,128)(2,1)S(1)}, bf16[256,512]{1,0:T(8,128)(2,1)S(1)}, u32[]{:S(2)}, u32[]{:S(2)}) collective-permute-start(bf16[256,512]{1,0:T(8,128)(2,1)S(1)} %get-tuple-element.125.refs_0_), channel_id=1, source_target_pairs={{0,16},{8,24},{16,0},{24,8},{1,17},{9,25},{17,1},{25,9},{2,18},{10... | collective-permute-start | bytes 786440 | tf_op jit(solution)/shard_map/ppermute | solution.py:223
  64.5 11.2 %collective-permute-start.22 = (bf16[256,512]{1,0:T(8,128)(2,1)S(1)}, bf16[256,512]{1,0:T(8,128)(2,1)S(1)}, u32[]{:S(2)}, u32[]{:S(2)}) collective-permute-start(bf16[256,512]{1,0:T(8,128)(2,1)S(1)} %get-tuple-element.145.refs_1_), channel_id=1, source_target_pairs={{0,16},{8,24},{16,0},{24,8},{1,17},{9,25},{17,1},{25,9},{2,18},{10... | collective-permute-start | bytes 786440 | tf_op jit(solution)/shard_map/ppermute | solution.py:223
  70.2 10.4 %collective-permute-start.24 = (bf16[256,512]{1,0:T(8,128)(2,1)S(1)}, bf16[256,512]{1,0:T(8,128)(2,1)S(1)}, u32[]{:S(2)}, u32[]{:S(2)}) collective-permute-start(bf16[256,512]{1,0:T(8,128)(2,1)S(1)} %get-tuple-element.154.refs_0_), channel_id=1, source_target_pairs={{0,8},{8,0},{16,24},{24,16},{1,9},{9,1},{17,25},{25,17},{2,10},{10... | collective-permute-start | bytes 786440 | tf_op jit(solution)/shard_map/ppermute | solution.py:223
  72.1 8.4 %collective-permute-start.25 = (bf16[256,512]{1,0:T(8,128)(2,1)S(1)}, bf16[256,512]{1,0:T(8,128)(2,1)S(1)}, u32[]{:S(2)}, u32[]{:S(2)}) collective-permute-start(bf16[256,512]{1,0:T(8,128)(2,1)S(1)} %get-tuple-element.154.refs_0_), channel_id=1, source_target_pairs={{0,16},{8,24},{16,0},{24,8},{1,17},{9,25},{17,1},{25,9},{2,18},{10... | collective-permute-start | bytes 786440 | tf_op jit(solution)/shard_map/ppermute | solution.py:223
  73.7 13.0 %collective-permute-start.26 = (bf16[256,512]{1,0:T(8,128)(2,1)S(1)}, bf16[256,512]{1,0:T(8,128)(2,1)S(1)}, u32[]{:S(2)}, u32[]{:S(2)}) collective-permute-start(bf16[256,512]{1,0:T(8,128)(2,1)S(1)} %get-tuple-element.156), channel_id=1, source_target_pairs={{0,7},{1,6},{2,5},{3,4},{4,3},{5,2},{6,1},{7,0},{8,15},{9,14},{10,... | collective-permute-start | bytes 786440 | tf_op jit(solution)/shard_map/ppermute | solution.py:223
  86.7 8.2 %collective-permute-start.28 = (bf16[256,512]{1,0:T(8,128)(2,1)S(1)}, bf16[256,512]{1,0:T(8,128)(2,1)S(1)}, u32[]{:S(2)}, u32[]{:S(2)}) collective-permute-start(bf16[256,512]{1,0:T(8,128)(2,1)S(1)} %get-tuple-element.157.refs_0_), channel_id=1, source_target_pairs={{0,8},{8,0},{16,24},{24,16},{1,9},{9,1},{17,25},{25,17},{2,10},{10... | collective-permute-start | bytes 786440 | tf_op jit(solution)/shard_map/ppermute | solution.py:223
  (19 other events, 113.4 us)

commit v9 on v8

--- a/solution.py
+++ b/solution.py
@@ -12,7 +12,6 @@
 QB = 128
 GROUP = 32
 VMEM_LIMIT = 60 * 1024 * 1024
-LATER_LIMIT = 54 * 1024 * 1024
 PRODUCT_LIMIT = 16 * 1024 * 1024
 
 beta_one = 0.9
@@ -55,9 +54,10 @@
     )(*arrays)
 
 
-def adam_kernel(base, blocks, passed, owner, *refs):
+def adam_kernel(groups, passed, owner, *refs):
     arrays, outs = refs[:4], refs[4 + passed : 7 + passed]
-    sends = refs[7 + passed : 7 + passed + blocks]
+    sends = refs[7 + passed : 7 + passed + len(groups)]
+    base, blocks = groups[0][0], sum(map(len, groups))
     *buffers, semaphores = refs[-9:]
     master, gradient, first, second, new_master, new_first, new_second, sent = buffers
     experts, rows, columns = arrays[0].shape
@@ -76,11 +76,11 @@
             pair = (far, near) if inward else (near, far)
             yield pltpu.make_async_copy(*pair, semaphores.at[chunk, k if inward else 4 + k])
 
-    def send_copy(chunk, block):
+    def send_copy(chunk, group, member):
         span = pl.ds(pl.multiple_of(chunk % bands * QB, QB), QB)
-        return pltpu.make_async_copy(
-            sent.at[block, span], sends[block].at[span], semaphores.at[chunk, 7]
-        )
+        n = groups[group][member] - base
+        far = sends[group].at[member, span]
+        return pltpu.make_async_copy(sent.at[n, span], far, semaphores.at[chunk, 7])
 
     def begin(chunk, carry):
         for copy in copies(chunk, True):
@@ -134,57 +134,84 @@
         lax.fori_loop(0, QB // GROUP, quantize, 0)
         for copy in copies(chunk, False):
             copy.start()
-        for block in range(blocks):
-
-            @pl.when(n == block)
-            def _():
-                send_copy(chunk, block).start()
+        for group, numbers in enumerate(groups):
+            for member, number in enumerate(numbers):
+
+                @pl.when(n == number - base)
+                def _():
+                    send_copy(chunk, group, member).start()
 
         return carry
 
     def finish(chunk, carry):
         for copy in copies(chunk, False):
             copy.wait()
-        send_copy(chunk, 0).wait()
+        send_copy(chunk, 0, 0).wait()
         return carry
 
     for part in (begin, work, finish):
         lax.fori_loop(0, blocks * bands, part, 0)
 
 
-def adam_blocks(base, blocks, owner, arrays, carried, token, fenced, limit):
+def adam_blocks(groups, owner, arrays, carried, fenced):
     _, rows, columns = arrays[0].shape
-    passed = len(carried) + len(token)
+    blocks, passed = sum(map(len, groups)), len(carried)
     made = [like(arrays[0]), like(arrays[2]), like(arrays[3])]
-    made += [jax.ShapeDtypeStruct((rows, columns), jnp.bfloat16)] * blocks
-    aliases = {5 + i: i for i in range(len(carried))}
-    if token:
-        aliases[5 + len(carried)] = len(made)
+    made += [jax.ShapeDtypeStruct((len(group), rows, columns), jnp.bfloat16) for group in groups]
     made += [jax.ShapeDtypeStruct(TOKEN, jnp.float32)] * fenced
     kinds = [jnp.float32, jnp.bfloat16, jnp.bfloat16, jnp.bfloat16] * 2
     results = pl.pallas_call(
-        functools.partial(adam_kernel, base, blocks, passed),
+        functools.partial(adam_kernel, groups, passed),
         in_specs=[pl.BlockSpec(memory_space=pltpu.SMEM)] + [WHOLE] * (4 + passed),
         out_specs=[WHOLE] * len(made),
         out_shape=made,
         scratch_shapes=[pltpu.VMEM((blocks, rows, columns), kind) for kind in kinds]
         + [pltpu.SemaphoreType.DMA((blocks * (rows // QB), 8))],
-        input_output_aliases=aliases,
-        compiler_params=pltpu.CompilerParams(vmem_limit_bytes=limit),
+        input_output_aliases={5 + i: i for i in range(passed)},
+        compiler_params=pltpu.CompilerParams(vmem_limit_bytes=VMEM_LIMIT),
         cost_estimate=SMALL_COST,
         name="adam_quantize",
-    )(owner, *arrays, *carried, *token)
-    return results[:3], results[3 : 3 + blocks], tuple(results[3 + blocks :])
+    )(owner, *arrays, *carried)
+    return results[:3], results[3 : 3 + len(groups)], tuple(results[3 + len(groups) :])
+
+
+def join_kernel(picks, *refs):
+    out, semaphores = refs[-2:]
+    pieces = [
+        pltpu.make_async_copy(refs[1 + place].at[pick], out.at[place], semaphores.at[place])
+        for place, pick in enumerate(picks)
+    ]
+    for piece in pieces:
+        piece.start()
+    for piece in pieces:
+        piece.wait()
+
+
+def join(token, arrays, picks):
+    count = len(arrays)
+    shape = jax.ShapeDtypeStruct((count, *arrays[0].shape[1:]), arrays[0].dtype)
+    return pl.pallas_call(
+        functools.partial(join_kernel, picks),
+        in_specs=[WHOLE] * (1 + count),
+        out_specs=[WHOLE] * 2,
+        out_shape=[like(token), shape],
+        scratch_shapes=[pltpu.SemaphoreType.DMA((count,))],
+        input_output_aliases={0: 0},
+        compiler_params=pltpu.CompilerParams(vmem_limit_bytes=1024 * 1024),
+        cost_estimate=SMALL_COST,
+        name="join_blocks",
+    )(token, *arrays)
 
 
 def product_kernel(slabs, sources, places, left, *refs):
     out = refs[-1]
-    rows, breadth = refs[0].shape[0], out.shape[1]
+    rows, breadth = refs[0].shape[1], out.shape[1]
     parts = [left[:, pl.ds(pl.multiple_of(places[i] * rows, QB), rows)] for i in range(slabs)]
-    span = pl.ds(pl.multiple_of(pl.program_id(0) * breadth, QB), breadth)
+    block = pl.program_id(0)
+    span = pl.ds(pl.multiple_of(pl.program_id(1) * breadth, QB), breadth)
     total = jnp.dot(
         jnp.concatenate(parts, axis=1),
-        jnp.concatenate([right[:, span] for right in refs[:slabs]], axis=0),
+        jnp.concatenate([right[block, :, span] for right in refs[:slabs]], axis=0),
         preferred_element_type=jnp.float32,
     )
     out[...] = total.astype(out.dtype)
@@ -193,18 +220,18 @@
 def product(number, sources, places, token_rows, weights, breadth, carried, token):
     slabs = len(weights)
     tokens, units = token_rows.shape
-    rows, columns = weights[0].shape
+    blocks, rows, columns = weights[0].shape
     passed = len(token) + len(carried)
     tile = math.gcd(columns, 2 * QB)
 
-    def place(i, sources, places):
-        return 0, sources[number] * (columns // tile) + i
+    def place(block, i, sources, places):
+        return 0, sources[number + block] * (columns // tile) + i
 
     *token, out = pl.pallas_call(
         functools.partial(product_kernel, slabs),
         grid_spec=pltpu.PrefetchScalarGridSpec(
             num_scalar_prefetch=2,
-            grid=(columns // tile,),
+            grid=(blocks, columns // tile),
             in_specs=[pl.BlockSpec(memory_space=pltpu.VMEM)] * (1 + slabs) + [WHOLE] * passed,
             out_specs=[WHOLE] * len(token)
             + [pl.BlockSpec((tokens, tile), place)],
@@ -236,17 +263,15 @@
         jnp.where((replica ^ members)[:, None] == members[None, :], slab_order[None, :], 0), axis=1
     ).astype(jnp.int32)
 
-    pairs = shards // 2
     fenced = (replicas, shards) == PLANNED
-    held = [{} for _ in range(shards)]
-    made, due, ready = {}, collections.defaultdict(list), set()
+    held, made, ready = collections.defaultdict(dict), {}, set()
     state = {"adam": (), "token": (), "out": ()}
 
-    def adam(base, blocks, limit):
+    def adam(*groups):
         state["adam"], sends, state["token"] = adam_blocks(
-            base, blocks, owner_of_expert, arrays, tuple(state["adam"]), state["token"], fenced, limit
+            groups, owner_of_expert, arrays, tuple(state["adam"]), fenced
         )
-        made.update(zip(range(base, base + blocks), sends))
+        made.update({group[0]: send for group, send in zip(groups, sends)})
 
     def deliver(block):
         held[block][0] = swap(made[block], "shard", shards, block) if block else made[block]
@@ -254,7 +279,7 @@
     def send(block, member, bit):
         held[block][member ^ bit] = swap(held[block][member], "replica", replicas, bit)
 
-    def arrived(keys, leaving):
+    def arrived(keys, leaving=()):
         waiting = [held[b][m] for b, m in keys] + [made[b] for b in leaving]
         token, *passed = fence([*state["token"], *waiting])
         state["token"] = (token,)
@@ -265,53 +290,62 @@
 
     def multiply(block):
         ordered = [held[block][member] for member in range(replicas)]
+        number = int(block)
         state["out"], state["token"] = product(
-            block, sources, places, token_rows, ordered, breadth, state["out"], state["token"]
+            number, sources, places, token_rows, ordered, breadth, state["out"], state["token"]
         )
 
-    waiting = list(range(shards))
     if fenced:
         plan = [
-            ([(1, 0), (0, 1), (0, 2)], [(1, 0, 1), (1, 0, 2)], []),
-            ([(1, 1), (1, 2)], [(0, 1, 2), (1, 2, 1)], []),
-            ([(2, 0), (3, 0), (4, 0)], [(3, 0, 2), (2, 0, 1)], []),
-            ([(0, 3), (1, 3)], [(2, 0, 2), (3, 0, 1)], [5]),
-            ([(2, 1), (3, 2)], [(2, 1, 2), (3, 2, 1)], []),
-            ([(2, 2), (3, 1), (5, 0)], [(4, 0, 1), (4, 0, 2)], [6]),
-            ([(2, 3), (3, 3)], [(5, 0, 1), (5, 0, 2)], []),
-            ([(4, 1), (4, 2)], [(4, 1, 2)], []),
-            ([(6, 0), (5, 1), (5, 2)], [(6, 0, 1), (6, 0, 2), (5, 2, 1)], [7]),
-            ([(4, 3), (5, 3)], [], []),
+            ([(0, 1), (0, 2), (1, 0)], [(1, 0, 1), (1, 0, 2), (0, 1, 2)], []),
+            ([(4, 0)], [], [5]),
+            (["pair", (1, 1), (1, 2)], [(1, 2, 1)], []),
+            (["join", 2.0], [(2.0, 0, 1), (2.0, 0, 2)], []),
+            ([(0, 3), (1, 3)], [], []),
+            (["join", 4.0], [(4.0, 0, 1), (4.0, 0, 2)], [6]),
+            ([(2.0, 1), (2.0, 2)], [(2.0, 1, 2)], []),
+            ([(6, 0), (4.0, 1), (4.0, 2)], [(4.0, 2, 1), (6, 0, 1), (6, 0, 2)], [7]),
+            ([(2.0, 3)], [], []),
+            ([(7, 0)], [(7, 0, 1), (7, 0, 2)], []),
+            ([(4.0, 3)], [], []),
             ([(6, 1), (6, 2)], [(6, 1, 2)], []),
-            ([(7, 0)], [(7, 0, 1), (7, 0, 2)], []),
+            ([(7, 1), (7, 2)], [(7, 2, 1)], []),
             ([(6, 3)], [], []),
-            ([(7, 1), (7, 2)], [(7, 2, 1)], []),
             ([(7, 3)], [], []),
         ]
-        adam(0, 2, VMEM_LIMIT)
-        deliver(0)
-        deliver(1)
+        waiting = [0, 1, 2.0, 4.0, 6, 7]
+        adam((0,), (1,), (2, 3), (4,), (5,), (6,), (7,))
+        for block in (0, 1, 2, 4):
+            deliver(block)
         ready.add((0, 0))
         send(0, 0, 1)
         send(0, 0, 2)
-        adam(2, 4, VMEM_LIMIT)
-        for block in (4, 2, 3):
-            deliver(block)
-        for step, (keys, sending, leaving) in enumerate(plan):
-            arrived(keys, leaving)
+        for keys, sending, leaving in plan:
+            if keys[0] == "pair":
+                arrived([(2, 0), *keys[1:]], leaving)
+                held[2.5][0] = swap(held[2][0], "shard", shards, 1)
+            elif keys[0] == "join":
+                pair = keys[1]
+                one, two = ((2, 2.5) if pair == 2 else (4, 5))
+                picks = (0, 1) if pair == 2 else (0, 0)
+                token, held[pair][0] = join(
+                    state["token"][0], [held[one][0], held[two][0]], picks
+                )
+                state["token"] = (token,)
+                ready.add((pair, 0))
+            else:
+                arrived(keys, leaving)
             for block in leaving:
                 deliver(block)
             for key in sending:
                 send(*key)
-            if not step:
-                adam(6, 2, LATER_LIMIT)
             for block in list(waiting):
                 if all((block, member) in ready for member in range(replicas)):
                     multiply(block)
                     waiting.remove(block)
     else:
-        for pair in range(pairs):
-            adam(2 * pair, 2, VMEM_LIMIT)
+        for pair in range(0, shards, 2):
+            adam((pair,), (pair + 1,))
         for block in range(shards):
             deliver(block)
             for number in range(len(bits)):

time: 105 us -> 103 us (0.981); the launches traced: 104 us -> 101 us
  starting transfers between devices: 30.9 us -> 23.1 us
  waiting for transfers between devices: 40 us -> 46.4 us
  Pallas kernels: 31.6 us -> 28.5 us
  local copies, waits for them, and re-layouts: 0.72 us -> 1.86 us
    ppermute x31 -> x25, starting transfers between devices: 30.9 us -> 23.1 us  [swap(): return lax.ppermute(value, axis, [(i, i ^ mask) for i in range(size)])]
    ppermute x31 -> x25, waiting for transfers between devices: 40 us -> 46.4 us  [swap(): return lax.ppermute(value, axis, [(i, i ^ mask) for i in range(size)])]
    pallas_call x3, Pallas kernels: 15.6 us -> 12.4 us  [the longest x1 10.5 us: adam_blocks(): pl.pallas_call(functools.partial(adam_kernel, groups, passed), in_specs=[...]
    unnamed x24 -> x18, local copies, waits for them, and re-layouts: 0.72 us -> 1.86 us
    pallas_call x8 -> x6, Pallas kernels: 16 us -> 16.2 us  [product(): pl.pallas_call(functools.partial(product_kernel, slabs), grid_spec=pltpu....]
  transfers between devices with their start and end apart: 31 -> 25, of which waited for: 15 -> 13; matrix products, arithmetic and copies ran while one was open for 0% -> 0% of each run, Pallas kernels for 24% -> 16%
where the time goes in v9:
time: 103 us; the launch traced here: 101 us
  waiting for transfers between devices  46.4 us (45%)
  Pallas kernels  28.5 us (28%)
  starting transfers between devices  23.1 us (22%)
  local copies, waits for them, and re-layouts  1.86 us (2%)
    ppermute x25, waiting for transfers between devices, swap(): return lax.ppermute(value, axis, [(i, i ^ mask) for i in range(size)])  46.4 us
    ppermute x25, starting transfers between devices, swap(): return lax.ppermute(value, axis, [(i, i ^ mask) for i in range(size)])  23.1 us
    pallas_call x6, Pallas kernels, product(): pl.pallas_call(functools.partial(product_kernel, slabs), grid_spec=pltpu....  16.2 us
    pallas_call x1, Pallas kernels, adam_blocks(): pl.pallas_call(functools.partial(adam_kernel, groups, passed), in_specs=[...  10.5 us
  transfers between devices with their start and end apart: 25, of which 13 were waited for; matrix products, arithmetic and copies ran while one was open for 0% of the time, Pallas kernels for 16%

profile of v9, /device:TPU:8, one launch (start us, length us, event | category | flops | bytes accessed | tf_op | source)
XLA Modules:
  0.0 100.8 jit_solution(14442048895372947017)
XLA Ops:
  0.6 10.5 %adam_quantize.1 = (f32[8,256,512]{2,1,0:T(8,128)}, bf16[8,256,512]{2,1,0:T(8,128)(2,1)}, bf16[8,256,512]{2,1,0:T(8,128)(2,1)}, bf16[1,256,512]{2,1,0:T(8,128)(2...) custom-call(s32[8]{0:T(128)} %owner.1, ...), custom_call_target="tpu_custom_call" | custom-call | bytes 65536 | tf_op jit(solution)/shard_map/adam_quantize/pallas_call | solution.py:163
  11.2 1.6 %collective-permute-start.1 = (bf16[1,256,512]{2,1,0:T(8,128)(2,1)}, bf16[1,256,512]{2,1,0:T(8,128)(2,1)S(1)}, u32[]{:S(2)}, u32[]{:S(2)}) collective-permute-start(bf16[1,256,512]{2,1,0:T(8,128)(2,1)} %get-tuple-element.72.refs_0_), channel_id=1, source_target_pairs={{0,16},{8,24},{16,0},{24,8},{1,17},{9,25},{17,1},{25,9},{2,18},{10... | collective-permute-start | bytes 786440 | tf_op jit(solution)/shard_map/ppermute | solution.py:250
  12.8 1.5 %collective-permute-start = (bf16[1,256,512]{2,1,0:T(8,128)(2,1)}, bf16[1,256,512]{2,1,0:T(8,128)(2,1)}, u32[]{:S(2)}, u32[]{:S(2)}) collective-permute-start(bf16[1,256,512]{2,1,0:T(8,128)(2,1)} %get-tuple-element.72.refs_0_), channel_id=1, source_target_pairs={{0,8},{8,0},{16,24},{24,16},{1,9},{9,1},{17,25},{25,17},{2,10},{10... | collective-permute-start | bytes 786440 | tf_op jit(solution)/shard_map/ppermute | solution.py:250
  14.8 2.6 %collective-permute-start.3 = (bf16[1,256,512]{2,1,0:T(8,128)(2,1)}, bf16[1,256,512]{2,1,0:T(8,128)(2,1)S(1)}, u32[]{:S(2)}, u32[]{:S(2)}) collective-permute-start(bf16[1,256,512]{2,1,0:T(8,128)(2,1)} %get-tuple-element.75), channel_id=1, source_target_pairs={{0,4},{1,5},{2,6},{3,7},{4,0},{5,1},{6,2},{7,3},{8,12},{9,13},{10,... | collective-permute-start | bytes 786440 | tf_op jit(solution)/shard_map/ppermute | solution.py:250
  17.3 2.8 %collective-permute-done.1.refs_2_ = bf16[1,256,512]{2,1,0:T(8,128)(2,1)S(1)} collective-permute-done((bf16[1,256,512]{2,1,0:T(8,128)(2,1)}, bf16[1,256,512]{2,1,0:T(8,128)(2,1)S(1)}, u32[]{:S(2)}, u32[]{:S(2)}) %collective-permute-start.1) | collective-permute-done | bytes 262176 | tf_op jit(solution)/shard_map/ppermute | solution.py:250
  22.0 1.5 %collective-permute-start.5 = (bf16[1,256,512]{2,1,0:T(8,128)(2,1)S(1)}, bf16[1,256,512]{2,1,0:T(8,128)(2,1)S(1)}, u32[]{:S(2)}, u32[]{:S(2)}) collective-permute-start(bf16[1,256,512]{2,1,0:T(8,128)(2,1)S(1)} %get-tuple-element.79.refs_0_), channel_id=1, source_target_pairs={{0,8},{8,0},{16,24},{24,16},{1,9},{9,1},{17,25},{25,17},{2,10},{10... | collective-permute-start | bytes 786440 | tf_op jit(solution)/shard_map/ppermute | solution.py:250
  23.5 11.4 %collective-permute-done.3.refs_1_ = bf16[1,256,512]{2,1,0:T(8,128)(2,1)S(1)} collective-permute-done((bf16[1,256,512]{2,1,0:T(8,128)(2,1)}, bf16[1,256,512]{2,1,0:T(8,128)(2,1)S(1)}, u32[]{:S(2)}, u32[]{:S(2)}) %collective-permute-start.3) | collective-permute-done | bytes 262176 | tf_op jit(solution)/shard_map/ppermute | solution.py:250
  35.0 1.6 %collective-permute-start.10 = (bf16[1,256,512]{2,1,0:T(8,128)(2,1)}, bf16[1,256,512]{2,1,0:T(8,128)(2,1)}, u32[]{:S(2)}, u32[]{:S(2)}) collective-permute-start(bf16[1,256,512]{2,1,0:T(8,128)(2,1)} %get-tuple-element.95), channel_id=1, source_target_pairs={{0,5},{1,4},{2,7},{3,6},{4,1},{5,0},{6,3},{7,2},{8,13},{9,12},{10,... | collective-permute-start | bytes 786440 | tf_op jit(solution)/shard_map/ppermute | solution.py:250
  40.3 1.6 %collective-permute-start.12 = (bf16[2,256,512]{2,1,0:T(8,128)(2,1)}, bf16[2,256,512]{2,1,0:T(8,128)(2,1)S(1)}, u32[]{:S(2)}, u32[]{:S(2)}) collective-permute-start(bf16[2,256,512]{2,1,0:T(8,128)(2,1)} %get-tuple-element.82.refs_0_), channel_id=1, source_target_pairs={{0,16},{8,24},{16,0},{24,8},{1,17},{9,25},{17,1},{25,9},{2,18},{10... | collective-permute-start | bytes 1572872 | tf_op jit(solution)/shard_map/ppermute | solution.py:250
  43.6 2.4 %collective-permute-done.8.refs_1_ = bf16[1,256,512]{2,1,0:T(8,128)(2,1)S(1)} collective-permute-done((bf16[1,256,512]{2,1,0:T(8,128)(2,1)}, bf16[1,256,512]{2,1,0:T(8,128)(2,1)S(1)}, u32[]{:S(2)}, u32[]{:S(2)}) %collective-permute-start.8) | collective-permute-done | bytes 262176 | tf_op jit(solution)/shard_map/ppermute | solution.py:250
  46.2 3.0 %expert_product.6 = (f32[135168,128]{1,0:T(8,128)}, bf16[384,4096]{1,0:T(8,128)(2,1)}) custom-call(s32[8]{0:T(128)S(1)} %iota_xor_fusion.1.sources, s32[4]{0:T(128)S(1)} %select_reduce_fusion.places, bf16[384,1024]{1,0:T(8,128)(2,1)S(1)} %bitcast.2, bf16[1,256,512]{2,1,0:T(8,128)(2,1)S(1)} %copy-done.6, ...), custom_call_target="tpu_custom_call", output_to_operand_aliasing={{0}: (7, {})} | custom-call | bytes 65536 | tf_op jit(solution)/shard_map/expert_product/pallas_call | solution.py:230
  49.2 2.0 %expert_product.7 = (f32[135168,128]{1,0:T(8,128)}, bf16[384,4096]{1,0:T(8,128)(2,1)}) custom-call(s32[8]{0:T(128)S(1)} %iota_xor_fusion.1.sources, s32[4]{0:T(128)S(1)} %select_reduce_fusion.places, bf16[384,1024]{1,0:T(8,128)(2,1)S(1)} %bitcast.3, ...), custom_call_target="tpu_custom_call", output_to_operand_aliasing={{0}: (7, {}), {1}: (8, {})} | custom-call | bytes 65536 | tf_op jit(solution)/shard_map/expert_product/pallas_call | solution.py:230
  52.2 1.7 %collective-permute-start.15 = (bf16[2,256,512]{2,1,0:T(8,128)(2,1)S(1)}, bf16[2,256,512]{2,1,0:T(8,128)(2,1)S(1)}, u32[]{:S(2)}, u32[]{:S(2)}) collective-permute-start(bf16[2,256,512]{2,1,0:T(8,128)(2,1)S(1)} %get-tuple-element.101.refs_0_), channel_id=1, source_target_pairs={{0,16},{8,24},{16,0},{24,8},{1,17},{9,25},{17,1},{25,9},{2,18},{10... | collective-permute-start | bytes 1572872 | tf_op jit(solution)/shard_map/ppermute | solution.py:250
  54.4 2.7 %collective-permute-done.12.refs_2_ = bf16[2,256,512]{2,1,0:T(8,128)(2,1)S(1)} collective-permute-done((bf16[2,256,512]{2,1,0:T(8,128)(2,1)}, bf16[2,256,512]{2,1,0:T(8,128)(2,1)S(1)}, u32[]{:S(2)}, u32[]{:S(2)}) %collective-permute-start.12) | collective-permute-done | bytes 524320 | tf_op jit(solution)/shard_map/ppermute | solution.py:250
  57.4 1.6 %collective-permute-start.16 = (bf16[2,256,512]{2,1,0:T(8,128)(2,1)S(1)}, bf16[2,256,512]{2,1,0:T(8,128)(2,1)S(1)}, u32[]{:S(2)}, u32[]{:S(2)}) collective-permute-start(bf16[2,256,512]{2,1,0:T(8,128)(2,1)S(1)} %get-tuple-element.97.refs_1_), channel_id=1, source_target_pairs={{0,16},{8,24},{16,0},{24,8},{1,17},{9,25},{17,1},{25,9},{2,18},{10... | collective-permute-start | bytes 1572872 | tf_op jit(solution)/shard_map/ppermute | solution.py:250
  59.0 6.4 %collective-permute-done.13.refs_1_ = bf16[1,256,512]{2,1,0:T(8,128)(2,1)S(1)} collective-permute-done((bf16[1,256,512]{2,1,0:T(8,128)(2,1)S(1)}, bf16[1,256,512]{2,1,0:T(8,128)(2,1)S(1)}, u32[]{:S(2)}, u32[]{:S(2)}) %collective-permute-start.13) | collective-permute-done | bytes 262176 | tf_op jit(solution)/shard_map/ppermute | solution.py:250
  65.4 3.0 %collective-permute-done.15.refs_3_ = bf16[2,256,512]{2,1,0:T(8,128)(2,1)S(1)} collective-permute-done((bf16[2,256,512]{2,1,0:T(8,128)(2,1)S(1)}, bf16[2,256,512]{2,1,0:T(8,128)(2,1)S(1)}, u32[]{:S(2)}, u32[]{:S(2)}) %collective-permute-start.15) | collective-permute-done | bytes 524320 | tf_op jit(solution)/shard_map/ppermute | solution.py:250
  71.1 8.5 %collective-permute-done.16.refs_1_ = bf16[2,256,512]{2,1,0:T(8,128)(2,1)S(1)} collective-permute-done((bf16[2,256,512]{2,1,0:T(8,128)(2,1)S(1)}, bf16[2,256,512]{2,1,0:T(8,128)(2,1)S(1)}, u32[]{:S(2)}, u32[]{:S(2)}) %collective-permute-start.16) | collective-permute-done | bytes 524320 | tf_op jit(solution)/shard_map/ppermute | solution.py:250
  79.6 4.1 %expert_product.8 = (f32[135168,128]{1,0:T(8,128)}, bf16[384,4096]{1,0:T(8,128)(2,1)}) custom-call(s32[8]{0:T(128)S(1)} %iota_xor_fusion.1.sources, s32[4]{0:T(128)S(1)} %select_reduce_fusion.places, bf16[384,1024]{1,0:T(8,128)(2,1)S(1)} %bitcast.4, bf16[2,256,512]{2,1,0:T(8,128)(2,1)} %get-tuple-element.82.refs_0_, ...), custom_call_target="tpu_custom_call", output_to_operand_aliasing={{0}: (7, {}), {1}: (8, {})} | custom-call | bytes 65536 | tf_op jit(solution)/shard_map/expert_product/pallas_call | solution.py:230
  85.0 3.1 %expert_product.9 = (f32[135168,128]{1,0:T(8,128)}, bf16[384,4096]{1,0:T(8,128)(2,1)}) custom-call(s32[8]{0:T(128)S(1)} %iota_xor_fusion.1.sources, s32[4]{0:T(128)S(1)} %select_reduce_fusion.places, bf16[384,1024]{1,0:T(8,128)(2,1)S(1)} %bitcast.5, ...), custom_call_target="tpu_custom_call", output_to_operand_aliasing={{0}: (7, {}), {1}: (8, {})} | custom-call | bytes 65536 | tf_op jit(solution)/shard_map/expert_product/pallas_call | solution.py:230
  89.5 3.0 %collective-permute-done.22.refs_2_ = bf16[1,256,512]{2,1,0:T(8,128)(2,1)S(1)} collective-permute-done((bf16[1,256,512]{2,1,0:T(8,128)(2,1)S(1)}, bf16[1,256,512]{2,1,0:T(8,128)(2,1)S(1)}, u32[]{:S(2)}, u32[]{:S(2)}) %collective-permute-start.22) | collective-permute-done | bytes 262176 | tf_op jit(solution)/shard_map/ppermute | solution.py:250
  92.5 3.5 %collective-permute-done.23.refs_1_ = bf16[1,256,512]{2,1,0:T(8,128)(2,1)S(1)} collective-permute-done((bf16[1,256,512]{2,1,0:T(8,128)(2,1)S(1)}, bf16[1,256,512]{2,1,0:T(8,128)(2,1)S(1)}, u32[]{:S(2)}, u32[]{:S(2)}) %collective-permute-start.23) | collective-permute-done | bytes 262176 | tf_op jit(solution)/shard_map/ppermute | solution.py:250
  95.9 2.0 %expert_product.10 = (f32[135168,128]{1,0:T(8,128)}, bf16[384,4096]{1,0:T(8,128)(2,1)}) custom-call(s32[8]{0:T(128)S(1)} %iota_xor_fusion.1.sources, s32[4]{0:T(128)S(1)} %select_reduce_fusion.places, bf16[384,1024]{1,0:T(8,128)(2,1)S(1)} %bitcast.6, ...), custom_call_target="tpu_custom_call", output_to_operand_aliasing={{0}: (7, {}), {1}: (8, {})} | custom-call | bytes 65536 | tf_op jit(solution)/shard_map/expert_product/pallas_call | solution.py:230
  98.8 2.0 %expert_product.11 = (f32[135168,128]{1,0:T(8,128)}, bf16[384,4096]{1,0:T(8,128)(2,1)}) custom-call(s32[8]{0:T(128)S(1)} %iota_xor_fusion.1.sources, s32[4]{0:T(128)S(1)} %select_reduce_fusion.places, bf16[384,1024]{1,0:T(8,128)(2,1)S(1)} %bitcast.7, ...), custom_call_target="tpu_custom_call", output_to_operand_aliasing={{0}: (7, {}), {1}: (8, {})} | custom-call | bytes 65536 | tf_op jit(solution)/shard_map/expert_product/pallas_call | solution.py:230
  (69 shorter events, 16.1 us)
Async XLA Ops:
  11.2 6.2 %collective-permute-start.2 = (bf16[1,256,512]{2,1,0:T(8,128)(2,1)}, bf16[1,256,512]{2,1,0:T(8,128)(2,1)S(1)}, u32[]{:S(2)}, u32[]{:S(2)}) collective-permute-start(bf16[1,256,512]{2,1,0:T(8,128)(2,1)} %get-tuple-element.73), channel_id=1, source_target_pairs={{0,1},{1,0},{2,3},{3,2},{4,5},{5,4},{6,7},{7,6},{8,9},{9,8},{10,11... | collective-permute-start | bytes 786440 | tf_op jit(solution)/shard_map/ppermute | solution.py:250
  11.2 8.9 %collective-permute-start.1 = (bf16[1,256,512]{2,1,0:T(8,128)(2,1)}, bf16[1,256,512]{2,1,0:T(8,128)(2,1)S(1)}, u32[]{:S(2)}, u32[]{:S(2)}) collective-permute-start(bf16[1,256,512]{2,1,0:T(8,128)(2,1)} %get-tuple-element.72.refs_0_), channel_id=1, source_target_pairs={{0,16},{8,24},{16,0},{24,8},{1,17},{9,25},{17,1},{25,9},{2,18},{10... | collective-permute-start | bytes 786440 | tf_op jit(solution)/shard_map/ppermute | solution.py:250
  12.8 8.7 %collective-permute-start = (bf16[1,256,512]{2,1,0:T(8,128)(2,1)}, bf16[1,256,512]{2,1,0:T(8,128)(2,1)}, u32[]{:S(2)}, u32[]{:S(2)}) collective-permute-start(bf16[1,256,512]{2,1,0:T(8,128)(2,1)} %get-tuple-element.72.refs_0_), channel_id=1, source_target_pairs={{0,8},{8,0},{16,24},{24,16},{1,9},{9,1},{17,25},{25,17},{2,10},{10... | collective-permute-start | bytes 786440 | tf_op jit(solution)/shard_map/ppermute | solution.py:250
  14.3 20.6 %collective-permute-start.4 = (bf16[2,256,512]{2,1,0:T(8,128)(2,1)}, bf16[2,256,512]{2,1,0:T(8,128)(2,1)S(1)}, u32[]{:S(2)}, u32[]{:S(2)}) collective-permute-start(bf16[2,256,512]{2,1,0:T(8,128)(2,1)} %get-tuple-element.78), channel_id=1, source_target_pairs={{0,2},{1,3},{2,0},{3,1},{4,6},{5,7},{6,4},{7,5},{8,10},{9,11},{10,... | collective-permute-start | bytes 1572872 | tf_op jit(solution)/shard_map/ppermute | solution.py:250
  14.8 20.1 %collective-permute-start.3 = (bf16[1,256,512]{2,1,0:T(8,128)(2,1)}, bf16[1,256,512]{2,1,0:T(8,128)(2,1)S(1)}, u32[]{:S(2)}, u32[]{:S(2)}) collective-permute-start(bf16[1,256,512]{2,1,0:T(8,128)(2,1)} %get-tuple-element.75), channel_id=1, source_target_pairs={{0,4},{1,5},{2,6},{3,7},{4,0},{5,1},{6,2},{7,3},{8,12},{9,13},{10,... | collective-permute-start | bytes 786440 | tf_op jit(solution)/shard_map/ppermute | solution.py:250
  21.5 13.4 %collective-permute-start.6 = (bf16[1,256,512]{2,1,0:T(8,128)(2,1)S(1)}, bf16[1,256,512]{2,1,0:T(8,128)(2,1)S(1)}, u32[]{:S(2)}, u32[]{:S(2)}) collective-permute-start(bf16[1,256,512]{2,1,0:T(8,128)(2,1)S(1)} %get-tuple-element.79.refs_0_), channel_id=1, source_target_pairs={{0,16},{8,24},{16,0},{24,8},{1,17},{9,25},{17,1},{25,9},{2,18},{10... | collective-permute-start | bytes 786440 | tf_op jit(solution)/shard_map/ppermute | solution.py:250
  22.0 12.9 %collective-permute-start.5 = (bf16[1,256,512]{2,1,0:T(8,128)(2,1)S(1)}, bf16[1,256,512]{2,1,0:T(8,128)(2,1)S(1)}, u32[]{:S(2)}, u32[]{:S(2)}) collective-permute-start(bf16[1,256,512]{2,1,0:T(8,128)(2,1)S(1)} %get-tuple-element.79.refs_0_), channel_id=1, source_target_pairs={{0,8},{8,0},{16,24},{24,16},{1,9},{9,1},{17,25},{25,17},{2,10},{10... | collective-permute-start | bytes 786440 | tf_op jit(solution)/shard_map/ppermute | solution.py:250
  35.0 16.2 %collective-permute-start.10 = (bf16[1,256,512]{2,1,0:T(8,128)(2,1)}, bf16[1,256,512]{2,1,0:T(8,128)(2,1)}, u32[]{:S(2)}, u32[]{:S(2)}) collective-permute-start(bf16[1,256,512]{2,1,0:T(8,128)(2,1)} %get-tuple-element.95), channel_id=1, source_target_pairs={{0,5},{1,4},{2,7},{3,6},{4,1},{5,0},{6,3},{7,2},{8,13},{9,12},{10,... | collective-permute-start | bytes 786440 | tf_op jit(solution)/shard_map/ppermute | solution.py:250
  36.6 9.4 %collective-permute-start.8 = (bf16[1,256,512]{2,1,0:T(8,128)(2,1)}, bf16[1,256,512]{2,1,0:T(8,128)(2,1)S(1)}, u32[]{:S(2)}, u32[]{:S(2)}) collective-permute-start(bf16[1,256,512]{2,1,0:T(8,128)(2,1)} %get-tuple-element.86.refs_1_), channel_id=1, source_target_pairs={{0,16},{8,24},{16,0},{24,8},{1,17},{9,25},{17,1},{25,9},{2,18},{10... | collective-permute-start | bytes 786440 | tf_op jit(solution)/shard_map/ppermute | solution.py:250
  37.1 9.1 %collective-permute-start.9 = (bf16[1,256,512]{2,1,0:T(8,128)(2,1)S(1)}, bf16[1,256,512]{2,1,0:T(8,128)(2,1)S(1)}, u32[]{:S(2)}, u32[]{:S(2)}) collective-permute-start(bf16[1,256,512]{2,1,0:T(8,128)(2,1)S(1)} %get-tuple-element.84.refs_2_), channel_id=1, source_target_pairs={{0,8},{8,0},{16,24},{24,16},{1,9},{9,1},{17,25},{25,17},{2,10},{10... | collective-permute-start | bytes 786440 | tf_op jit(solution)/shard_map/ppermute | solution.py:250
  40.3 16.9 %collective-permute-start.12 = (bf16[2,256,512]{2,1,0:T(8,128)(2,1)}, bf16[2,256,512]{2,1,0:T(8,128)(2,1)S(1)}, u32[]{:S(2)}, u32[]{:S(2)}) collective-permute-start(bf16[2,256,512]{2,1,0:T(8,128)(2,1)} %get-tuple-element.82.refs_0_), channel_id=1, source_target_pairs={{0,16},{8,24},{16,0},{24,8},{1,17},{9,25},{17,1},{25,9},{2,18},{10... | collective-permute-start | bytes 1572872 | tf_op jit(solution)/shard_map/ppermute | solution.py:250
  41.9 15.5 %collective-permute-start.11 = (bf16[2,256,512]{2,1,0:T(8,128)(2,1)}, bf16[2,256,512]{2,1,0:T(8,128)(2,1)S(1)}, u32[]{:S(2)}, u32[]{:S(2)}) collective-permute-start(bf16[2,256,512]{2,1,0:T(8,128)(2,1)} %get-tuple-element.82.refs_0_), channel_id=1, source_target_pairs={{0,8},{8,0},{16,24},{24,16},{1,9},{9,1},{17,25},{25,17},{2,10},{10... | collective-permute-start | bytes 1572872 | tf_op jit(solution)/shard_map/ppermute | solution.py:250
  52.2 16.2 %collective-permute-start.15 = (bf16[2,256,512]{2,1,0:T(8,128)(2,1)S(1)}, bf16[2,256,512]{2,1,0:T(8,128)(2,1)S(1)}, u32[]{:S(2)}, u32[]{:S(2)}) collective-permute-start(bf16[2,256,512]{2,1,0:T(8,128)(2,1)S(1)} %get-tuple-element.101.refs_0_), channel_id=1, source_target_pairs={{0,16},{8,24},{16,0},{24,8},{1,17},{9,25},{17,1},{25,9},{2,18},{10... | collective-permute-start | bytes 1572872 | tf_op jit(solution)/shard_map/ppermute | solution.py:250
  53.9 14.5 %collective-permute-start.14 = (bf16[2,256,512]{2,1,0:T(8,128)(2,1)S(1)}, bf16[2,256,512]{2,1,0:T(8,128)(2,1)S(1)}, u32[]{:S(2)}, u32[]{:S(2)}) collective-permute-start(bf16[2,256,512]{2,1,0:T(8,128)(2,1)S(1)} %get-tuple-element.101.refs_0_), channel_id=1, source_target_pairs={{0,8},{8,0},{16,24},{24,16},{1,9},{9,1},{17,25},{25,17},{2,10},{10... | collective-permute-start | bytes 1572872 | tf_op jit(solution)/shard_map/ppermute | solution.py:250
  54.4 11.0 %collective-permute-start.13 = (bf16[1,256,512]{2,1,0:T(8,128)(2,1)S(1)}, bf16[1,256,512]{2,1,0:T(8,128)(2,1)S(1)}, u32[]{:S(2)}, u32[]{:S(2)}) collective-permute-start(bf16[1,256,512]{2,1,0:T(8,128)(2,1)S(1)} %copy-done.7), channel_id=1, source_target_pairs={{0,6},{1,7},{2,4},{3,5},{4,2},{5,3},{6,0},{7,1},{8,14},{9,15},{10,... | collective-permute-start | bytes 786440 | tf_op jit(solution)/shard_map/ppermute | solution.py:250
  57.4 22.2 %collective-permute-start.16 = (bf16[2,256,512]{2,1,0:T(8,128)(2,1)S(1)}, bf16[2,256,512]{2,1,0:T(8,128)(2,1)S(1)}, u32[]{:S(2)}, u32[]{:S(2)}) collective-permute-start(bf16[2,256,512]{2,1,0:T(8,128)(2,1)S(1)} %get-tuple-element.97.refs_1_), channel_id=1, source_target_pairs={{0,16},{8,24},{16,0},{24,8},{1,17},{9,25},{17,1},{25,9},{2,18},{10... | collective-permute-start | bytes 1572872 | tf_op jit(solution)/shard_map/ppermute | solution.py:250
  68.4 16.6 %collective-permute-start.18 = (bf16[2,256,512]{2,1,0:T(8,128)(2,1)S(1)}, bf16[2,256,512]{2,1,0:T(8,128)(2,1)S(1)}, u32[]{:S(2)}, u32[]{:S(2)}) collective-permute-start(bf16[2,256,512]{2,1,0:T(8,128)(2,1)S(1)} %get-tuple-element.111.refs_2_), channel_id=1, source_target_pairs={{0,8},{8,0},{16,24},{24,16},{1,9},{9,1},{17,25},{25,17},{2,10},{10... | collective-permute-start | bytes 1572872 | tf_op jit(solution)/shard_map/ppermute | solution.py:250
  68.9 14.8 %collective-permute-start.17 = (bf16[1,256,512]{2,1,0:T(8,128)(2,1)S(1)}, bf16[1,256,512]{2,1,0:T(8,128)(2,1)S(1)}, u32[]{:S(2)}, u32[]{:S(2)}) collective-permute-start(bf16[1,256,512]{2,1,0:T(8,128)(2,1)S(1)} %get-tuple-element.108), channel_id=1, source_target_pairs={{0,7},{1,6},{2,5},{3,4},{4,3},{5,2},{6,1},{7,0},{8,15},{9,14},{10,... | collective-permute-start | bytes 786440 | tf_op jit(solution)/shard_map/ppermute | solution.py:250
  69.0 19.1 %collective-permute-start.20 = (bf16[1,256,512]{2,1,0:T(8,128)(2,1)S(1)}, bf16[1,256,512]{2,1,0:T(8,128)(2,1)S(1)}, u32[]{:S(2)}, u32[]{:S(2)}) collective-permute-start(bf16[1,256,512]{2,1,0:T(8,128)(2,1)S(1)} %get-tuple-element.117.refs_0_), channel_id=1, source_target_pairs={{0,16},{8,24},{16,0},{24,8},{1,17},{9,25},{17,1},{25,9},{2,18},{10... | collective-permute-start | bytes 786440 | tf_op jit(solution)/shard_map/ppermute | solution.py:250
  69.7 18.4 %collective-permute-start.19 = (bf16[1,256,512]{2,1,0:T(8,128)(2,1)S(1)}, bf16[1,256,512]{2,1,0:T(8,128)(2,1)S(1)}, u32[]{:S(2)}, u32[]{:S(2)}) collective-permute-start(bf16[1,256,512]{2,1,0:T(8,128)(2,1)S(1)} %get-tuple-element.117.refs_0_), channel_id=1, source_target_pairs={{0,8},{8,0},{16,24},{24,16},{1,9},{9,1},{17,25},{25,17},{2,10},{10... | collective-permute-start | bytes 786440 | tf_op jit(solution)/shard_map/ppermute | solution.py:250
  83.8 8.7 %collective-permute-start.22 = (bf16[1,256,512]{2,1,0:T(8,128)(2,1)S(1)}, bf16[1,256,512]{2,1,0:T(8,128)(2,1)S(1)}, u32[]{:S(2)}, u32[]{:S(2)}) collective-permute-start(bf16[1,256,512]{2,1,0:T(8,128)(2,1)S(1)} %get-tuple-element.109.refs_0_), channel_id=1, source_target_pairs={{0,16},{8,24},{16,0},{24,8},{1,17},{9,25},{17,1},{25,9},{2,18},{10... | collective-permute-start | bytes 786440 | tf_op jit(solution)/shard_map/ppermute | solution.py:250
  84.3 8.2 %collective-permute-start.21 = (bf16[1,256,512]{2,1,0:T(8,128)(2,1)S(1)}, bf16[1,256,512]{2,1,0:T(8,128)(2,1)S(1)}, u32[]{:S(2)}, u32[]{:S(2)}) collective-permute-start(bf16[1,256,512]{2,1,0:T(8,128)(2,1)S(1)} %get-tuple-element.109.refs_0_), channel_id=1, source_target_pairs={{0,8},{8,0},{16,24},{24,16},{1,9},{9,1},{17,25},{25,17},{2,10},{10... | collective-permute-start | bytes 786440 | tf_op jit(solution)/shard_map/ppermute | solution.py:250
  88.1 7.9 %collective-permute-start.23 = (bf16[1,256,512]{2,1,0:T(8,128)(2,1)S(1)}, bf16[1,256,512]{2,1,0:T(8,128)(2,1)S(1)}, u32[]{:S(2)}, u32[]{:S(2)}) collective-permute-start(bf16[1,256,512]{2,1,0:T(8,128)(2,1)S(1)} %get-tuple-element.121.refs_1_), channel_id=1, source_target_pairs={{0,16},{8,24},{16,0},{24,8},{1,17},{9,25},{17,1},{25,9},{2,18},{10... | collective-permute-start | bytes 786440 | tf_op jit(solution)/shard_map/ppermute | solution.py:250
  92.5 6.4 %collective-permute-start.24 = (bf16[1,256,512]{2,1,0:T(8,128)(2,1)S(1)}, bf16[1,256,512]{2,1,0:T(8,128)(2,1)S(1)}, u32[]{:S(2)}, u32[]{:S(2)}) collective-permute-start(bf16[1,256,512]{2,1,0:T(8,128)(2,1)S(1)} %get-tuple-element.120.refs_2_), channel_id=1, source_target_pairs={{0,8},{8,0},{16,24},{24,16},{1,9},{9,1},{17,25},{25,17},{2,10},{10... | collective-permute-start | bytes 786440 | tf_op jit(solution)/shard_map/ppermute | solution.py:250
  (10 other events, 53.4 us)

commit v10 on v9

--- a/solution.py
+++ b/solution.py
@@ -217,7 +217,7 @@
     out[...] = total.astype(out.dtype)
 
 
-def product(number, sources, places, token_rows, weights, breadth, carried, token):
+def product(numbers, sources, places, token_rows, weights, breadth, carried, token):
     slabs = len(weights)
     tokens, units = token_rows.shape
     blocks, rows, columns = weights[0].shape
@@ -225,7 +225,8 @@
     tile = math.gcd(columns, 2 * QB)
 
     def place(block, i, sources, places):
-        return 0, sources[number + block] * (columns // tile) + i
+        number = numbers[0] + block * (numbers[-1] - numbers[0])
+        return 0, sources[number] * (columns // tile) + i
 
     *token, out = pl.pallas_call(
         functools.partial(product_kernel, slabs),
@@ -290,49 +291,43 @@
 
     def multiply(block):
         ordered = [held[block][member] for member in range(replicas)]
-        number = int(block)
+        numbers = block if isinstance(block, tuple) else (block,)
         state["out"], state["token"] = product(
-            number, sources, places, token_rows, ordered, breadth, state["out"], state["token"]
+            numbers, sources, places, token_rows, ordered, breadth, state["out"], state["token"]
         )
 
     if fenced:
+        one, two = (2, 4), (3, 5)
         plan = [
-            ([(0, 1), (0, 2), (1, 0)], [(1, 0, 1), (1, 0, 2), (0, 1, 2)], []),
-            ([(4, 0)], [], [5]),
-            (["pair", (1, 1), (1, 2)], [(1, 2, 1)], []),
-            (["join", 2.0], [(2.0, 0, 1), (2.0, 0, 2)], []),
-            ([(0, 3), (1, 3)], [], []),
-            (["join", 4.0], [(4.0, 0, 1), (4.0, 0, 2)], [6]),
-            ([(2.0, 1), (2.0, 2)], [(2.0, 1, 2)], []),
-            ([(6, 0), (4.0, 1), (4.0, 2)], [(4.0, 2, 1), (6, 0, 1), (6, 0, 2)], [7]),
-            ([(2.0, 3)], [], []),
+            ([(0, 1), (0, 2), (1, 0)], [(1, 0, 1), (1, 0, 2)], []),
+            ([(2, 0), (4, 0)], [], [5]),
+            ([(1, 1), (1, 2)], [(1, 2, 1), (0, 1, 2)], []),
+            (one, [(one, 0, 1), (one, 0, 2)], []),
+            ([(0, 3), (1, 3)], [], [3]),
+            (two, [(two, 0, 1), (two, 0, 2)], [6]),
+            ([(one, 1), (one, 2)], [(one, 1, 2)], []),
+            ([(6, 0), (two, 1), (two, 2)], [(two, 2, 1), (6, 0, 1), (6, 0, 2)], [7]),
+            ([(one, 3)], [], []),
             ([(7, 0)], [(7, 0, 1), (7, 0, 2)], []),
-            ([(4.0, 3)], [], []),
+            ([(two, 3)], [], []),
             ([(6, 1), (6, 2)], [(6, 1, 2)], []),
             ([(7, 1), (7, 2)], [(7, 2, 1)], []),
             ([(6, 3)], [], []),
             ([(7, 3)], [], []),
         ]
-        waiting = [0, 1, 2.0, 4.0, 6, 7]
-        adam((0,), (1,), (2, 3), (4,), (5,), (6,), (7,))
+        waiting = [0, 1, one, two, 6, 7]
+        adam(*[(block,) for block in range(shards)])
         for block in (0, 1, 2, 4):
             deliver(block)
         ready.add((0, 0))
         send(0, 0, 1)
         send(0, 0, 2)
         for keys, sending, leaving in plan:
-            if keys[0] == "pair":
-                arrived([(2, 0), *keys[1:]], leaving)
-                held[2.5][0] = swap(held[2][0], "shard", shards, 1)
-            elif keys[0] == "join":
-                pair = keys[1]
-                one, two = ((2, 2.5) if pair == 2 else (4, 5))
-                picks = (0, 1) if pair == 2 else (0, 0)
-                token, held[pair][0] = join(
-                    state["token"][0], [held[one][0], held[two][0]], picks
-                )
+            if isinstance(keys, tuple):
+                pieces = [held[block][0] for block in keys]
+                token, held[keys][0] = join(state["token"][0], pieces, (0, 0))
                 state["token"] = (token,)
-                ready.add((pair, 0))
+                ready.add((keys, 0))
             else:
                 arrived(keys, leaving)
             for block in leaving:

time: 103 us -> 103 us (level)
  waiting for transfers between devices: 46.4 us -> 44.7 us
    ppermute x25, waiting for transfers between devices: 46.4 us -> 44.7 us  [swap(): return lax.ppermute(value, axis, [(i, i ^ mask) for i in range(size)])]
    unnamed x18 -> x14, local copies, waits for them, and re-layouts: 1.86 us -> 2.6 us
  transfers between devices with their start and end apart: 25 -> 25, of which waited for: 13 -> 15; matrix products, arithmetic and copies ran while one was open for 0% -> 0% of each run, Pallas kernels for 16% -> 16%
where the time goes in v10:
time: 103 us; the launch traced here: 101 us
  waiting for transfers between devices  44.7 us (43%)
  Pallas kernels  28.6 us (28%)
  starting transfers between devices  23.9 us (23%)
  local copies, waits for them, and re-layouts  2.6 us (3%)
    ppermute x25, waiting for transfers between devices, swap(): return lax.ppermute(value, axis, [(i, i ^ mask) for i in range(size)])  44.7 us
    ppermute x25, starting transfers between devices, swap(): return lax.ppermute(value, axis, [(i, i ^ mask) for i in range(size)])  23.9 us
    pallas_call x6, Pallas kernels, product(): pl.pallas_call(functools.partial(product_kernel, slabs), grid_spec=pltpu....  16.2 us
    pallas_call x1, Pallas kernels, adam_blocks(): pl.pallas_call(functools.partial(adam_kernel, groups, passed), in_specs=[...  10.5 us
    unnamed x14, local copies, waits for them, and re-layouts  2.6 us
  transfers between devices with their start and end apart: 25, of which 15 were waited for; matrix products, arithmetic and copies ran while one was open for 0% of the time, Pallas kernels for 16%

profile of v10, /device:TPU:8, one launch (start us, length us, event | category | flops | bytes accessed | tf_op | source)
XLA Modules:
  0.0 100.7 jit_solution(8112611911335105329)
XLA Ops:
  0.6 10.5 %adam_quantize.1 = (f32[8,256,512]{2,1,0:T(8,128)}, bf16[8,256,512]{2,1,0:T(8,128)(2,1)}, bf16[8,256,512]{2,1,0:T(8,128)(2,1)}, bf16[1,256,512]{2,1,0:T(8,128)(2...) custom-call(s32[8]{0:T(128)} %owner.1, ...), custom_call_target="tpu_custom_call" | custom-call | bytes 65536 | tf_op jit(solution)/shard_map/adam_quantize/pallas_call | solution.py:163
  11.2 1.6 %collective-permute-start.1 = (bf16[1,256,512]{2,1,0:T(8,128)(2,1)}, bf16[1,256,512]{2,1,0:T(8,128)(2,1)S(1)}, u32[]{:S(2)}, u32[]{:S(2)}) collective-permute-start(bf16[1,256,512]{2,1,0:T(8,128)(2,1)} %get-tuple-element.74.refs_0_), channel_id=1, source_target_pairs={{0,16},{8,24},{16,0},{24,8},{1,17},{9,25},{17,1},{25,9},{2,18},{10... | collective-permute-start | bytes 786440 | tf_op jit(solution)/shard_map/ppermute | solution.py:251
  12.8 1.5 %collective-permute-start = (bf16[1,256,512]{2,1,0:T(8,128)(2,1)}, bf16[1,256,512]{2,1,0:T(8,128)(2,1)}, u32[]{:S(2)}, u32[]{:S(2)}) collective-permute-start(bf16[1,256,512]{2,1,0:T(8,128)(2,1)} %get-tuple-element.74.refs_0_), channel_id=1, source_target_pairs={{0,8},{8,0},{16,24},{24,16},{1,9},{9,1},{17,25},{25,17},{2,10},{10... | collective-permute-start | bytes 786440 | tf_op jit(solution)/shard_map/ppermute | solution.py:251
  14.8 2.6 %collective-permute-start.4 = (bf16[1,256,512]{2,1,0:T(8,128)(2,1)}, bf16[1,256,512]{2,1,0:T(8,128)(2,1)S(1)}, u32[]{:S(2)}, u32[]{:S(2)}) collective-permute-start(bf16[1,256,512]{2,1,0:T(8,128)(2,1)} %get-tuple-element.78), channel_id=1, source_target_pairs={{0,4},{1,5},{2,6},{3,7},{4,0},{5,1},{6,2},{7,3},{8,12},{9,13},{10,... | collective-permute-start | bytes 786440 | tf_op jit(solution)/shard_map/ppermute | solution.py:251
  17.4 2.8 %collective-permute-done.1.refs_2_ = bf16[1,256,512]{2,1,0:T(8,128)(2,1)S(1)} collective-permute-done((bf16[1,256,512]{2,1,0:T(8,128)(2,1)}, bf16[1,256,512]{2,1,0:T(8,128)(2,1)S(1)}, u32[]{:S(2)}, u32[]{:S(2)}) %collective-permute-start.1) | collective-permute-done | bytes 262176 | tf_op jit(solution)/shard_map/ppermute | solution.py:251
  22.0 1.5 %collective-permute-start.5 = (bf16[1,256,512]{2,1,0:T(8,128)(2,1)S(1)}, bf16[1,256,512]{2,1,0:T(8,128)(2,1)S(1)}, u32[]{:S(2)}, u32[]{:S(2)}) collective-permute-start(bf16[1,256,512]{2,1,0:T(8,128)(2,1)S(1)} %get-tuple-element.81.refs_0_), channel_id=1, source_target_pairs={{0,8},{8,0},{16,24},{24,16},{1,9},{9,1},{17,25},{25,17},{2,10},{10... | collective-permute-start | bytes 786440 | tf_op jit(solution)/shard_map/ppermute | solution.py:251
  23.5 1.5 %collective-permute-start.7 = (bf16[1,256,512]{2,1,0:T(8,128)(2,1)}, bf16[1,256,512]{2,1,0:T(8,128)(2,1)S(1)}, u32[]{:S(2)}, u32[]{:S(2)}) collective-permute-start(bf16[1,256,512]{2,1,0:T(8,128)(2,1)} %get-tuple-element.89.refs_1_), channel_id=1, source_target_pairs={{0,16},{8,24},{16,0},{24,8},{1,17},{9,25},{17,1},{25,9},{2,18},{10... | collective-permute-start | bytes 786440 | tf_op jit(solution)/shard_map/ppermute | solution.py:251
  26.2 3.2 %collective-permute-done.4.refs_2_ = bf16[1,256,512]{2,1,0:T(8,128)(2,1)S(1)} collective-permute-done((bf16[1,256,512]{2,1,0:T(8,128)(2,1)}, bf16[1,256,512]{2,1,0:T(8,128)(2,1)S(1)}, u32[]{:S(2)}, u32[]{:S(2)}) %collective-permute-start.4) | collective-permute-done | bytes 262176 | tf_op jit(solution)/shard_map/ppermute | solution.py:251
  29.4 1.4 %collective-permute-done.6.refs_2_ = bf16[1,256,512]{2,1,0:T(8,128)(2,1)S(1)} collective-permute-done((bf16[1,256,512]{2,1,0:T(8,128)(2,1)S(1)}, bf16[1,256,512]{2,1,0:T(8,128)(2,1)S(1)}, u32[]{:S(2)}, u32[]{:S(2)}) %collective-permute-start.6) | collective-permute-done | bytes 262176 | tf_op jit(solution)/shard_map/ppermute | solution.py:251
  30.8 1.5 %collective-permute-start.8 = (bf16[1,256,512]{2,1,0:T(8,128)(2,1)S(1)}, bf16[1,256,512]{2,1,0:T(8,128)(2,1)S(1)}, u32[]{:S(2)}, u32[]{:S(2)}) collective-permute-start(bf16[1,256,512]{2,1,0:T(8,128)(2,1)S(1)} %get-tuple-element.87.refs_2_), channel_id=1, source_target_pairs={{0,8},{8,0},{16,24},{24,16},{1,9},{9,1},{17,25},{25,17},{2,10},{10... | collective-permute-start | bytes 786440 | tf_op jit(solution)/shard_map/ppermute | solution.py:251
  34.7 2.5 %collective-permute-done.8.refs_2_ = bf16[1,256,512]{2,1,0:T(8,128)(2,1)S(1)} collective-permute-done((bf16[1,256,512]{2,1,0:T(8,128)(2,1)S(1)}, bf16[1,256,512]{2,1,0:T(8,128)(2,1)S(1)}, u32[]{:S(2)}, u32[]{:S(2)}) %collective-permute-start.8) | collective-permute-done | bytes 262176 | tf_op jit(solution)/shard_map/ppermute | solution.py:251
  40.0 3.0 %expert_product.6 = (f32[135168,128]{1,0:T(8,128)}, bf16[384,4096]{1,0:T(8,128)(2,1)}) custom-call(s32[8]{0:T(128)S(1)} %iota_xor_fusion.1.sources, s32[4]{0:T(128)S(1)} %select_reduce_fusion.places, bf16[384,1024]{1,0:T(8,128)(2,1)S(1)} %bitcast.2, bf16[1,256,512]{2,1,0:T(8,128)(2,1)S(1)} %copy-done.2, ...), custom_call_target="tpu_custom_call", output_to_operand_aliasing={{0}: (7, {})} | custom-call | bytes 65536 | tf_op jit(solution)/shard_map/expert_product/pallas_call | solution.py:231
  42.9 2.0 %expert_product.7 = (f32[135168,128]{1,0:T(8,128)}, bf16[384,4096]{1,0:T(8,128)(2,1)}) custom-call(s32[8]{0:T(128)S(1)} %iota_xor_fusion.1.sources, s32[4]{0:T(128)S(1)} %select_reduce_fusion.places, bf16[384,1024]{1,0:T(8,128)(2,1)S(1)} %bitcast.3, ...), custom_call_target="tpu_custom_call", output_to_operand_aliasing={{0}: (7, {}), {1}: (8, {})} | custom-call | bytes 65536 | tf_op jit(solution)/shard_map/expert_product/pallas_call | solution.py:231
  44.9 5.3 %collective-permute-done.9.refs_1_ = bf16[1,256,512]{2,1,0:T(8,128)(2,1)} collective-permute-done((bf16[1,256,512]{2,1,0:T(8,128)(2,1)}, bf16[1,256,512]{2,1,0:T(8,128)(2,1)}, u32[]{:S(2)}, u32[]{:S(2)}) %collective-permute-start.9) | collective-permute-done | bytes 262176 | tf_op jit(solution)/shard_map/ppermute | solution.py:251
  51.7 1.5 %collective-permute-start.14 = (bf16[2,256,512]{2,1,0:T(8,128)(2,1)S(1)}, bf16[2,256,512]{2,1,0:T(8,128)(2,1)S(1)}, u32[]{:S(2)}, u32[]{:S(2)}) collective-permute-start(bf16[2,256,512]{2,1,0:T(8,128)(2,1)S(1)} %get-tuple-element.105.refs_0_), channel_id=1, source_target_pairs={{0,8},{8,0},{16,24},{24,16},{1,9},{9,1},{17,25},{25,17},{2,10},{10... | collective-permute-start | bytes 1572872 | tf_op jit(solution)/shard_map/ppermute | solution.py:251
  53.8 1.7 %collective-permute-start.16 = (bf16[2,256,512]{2,1,0:T(8,128)(2,1)S(1)}, bf16[2,256,512]{2,1,0:T(8,128)(2,1)S(1)}, u32[]{:S(2)}, u32[]{:S(2)}) collective-permute-start(bf16[2,256,512]{2,1,0:T(8,128)(2,1)S(1)} %get-tuple-element.101.refs_1_), channel_id=1, source_target_pairs={{0,16},{8,24},{16,0},{24,8},{1,17},{9,25},{17,1},{25,9},{2,18},{10... | collective-permute-start | bytes 1572872 | tf_op jit(solution)/shard_map/ppermute | solution.py:251
  55.5 10.9 %collective-permute-done.13.refs_1_ = bf16[1,256,512]{2,1,0:T(8,128)(2,1)S(1)} collective-permute-done((bf16[1,256,512]{2,1,0:T(8,128)(2,1)S(1)}, bf16[1,256,512]{2,1,0:T(8,128)(2,1)S(1)}, u32[]{:S(2)}, u32[]{:S(2)}) %collective-permute-start.13) | collective-permute-done | bytes 262176 | tf_op jit(solution)/shard_map/ppermute | solution.py:251
  70.2 7.1 %collective-permute-done.16.refs_1_ = bf16[2,256,512]{2,1,0:T(8,128)(2,1)S(1)} collective-permute-done((bf16[2,256,512]{2,1,0:T(8,128)(2,1)S(1)}, bf16[2,256,512]{2,1,0:T(8,128)(2,1)S(1)}, u32[]{:S(2)}, u32[]{:S(2)}) %collective-permute-start.16) | collective-permute-done | bytes 524320 | tf_op jit(solution)/shard_map/ppermute | solution.py:251
  77.4 4.1 %expert_product.8 = (f32[135168,128]{1,0:T(8,128)}, bf16[384,4096]{1,0:T(8,128)(2,1)}) custom-call(s32[8]{0:T(128)S(1)} %iota_xor_fusion.1.sources, s32[4]{0:T(128)S(1)} %select_reduce_fusion.places, bf16[384,1024]{1,0:T(8,128)(2,1)S(1)} %bitcast.4, bf16[2,256,512]{2,1,0:T(8,128)(2,1)} %get-tuple-element.85.refs_0_, ...), custom_call_target="tpu_custom_call", output_to_operand_aliasing={{0}: (7, {}), {1}: (8, {})} | custom-call | bytes 65536 | tf_op jit(solution)/shard_map/expert_product/pallas_call | solution.py:231
  83.9 3.1 %expert_product.9 = (f32[135168,128]{1,0:T(8,128)}, bf16[384,4096]{1,0:T(8,128)(2,1)}) custom-call(s32[8]{0:T(128)S(1)} %iota_xor_fusion.1.sources, s32[4]{0:T(128)S(1)} %select_reduce_fusion.places, bf16[384,1024]{1,0:T(8,128)(2,1)S(1)} %bitcast.5, ...), custom_call_target="tpu_custom_call", output_to_operand_aliasing={{0}: (7, {}), {1}: (8, {})} | custom-call | bytes 65536 | tf_op jit(solution)/shard_map/expert_product/pallas_call | solution.py:231
  88.2 2.8 %collective-permute-done.22.refs_2_ = bf16[1,256,512]{2,1,0:T(8,128)(2,1)S(1)} collective-permute-done((bf16[1,256,512]{2,1,0:T(8,128)(2,1)S(1)}, bf16[1,256,512]{2,1,0:T(8,128)(2,1)S(1)}, u32[]{:S(2)}, u32[]{:S(2)}) %collective-permute-start.22) | collective-permute-done | bytes 262176 | tf_op jit(solution)/shard_map/ppermute | solution.py:251
  91.5 4.3 %collective-permute-done.23.refs_1_ = bf16[1,256,512]{2,1,0:T(8,128)(2,1)S(1)} collective-permute-done((bf16[1,256,512]{2,1,0:T(8,128)(2,1)S(1)}, bf16[1,256,512]{2,1,0:T(8,128)(2,1)S(1)}, u32[]{:S(2)}, u32[]{:S(2)}) %collective-permute-start.23) | collective-permute-done | bytes 262176 | tf_op jit(solution)/shard_map/ppermute | solution.py:251
  95.8 2.0 %expert_product.10 = (f32[135168,128]{1,0:T(8,128)}, bf16[384,4096]{1,0:T(8,128)(2,1)}) custom-call(s32[8]{0:T(128)S(1)} %iota_xor_fusion.1.sources, s32[4]{0:T(128)S(1)} %select_reduce_fusion.places, bf16[384,1024]{1,0:T(8,128)(2,1)S(1)} %bitcast.6, ...), custom_call_target="tpu_custom_call", output_to_operand_aliasing={{0}: (7, {}), {1}: (8, {})} | custom-call | bytes 65536 | tf_op jit(solution)/shard_map/expert_product/pallas_call | solution.py:231
  98.7 2.0 %expert_product.11 = (f32[135168,128]{1,0:T(8,128)}, bf16[384,4096]{1,0:T(8,128)(2,1)}) custom-call(s32[8]{0:T(128)S(1)} %iota_xor_fusion.1.sources, s32[4]{0:T(128)S(1)} %select_reduce_fusion.places, bf16[384,1024]{1,0:T(8,128)(2,1)S(1)} %bitcast.7, ...), custom_call_target="tpu_custom_call", output_to_operand_aliasing={{0}: (7, {}), {1}: (8, {})} | custom-call | bytes 65536 | tf_op jit(solution)/shard_map/expert_product/pallas_call | solution.py:231
  (65 shorter events, 19.6 us)
Async XLA Ops:
  11.2 8.9 %collective-permute-start.1 = (bf16[1,256,512]{2,1,0:T(8,128)(2,1)}, bf16[1,256,512]{2,1,0:T(8,128)(2,1)S(1)}, u32[]{:S(2)}, u32[]{:S(2)}) collective-permute-start(bf16[1,256,512]{2,1,0:T(8,128)(2,1)} %get-tuple-element.74.refs_0_), channel_id=1, source_target_pairs={{0,16},{8,24},{16,0},{24,8},{1,17},{9,25},{17,1},{25,9},{2,18},{10... | collective-permute-start | bytes 786440 | tf_op jit(solution)/shard_map/ppermute | solution.py:251
  12.8 8.7 %collective-permute-start = (bf16[1,256,512]{2,1,0:T(8,128)(2,1)}, bf16[1,256,512]{2,1,0:T(8,128)(2,1)}, u32[]{:S(2)}, u32[]{:S(2)}) collective-permute-start(bf16[1,256,512]{2,1,0:T(8,128)(2,1)} %get-tuple-element.74.refs_0_), channel_id=1, source_target_pairs={{0,8},{8,0},{16,24},{24,16},{1,9},{9,1},{17,25},{25,17},{2,10},{10... | collective-permute-start | bytes 786440 | tf_op jit(solution)/shard_map/ppermute | solution.py:251
  14.3 11.9 %collective-permute-start.3 = (bf16[1,256,512]{2,1,0:T(8,128)(2,1)}, bf16[1,256,512]{2,1,0:T(8,128)(2,1)S(1)}, u32[]{:S(2)}, u32[]{:S(2)}) collective-permute-start(bf16[1,256,512]{2,1,0:T(8,128)(2,1)} %get-tuple-element.77), channel_id=1, source_target_pairs={{0,2},{1,3},{2,0},{3,1},{4,6},{5,7},{6,4},{7,5},{8,10},{9,11},{10,... | collective-permute-start | bytes 786440 | tf_op jit(solution)/shard_map/ppermute | solution.py:251
  14.8 14.6 %collective-permute-start.4 = (bf16[1,256,512]{2,1,0:T(8,128)(2,1)}, bf16[1,256,512]{2,1,0:T(8,128)(2,1)S(1)}, u32[]{:S(2)}, u32[]{:S(2)}) collective-permute-start(bf16[1,256,512]{2,1,0:T(8,128)(2,1)} %get-tuple-element.78), channel_id=1, source_target_pairs={{0,4},{1,5},{2,6},{3,7},{4,0},{5,1},{6,2},{7,3},{8,12},{9,13},{10,... | collective-permute-start | bytes 786440 | tf_op jit(solution)/shard_map/ppermute | solution.py:251
  21.5 9.2 %collective-permute-start.6 = (bf16[1,256,512]{2,1,0:T(8,128)(2,1)S(1)}, bf16[1,256,512]{2,1,0:T(8,128)(2,1)S(1)}, u32[]{:S(2)}, u32[]{:S(2)}) collective-permute-start(bf16[1,256,512]{2,1,0:T(8,128)(2,1)S(1)} %get-tuple-element.81.refs_0_), channel_id=1, source_target_pairs={{0,16},{8,24},{16,0},{24,8},{1,17},{9,25},{17,1},{25,9},{2,18},{10... | collective-permute-start | bytes 786440 | tf_op jit(solution)/shard_map/ppermute | solution.py:251
  22.0 8.7 %collective-permute-start.5 = (bf16[1,256,512]{2,1,0:T(8,128)(2,1)S(1)}, bf16[1,256,512]{2,1,0:T(8,128)(2,1)S(1)}, u32[]{:S(2)}, u32[]{:S(2)}) collective-permute-start(bf16[1,256,512]{2,1,0:T(8,128)(2,1)S(1)} %get-tuple-element.81.refs_0_), channel_id=1, source_target_pairs={{0,8},{8,0},{16,24},{24,16},{1,9},{9,1},{17,25},{25,17},{2,10},{10... | collective-permute-start | bytes 786440 | tf_op jit(solution)/shard_map/ppermute | solution.py:251
  23.5 11.2 %collective-permute-start.7 = (bf16[1,256,512]{2,1,0:T(8,128)(2,1)}, bf16[1,256,512]{2,1,0:T(8,128)(2,1)S(1)}, u32[]{:S(2)}, u32[]{:S(2)}) collective-permute-start(bf16[1,256,512]{2,1,0:T(8,128)(2,1)} %get-tuple-element.89.refs_1_), channel_id=1, source_target_pairs={{0,16},{8,24},{16,0},{24,8},{1,17},{9,25},{17,1},{25,9},{2,18},{10... | collective-permute-start | bytes 786440 | tf_op jit(solution)/shard_map/ppermute | solution.py:251
  30.8 6.4 %collective-permute-start.8 = (bf16[1,256,512]{2,1,0:T(8,128)(2,1)S(1)}, bf16[1,256,512]{2,1,0:T(8,128)(2,1)S(1)}, u32[]{:S(2)}, u32[]{:S(2)}) collective-permute-start(bf16[1,256,512]{2,1,0:T(8,128)(2,1)S(1)} %get-tuple-element.87.refs_2_), channel_id=1, source_target_pairs={{0,8},{8,0},{16,24},{24,16},{1,9},{9,1},{17,25},{25,17},{2,10},{10... | collective-permute-start | bytes 786440 | tf_op jit(solution)/shard_map/ppermute | solution.py:251
  32.3 12.7 %collective-permute-start.10 = (bf16[1,256,512]{2,1,0:T(8,128)(2,1)}, bf16[1,256,512]{2,1,0:T(8,128)(2,1)}, u32[]{:S(2)}, u32[]{:S(2)}) collective-permute-start(bf16[1,256,512]{2,1,0:T(8,128)(2,1)} %get-tuple-element.99), channel_id=1, source_target_pairs={{0,5},{1,4},{2,7},{3,6},{4,1},{5,0},{6,3},{7,2},{8,13},{9,12},{10,... | collective-permute-start | bytes 786440 | tf_op jit(solution)/shard_map/ppermute | solution.py:251
  33.1 20.7 %collective-permute-start.12 = (bf16[2,256,512]{2,1,0:T(8,128)(2,1)}, bf16[2,256,512]{2,1,0:T(8,128)(2,1)S(1)}, u32[]{:S(2)}, u32[]{:S(2)}) collective-permute-start(bf16[2,256,512]{2,1,0:T(8,128)(2,1)} %get-tuple-element.85.refs_0_), channel_id=1, source_target_pairs={{0,16},{8,24},{16,0},{24,8},{1,17},{9,25},{17,1},{25,9},{2,18},{10... | collective-permute-start | bytes 1572872 | tf_op jit(solution)/shard_map/ppermute | solution.py:251
  33.7 20.1 %collective-permute-start.11 = (bf16[2,256,512]{2,1,0:T(8,128)(2,1)}, bf16[2,256,512]{2,1,0:T(8,128)(2,1)S(1)}, u32[]{:S(2)}, u32[]{:S(2)}) collective-permute-start(bf16[2,256,512]{2,1,0:T(8,128)(2,1)} %get-tuple-element.85.refs_0_), channel_id=1, source_target_pairs={{0,8},{8,0},{16,24},{24,16},{1,9},{9,1},{17,25},{25,17},{2,10},{10... | collective-permute-start | bytes 1572872 | tf_op jit(solution)/shard_map/ppermute | solution.py:251
  38.8 11.4 %collective-permute-start.9 = (bf16[1,256,512]{2,1,0:T(8,128)(2,1)}, bf16[1,256,512]{2,1,0:T(8,128)(2,1)}, u32[]{:S(2)}, u32[]{:S(2)}) collective-permute-start(bf16[1,256,512]{2,1,0:T(8,128)(2,1)} %copy-done.4), channel_id=1, source_target_pairs={{0,3},{1,2},{2,1},{3,0},{4,7},{5,6},{6,5},{7,4},{8,11},{9,10},{10,... | collective-permute-start | bytes 786440 | tf_op jit(solution)/shard_map/ppermute | solution.py:251
  51.3 15.2 %collective-permute-start.15 = (bf16[2,256,512]{2,1,0:T(8,128)(2,1)S(1)}, bf16[2,256,512]{2,1,0:T(8,128)(2,1)S(1)}, u32[]{:S(2)}, u32[]{:S(2)}) collective-permute-start(bf16[2,256,512]{2,1,0:T(8,128)(2,1)S(1)} %get-tuple-element.105.refs_0_), channel_id=1, source_target_pairs={{0,16},{8,24},{16,0},{24,8},{1,17},{9,25},{17,1},{25,9},{2,18},{10... | collective-permute-start | bytes 1572872 | tf_op jit(solution)/shard_map/ppermute | solution.py:251
  51.7 14.8 %collective-permute-start.14 = (bf16[2,256,512]{2,1,0:T(8,128)(2,1)S(1)}, bf16[2,256,512]{2,1,0:T(8,128)(2,1)S(1)}, u32[]{:S(2)}, u32[]{:S(2)}) collective-permute-start(bf16[2,256,512]{2,1,0:T(8,128)(2,1)S(1)} %get-tuple-element.105.refs_0_), channel_id=1, source_target_pairs={{0,8},{8,0},{16,24},{24,16},{1,9},{9,1},{17,25},{25,17},{2,10},{10... | collective-permute-start | bytes 1572872 | tf_op jit(solution)/shard_map/ppermute | solution.py:251
  53.1 13.3 %collective-permute-start.13 = (bf16[1,256,512]{2,1,0:T(8,128)(2,1)S(1)}, bf16[1,256,512]{2,1,0:T(8,128)(2,1)S(1)}, u32[]{:S(2)}, u32[]{:S(2)}) collective-permute-start(bf16[1,256,512]{2,1,0:T(8,128)(2,1)S(1)} %copy-done.5), channel_id=1, source_target_pairs={{0,6},{1,7},{2,4},{3,5},{4,2},{5,3},{6,0},{7,1},{8,14},{9,15},{10,... | collective-permute-start | bytes 786440 | tf_op jit(solution)/shard_map/ppermute | solution.py:251
  53.8 23.6 %collective-permute-start.16 = (bf16[2,256,512]{2,1,0:T(8,128)(2,1)S(1)}, bf16[2,256,512]{2,1,0:T(8,128)(2,1)S(1)}, u32[]{:S(2)}, u32[]{:S(2)}) collective-permute-start(bf16[2,256,512]{2,1,0:T(8,128)(2,1)S(1)} %get-tuple-element.101.refs_1_), channel_id=1, source_target_pairs={{0,16},{8,24},{16,0},{24,8},{1,17},{9,25},{17,1},{25,9},{2,18},{10... | collective-permute-start | bytes 1572872 | tf_op jit(solution)/shard_map/ppermute | solution.py:251
  66.5 17.4 %collective-permute-start.18 = (bf16[2,256,512]{2,1,0:T(8,128)(2,1)S(1)}, bf16[2,256,512]{2,1,0:T(8,128)(2,1)S(1)}, u32[]{:S(2)}, u32[]{:S(2)}) collective-permute-start(bf16[2,256,512]{2,1,0:T(8,128)(2,1)S(1)} %get-tuple-element.115.refs_2_), channel_id=1, source_target_pairs={{0,8},{8,0},{16,24},{24,16},{1,9},{9,1},{17,25},{25,17},{2,10},{10... | collective-permute-start | bytes 1572872 | tf_op jit(solution)/shard_map/ppermute | solution.py:251
  67.6 14.2 %collective-permute-start.17 = (bf16[1,256,512]{2,1,0:T(8,128)(2,1)S(1)}, bf16[1,256,512]{2,1,0:T(8,128)(2,1)S(1)}, u32[]{:S(2)}, u32[]{:S(2)}) collective-permute-start(bf16[1,256,512]{2,1,0:T(8,128)(2,1)S(1)} %get-tuple-element.112), channel_id=1, source_target_pairs={{0,7},{1,6},{2,5},{3,4},{4,3},{5,2},{6,1},{7,0},{8,15},{9,14},{10,... | collective-permute-start | bytes 786440 | tf_op jit(solution)/shard_map/ppermute | solution.py:251
  67.6 19.3 %collective-permute-start.20 = (bf16[1,256,512]{2,1,0:T(8,128)(2,1)S(1)}, bf16[1,256,512]{2,1,0:T(8,128)(2,1)S(1)}, u32[]{:S(2)}, u32[]{:S(2)}) collective-permute-start(bf16[1,256,512]{2,1,0:T(8,128)(2,1)S(1)} %get-tuple-element.121.refs_0_), channel_id=1, source_target_pairs={{0,16},{8,24},{16,0},{24,8},{1,17},{9,25},{17,1},{25,9},{2,18},{10... | collective-permute-start | bytes 786440 | tf_op jit(solution)/shard_map/ppermute | solution.py:251
  68.9 18.1 %collective-permute-start.19 = (bf16[1,256,512]{2,1,0:T(8,128)(2,1)S(1)}, bf16[1,256,512]{2,1,0:T(8,128)(2,1)S(1)}, u32[]{:S(2)}, u32[]{:S(2)}) collective-permute-start(bf16[1,256,512]{2,1,0:T(8,128)(2,1)S(1)} %get-tuple-element.121.refs_0_), channel_id=1, source_target_pairs={{0,8},{8,0},{16,24},{24,16},{1,9},{9,1},{17,25},{25,17},{2,10},{10... | collective-permute-start | bytes 786440 | tf_op jit(solution)/shard_map/ppermute | solution.py:251
  81.8 9.2 %collective-permute-start.22 = (bf16[1,256,512]{2,1,0:T(8,128)(2,1)S(1)}, bf16[1,256,512]{2,1,0:T(8,128)(2,1)S(1)}, u32[]{:S(2)}, u32[]{:S(2)}) collective-permute-start(bf16[1,256,512]{2,1,0:T(8,128)(2,1)S(1)} %get-tuple-element.113.refs_0_), channel_id=1, source_target_pairs={{0,16},{8,24},{16,0},{24,8},{1,17},{9,25},{17,1},{25,9},{2,18},{10... | collective-permute-start | bytes 786440 | tf_op jit(solution)/shard_map/ppermute | solution.py:251
  82.8 8.4 %collective-permute-start.21 = (bf16[1,256,512]{2,1,0:T(8,128)(2,1)S(1)}, bf16[1,256,512]{2,1,0:T(8,128)(2,1)S(1)}, u32[]{:S(2)}, u32[]{:S(2)}) collective-permute-start(bf16[1,256,512]{2,1,0:T(8,128)(2,1)S(1)} %get-tuple-element.113.refs_0_), channel_id=1, source_target_pairs={{0,8},{8,0},{16,24},{24,16},{1,9},{9,1},{17,25},{25,17},{2,10},{10... | collective-permute-start | bytes 786440 | tf_op jit(solution)/shard_map/ppermute | solution.py:251
  87.0 8.8 %collective-permute-start.23 = (bf16[1,256,512]{2,1,0:T(8,128)(2,1)S(1)}, bf16[1,256,512]{2,1,0:T(8,128)(2,1)S(1)}, u32[]{:S(2)}, u32[]{:S(2)}) collective-permute-start(bf16[1,256,512]{2,1,0:T(8,128)(2,1)S(1)} %get-tuple-element.125.refs_1_), channel_id=1, source_target_pairs={{0,16},{8,24},{16,0},{24,8},{1,17},{9,25},{17,1},{25,9},{2,18},{10... | collective-permute-start | bytes 786440 | tf_op jit(solution)/shard_map/ppermute | solution.py:251
  91.1 7.5 %collective-permute-start.24 = (bf16[1,256,512]{2,1,0:T(8,128)(2,1)S(1)}, bf16[1,256,512]{2,1,0:T(8,128)(2,1)S(1)}, u32[]{:S(2)}, u32[]{:S(2)}) collective-permute-start(bf16[1,256,512]{2,1,0:T(8,128)(2,1)S(1)} %get-tuple-element.124.refs_2_), channel_id=1, source_target_pairs={{0,8},{8,0},{16,24},{24,16},{1,9},{9,1},{17,25},{25,17},{2,10},{10... | collective-permute-start | bytes 786440 | tf_op jit(solution)/shard_map/ppermute | solution.py:251
  (8 other events, 48.6 us)

commit v11 on v10

--- a/solution.py
+++ b/solution.py
@@ -12,6 +12,7 @@
 QB = 128
 GROUP = 32
 VMEM_LIMIT = 60 * 1024 * 1024
+LATER_LIMIT = 56 * 1024 * 1024
 PRODUCT_LIMIT = 16 * 1024 * 1024
 
 beta_one = 0.9
@@ -33,6 +34,9 @@
 SMALL_COST = pl.CostEstimate(flops=0, bytes_accessed=65536, transcendentals=0)
 
 
+PAIR_COST = pl.CostEstimate(flops=0, bytes_accessed=16 * 1024 * 1024, transcendentals=0)
+
+
 def like(array):
     return jax.ShapeDtypeStruct(array.shape, array.dtype)
 
@@ -57,7 +61,8 @@
 def adam_kernel(groups, passed, owner, *refs):
     arrays, outs = refs[:4], refs[4 + passed : 7 + passed]
     sends = refs[7 + passed : 7 + passed + len(groups)]
-    base, blocks = groups[0][0], sum(map(len, groups))
+    order = [number for group in groups for number in group]
+    blocks = len(order)
     *buffers, semaphores = refs[-9:]
     master, gradient, first, second, new_master, new_first, new_second, sent = buffers
     experts, rows, columns = arrays[0].shape
@@ -67,9 +72,11 @@
 
     def copies(chunk, inward):
         n, i = chunk // bands, chunk % bands
-        expert = jnp.int32(0)
+        number, expert = jnp.int32(order[0]), jnp.int32(0)
+        for position in range(1, blocks):
+            number = jnp.where(n == position, order[position], number)
         for candidate in range(experts):
-            expert = jnp.where(owner[candidate] == shard ^ (base + n), candidate, expert)
+            expert = jnp.where(owner[candidate] == shard ^ number, candidate, expert)
         span = pl.ds(pl.multiple_of(i * QB, QB), QB)
         for k, ref in enumerate(arrays if inward else outs):
             far, near = ref.at[expert, span], buffers[k if inward else 4 + k].at[n, span]
@@ -78,7 +85,7 @@
 
     def send_copy(chunk, group, member):
         span = pl.ds(pl.multiple_of(chunk % bands * QB, QB), QB)
-        n = groups[group][member] - base
+        n = order.index(groups[group][member])
         far = sends[group].at[member, span]
         return pltpu.make_async_copy(sent.at[n, span], far, semaphores.at[chunk, 7])
 
@@ -137,7 +144,7 @@
         for group, numbers in enumerate(groups):
             for member, number in enumerate(numbers):
 
-                @pl.when(n == number - base)
+                @pl.when(n == order.index(number))
                 def _():
                     send_copy(chunk, group, member).start()
 
@@ -153,11 +160,14 @@
         lax.fori_loop(0, blocks * bands, part, 0)
 
 
-def adam_blocks(groups, owner, arrays, carried, fenced):
+def adam_blocks(groups, owner, arrays, carried, token, fenced, limit):
     _, rows, columns = arrays[0].shape
-    blocks, passed = sum(map(len, groups)), len(carried)
+    blocks, passed = sum(map(len, groups)), len(carried) + len(token)
     made = [like(arrays[0]), like(arrays[2]), like(arrays[3])]
     made += [jax.ShapeDtypeStruct((len(group), rows, columns), jnp.bfloat16) for group in groups]
+    aliases = {5 + i: i for i in range(len(carried))}
+    if token:
+        aliases[5 + len(carried)] = len(made)
     made += [jax.ShapeDtypeStruct(TOKEN, jnp.float32)] * fenced
     kinds = [jnp.float32, jnp.bfloat16, jnp.bfloat16, jnp.bfloat16] * 2
     results = pl.pallas_call(
@@ -167,11 +177,11 @@
         out_shape=made,
         scratch_shapes=[pltpu.VMEM((blocks, rows, columns), kind) for kind in kinds]
         + [pltpu.SemaphoreType.DMA((blocks * (rows // QB), 8))],
-        input_output_aliases={5 + i: i for i in range(passed)},
-        compiler_params=pltpu.CompilerParams(vmem_limit_bytes=VMEM_LIMIT),
+        input_output_aliases=aliases,
+        compiler_params=pltpu.CompilerParams(vmem_limit_bytes=limit),
         cost_estimate=SMALL_COST,
         name="adam_quantize",
-    )(owner, *arrays, *carried)
+    )(owner, *arrays, *carried, *token)
     return results[:3], results[3 : 3 + len(groups)], tuple(results[3 + len(groups) :])
 
 
@@ -241,7 +251,7 @@
             + [jax.ShapeDtypeStruct((tokens, breadth), jnp.bfloat16)],
         input_output_aliases={3 + slabs + i: i for i in range(passed)},
         compiler_params=pltpu.CompilerParams(vmem_limit_bytes=PRODUCT_LIMIT),
-        cost_estimate=SMALL_COST,
+        cost_estimate=SMALL_COST if blocks == 1 else PAIR_COST,
         name="expert_product",
     )(sources, places, token_rows, *weights, *token, *carried)
     return (out,), tuple(token)
@@ -268,9 +278,9 @@
     held, made, ready = collections.defaultdict(dict), {}, set()
     state = {"adam": (), "token": (), "out": ()}
 
-    def adam(*groups):
+    def adam(groups, limit=VMEM_LIMIT):
         state["adam"], sends, state["token"] = adam_blocks(
-            groups, owner_of_expert, arrays, tuple(state["adam"]), fenced
+            groups, owner_of_expert, arrays, tuple(state["adam"]), state["token"], fenced, limit
         )
         made.update({group[0]: send for group, send in zip(groups, sends)})
 
@@ -299,16 +309,17 @@
     if fenced:
         one, two = (2, 4), (3, 5)
         plan = [
-            ([(0, 1), (0, 2), (1, 0)], [(1, 0, 1), (1, 0, 2)], []),
-            ([(2, 0), (4, 0)], [], [5]),
-            ([(1, 1), (1, 2)], [(1, 2, 1), (0, 1, 2)], []),
+            ([(0, 1), (0, 2), (1, 0)], [(1, 0, 1), (1, 0, 2), (0, 1, 2)], []),
+            ([(2, 0), (4, 0)], [], [3, 5]),
+            ([(1, 1), (1, 2), (0, 3)], [(1, 2, 1)], []),
             (one, [(one, 0, 1), (one, 0, 2)], []),
-            ([(0, 3), (1, 3)], [], [3]),
+            ([(1, 3)], [], []),
             (two, [(two, 0, 1), (two, 0, 2)], [6]),
             ([(one, 1), (one, 2)], [(one, 1, 2)], []),
-            ([(6, 0), (two, 1), (two, 2)], [(two, 2, 1), (6, 0, 1), (6, 0, 2)], [7]),
+            ([(6, 0)], [], [7]),
+            ([(two, 1), (two, 2)], [(two, 2, 1), (6, 0, 1), (6, 0, 2)], []),
+            ([(7, 0)], [(7, 0, 1), (7, 0, 2)], []),
             ([(one, 3)], [], []),
-            ([(7, 0)], [(7, 0, 1), (7, 0, 2)], []),
             ([(two, 3)], [], []),
             ([(6, 1), (6, 2)], [(6, 1, 2)], []),
             ([(7, 1), (7, 2)], [(7, 2, 1)], []),
@@ -316,12 +327,13 @@
             ([(7, 3)], [], []),
         ]
         waiting = [0, 1, one, two, 6, 7]
-        adam(*[(block,) for block in range(shards)])
+        adam(((0,), (1,), (2,), (4,)))
         for block in (0, 1, 2, 4):
             deliver(block)
         ready.add((0, 0))
         send(0, 0, 1)
         send(0, 0, 2)
+        adam(((3,), (5,), (6,), (7,)), LATER_LIMIT)
         for keys, sending, leaving in plan:
             if isinstance(keys, tuple):
                 pieces = [held[block][0] for block in keys]
@@ -334,13 +346,13 @@
                 deliver(block)
             for key in sending:
                 send(*key)
-            for block in list(waiting):
+            for block in [] if sending or leaving else list(waiting):
                 if all((block, member) in ready for member in range(replicas)):
                     multiply(block)
                     waiting.remove(block)
     else:
         for pair in range(0, shards, 2):
-            adam((pair,), (pair + 1,))
+            adam(((pair,), (pair + 1,)))
         for block in range(shards):
             deliver(block)
             for number in range(len(bits)):

time: 103 us -> 111 us (1.078); the launches traced: 101 us -> 110 us
  waiting for transfers between devices: 44.7 us -> 54.9 us
  local copies, waits for them, and re-layouts: 2.6 us -> 0.02 us
  Pallas kernels: 28.6 us -> 31.1 us
    ppermute x25, waiting for transfers between devices: 44.7 us -> 54.9 us  [swap(): return lax.ppermute(value, axis, [(i, i ^ mask) for i in range(size)])]
    unnamed x14 -> x10, local copies, waits for them, and re-layouts: 2.6 us -> 0.02 us
    pallas_call x1 -> x2, Pallas kernels: 10.5 us -> 13 us  [adam_blocks(): pl.pallas_call(functools.partial(adam_kernel, groups, passed), in_specs=[...]
  transfers between devices with their start and end apart: 25 -> 25, of which waited for: 15 -> 10; matrix products, arithmetic and copies ran while one was open for 0% -> 0% of each run, Pallas kernels for 16% -> 20%
where the time goes in v11:
time: 111 us; the launch traced here: 110 us
  waiting for transfers between devices  54.9 us (49%)
  Pallas kernels  31.1 us (28%)
  starting transfers between devices  23.6 us (21%)
    ppermute x25, waiting for transfers between devices, swap(): return lax.ppermute(value, axis, [(i, i ^ mask) for i in range(size)])  54.9 us
    ppermute x25, starting transfers between devices, swap(): return lax.ppermute(value, axis, [(i, i ^ mask) for i in range(size)])  23.6 us
    pallas_call x6, Pallas kernels, product(): pl.pallas_call(functools.partial(product_kernel, slabs), grid_spec=pltpu....  16.2 us
    pallas_call x2, Pallas kernels, adam_blocks(): pl.pallas_call(functools.partial(adam_kernel, groups, passed), in_specs=[...  13 us
  transfers between devices with their start and end apart: 25, of which 10 were waited for; matrix products, arithmetic and copies ran while one was open for 0% of the time, Pallas kernels for 20%

profile of v11, /device:TPU:8, one launch (start us, length us, event | category | flops | bytes accessed | tf_op | source)
XLA Modules:
  0.0 110.5 jit_solution(10157441867068902311)
XLA Ops:
  0.6 6.5 %adam_quantize.2 = (f32[8,256,512]{2,1,0:T(8,128)}, bf16[8,256,512]{2,1,0:T(8,128)(2,1)}, bf16[8,256,512]{2,1,0:T(8,128)(2,1)}, bf16[1,256,512]{2,1,0:T(8,128)(2...) custom-call(s32[8]{0:T(128)} %owner.3, ...), custom_call_target="tpu_custom_call" | custom-call | bytes 65536 | tf_op jit(solution)/shard_map/adam_quantize/pallas_call | solution.py:173
  7.1 1.6 %collective-permute-start = (bf16[1,256,512]{2,1,0:T(8,128)(2,1)}, bf16[1,256,512]{2,1,0:T(8,128)(2,1)S(1)}, u32[]{:S(2)}, u32[]{:S(2)}) collective-permute-start(bf16[1,256,512]{2,1,0:T(8,128)(2,1)} %get-tuple-element.83.refs_0_), channel_id=1, source_target_pairs={{0,8},{8,0},{16,24},{24,16},{1,9},{9,1},{17,25},{25,17},{2,10},{10... | collective-permute-start | bytes 786440 | tf_op jit(solution)/shard_map/ppermute | solution.py:261
  8.7 1.5 %collective-permute-start.1 = (bf16[1,256,512]{2,1,0:T(8,128)(2,1)}, bf16[1,256,512]{2,1,0:T(8,128)(2,1)S(1)}, u32[]{:S(2)}, u32[]{:S(2)}) collective-permute-start(bf16[1,256,512]{2,1,0:T(8,128)(2,1)} %get-tuple-element.83.refs_0_), channel_id=1, source_target_pairs={{0,16},{8,24},{16,0},{24,8},{1,17},{9,25},{17,1},{25,9},{2,18},{10... | collective-permute-start | bytes 786440 | tf_op jit(solution)/shard_map/ppermute | solution.py:261
  10.7 2.6 %collective-permute-start.4 = (bf16[1,256,512]{2,1,0:T(8,128)(2,1)}, bf16[1,256,512]{2,1,0:T(8,128)(2,1)S(1)}, u32[]{:S(2)}, u32[]{:S(2)}) collective-permute-start(bf16[1,256,512]{2,1,0:T(8,128)(2,1)} %get-tuple-element.88), channel_id=1, source_target_pairs={{0,4},{1,5},{2,6},{3,7},{4,0},{5,1},{6,2},{7,3},{8,12},{9,13},{10,... | collective-permute-start | bytes 786440 | tf_op jit(solution)/shard_map/ppermute | solution.py:261
  13.3 6.5 %adam_quantize.3 = (f32[8,256,512]{2,1,0:T(8,128)}, bf16[8,256,512]{2,1,0:T(8,128)(2,1)}, bf16[8,256,512]{2,1,0:T(8,128)(2,1)}, bf16[1,256,512]{2,1,0:T(8,128)(2...) custom-call(s32[8]{0:T(128)} %owner.3, ...), custom_call_target="tpu_custom_call", output_to_operand_aliasing={{0}: (5, {}), {1}: (6, {}), {2}: (7, {}), {7}: (8, {})} | custom-call | bytes 65536 | tf_op jit(solution)/shard_map/adam_quantize/pallas_call | solution.py:173
  20.9 1.5 %collective-permute-start.7 = (bf16[1,256,512]{2,1,0:T(8,128)(2,1)S(1)}, bf16[1,256,512]{2,1,0:T(8,128)(2,1)S(1)}, u32[]{:S(2)}, u32[]{:S(2)}) collective-permute-start(bf16[1,256,512]{2,1,0:T(8,128)(2,1)S(1)} %get-tuple-element.92.refs_1_), channel_id=1, source_target_pairs={{0,16},{8,24},{16,0},{24,8},{1,17},{9,25},{17,1},{25,9},{2,18},{10... | collective-permute-start | bytes 786440 | tf_op jit(solution)/shard_map/ppermute | solution.py:261
  22.7 3.2 %collective-permute-done.4.refs_2_ = bf16[1,256,512]{2,1,0:T(8,128)(2,1)S(1)} collective-permute-done((bf16[1,256,512]{2,1,0:T(8,128)(2,1)}, bf16[1,256,512]{2,1,0:T(8,128)(2,1)S(1)}, u32[]{:S(2)}, u32[]{:S(2)}) %collective-permute-start.4) | collective-permute-done | bytes 262176 | tf_op jit(solution)/shard_map/ppermute | solution.py:261
  25.9 1.6 %collective-permute-start.10 = (bf16[1,256,512]{2,1,0:T(8,128)(2,1)}, bf16[1,256,512]{2,1,0:T(8,128)(2,1)}, u32[]{:S(2)}, u32[]{:S(2)}) collective-permute-start(bf16[1,256,512]{2,1,0:T(8,128)(2,1)} %get-tuple-element.107), channel_id=1, source_target_pairs={{0,5},{1,4},{2,7},{3,6},{4,1},{5,0},{6,3},{7,2},{8,13},{9,12},{10,... | collective-permute-start | bytes 786440 | tf_op jit(solution)/shard_map/ppermute | solution.py:261
  28.0 1.6 %collective-permute-done.6.refs_2_ = bf16[1,256,512]{2,1,0:T(8,128)(2,1)S(1)} collective-permute-done((bf16[1,256,512]{2,1,0:T(8,128)(2,1)S(1)}, bf16[1,256,512]{2,1,0:T(8,128)(2,1)S(1)}, u32[]{:S(2)}, u32[]{:S(2)}) %collective-permute-start.6) | collective-permute-done | bytes 262176 | tf_op jit(solution)/shard_map/ppermute | solution.py:261
  29.6 4.3 %collective-permute-done.7.refs_3_ = bf16[1,256,512]{2,1,0:T(8,128)(2,1)S(1)} collective-permute-done((bf16[1,256,512]{2,1,0:T(8,128)(2,1)S(1)}, bf16[1,256,512]{2,1,0:T(8,128)(2,1)S(1)}, u32[]{:S(2)}, u32[]{:S(2)}) %collective-permute-start.7) | collective-permute-done | bytes 262176 | tf_op jit(solution)/shard_map/ppermute | solution.py:261
  34.7 1.6 %collective-permute-start.11 = (bf16[2,256,512]{2,1,0:T(8,128)(2,1)}, bf16[2,256,512]{2,1,0:T(8,128)(2,1)S(1)}, u32[]{:S(2)}, u32[]{:S(2)}) collective-permute-start(bf16[2,256,512]{2,1,0:T(8,128)(2,1)} %get-tuple-element.109.refs_0_), channel_id=1, source_target_pairs={{0,8},{8,0},{16,24},{24,16},{1,9},{9,1},{17,25},{25,17},{2,10},{10... | collective-permute-start | bytes 1572872 | tf_op jit(solution)/shard_map/ppermute | solution.py:261
  37.5 15.9 %collective-permute-done.8.refs_1_ = bf16[1,256,512]{2,1,0:T(8,128)(2,1)} collective-permute-done((bf16[1,256,512]{2,1,0:T(8,128)(2,1)S(1)}, bf16[1,256,512]{2,1,0:T(8,128)(2,1)}, u32[]{:S(2)}, u32[]{:S(2)}) %collective-permute-start.8) | collective-permute-done | bytes 262176 | tf_op jit(solution)/shard_map/ppermute | solution.py:261
  53.5 2.0 %expert_product.6 = (f32[135168,128]{1,0:T(8,128)}, bf16[384,4096]{1,0:T(8,128)(2,1)}) custom-call(s32[8]{0:T(128)S(1)} %iota_xor_fusion.1.sources, s32[4]{0:T(128)S(1)} %select_reduce_fusion.places, bf16[384,1024]{1,0:T(8,128)(2,1)S(1)} %bitcast.2, bf16[1,256,512]{2,1,0:T(8,128)(2,1)S(1)} %copy-done.2, ...), custom_call_target="tpu_custom_call", output_to_operand_aliasing={{0}: (7, {})} | custom-call | bytes 65536 | tf_op jit(solution)/shard_map/expert_product/pallas_call | solution.py:241
  55.5 3.0 %expert_product.7 = (f32[135168,128]{1,0:T(8,128)}, bf16[384,4096]{1,0:T(8,128)(2,1)}) custom-call(s32[8]{0:T(128)S(1)} %iota_xor_fusion.1.sources, s32[4]{0:T(128)S(1)} %select_reduce_fusion.places, bf16[384,1024]{1,0:T(8,128)(2,1)S(1)} %bitcast.3, ...), custom_call_target="tpu_custom_call", output_to_operand_aliasing={{0}: (7, {}), {1}: (8, {})} | custom-call | bytes 65536 | tf_op jit(solution)/shard_map/expert_product/pallas_call | solution.py:241
  59.5 1.6 %collective-permute-start.14 = (bf16[2,256,512]{2,1,0:T(8,128)(2,1)S(1)}, bf16[2,256,512]{2,1,0:T(8,128)(2,1)S(1)}, u32[]{:S(2)}, u32[]{:S(2)}) collective-permute-start(bf16[2,256,512]{2,1,0:T(8,128)(2,1)S(1)} %get-tuple-element.114.refs_0_), channel_id=1, source_target_pairs={{0,8},{8,0},{16,24},{24,16},{1,9},{9,1},{17,25},{25,17},{2,10},{10... | collective-permute-start | bytes 1572872 | tf_op jit(solution)/shard_map/ppermute | solution.py:261
  63.5 9.3 %collective-permute-done.13.refs_1_ = bf16[1,256,512]{2,1,0:T(8,128)(2,1)S(1)} collective-permute-done((bf16[1,256,512]{2,1,0:T(8,128)(2,1)S(1)}, bf16[1,256,512]{2,1,0:T(8,128)(2,1)S(1)}, u32[]{:S(2)}, u32[]{:S(2)}) %collective-permute-start.13) | collective-permute-done | bytes 262176 | tf_op jit(solution)/shard_map/ppermute | solution.py:261
  72.8 3.1 %collective-permute-done.15.refs_2_ = bf16[2,256,512]{2,1,0:T(8,128)(2,1)S(1)} collective-permute-done((bf16[2,256,512]{2,1,0:T(8,128)(2,1)S(1)}, bf16[2,256,512]{2,1,0:T(8,128)(2,1)S(1)}, u32[]{:S(2)}, u32[]{:S(2)}) %collective-permute-start.15) | collective-permute-done | bytes 524320 | tf_op jit(solution)/shard_map/ppermute | solution.py:261
  78.5 11.1 %collective-permute-done.16.refs_1_ = bf16[1,256,512]{2,1,0:T(8,128)(2,1)S(1)} collective-permute-done((bf16[1,256,512]{2,1,0:T(8,128)(2,1)S(1)}, bf16[1,256,512]{2,1,0:T(8,128)(2,1)S(1)}, u32[]{:S(2)}, u32[]{:S(2)}) %collective-permute-start.16) | collective-permute-done | bytes 262176 | tf_op jit(solution)/shard_map/ppermute | solution.py:261
  91.5 4.1 %expert_product.8 = (f32[135168,128]{1,0:T(8,128)}, bf16[384,4096]{1,0:T(8,128)(2,1)}) custom-call(s32[8]{0:T(128)S(1)} %iota_xor_fusion.1.sources, s32[4]{0:T(128)S(1)} %select_reduce_fusion.places, bf16[384,1024]{1,0:T(8,128)(2,1)S(1)} %bitcast.4, bf16[2,256,512]{2,1,0:T(8,128)(2,1)} %get-tuple-element.109.refs_0_, ...), custom_call_target="tpu_custom_call", output_to_operand_aliasing={{0}: (7, {}), {1}: (8, {})} | custom-call | bytes 16777216 | tf_op jit(solution)/shard_map/expert_product/pallas_call | solution.py:241
  95.7 3.1 %expert_product.9 = (f32[135168,128]{1,0:T(8,128)}, bf16[384,4096]{1,0:T(8,128)(2,1)}) custom-call(s32[8]{0:T(128)S(1)} %iota_xor_fusion.1.sources, s32[4]{0:T(128)S(1)} %select_reduce_fusion.places, bf16[384,1024]{1,0:T(8,128)(2,1)S(1)} %bitcast.5, ...), custom_call_target="tpu_custom_call", output_to_operand_aliasing={{0}: (7, {}), {1}: (8, {})} | custom-call | bytes 16777216 | tf_op jit(solution)/shard_map/expert_product/pallas_call | solution.py:241
  98.7 1.7 %collective-permute-start.23 = (bf16[1,256,512]{2,1,0:T(8,128)(2,1)S(1)}, bf16[1,256,512]{2,1,0:T(8,128)(2,1)S(1)}, u32[]{:S(2)}, u32[]{:S(2)}) collective-permute-start(bf16[1,256,512]{2,1,0:T(8,128)(2,1)S(1)} %get-tuple-element.135.refs_1_), channel_id=1, source_target_pairs={{0,16},{8,24},{16,0},{24,8},{1,17},{9,25},{17,1},{25,9},{2,18},{10... | collective-permute-start | bytes 786440 | tf_op jit(solution)/shard_map/ppermute | solution.py:261
  100.9 5.5 %collective-permute-done.23.refs_1_ = bf16[1,256,512]{2,1,0:T(8,128)(2,1)S(1)} collective-permute-done((bf16[1,256,512]{2,1,0:T(8,128)(2,1)S(1)}, bf16[1,256,512]{2,1,0:T(8,128)(2,1)S(1)}, u32[]{:S(2)}, u32[]{:S(2)}) %collective-permute-start.23) | collective-permute-done | bytes 262176 | tf_op jit(solution)/shard_map/ppermute | solution.py:261
  106.5 2.0 %expert_product.10 = (f32[135168,128]{1,0:T(8,128)}, bf16[384,4096]{1,0:T(8,128)(2,1)}) custom-call(s32[8]{0:T(128)S(1)} %iota_xor_fusion.1.sources, s32[4]{0:T(128)S(1)} %select_reduce_fusion.places, bf16[384,1024]{1,0:T(8,128)(2,1)S(1)} %bitcast.6, ...), custom_call_target="tpu_custom_call", output_to_operand_aliasing={{0}: (7, {}), {1}: (8, {})} | custom-call | bytes 65536 | tf_op jit(solution)/shard_map/expert_product/pallas_call | solution.py:241
  108.5 2.0 %expert_product.11 = (f32[135168,128]{1,0:T(8,128)}, bf16[384,4096]{1,0:T(8,128)(2,1)}) custom-call(s32[8]{0:T(128)S(1)} %iota_xor_fusion.1.sources, s32[4]{0:T(128)S(1)} %select_reduce_fusion.places, bf16[384,1024]{1,0:T(8,128)(2,1)S(1)} %bitcast.7, ...), custom_call_target="tpu_custom_call", output_to_operand_aliasing={{0}: (7, {}), {1}: (8, {})} | custom-call | bytes 65536 | tf_op jit(solution)/shard_map/expert_product/pallas_call | solution.py:241
  (63 shorter events, 12.9 us)
Async XLA Ops:
  7.1 12.6 %collective-permute-start = (bf16[1,256,512]{2,1,0:T(8,128)(2,1)}, bf16[1,256,512]{2,1,0:T(8,128)(2,1)S(1)}, u32[]{:S(2)}, u32[]{:S(2)}) collective-permute-start(bf16[1,256,512]{2,1,0:T(8,128)(2,1)} %get-tuple-element.83.refs_0_), channel_id=1, source_target_pairs={{0,8},{8,0},{16,24},{24,16},{1,9},{9,1},{17,25},{25,17},{2,10},{10... | collective-permute-start | bytes 786440 | tf_op jit(solution)/shard_map/ppermute | solution.py:261
  8.7 11.1 %collective-permute-start.1 = (bf16[1,256,512]{2,1,0:T(8,128)(2,1)}, bf16[1,256,512]{2,1,0:T(8,128)(2,1)S(1)}, u32[]{:S(2)}, u32[]{:S(2)}) collective-permute-start(bf16[1,256,512]{2,1,0:T(8,128)(2,1)} %get-tuple-element.83.refs_0_), channel_id=1, source_target_pairs={{0,16},{8,24},{16,0},{24,8},{1,17},{9,25},{17,1},{25,9},{2,18},{10... | collective-permute-start | bytes 786440 | tf_op jit(solution)/shard_map/ppermute | solution.py:261
  10.2 9.6 %collective-permute-start.2 = (bf16[1,256,512]{2,1,0:T(8,128)(2,1)}, bf16[1,256,512]{2,1,0:T(8,128)(2,1)S(1)}, u32[]{:S(2)}, u32[]{:S(2)}) collective-permute-start(bf16[1,256,512]{2,1,0:T(8,128)(2,1)} %get-tuple-element.84), channel_id=1, source_target_pairs={{0,1},{1,0},{2,3},{3,2},{4,5},{5,4},{6,7},{7,6},{8,9},{9,8},{10,11... | collective-permute-start | bytes 786440 | tf_op jit(solution)/shard_map/ppermute | solution.py:261
  10.2 12.5 %collective-permute-start.3 = (bf16[1,256,512]{2,1,0:T(8,128)(2,1)}, bf16[1,256,512]{2,1,0:T(8,128)(2,1)S(1)}, u32[]{:S(2)}, u32[]{:S(2)}) collective-permute-start(bf16[1,256,512]{2,1,0:T(8,128)(2,1)} %get-tuple-element.87), channel_id=1, source_target_pairs={{0,2},{1,3},{2,0},{3,1},{4,6},{5,7},{6,4},{7,5},{8,10},{9,11},{10,... | collective-permute-start | bytes 786440 | tf_op jit(solution)/shard_map/ppermute | solution.py:261
  10.7 15.2 %collective-permute-start.4 = (bf16[1,256,512]{2,1,0:T(8,128)(2,1)}, bf16[1,256,512]{2,1,0:T(8,128)(2,1)S(1)}, u32[]{:S(2)}, u32[]{:S(2)}) collective-permute-start(bf16[1,256,512]{2,1,0:T(8,128)(2,1)} %get-tuple-element.88), channel_id=1, source_target_pairs={{0,4},{1,5},{2,6},{3,7},{4,0},{5,1},{6,2},{7,3},{8,12},{9,13},{10,... | collective-permute-start | bytes 786440 | tf_op jit(solution)/shard_map/ppermute | solution.py:261
  19.8 8.2 %collective-permute-start.5 = (bf16[1,256,512]{2,1,0:T(8,128)(2,1)S(1)}, bf16[1,256,512]{2,1,0:T(8,128)(2,1)S(1)}, u32[]{:S(2)}, u32[]{:S(2)}) collective-permute-start(bf16[1,256,512]{2,1,0:T(8,128)(2,1)S(1)} %get-tuple-element.85.refs_0_), channel_id=1, source_target_pairs={{0,8},{8,0},{16,24},{24,16},{1,9},{9,1},{17,25},{25,17},{2,10},{10... | collective-permute-start | bytes 786440 | tf_op jit(solution)/shard_map/ppermute | solution.py:261
  20.4 9.2 %collective-permute-start.6 = (bf16[1,256,512]{2,1,0:T(8,128)(2,1)S(1)}, bf16[1,256,512]{2,1,0:T(8,128)(2,1)S(1)}, u32[]{:S(2)}, u32[]{:S(2)}) collective-permute-start(bf16[1,256,512]{2,1,0:T(8,128)(2,1)S(1)} %get-tuple-element.85.refs_0_), channel_id=1, source_target_pairs={{0,16},{8,24},{16,0},{24,8},{1,17},{9,25},{17,1},{25,9},{2,18},{10... | collective-permute-start | bytes 786440 | tf_op jit(solution)/shard_map/ppermute | solution.py:261
  20.9 13.0 %collective-permute-start.7 = (bf16[1,256,512]{2,1,0:T(8,128)(2,1)S(1)}, bf16[1,256,512]{2,1,0:T(8,128)(2,1)S(1)}, u32[]{:S(2)}, u32[]{:S(2)}) collective-permute-start(bf16[1,256,512]{2,1,0:T(8,128)(2,1)S(1)} %get-tuple-element.92.refs_1_), channel_id=1, source_target_pairs={{0,16},{8,24},{16,0},{24,8},{1,17},{9,25},{17,1},{25,9},{2,18},{10... | collective-permute-start | bytes 786440 | tf_op jit(solution)/shard_map/ppermute | solution.py:261
  25.9 32.5 %collective-permute-start.9 = (bf16[1,256,512]{2,1,0:T(8,128)(2,1)}, bf16[1,256,512]{2,1,0:T(8,128)(2,1)}, u32[]{:S(2)}, u32[]{:S(2)}) collective-permute-start(bf16[1,256,512]{2,1,0:T(8,128)(2,1)} %get-tuple-element.106), channel_id=1, source_target_pairs={{0,3},{1,2},{2,1},{3,0},{4,7},{5,6},{6,5},{7,4},{8,11},{9,10},{10,... | collective-permute-start | bytes 786440 | tf_op jit(solution)/shard_map/ppermute | solution.py:261
  25.9 32.5 %collective-permute-start.10 = (bf16[1,256,512]{2,1,0:T(8,128)(2,1)}, bf16[1,256,512]{2,1,0:T(8,128)(2,1)}, u32[]{:S(2)}, u32[]{:S(2)}) collective-permute-start(bf16[1,256,512]{2,1,0:T(8,128)(2,1)} %get-tuple-element.107), channel_id=1, source_target_pairs={{0,5},{1,4},{2,7},{3,6},{4,1},{5,0},{6,3},{7,2},{8,13},{9,12},{10,... | collective-permute-start | bytes 786440 | tf_op jit(solution)/shard_map/ppermute | solution.py:261
  34.7 27.2 %collective-permute-start.11 = (bf16[2,256,512]{2,1,0:T(8,128)(2,1)}, bf16[2,256,512]{2,1,0:T(8,128)(2,1)S(1)}, u32[]{:S(2)}, u32[]{:S(2)}) collective-permute-start(bf16[2,256,512]{2,1,0:T(8,128)(2,1)} %get-tuple-element.109.refs_0_), channel_id=1, source_target_pairs={{0,8},{8,0},{16,24},{24,16},{1,9},{9,1},{17,25},{25,17},{2,10},{10... | collective-permute-start | bytes 1572872 | tf_op jit(solution)/shard_map/ppermute | solution.py:261
  36.3 25.7 %collective-permute-start.12 = (bf16[2,256,512]{2,1,0:T(8,128)(2,1)}, bf16[2,256,512]{2,1,0:T(8,128)(2,1)S(1)}, u32[]{:S(2)}, u32[]{:S(2)}) collective-permute-start(bf16[2,256,512]{2,1,0:T(8,128)(2,1)} %get-tuple-element.109.refs_0_), channel_id=1, source_target_pairs={{0,16},{8,24},{16,0},{24,8},{1,17},{9,25},{17,1},{25,9},{2,18},{10... | collective-permute-start | bytes 1572872 | tf_op jit(solution)/shard_map/ppermute | solution.py:261
  36.8 16.6 %collective-permute-start.8 = (bf16[1,256,512]{2,1,0:T(8,128)(2,1)S(1)}, bf16[1,256,512]{2,1,0:T(8,128)(2,1)}, u32[]{:S(2)}, u32[]{:S(2)}) collective-permute-start(bf16[1,256,512]{2,1,0:T(8,128)(2,1)S(1)} %get-tuple-element.94.refs_2_), channel_id=1, source_target_pairs={{0,8},{8,0},{16,24},{24,16},{1,9},{9,1},{17,25},{25,17},{2,10},{10... | collective-permute-start | bytes 786440 | tf_op jit(solution)/shard_map/ppermute | solution.py:261
  59.5 13.3 %collective-permute-start.14 = (bf16[2,256,512]{2,1,0:T(8,128)(2,1)S(1)}, bf16[2,256,512]{2,1,0:T(8,128)(2,1)S(1)}, u32[]{:S(2)}, u32[]{:S(2)}) collective-permute-start(bf16[2,256,512]{2,1,0:T(8,128)(2,1)S(1)} %get-tuple-element.114.refs_0_), channel_id=1, source_target_pairs={{0,8},{8,0},{16,24},{24,16},{1,9},{9,1},{17,25},{25,17},{2,10},{10... | collective-permute-start | bytes 1572872 | tf_op jit(solution)/shard_map/ppermute | solution.py:261
  61.1 14.9 %collective-permute-start.15 = (bf16[2,256,512]{2,1,0:T(8,128)(2,1)S(1)}, bf16[2,256,512]{2,1,0:T(8,128)(2,1)S(1)}, u32[]{:S(2)}, u32[]{:S(2)}) collective-permute-start(bf16[2,256,512]{2,1,0:T(8,128)(2,1)S(1)} %get-tuple-element.114.refs_0_), channel_id=1, source_target_pairs={{0,16},{8,24},{16,0},{24,8},{1,17},{9,25},{17,1},{25,9},{2,18},{10... | collective-permute-start | bytes 1572872 | tf_op jit(solution)/shard_map/ppermute | solution.py:261
  61.6 11.2 %collective-permute-start.13 = (bf16[1,256,512]{2,1,0:T(8,128)(2,1)S(1)}, bf16[1,256,512]{2,1,0:T(8,128)(2,1)S(1)}, u32[]{:S(2)}, u32[]{:S(2)}) collective-permute-start(bf16[1,256,512]{2,1,0:T(8,128)(2,1)S(1)} %copy-done.3), channel_id=1, source_target_pairs={{0,6},{1,7},{2,4},{3,5},{4,2},{5,3},{6,0},{7,1},{8,14},{9,15},{10,... | collective-permute-start | bytes 786440 | tf_op jit(solution)/shard_map/ppermute | solution.py:261
  62.0 29.1 %collective-permute-start.17 = (bf16[2,256,512]{2,1,0:T(8,128)(2,1)S(1)}, bf16[2,256,512]{2,1,0:T(8,128)(2,1)S(1)}, u32[]{:S(2)}, u32[]{:S(2)}) collective-permute-start(bf16[2,256,512]{2,1,0:T(8,128)(2,1)S(1)} %get-tuple-element.120.refs_1_), channel_id=1, source_target_pairs={{0,16},{8,24},{16,0},{24,8},{1,17},{9,25},{17,1},{25,9},{2,18},{10... | collective-permute-start | bytes 1572872 | tf_op jit(solution)/shard_map/ppermute | solution.py:261
  76.0 19.7 %collective-permute-start.18 = (bf16[2,256,512]{2,1,0:T(8,128)(2,1)S(1)}, bf16[2,256,512]{2,1,0:T(8,128)(2,1)S(1)}, u32[]{:S(2)}, u32[]{:S(2)}) collective-permute-start(bf16[2,256,512]{2,1,0:T(8,128)(2,1)S(1)} %get-tuple-element.119.refs_2_), channel_id=1, source_target_pairs={{0,8},{8,0},{16,24},{24,16},{1,9},{9,1},{17,25},{25,17},{2,10},{10... | collective-permute-start | bytes 1572872 | tf_op jit(solution)/shard_map/ppermute | solution.py:261
  76.5 13.1 %collective-permute-start.16 = (bf16[1,256,512]{2,1,0:T(8,128)(2,1)S(1)}, bf16[1,256,512]{2,1,0:T(8,128)(2,1)S(1)}, u32[]{:S(2)}, u32[]{:S(2)}) collective-permute-start(bf16[1,256,512]{2,1,0:T(8,128)(2,1)S(1)} %get-tuple-element.116), channel_id=1, source_target_pairs={{0,7},{1,6},{2,5},{3,4},{4,3},{5,2},{6,1},{7,0},{8,15},{9,14},{10,... | collective-permute-start | bytes 786440 | tf_op jit(solution)/shard_map/ppermute | solution.py:261
  76.5 22.2 %collective-permute-start.19 = (bf16[1,256,512]{2,1,0:T(8,128)(2,1)S(1)}, bf16[1,256,512]{2,1,0:T(8,128)(2,1)S(1)}, u32[]{:S(2)}, u32[]{:S(2)}) collective-permute-start(bf16[1,256,512]{2,1,0:T(8,128)(2,1)S(1)} %get-tuple-element.131.refs_0_), channel_id=1, source_target_pairs={{0,8},{8,0},{16,24},{24,16},{1,9},{9,1},{17,25},{25,17},{2,10},{10... | collective-permute-start | bytes 786440 | tf_op jit(solution)/shard_map/ppermute | solution.py:261
  78.0 20.7 %collective-permute-start.20 = (bf16[1,256,512]{2,1,0:T(8,128)(2,1)S(1)}, bf16[1,256,512]{2,1,0:T(8,128)(2,1)S(1)}, u32[]{:S(2)}, u32[]{:S(2)}) collective-permute-start(bf16[1,256,512]{2,1,0:T(8,128)(2,1)S(1)} %get-tuple-element.131.refs_0_), channel_id=1, source_target_pairs={{0,16},{8,24},{16,0},{24,8},{1,17},{9,25},{17,1},{25,9},{2,18},{10... | collective-permute-start | bytes 786440 | tf_op jit(solution)/shard_map/ppermute | solution.py:261
  89.6 10.8 %collective-permute-start.21 = (bf16[1,256,512]{2,1,0:T(8,128)(2,1)S(1)}, bf16[1,256,512]{2,1,0:T(8,128)(2,1)S(1)}, u32[]{:S(2)}, u32[]{:S(2)}) collective-permute-start(bf16[1,256,512]{2,1,0:T(8,128)(2,1)S(1)} %get-tuple-element.117.refs_0_), channel_id=1, source_target_pairs={{0,8},{8,0},{16,24},{24,16},{1,9},{9,1},{17,25},{25,17},{2,10},{10... | collective-permute-start | bytes 786440 | tf_op jit(solution)/shard_map/ppermute | solution.py:261
  91.1 9.3 %collective-permute-start.22 = (bf16[1,256,512]{2,1,0:T(8,128)(2,1)S(1)}, bf16[1,256,512]{2,1,0:T(8,128)(2,1)S(1)}, u32[]{:S(2)}, u32[]{:S(2)}) collective-permute-start(bf16[1,256,512]{2,1,0:T(8,128)(2,1)S(1)} %get-tuple-element.117.refs_0_), channel_id=1, source_target_pairs={{0,16},{8,24},{16,0},{24,8},{1,17},{9,25},{17,1},{25,9},{2,18},{10... | collective-permute-start | bytes 786440 | tf_op jit(solution)/shard_map/ppermute | solution.py:261
  100.4 8.1 %collective-permute-start.24 = (bf16[1,256,512]{2,1,0:T(8,128)(2,1)S(1)}, bf16[1,256,512]{2,1,0:T(8,128)(2,1)S(1)}, u32[]{:S(2)}, u32[]{:S(2)}) collective-permute-start(bf16[1,256,512]{2,1,0:T(8,128)(2,1)S(1)} %get-tuple-element.134.refs_2_), channel_id=1, source_target_pairs={{0,8},{8,0},{16,24},{24,16},{1,9},{9,1},{17,25},{25,17},{2,10},{10... | collective-permute-start | bytes 786440 | tf_op jit(solution)/shard_map/ppermute | solution.py:261
  (6 other events, 67.3 us)

commit v12 on v11

--- a/solution.py
+++ b/solution.py
@@ -32,9 +32,6 @@
 PLANNED = (4, 8)
 WHOLE = pl.BlockSpec(memory_space=pl.ANY)
 SMALL_COST = pl.CostEstimate(flops=0, bytes_accessed=65536, transcendentals=0)
-
-
-PAIR_COST = pl.CostEstimate(flops=0, bytes_accessed=16 * 1024 * 1024, transcendentals=0)
 
 
 def like(array):
@@ -251,7 +248,7 @@
             + [jax.ShapeDtypeStruct((tokens, breadth), jnp.bfloat16)],
         input_output_aliases={3 + slabs + i: i for i in range(passed)},
         compiler_params=pltpu.CompilerParams(vmem_limit_bytes=PRODUCT_LIMIT),
-        cost_estimate=SMALL_COST if blocks == 1 else PAIR_COST,
+        cost_estimate=SMALL_COST,
         name="expert_product",
     )(sources, places, token_rows, *weights, *token, *carried)
     return (out,), tuple(token)
@@ -309,17 +306,16 @@
     if fenced:
         one, two = (2, 4), (3, 5)
         plan = [
-            ([(0, 1), (0, 2), (1, 0)], [(1, 0, 1), (1, 0, 2), (0, 1, 2)], []),
-            ([(2, 0), (4, 0)], [], [3, 5]),
-            ([(1, 1), (1, 2), (0, 3)], [(1, 2, 1)], []),
+            ([(0, 1), (0, 2), (1, 0)], [(1, 0, 1), (1, 0, 2)], []),
+            ([(2, 0), (4, 0)], [], [5]),
+            ([(1, 1), (1, 2)], [(1, 2, 1), (0, 1, 2)], []),
             (one, [(one, 0, 1), (one, 0, 2)], []),
-            ([(1, 3)], [], []),
+            ([(0, 3), (1, 3)], [], [3]),
             (two, [(two, 0, 1), (two, 0, 2)], [6]),
             ([(one, 1), (one, 2)], [(one, 1, 2)], []),
-            ([(6, 0)], [], [7]),
-            ([(two, 1), (two, 2)], [(two, 2, 1), (6, 0, 1), (6, 0, 2)], []),
+            ([(6, 0), (two, 1), (two, 2)], [(two, 2, 1), (6, 0, 1), (6, 0, 2)], [7]),
+            ([(one, 3)], [], []),
             ([(7, 0)], [(7, 0, 1), (7, 0, 2)], []),
-            ([(one, 3)], [], []),
             ([(two, 3)], [], []),
             ([(6, 1), (6, 2)], [(6, 1, 2)], []),
             ([(7, 1), (7, 2)], [(7, 2, 1)], []),
@@ -346,7 +342,7 @@
                 deliver(block)
             for key in sending:
                 send(*key)
-            for block in [] if sending or leaving else list(waiting):
+            for block in list(waiting):
                 if all((block, member) in ready for member in range(replicas)):
                     multiply(block)
                     waiting.remove(block)

time: 111 us -> 104 us (0.937)
  the two profiles are of different devices: /device:TPU:8 before, /device:TPU:0 now
where the time goes in v12:
time: 104 us; the launch traced here: 103 us
  waiting for transfers between devices  43.2 us (42%)
  Pallas kernels  31.1 us (30%)
  starting transfers between devices  25.6 us (25%)
  local copies, waits for them, and re-layouts  2.61 us (3%)
    ppermute x25, waiting for transfers between devices, swap(): return lax.ppermute(value, axis, [(i, i ^ mask) for i in range(size)])  43.2 us
    ppermute x25, starting transfers between devices, swap(): return lax.ppermute(value, axis, [(i, i ^ mask) for i in range(size)])  25.6 us
    pallas_call x6, Pallas kernels, product(): pl.pallas_call(functools.partial(product_kernel, slabs), grid_spec=pltpu....  16.2 us
    pallas_call x2, Pallas kernels, adam_blocks(): pl.pallas_call(functools.partial(adam_kernel, groups, passed), in_specs=[...  13 us
    unnamed x14, local copies, waits for them, and re-layouts  2.61 us
  transfers between devices with their start and end apart: 25, of which 15 were waited for; matrix products, arithmetic and copies ran while one was open for 0% of the time, Pallas kernels for 22%

profile of v12, /device:TPU:0, one launch (start us, length us, event | category | flops | bytes accessed | tf_op | source)
XLA Modules:
  0.0 103.5 jit_solution(3443890772828653312)
XLA Ops:
  0.6 6.5 %adam_quantize.2 = (f32[8,256,512]{2,1,0:T(8,128)}, bf16[8,256,512]{2,1,0:T(8,128)(2,1)}, bf16[8,256,512]{2,1,0:T(8,128)(2,1)}, bf16[1,256,512]{2,1,0:T(8,128)(2...) custom-call(s32[8]{0:T(128)} %owner.3, ...), custom_call_target="tpu_custom_call" | custom-call | bytes 65536 | tf_op jit(solution)/shard_map/adam_quantize/pallas_call | solution.py:170
  7.2 3.0 %collective-permute-start = (bf16[1,256,512]{2,1,0:T(8,128)(2,1)}, bf16[1,256,512]{2,1,0:T(8,128)(2,1)S(1)}, u32[]{:S(2)}, u32[]{:S(2)}) collective-permute-start(bf16[1,256,512]{2,1,0:T(8,128)(2,1)} %get-tuple-element.82.refs_0_), channel_id=1, source_target_pairs={{0,8},{8,0},{16,24},{24,16},{1,9},{9,1},{17,25},{25,17},{2,10},{10... | collective-permute-start | bytes 786440 | tf_op jit(solution)/shard_map/ppermute | solution.py:258
  10.2 1.5 %collective-permute-start.1 = (bf16[1,256,512]{2,1,0:T(8,128)(2,1)}, bf16[1,256,512]{2,1,0:T(8,128)(2,1)S(1)}, u32[]{:S(2)}, u32[]{:S(2)}) collective-permute-start(bf16[1,256,512]{2,1,0:T(8,128)(2,1)} %get-tuple-element.82.refs_0_), channel_id=1, source_target_pairs={{0,16},{8,24},{16,0},{24,8},{1,17},{9,25},{17,1},{25,9},{2,18},{10... | collective-permute-start | bytes 786440 | tf_op jit(solution)/shard_map/ppermute | solution.py:258
  11.7 1.6 %collective-permute-start.3 = (bf16[1,256,512]{2,1,0:T(8,128)(2,1)}, bf16[1,256,512]{2,1,0:T(8,128)(2,1)S(1)}, u32[]{:S(2)}, u32[]{:S(2)}) collective-permute-start(bf16[1,256,512]{2,1,0:T(8,128)(2,1)} %get-tuple-element.85), channel_id=1, source_target_pairs={{0,2},{1,3},{2,0},{3,1},{4,6},{5,7},{6,4},{7,5},{8,10},{9,11},{10,... | collective-permute-start | bytes 786440 | tf_op jit(solution)/shard_map/ppermute | solution.py:258
  13.3 2.6 %collective-permute-start.4 = (bf16[1,256,512]{2,1,0:T(8,128)(2,1)}, bf16[1,256,512]{2,1,0:T(8,128)(2,1)S(1)}, u32[]{:S(2)}, u32[]{:S(2)}) collective-permute-start(bf16[1,256,512]{2,1,0:T(8,128)(2,1)} %get-tuple-element.86), channel_id=1, source_target_pairs={{0,4},{1,5},{2,6},{3,7},{4,0},{5,1},{6,2},{7,3},{8,12},{9,13},{10,... | collective-permute-start | bytes 786440 | tf_op jit(solution)/shard_map/ppermute | solution.py:258
  15.9 6.5 %adam_quantize.3 = (f32[8,256,512]{2,1,0:T(8,128)}, bf16[8,256,512]{2,1,0:T(8,128)(2,1)}, bf16[8,256,512]{2,1,0:T(8,128)(2,1)}, bf16[1,256,512]{2,1,0:T(8,128)(2...) custom-call(s32[8]{0:T(128)} %owner.3, ...), custom_call_target="tpu_custom_call", output_to_operand_aliasing={{0}: (5, {}), {1}: (6, {}), {2}: (7, {}), {7}: (8, {})} | custom-call | bytes 65536 | tf_op jit(solution)/shard_map/adam_quantize/pallas_call | solution.py:170
  26.1 2.4 %collective-permute-done.4.refs_2_ = bf16[1,256,512]{2,1,0:T(8,128)(2,1)S(1)} collective-permute-done((bf16[1,256,512]{2,1,0:T(8,128)(2,1)}, bf16[1,256,512]{2,1,0:T(8,128)(2,1)S(1)}, u32[]{:S(2)}, u32[]{:S(2)}) %collective-permute-start.4) | collective-permute-done | bytes 262176 | tf_op jit(solution)/shard_map/ppermute | solution.py:258
  28.5 2.2 %collective-permute-done.5.refs_1_ = bf16[1,256,512]{2,1,0:T(8,128)(2,1)S(1)} collective-permute-done((bf16[1,256,512]{2,1,0:T(8,128)(2,1)S(1)}, bf16[1,256,512]{2,1,0:T(8,128)(2,1)S(1)}, u32[]{:S(2)}, u32[]{:S(2)}) %collective-permute-start.5) | collective-permute-done | bytes 262176 | tf_op jit(solution)/shard_map/ppermute | solution.py:258
  30.6 1.7 %collective-permute-done.6.refs_2_ = bf16[1,256,512]{2,1,0:T(8,128)(2,1)} collective-permute-done((bf16[1,256,512]{2,1,0:T(8,128)(2,1)S(1)}, bf16[1,256,512]{2,1,0:T(8,128)(2,1)}, u32[]{:S(2)}, u32[]{:S(2)}) %collective-permute-start.6) | collective-permute-done | bytes 262176 | tf_op jit(solution)/shard_map/ppermute | solution.py:258
  36.5 3.4 %collective-permute-done.8.refs_2_ = bf16[1,256,512]{2,1,0:T(8,128)(2,1)S(1)} collective-permute-done((bf16[1,256,512]{2,1,0:T(8,128)(2,1)}, bf16[1,256,512]{2,1,0:T(8,128)(2,1)S(1)}, u32[]{:S(2)}, u32[]{:S(2)}) %collective-permute-start.8) | collective-permute-done | bytes 262176 | tf_op jit(solution)/shard_map/ppermute | solution.py:258
  42.8 2.0 %expert_product.6 = (f32[135168,128]{1,0:T(8,128)}, bf16[384,4096]{1,0:T(8,128)(2,1)}) custom-call(s32[8]{0:T(128)S(1)} %iota_xor_fusion.1.sources, s32[4]{0:T(128)S(1)} %select_reduce_fusion.places, bf16[384,1024]{1,0:T(8,128)(2,1)S(1)} %bitcast.2, bf16[1,256,512]{2,1,0:T(8,128)(2,1)S(1)} %copy-done.2, ...), custom_call_target="tpu_custom_call", output_to_operand_aliasing={{0}: (7, {})} | custom-call | bytes 65536 | tf_op jit(solution)/shard_map/expert_product/pallas_call | solution.py:238
  44.8 3.0 %expert_product.7 = (f32[135168,128]{1,0:T(8,128)}, bf16[384,4096]{1,0:T(8,128)(2,1)}) custom-call(s32[8]{0:T(128)S(1)} %iota_xor_fusion.1.sources, s32[4]{0:T(128)S(1)} %select_reduce_fusion.places, bf16[384,1024]{1,0:T(8,128)(2,1)S(1)} %bitcast.3, ...), custom_call_target="tpu_custom_call", output_to_operand_aliasing={{0}: (7, {}), {1}: (8, {})} | custom-call | bytes 65536 | tf_op jit(solution)/shard_map/expert_product/pallas_call | solution.py:238
  47.7 5.0 %collective-permute-done.9.refs_1_ = bf16[1,256,512]{2,1,0:T(8,128)(2,1)} collective-permute-done((bf16[1,256,512]{2,1,0:T(8,128)(2,1)}, bf16[1,256,512]{2,1,0:T(8,128)(2,1)}, u32[]{:S(2)}, u32[]{:S(2)}) %collective-permute-start.9) | collective-permute-done | bytes 262176 | tf_op jit(solution)/shard_map/ppermute | solution.py:258
  55.0 2.3 %collective-permute-start.13 = (bf16[1,256,512]{2,1,0:T(8,128)(2,1)S(1)}, bf16[1,256,512]{2,1,0:T(8,128)(2,1)S(1)}, u32[]{:S(2)}, u32[]{:S(2)}) collective-permute-start(bf16[1,256,512]{2,1,0:T(8,128)(2,1)S(1)} %copy-done.5), channel_id=1, source_target_pairs={{0,6},{1,7},{2,4},{3,5},{4,2},{5,3},{6,0},{7,1},{8,14},{9,15},{10,... | collective-permute-start | bytes 786440 | tf_op jit(solution)/shard_map/ppermute | solution.py:258
  58.8 5.8 %collective-permute-done.13.refs_1_ = bf16[1,256,512]{2,1,0:T(8,128)(2,1)S(1)} collective-permute-done((bf16[1,256,512]{2,1,0:T(8,128)(2,1)S(1)}, bf16[1,256,512]{2,1,0:T(8,128)(2,1)S(1)}, u32[]{:S(2)}, u32[]{:S(2)}) %collective-permute-start.13) | collective-permute-done | bytes 262176 | tf_op jit(solution)/shard_map/ppermute | solution.py:258
  64.6 3.2 %collective-permute-done.14.refs_2_ = bf16[2,256,512]{2,1,0:T(8,128)(2,1)S(1)} collective-permute-done((bf16[2,256,512]{2,1,0:T(8,128)(2,1)S(1)}, bf16[2,256,512]{2,1,0:T(8,128)(2,1)S(1)}, u32[]{:S(2)}, u32[]{:S(2)}) %collective-permute-start.14) | collective-permute-done | bytes 524320 | tf_op jit(solution)/shard_map/ppermute | solution.py:258
  71.9 8.6 %collective-permute-done.16.refs_1_ = bf16[2,256,512]{2,1,0:T(8,128)(2,1)S(1)} collective-permute-done((bf16[2,256,512]{2,1,0:T(8,128)(2,1)S(1)}, bf16[2,256,512]{2,1,0:T(8,128)(2,1)S(1)}, u32[]{:S(2)}, u32[]{:S(2)}) %collective-permute-start.16) | collective-permute-done | bytes 524320 | tf_op jit(solution)/shard_map/ppermute | solution.py:258
  80.5 4.1 %expert_product.8 = (f32[135168,128]{1,0:T(8,128)}, bf16[384,4096]{1,0:T(8,128)(2,1)}) custom-call(s32[8]{0:T(128)S(1)} %iota_xor_fusion.1.sources, s32[4]{0:T(128)S(1)} %select_reduce_fusion.places, bf16[384,1024]{1,0:T(8,128)(2,1)S(1)} %bitcast.4, bf16[2,256,512]{2,1,0:T(8,128)(2,1)} %get-tuple-element.93.refs_0_, ...), custom_call_target="tpu_custom_call", output_to_operand_aliasing={{0}: (7, {}), {1}: (8, {})} | custom-call | bytes 65536 | tf_op jit(solution)/shard_map/expert_product/pallas_call | solution.py:238
  86.7 3.1 %expert_product.9 = (f32[135168,128]{1,0:T(8,128)}, bf16[384,4096]{1,0:T(8,128)(2,1)}) custom-call(s32[8]{0:T(128)S(1)} %iota_xor_fusion.1.sources, s32[4]{0:T(128)S(1)} %select_reduce_fusion.places, bf16[384,1024]{1,0:T(8,128)(2,1)S(1)} %bitcast.5, ...), custom_call_target="tpu_custom_call", output_to_operand_aliasing={{0}: (7, {}), {1}: (8, {})} | custom-call | bytes 65536 | tf_op jit(solution)/shard_map/expert_product/pallas_call | solution.py:238
  92.0 3.1 %collective-permute-done.22.refs_2_ = bf16[1,256,512]{2,1,0:T(8,128)(2,1)S(1)} collective-permute-done((bf16[1,256,512]{2,1,0:T(8,128)(2,1)S(1)}, bf16[1,256,512]{2,1,0:T(8,128)(2,1)S(1)}, u32[]{:S(2)}, u32[]{:S(2)}) %collective-permute-start.22) | collective-permute-done | bytes 262176 | tf_op jit(solution)/shard_map/ppermute | solution.py:258
  95.6 2.3 %collective-permute-done.23.refs_1_ = bf16[1,256,512]{2,1,0:T(8,128)(2,1)S(1)} collective-permute-done((bf16[1,256,512]{2,1,0:T(8,128)(2,1)S(1)}, bf16[1,256,512]{2,1,0:T(8,128)(2,1)S(1)}, u32[]{:S(2)}, u32[]{:S(2)}) %collective-permute-start.23) | collective-permute-done | bytes 262176 | tf_op jit(solution)/shard_map/ppermute | solution.py:258
  97.9 2.0 %expert_product.10 = (f32[135168,128]{1,0:T(8,128)}, bf16[384,4096]{1,0:T(8,128)(2,1)}) custom-call(s32[8]{0:T(128)S(1)} %iota_xor_fusion.1.sources, s32[4]{0:T(128)S(1)} %select_reduce_fusion.places, bf16[384,1024]{1,0:T(8,128)(2,1)S(1)} %bitcast.6, ...), custom_call_target="tpu_custom_call", output_to_operand_aliasing={{0}: (7, {}), {1}: (8, {})} | custom-call | bytes 65536 | tf_op jit(solution)/shard_map/expert_product/pallas_call | solution.py:238
  99.9 1.6 %collective-permute-done.24.refs_1_ = bf16[1,256,512]{2,1,0:T(8,128)(2,1)S(1)} collective-permute-done((bf16[1,256,512]{2,1,0:T(8,128)(2,1)S(1)}, bf16[1,256,512]{2,1,0:T(8,128)(2,1)S(1)}, u32[]{:S(2)}, u32[]{:S(2)}) %collective-permute-start.24) | collective-permute-done | bytes 262176 | tf_op jit(solution)/shard_map/ppermute | solution.py:258
  101.5 2.0 %expert_product.11 = (f32[135168,128]{1,0:T(8,128)}, bf16[384,4096]{1,0:T(8,128)(2,1)}) custom-call(s32[8]{0:T(128)S(1)} %iota_xor_fusion.1.sources, s32[4]{0:T(128)S(1)} %select_reduce_fusion.places, bf16[384,1024]{1,0:T(8,128)(2,1)S(1)} %bitcast.7, ...), custom_call_target="tpu_custom_call", output_to_operand_aliasing={{0}: (7, {}), {1}: (8, {})} | custom-call | bytes 65536 | tf_op jit(solution)/shard_map/expert_product/pallas_call | solution.py:238
  (66 shorter events, 23.4 us)
Async XLA Ops:
  7.2 15.2 %collective-permute-start = (bf16[1,256,512]{2,1,0:T(8,128)(2,1)}, bf16[1,256,512]{2,1,0:T(8,128)(2,1)S(1)}, u32[]{:S(2)}, u32[]{:S(2)}) collective-permute-start(bf16[1,256,512]{2,1,0:T(8,128)(2,1)} %get-tuple-element.82.refs_0_), channel_id=1, source_target_pairs={{0,8},{8,0},{16,24},{24,16},{1,9},{9,1},{17,25},{25,17},{2,10},{10... | collective-permute-start | bytes 786440 | tf_op jit(solution)/shard_map/ppermute | solution.py:258
  10.2 12.2 %collective-permute-start.1 = (bf16[1,256,512]{2,1,0:T(8,128)(2,1)}, bf16[1,256,512]{2,1,0:T(8,128)(2,1)S(1)}, u32[]{:S(2)}, u32[]{:S(2)}) collective-permute-start(bf16[1,256,512]{2,1,0:T(8,128)(2,1)} %get-tuple-element.82.refs_0_), channel_id=1, source_target_pairs={{0,16},{8,24},{16,0},{24,8},{1,17},{9,25},{17,1},{25,9},{2,18},{10... | collective-permute-start | bytes 786440 | tf_op jit(solution)/shard_map/ppermute | solution.py:258
  11.7 10.7 %collective-permute-start.2 = (bf16[1,256,512]{2,1,0:T(8,128)(2,1)}, bf16[1,256,512]{2,1,0:T(8,128)(2,1)S(1)}, u32[]{:S(2)}, u32[]{:S(2)}) collective-permute-start(bf16[1,256,512]{2,1,0:T(8,128)(2,1)} %get-tuple-element.83), channel_id=1, source_target_pairs={{0,1},{1,0},{2,3},{3,2},{4,5},{5,4},{6,7},{7,6},{8,9},{9,8},{10,11... | collective-permute-start | bytes 786440 | tf_op jit(solution)/shard_map/ppermute | solution.py:258
  11.7 14.4 %collective-permute-start.3 = (bf16[1,256,512]{2,1,0:T(8,128)(2,1)}, bf16[1,256,512]{2,1,0:T(8,128)(2,1)S(1)}, u32[]{:S(2)}, u32[]{:S(2)}) collective-permute-start(bf16[1,256,512]{2,1,0:T(8,128)(2,1)} %get-tuple-element.85), channel_id=1, source_target_pairs={{0,2},{1,3},{2,0},{3,1},{4,6},{5,7},{6,4},{7,5},{8,10},{9,11},{10,... | collective-permute-start | bytes 786440 | tf_op jit(solution)/shard_map/ppermute | solution.py:258
  13.3 15.2 %collective-permute-start.4 = (bf16[1,256,512]{2,1,0:T(8,128)(2,1)}, bf16[1,256,512]{2,1,0:T(8,128)(2,1)S(1)}, u32[]{:S(2)}, u32[]{:S(2)}) collective-permute-start(bf16[1,256,512]{2,1,0:T(8,128)(2,1)} %get-tuple-element.86), channel_id=1, source_target_pairs={{0,4},{1,5},{2,6},{3,7},{4,0},{5,1},{6,2},{7,3},{8,12},{9,13},{10,... | collective-permute-start | bytes 786440 | tf_op jit(solution)/shard_map/ppermute | solution.py:258
  22.4 8.2 %collective-permute-start.5 = (bf16[1,256,512]{2,1,0:T(8,128)(2,1)S(1)}, bf16[1,256,512]{2,1,0:T(8,128)(2,1)S(1)}, u32[]{:S(2)}, u32[]{:S(2)}) collective-permute-start(bf16[1,256,512]{2,1,0:T(8,128)(2,1)S(1)} %get-tuple-element.89.refs_0_), channel_id=1, source_target_pairs={{0,8},{8,0},{16,24},{24,16},{1,9},{9,1},{17,25},{25,17},{2,10},{10... | collective-permute-start | bytes 786440 | tf_op jit(solution)/shard_map/ppermute | solution.py:258
  23.0 9.3 %collective-permute-start.6 = (bf16[1,256,512]{2,1,0:T(8,128)(2,1)S(1)}, bf16[1,256,512]{2,1,0:T(8,128)(2,1)}, u32[]{:S(2)}, u32[]{:S(2)}) collective-permute-start(bf16[1,256,512]{2,1,0:T(8,128)(2,1)S(1)} %get-tuple-element.89.refs_0_), channel_id=1, source_target_pairs={{0,16},{8,24},{16,0},{24,8},{1,17},{9,25},{17,1},{25,9},{2,18},{10... | collective-permute-start | bytes 786440 | tf_op jit(solution)/shard_map/ppermute | solution.py:258
  23.5 13.0 %collective-permute-start.7 = (bf16[1,256,512]{2,1,0:T(8,128)(2,1)S(1)}, bf16[1,256,512]{2,1,0:T(8,128)(2,1)S(1)}, u32[]{:S(2)}, u32[]{:S(2)}) collective-permute-start(bf16[1,256,512]{2,1,0:T(8,128)(2,1)S(1)} %get-tuple-element.97.refs_1_), channel_id=1, source_target_pairs={{0,16},{8,24},{16,0},{24,8},{1,17},{9,25},{17,1},{25,9},{2,18},{10... | collective-permute-start | bytes 786440 | tf_op jit(solution)/shard_map/ppermute | solution.py:258
  32.3 7.6 %collective-permute-start.8 = (bf16[1,256,512]{2,1,0:T(8,128)(2,1)}, bf16[1,256,512]{2,1,0:T(8,128)(2,1)S(1)}, u32[]{:S(2)}, u32[]{:S(2)}) collective-permute-start(bf16[1,256,512]{2,1,0:T(8,128)(2,1)} %get-tuple-element.95.refs_2_), channel_id=1, source_target_pairs={{0,8},{8,0},{16,24},{24,16},{1,9},{9,1},{17,25},{25,17},{2,10},{10... | collective-permute-start | bytes 786440 | tf_op jit(solution)/shard_map/ppermute | solution.py:258
  33.8 13.9 %collective-permute-start.10 = (bf16[1,256,512]{2,1,0:T(8,128)(2,1)}, bf16[1,256,512]{2,1,0:T(8,128)(2,1)}, u32[]{:S(2)}, u32[]{:S(2)}) collective-permute-start(bf16[1,256,512]{2,1,0:T(8,128)(2,1)} %get-tuple-element.107), channel_id=1, source_target_pairs={{0,5},{1,4},{2,7},{3,6},{4,1},{5,0},{6,3},{7,2},{8,13},{9,12},{10,... | collective-permute-start | bytes 786440 | tf_op jit(solution)/shard_map/ppermute | solution.py:258
  34.7 22.7 %collective-permute-start.11 = (bf16[2,256,512]{2,1,0:T(8,128)(2,1)}, bf16[2,256,512]{2,1,0:T(8,128)(2,1)S(1)}, u32[]{:S(2)}, u32[]{:S(2)}) collective-permute-start(bf16[2,256,512]{2,1,0:T(8,128)(2,1)} %get-tuple-element.93.refs_0_), channel_id=1, source_target_pairs={{0,8},{8,0},{16,24},{24,16},{1,9},{9,1},{17,25},{25,17},{2,10},{10... | collective-permute-start | bytes 1572872 | tf_op jit(solution)/shard_map/ppermute | solution.py:258
  35.3 22.1 %collective-permute-start.12 = (bf16[2,256,512]{2,1,0:T(8,128)(2,1)}, bf16[2,256,512]{2,1,0:T(8,128)(2,1)S(1)}, u32[]{:S(2)}, u32[]{:S(2)}) collective-permute-start(bf16[2,256,512]{2,1,0:T(8,128)(2,1)} %get-tuple-element.93.refs_0_), channel_id=1, source_target_pairs={{0,16},{8,24},{16,0},{24,8},{1,17},{9,25},{17,1},{25,9},{2,18},{10... | collective-permute-start | bytes 1572872 | tf_op jit(solution)/shard_map/ppermute | solution.py:258
  41.6 11.2 %collective-permute-start.9 = (bf16[1,256,512]{2,1,0:T(8,128)(2,1)}, bf16[1,256,512]{2,1,0:T(8,128)(2,1)}, u32[]{:S(2)}, u32[]{:S(2)}) collective-permute-start(bf16[1,256,512]{2,1,0:T(8,128)(2,1)} %copy-done.4), channel_id=1, source_target_pairs={{0,3},{1,2},{2,1},{3,0},{4,7},{5,6},{6,5},{7,4},{8,11},{9,10},{10,... | collective-permute-start | bytes 786440 | tf_op jit(solution)/shard_map/ppermute | solution.py:258
  53.9 13.9 %collective-permute-start.14 = (bf16[2,256,512]{2,1,0:T(8,128)(2,1)S(1)}, bf16[2,256,512]{2,1,0:T(8,128)(2,1)S(1)}, u32[]{:S(2)}, u32[]{:S(2)}) collective-permute-start(bf16[2,256,512]{2,1,0:T(8,128)(2,1)S(1)} %get-tuple-element.113.refs_0_), channel_id=1, source_target_pairs={{0,8},{8,0},{16,24},{24,16},{1,9},{9,1},{17,25},{25,17},{2,10},{10... | collective-permute-start | bytes 1572872 | tf_op jit(solution)/shard_map/ppermute | solution.py:258
  54.5 14.8 %collective-permute-start.15 = (bf16[2,256,512]{2,1,0:T(8,128)(2,1)S(1)}, bf16[2,256,512]{2,1,0:T(8,128)(2,1)S(1)}, u32[]{:S(2)}, u32[]{:S(2)}) collective-permute-start(bf16[2,256,512]{2,1,0:T(8,128)(2,1)S(1)} %get-tuple-element.113.refs_0_), channel_id=1, source_target_pairs={{0,16},{8,24},{16,0},{24,8},{1,17},{9,25},{17,1},{25,9},{2,18},{10... | collective-permute-start | bytes 1572872 | tf_op jit(solution)/shard_map/ppermute | solution.py:258
  55.0 9.6 %collective-permute-start.13 = (bf16[1,256,512]{2,1,0:T(8,128)(2,1)S(1)}, bf16[1,256,512]{2,1,0:T(8,128)(2,1)S(1)}, u32[]{:S(2)}, u32[]{:S(2)}) collective-permute-start(bf16[1,256,512]{2,1,0:T(8,128)(2,1)S(1)} %copy-done.5), channel_id=1, source_target_pairs={{0,6},{1,7},{2,4},{3,5},{4,2},{5,3},{6,0},{7,1},{8,14},{9,15},{10,... | collective-permute-start | bytes 786440 | tf_op jit(solution)/shard_map/ppermute | solution.py:258
  57.4 23.1 %collective-permute-start.16 = (bf16[2,256,512]{2,1,0:T(8,128)(2,1)S(1)}, bf16[2,256,512]{2,1,0:T(8,128)(2,1)S(1)}, u32[]{:S(2)}, u32[]{:S(2)}) collective-permute-start(bf16[2,256,512]{2,1,0:T(8,128)(2,1)S(1)} %get-tuple-element.109.refs_1_), channel_id=1, source_target_pairs={{0,16},{8,24},{16,0},{24,8},{1,17},{9,25},{17,1},{25,9},{2,18},{10... | collective-permute-start | bytes 1572872 | tf_op jit(solution)/shard_map/ppermute | solution.py:258
  69.3 17.4 %collective-permute-start.18 = (bf16[2,256,512]{2,1,0:T(8,128)(2,1)S(1)}, bf16[2,256,512]{2,1,0:T(8,128)(2,1)S(1)}, u32[]{:S(2)}, u32[]{:S(2)}) collective-permute-start(bf16[2,256,512]{2,1,0:T(8,128)(2,1)S(1)} %get-tuple-element.123.refs_2_), channel_id=1, source_target_pairs={{0,8},{8,0},{16,24},{24,16},{1,9},{9,1},{17,25},{25,17},{2,10},{10... | collective-permute-start | bytes 1572872 | tf_op jit(solution)/shard_map/ppermute | solution.py:258
  70.8 13.9 %collective-permute-start.17 = (bf16[1,256,512]{2,1,0:T(8,128)(2,1)S(1)}, bf16[1,256,512]{2,1,0:T(8,128)(2,1)S(1)}, u32[]{:S(2)}, u32[]{:S(2)}) collective-permute-start(bf16[1,256,512]{2,1,0:T(8,128)(2,1)S(1)} %get-tuple-element.120), channel_id=1, source_target_pairs={{0,7},{1,6},{2,5},{3,4},{4,3},{5,2},{6,1},{7,0},{8,15},{9,14},{10,... | collective-permute-start | bytes 786440 | tf_op jit(solution)/shard_map/ppermute | solution.py:258
  70.8 19.0 %collective-permute-start.19 = (bf16[1,256,512]{2,1,0:T(8,128)(2,1)S(1)}, bf16[1,256,512]{2,1,0:T(8,128)(2,1)S(1)}, u32[]{:S(2)}, u32[]{:S(2)}) collective-permute-start(bf16[1,256,512]{2,1,0:T(8,128)(2,1)S(1)} %get-tuple-element.129.refs_0_), channel_id=1, source_target_pairs={{0,8},{8,0},{16,24},{24,16},{1,9},{9,1},{17,25},{25,17},{2,10},{10... | collective-permute-start | bytes 786440 | tf_op jit(solution)/shard_map/ppermute | solution.py:258
  71.3 18.5 %collective-permute-start.20 = (bf16[1,256,512]{2,1,0:T(8,128)(2,1)S(1)}, bf16[1,256,512]{2,1,0:T(8,128)(2,1)S(1)}, u32[]{:S(2)}, u32[]{:S(2)}) collective-permute-start(bf16[1,256,512]{2,1,0:T(8,128)(2,1)S(1)} %get-tuple-element.129.refs_0_), channel_id=1, source_target_pairs={{0,16},{8,24},{16,0},{24,8},{1,17},{9,25},{17,1},{25,9},{2,18},{10... | collective-permute-start | bytes 786440 | tf_op jit(solution)/shard_map/ppermute | solution.py:258
  84.6 7.4 %collective-permute-start.21 = (bf16[1,256,512]{2,1,0:T(8,128)(2,1)S(1)}, bf16[1,256,512]{2,1,0:T(8,128)(2,1)S(1)}, u32[]{:S(2)}, u32[]{:S(2)}) collective-permute-start(bf16[1,256,512]{2,1,0:T(8,128)(2,1)S(1)} %get-tuple-element.121.refs_0_), channel_id=1, source_target_pairs={{0,8},{8,0},{16,24},{24,16},{1,9},{9,1},{17,25},{25,17},{2,10},{10... | collective-permute-start | bytes 786440 | tf_op jit(solution)/shard_map/ppermute | solution.py:258
  86.1 9.0 %collective-permute-start.22 = (bf16[1,256,512]{2,1,0:T(8,128)(2,1)S(1)}, bf16[1,256,512]{2,1,0:T(8,128)(2,1)S(1)}, u32[]{:S(2)}, u32[]{:S(2)}) collective-permute-start(bf16[1,256,512]{2,1,0:T(8,128)(2,1)S(1)} %get-tuple-element.121.refs_0_), channel_id=1, source_target_pairs={{0,16},{8,24},{16,0},{24,8},{1,17},{9,25},{17,1},{25,9},{2,18},{10... | collective-permute-start | bytes 786440 | tf_op jit(solution)/shard_map/ppermute | solution.py:258
  89.8 8.1 %collective-permute-start.23 = (bf16[1,256,512]{2,1,0:T(8,128)(2,1)S(1)}, bf16[1,256,512]{2,1,0:T(8,128)(2,1)S(1)}, u32[]{:S(2)}, u32[]{:S(2)}) collective-permute-start(bf16[1,256,512]{2,1,0:T(8,128)(2,1)S(1)} %get-tuple-element.133.refs_1_), channel_id=1, source_target_pairs={{0,16},{8,24},{16,0},{24,8},{1,17},{9,25},{17,1},{25,9},{2,18},{10... | collective-permute-start | bytes 786440 | tf_op jit(solution)/shard_map/ppermute | solution.py:258
  (8 other events, 51.5 us)

commit v13 on v12

--- a/solution.py
+++ b/solution.py
@@ -12,7 +12,7 @@
 QB = 128
 GROUP = 32
 VMEM_LIMIT = 60 * 1024 * 1024
-LATER_LIMIT = 56 * 1024 * 1024
+LATER_LIMIT = 52 * 1024 * 1024
 PRODUCT_LIMIT = 16 * 1024 * 1024
 
 beta_one = 0.9
@@ -306,16 +306,16 @@
     if fenced:
         one, two = (2, 4), (3, 5)
         plan = [
-            ([(0, 1), (0, 2), (1, 0)], [(1, 0, 1), (1, 0, 2)], []),
-            ([(2, 0), (4, 0)], [], [5]),
-            ([(1, 1), (1, 2)], [(1, 2, 1), (0, 1, 2)], []),
+            ([(0, 1), (0, 2), (1, 0)], [(1, 0, 1), (1, 0, 2), (0, 1, 2)], []),
+            ([(2, 0), (4, 0)], [], []),
+            ([(1, 1), (1, 2)], [(1, 2, 1)], []),
+            ([(1, 3)], [], []),
             (one, [(one, 0, 1), (one, 0, 2)], []),
-            ([(0, 3), (1, 3)], [], [3]),
-            (two, [(two, 0, 1), (two, 0, 2)], [6]),
-            ([(one, 1), (one, 2)], [(one, 1, 2)], []),
-            ([(6, 0), (two, 1), (two, 2)], [(two, 2, 1), (6, 0, 1), (6, 0, 2)], [7]),
-            ([(one, 3)], [], []),
-            ([(7, 0)], [(7, 0, 1), (7, 0, 2)], []),
+            ([(0, 3)], [], [6]),
+            (two, [(two, 0, 1), (two, 0, 2)], []),
+            ([(6, 0), (one, 1), (one, 2)], [(one, 1, 2)], [7]),
+            ([(two, 1), (two, 2)], [(two, 2, 1), (6, 0, 1), (6, 0, 2)], []),
+            ([(one, 3), (7, 0)], [(7, 0, 1), (7, 0, 2)], []),
             ([(two, 3)], [], []),
             ([(6, 1), (6, 2)], [(6, 1, 2)], []),
             ([(7, 1), (7, 2)], [(7, 2, 1)], []),
@@ -329,8 +329,7 @@
         ready.add((0, 0))
         send(0, 0, 1)
         send(0, 0, 2)
-        adam(((3,), (5,), (6,), (7,)), LATER_LIMIT)
-        for keys, sending, leaving in plan:
+        for step, (keys, sending, leaving) in enumerate(plan):
             if isinstance(keys, tuple):
                 pieces = [held[block][0] for block in keys]
                 token, held[keys][0] = join(state["token"][0], pieces, (0, 0))
@@ -342,7 +341,11 @@
                 deliver(block)
             for key in sending:
                 send(*key)
-            for block in list(waiting):
+            if not step:
+                adam(((3,), (5,), (6,), (7,)), LATER_LIMIT)
+                deliver(5)
+                deliver(3)
+            for block in list(waiting) if step > 3 else []:
                 if all((block, member) in ready for member in range(replicas)):
                     multiply(block)
                     waiting.remove(block)

time: 104 us -> 97 us (0.933)
  the two profiles are of different devices: /device:TPU:0 before, /device:TPU:8 now
where the time goes in v13:
time: 97 us; the launch traced here: 96.7 us
  waiting for transfers between devices  37.1 us (38%)
  Pallas kernels  30.6 us (32%)
  starting transfers between devices  26.5 us (27%)
  local copies, waits for them, and re-layouts  1.59 us (2%)
    ppermute x25, waiting for transfers between devices, swap(): return lax.ppermute(value, axis, [(i, i ^ mask) for i in range(size)])  37.1 us
    ppermute x25, starting transfers between devices, swap(): return lax.ppermute(value, axis, [(i, i ^ mask) for i in range(size)])  26.5 us
    pallas_call x6, Pallas kernels, product(): pl.pallas_call(functools.partial(product_kernel, slabs), grid_spec=pltpu....  15.2 us
    pallas_call x2, Pallas kernels, adam_blocks(): pl.pallas_call(functools.partial(adam_kernel, groups, passed), in_specs=[...  13.5 us
  transfers between devices with their start and end apart: 25, of which 8 were waited for; matrix products, arithmetic and copies ran while one was open for 0% of the time, Pallas kernels for 23%

profile of v13, /device:TPU:8, one launch (start us, length us, event | category | flops | bytes accessed | tf_op | source)
XLA Modules:
  0.0 96.7 jit_solution(13195219270182453962)
XLA Ops:
  0.6 6.6 %adam_quantize.2 = (f32[8,256,512]{2,1,0:T(8,128)}, bf16[8,256,512]{2,1,0:T(8,128)(2,1)}, bf16[8,256,512]{2,1,0:T(8,128)(2,1)}, bf16[1,256,512]{2,1,0:T(8,128)(2...) custom-call(s32[8]{0:T(128)} %owner.3, ...), custom_call_target="tpu_custom_call" | custom-call | bytes 65536 | tf_op jit(solution)/shard_map/adam_quantize/pallas_call | solution.py:170
  7.2 1.6 %collective-permute-start = (bf16[1,256,512]{2,1,0:T(8,128)(2,1)}, bf16[1,256,512]{2,1,0:T(8,128)(2,1)S(1)}, u32[]{:S(2)}, u32[]{:S(2)}) collective-permute-start(bf16[1,256,512]{2,1,0:T(8,128)(2,1)} %get-tuple-element.77.refs_0_), channel_id=1, source_target_pairs={{0,8},{8,0},{16,24},{24,16},{1,9},{9,1},{17,25},{25,17},{2,10},{10... | collective-permute-start | bytes 786440 | tf_op jit(solution)/shard_map/ppermute | solution.py:258
  8.8 1.5 %collective-permute-start.1 = (bf16[1,256,512]{2,1,0:T(8,128)(2,1)}, bf16[1,256,512]{2,1,0:T(8,128)(2,1)S(1)}, u32[]{:S(2)}, u32[]{:S(2)}) collective-permute-start(bf16[1,256,512]{2,1,0:T(8,128)(2,1)} %get-tuple-element.77.refs_0_), channel_id=1, source_target_pairs={{0,16},{8,24},{16,0},{24,8},{1,17},{9,25},{17,1},{25,9},{2,18},{10... | collective-permute-start | bytes 786440 | tf_op jit(solution)/shard_map/ppermute | solution.py:258
  10.7 2.6 %collective-permute-start.4 = (bf16[1,256,512]{2,1,0:T(8,128)(2,1)}, bf16[1,256,512]{2,1,0:T(8,128)(2,1)S(1)}, u32[]{:S(2)}, u32[]{:S(2)}) collective-permute-start(bf16[1,256,512]{2,1,0:T(8,128)(2,1)} %get-tuple-element.88), channel_id=1, source_target_pairs={{0,4},{1,5},{2,6},{3,7},{4,0},{5,1},{6,2},{7,3},{8,12},{9,13},{10,... | collective-permute-start | bytes 786440 | tf_op jit(solution)/shard_map/ppermute | solution.py:258
  13.3 2.2 %collective-permute-done.refs_1_ = bf16[1,256,512]{2,1,0:T(8,128)(2,1)S(1)} collective-permute-done((bf16[1,256,512]{2,1,0:T(8,128)(2,1)}, bf16[1,256,512]{2,1,0:T(8,128)(2,1)S(1)}, u32[]{:S(2)}, u32[]{:S(2)}) %collective-permute-start) | collective-permute-done | bytes 262176 | tf_op jit(solution)/shard_map/ppermute | solution.py:258
  17.3 1.5 %collective-permute-start.6 = (bf16[1,256,512]{2,1,0:T(8,128)(2,1)S(1)}, bf16[1,256,512]{2,1,0:T(8,128)(2,1)S(1)}, u32[]{:S(2)}, u32[]{:S(2)}) collective-permute-start(bf16[1,256,512]{2,1,0:T(8,128)(2,1)S(1)} %get-tuple-element.85.refs_0_), channel_id=1, source_target_pairs={{0,16},{8,24},{16,0},{24,8},{1,17},{9,25},{17,1},{25,9},{2,18},{10... | collective-permute-start | bytes 786440 | tf_op jit(solution)/shard_map/ppermute | solution.py:258
  18.8 6.9 %adam_quantize.3 = (f32[8,256,512]{2,1,0:T(8,128)}, bf16[8,256,512]{2,1,0:T(8,128)(2,1)}, bf16[8,256,512]{2,1,0:T(8,128)(2,1)}, bf16[1,256,512]{2,1,0:T(8,128)(2...) custom-call(s32[8]{0:T(128)S(1)} %copy-done.8, ...), custom_call_target="tpu_custom_call", output_to_operand_aliasing={{0}: (5, {}), {1}: (6, {}), {2}: (7, {}), {7}: (8, {})} | custom-call | bytes 65536 | tf_op jit(solution)/shard_map/adam_quantize/pallas_call | solution.py:170
  28.5 2.8 %collective-permute-start.9 = (bf16[1,256,512]{2,1,0:T(8,128)(2,1)}, bf16[1,256,512]{2,1,0:T(8,128)(2,1)}, u32[]{:S(2)}, u32[]{:S(2)}) collective-permute-start(bf16[1,256,512]{2,1,0:T(8,128)(2,1)} %get-tuple-element.104), channel_id=1, source_target_pairs={{0,3},{1,2},{2,1},{3,0},{4,7},{5,6},{6,5},{7,4},{8,11},{9,10},{10,... | collective-permute-start | bytes 786440 | tf_op jit(solution)/shard_map/ppermute | solution.py:258
  31.3 2.7 %collective-permute-done.7.refs_1_ = bf16[1,256,512]{2,1,0:T(8,128)(2,1)S(1)} collective-permute-done((bf16[1,256,512]{2,1,0:T(8,128)(2,1)S(1)}, bf16[1,256,512]{2,1,0:T(8,128)(2,1)S(1)}, u32[]{:S(2)}, u32[]{:S(2)}) %collective-permute-start.7) | collective-permute-done | bytes 262176 | tf_op jit(solution)/shard_map/ppermute | solution.py:258
  37.0 2.0 %expert_product.6 = (f32[135168,128]{1,0:T(8,128)}, bf16[384,4096]{1,0:T(8,128)(2,1)}) custom-call(s32[8]{0:T(128)S(1)} %iota_xor_fusion.1.sources, s32[4]{0:T(128)S(1)} %select_reduce_fusion.places, bf16[384,1024]{1,0:T(8,128)(2,1)S(1)} %bitcast.2, bf16[1,256,512]{2,1,0:T(8,128)(2,1)S(1)} %get-tuple-element.85.refs_0_, ...), custom_call_target="tpu_custom_call", output_to_operand_aliasing={{0}: (7, {})} | custom-call | bytes 65536 | tf_op jit(solution)/shard_map/expert_product/pallas_call | solution.py:238
  39.1 2.0 %expert_product.7 = (f32[135168,128]{1,0:T(8,128)}, bf16[384,4096]{1,0:T(8,128)(2,1)}) custom-call(s32[8]{0:T(128)S(1)} %iota_xor_fusion.1.sources, s32[4]{0:T(128)S(1)} %select_reduce_fusion.places, bf16[384,1024]{1,0:T(8,128)(2,1)S(1)} %bitcast.3, bf16[1,256,512]{2,1,0:T(8,128)(2,1)S(1)} %copy-done.3, ...), custom_call_target="tpu_custom_call", output_to_operand_aliasing={{0}: (7, {}), {1}: (8, {})} | custom-call | bytes 65536 | tf_op jit(solution)/shard_map/expert_product/pallas_call | solution.py:238
  44.4 1.5 %collective-permute-start.15 = (bf16[2,256,512]{2,1,0:T(8,128)(2,1)S(1)}, bf16[2,256,512]{2,1,0:T(8,128)(2,1)S(1)}, u32[]{:S(2)}, u32[]{:S(2)}) collective-permute-start(bf16[2,256,512]{2,1,0:T(8,128)(2,1)S(1)} %get-tuple-element.111.refs_0_), channel_id=1, source_target_pairs={{0,16},{8,24},{16,0},{24,8},{1,17},{9,25},{17,1},{25,9},{2,18},{10... | collective-permute-start | bytes 1572872 | tf_op jit(solution)/shard_map/ppermute | solution.py:258
  45.9 1.6 %collective-permute-start.11 = (bf16[1,256,512]{2,1,0:T(8,128)(2,1)S(1)}, bf16[1,256,512]{2,1,0:T(8,128)(2,1)S(1)}, u32[]{:S(2)}, u32[]{:S(2)}) collective-permute-start(bf16[1,256,512]{2,1,0:T(8,128)(2,1)S(1)} %get-tuple-element.107), channel_id=1, source_target_pairs={{0,6},{1,7},{2,4},{3,5},{4,2},{5,3},{6,0},{7,1},{8,14},{9,15},{10,... | collective-permute-start | bytes 786440 | tf_op jit(solution)/shard_map/ppermute | solution.py:258
  47.5 11.8 %collective-permute-done.11.refs_1_ = bf16[1,256,512]{2,1,0:T(8,128)(2,1)S(1)} collective-permute-done((bf16[1,256,512]{2,1,0:T(8,128)(2,1)S(1)}, bf16[1,256,512]{2,1,0:T(8,128)(2,1)S(1)}, u32[]{:S(2)}, u32[]{:S(2)}) %collective-permute-start.11) | collective-permute-done | bytes 262176 | tf_op jit(solution)/shard_map/ppermute | solution.py:258
  59.9 1.5 %collective-permute-start.18 = (bf16[2,256,512]{2,1,0:T(8,128)(2,1)S(1)}, bf16[2,256,512]{2,1,0:T(8,128)(2,1)S(1)}, u32[]{:S(2)}, u32[]{:S(2)}) collective-permute-start(bf16[2,256,512]{2,1,0:T(8,128)(2,1)S(1)} %get-tuple-element.117.refs_2_), channel_id=1, source_target_pairs={{0,8},{8,0},{16,24},{24,16},{1,9},{9,1},{17,25},{25,17},{2,10},{10... | collective-permute-start | bytes 1572872 | tf_op jit(solution)/shard_map/ppermute | solution.py:258
  61.9 1.5 %collective-permute-start.20 = (bf16[1,256,512]{2,1,0:T(8,128)(2,1)S(1)}, bf16[1,256,512]{2,1,0:T(8,128)(2,1)S(1)}, u32[]{:S(2)}, u32[]{:S(2)}) collective-permute-start(bf16[1,256,512]{2,1,0:T(8,128)(2,1)S(1)} %get-tuple-element.127.refs_0_), channel_id=1, source_target_pairs={{0,16},{8,24},{16,0},{24,8},{1,17},{9,25},{17,1},{25,9},{2,18},{10... | collective-permute-start | bytes 786440 | tf_op jit(solution)/shard_map/ppermute | solution.py:258
  63.4 12.0 %collective-permute-done.17.refs_2_ = bf16[1,256,512]{2,1,0:T(8,128)(2,1)S(1)} collective-permute-done((bf16[1,256,512]{2,1,0:T(8,128)(2,1)S(1)}, bf16[1,256,512]{2,1,0:T(8,128)(2,1)S(1)}, u32[]{:S(2)}, u32[]{:S(2)}) %collective-permute-start.17) | collective-permute-done | bytes 262176 | tf_op jit(solution)/shard_map/ppermute | solution.py:258
  75.8 1.5 %collective-permute-start.22 = (bf16[1,256,512]{2,1,0:T(8,128)(2,1)S(1)}, bf16[1,256,512]{2,1,0:T(8,128)(2,1)S(1)}, u32[]{:S(2)}, u32[]{:S(2)}) collective-permute-start(bf16[1,256,512]{2,1,0:T(8,128)(2,1)S(1)} %get-tuple-element.115.refs_0_), channel_id=1, source_target_pairs={{0,16},{8,24},{16,0},{24,8},{1,17},{9,25},{17,1},{25,9},{2,18},{10... | collective-permute-start | bytes 786440 | tf_op jit(solution)/shard_map/ppermute | solution.py:258
  77.4 4.1 %expert_product.8 = (f32[135168,128]{1,0:T(8,128)}, bf16[384,4096]{1,0:T(8,128)(2,1)}) custom-call(s32[8]{0:T(128)S(1)} %iota_xor_fusion.1.sources, s32[4]{0:T(128)S(1)} %select_reduce_fusion.places, bf16[384,1024]{1,0:T(8,128)(2,1)S(1)} %bitcast.4, bf16[2,256,512]{2,1,0:T(8,128)(2,1)} %get-tuple-element.108.refs_0_, ...), custom_call_target="tpu_custom_call", output_to_operand_aliasing={{0}: (7, {}), {1}: (8, {})} | custom-call | bytes 65536 | tf_op jit(solution)/shard_map/expert_product/pallas_call | solution.py:238
  81.5 3.1 %expert_product.9 = (f32[135168,128]{1,0:T(8,128)}, bf16[384,4096]{1,0:T(8,128)(2,1)}) custom-call(s32[8]{0:T(128)S(1)} %iota_xor_fusion.1.sources, s32[4]{0:T(128)S(1)} %select_reduce_fusion.places, bf16[384,1024]{1,0:T(8,128)(2,1)S(1)} %bitcast.5, ...), custom_call_target="tpu_custom_call", output_to_operand_aliasing={{0}: (7, {}), {1}: (8, {})} | custom-call | bytes 65536 | tf_op jit(solution)/shard_map/expert_product/pallas_call | solution.py:238
  85.1 1.6 %collective-permute-start.24 = (bf16[1,256,512]{2,1,0:T(8,128)(2,1)S(1)}, bf16[1,256,512]{2,1,0:T(8,128)(2,1)S(1)}, u32[]{:S(2)}, u32[]{:S(2)}) collective-permute-start(bf16[1,256,512]{2,1,0:T(8,128)(2,1)S(1)} %get-tuple-element.130.refs_2_), channel_id=1, source_target_pairs={{0,8},{8,0},{16,24},{24,16},{1,9},{9,1},{17,25},{25,17},{2,10},{10... | collective-permute-start | bytes 786440 | tf_op jit(solution)/shard_map/ppermute | solution.py:258
  86.8 5.9 %collective-permute-done.23.refs_1_ = bf16[1,256,512]{2,1,0:T(8,128)(2,1)S(1)} collective-permute-done((bf16[1,256,512]{2,1,0:T(8,128)(2,1)S(1)}, bf16[1,256,512]{2,1,0:T(8,128)(2,1)S(1)}, u32[]{:S(2)}, u32[]{:S(2)}) %collective-permute-start.23) | collective-permute-done | bytes 262176 | tf_op jit(solution)/shard_map/ppermute | solution.py:258
  92.7 2.0 %expert_product.10 = (f32[135168,128]{1,0:T(8,128)}, bf16[384,4096]{1,0:T(8,128)(2,1)}) custom-call(s32[8]{0:T(128)S(1)} %iota_xor_fusion.1.sources, s32[4]{0:T(128)S(1)} %select_reduce_fusion.places, bf16[384,1024]{1,0:T(8,128)(2,1)S(1)} %bitcast.6, ...), custom_call_target="tpu_custom_call", output_to_operand_aliasing={{0}: (7, {}), {1}: (8, {})} | custom-call | bytes 65536 | tf_op jit(solution)/shard_map/expert_product/pallas_call | solution.py:238
  94.7 2.0 %expert_product.11 = (f32[135168,128]{1,0:T(8,128)}, bf16[384,4096]{1,0:T(8,128)(2,1)}) custom-call(s32[8]{0:T(128)S(1)} %iota_xor_fusion.1.sources, s32[4]{0:T(128)S(1)} %select_reduce_fusion.places, bf16[384,1024]{1,0:T(8,128)(2,1)S(1)} %bitcast.7, ...), custom_call_target="tpu_custom_call", output_to_operand_aliasing={{0}: (7, {}), {1}: (8, {})} | custom-call | bytes 65536 | tf_op jit(solution)/shard_map/expert_product/pallas_call | solution.py:238
  (72 shorter events, 13.5 us)
Async XLA Ops:
  7.2 8.3 %collective-permute-start = (bf16[1,256,512]{2,1,0:T(8,128)(2,1)}, bf16[1,256,512]{2,1,0:T(8,128)(2,1)S(1)}, u32[]{:S(2)}, u32[]{:S(2)}) collective-permute-start(bf16[1,256,512]{2,1,0:T(8,128)(2,1)} %get-tuple-element.77.refs_0_), channel_id=1, source_target_pairs={{0,8},{8,0},{16,24},{24,16},{1,9},{9,1},{17,25},{25,17},{2,10},{10... | collective-permute-start | bytes 786440 | tf_op jit(solution)/shard_map/ppermute | solution.py:258
  8.8 8.0 %collective-permute-start.1 = (bf16[1,256,512]{2,1,0:T(8,128)(2,1)}, bf16[1,256,512]{2,1,0:T(8,128)(2,1)S(1)}, u32[]{:S(2)}, u32[]{:S(2)}) collective-permute-start(bf16[1,256,512]{2,1,0:T(8,128)(2,1)} %get-tuple-element.77.refs_0_), channel_id=1, source_target_pairs={{0,16},{8,24},{16,0},{24,8},{1,17},{9,25},{17,1},{25,9},{2,18},{10... | collective-permute-start | bytes 786440 | tf_op jit(solution)/shard_map/ppermute | solution.py:258
  10.3 15.5 %collective-permute-start.3 = (bf16[1,256,512]{2,1,0:T(8,128)(2,1)}, bf16[1,256,512]{2,1,0:T(8,128)(2,1)S(1)}, u32[]{:S(2)}, u32[]{:S(2)}) collective-permute-start(bf16[1,256,512]{2,1,0:T(8,128)(2,1)} %get-tuple-element.87), channel_id=1, source_target_pairs={{0,2},{1,3},{2,0},{3,1},{4,6},{5,7},{6,4},{7,5},{8,10},{9,11},{10,... | collective-permute-start | bytes 786440 | tf_op jit(solution)/shard_map/ppermute | solution.py:258
  10.7 15.2 %collective-permute-start.4 = (bf16[1,256,512]{2,1,0:T(8,128)(2,1)}, bf16[1,256,512]{2,1,0:T(8,128)(2,1)S(1)}, u32[]{:S(2)}, u32[]{:S(2)}) collective-permute-start(bf16[1,256,512]{2,1,0:T(8,128)(2,1)} %get-tuple-element.88), channel_id=1, source_target_pairs={{0,4},{1,5},{2,6},{3,7},{4,0},{5,1},{6,2},{7,3},{8,12},{9,13},{10,... | collective-permute-start | bytes 786440 | tf_op jit(solution)/shard_map/ppermute | solution.py:258
  16.8 9.2 %collective-permute-start.5 = (bf16[1,256,512]{2,1,0:T(8,128)(2,1)S(1)}, bf16[1,256,512]{2,1,0:T(8,128)(2,1)S(1)}, u32[]{:S(2)}, u32[]{:S(2)}) collective-permute-start(bf16[1,256,512]{2,1,0:T(8,128)(2,1)S(1)} %get-tuple-element.85.refs_0_), channel_id=1, source_target_pairs={{0,8},{8,0},{16,24},{24,16},{1,9},{9,1},{17,25},{25,17},{2,10},{10... | collective-permute-start | bytes 786440 | tf_op jit(solution)/shard_map/ppermute | solution.py:258
  17.3 8.7 %collective-permute-start.6 = (bf16[1,256,512]{2,1,0:T(8,128)(2,1)S(1)}, bf16[1,256,512]{2,1,0:T(8,128)(2,1)S(1)}, u32[]{:S(2)}, u32[]{:S(2)}) collective-permute-start(bf16[1,256,512]{2,1,0:T(8,128)(2,1)S(1)} %get-tuple-element.85.refs_0_), channel_id=1, source_target_pairs={{0,16},{8,24},{16,0},{24,8},{1,17},{9,25},{17,1},{25,9},{2,18},{10... | collective-permute-start | bytes 786440 | tf_op jit(solution)/shard_map/ppermute | solution.py:258
  26.5 7.4 %collective-permute-start.7 = (bf16[1,256,512]{2,1,0:T(8,128)(2,1)S(1)}, bf16[1,256,512]{2,1,0:T(8,128)(2,1)S(1)}, u32[]{:S(2)}, u32[]{:S(2)}) collective-permute-start(bf16[1,256,512]{2,1,0:T(8,128)(2,1)S(1)} %get-tuple-element.91.refs_2_), channel_id=1, source_target_pairs={{0,8},{8,0},{16,24},{24,16},{1,9},{9,1},{17,25},{25,17},{2,10},{10... | collective-permute-start | bytes 786440 | tf_op jit(solution)/shard_map/ppermute | solution.py:258
  28.0 11.0 %collective-permute-start.8 = (bf16[1,256,512]{2,1,0:T(8,128)(2,1)S(1)}, bf16[1,256,512]{2,1,0:T(8,128)(2,1)S(1)}, u32[]{:S(2)}, u32[]{:S(2)}) collective-permute-start(bf16[1,256,512]{2,1,0:T(8,128)(2,1)S(1)} %get-tuple-element.83.refs_1_), channel_id=1, source_target_pairs={{0,16},{8,24},{16,0},{24,8},{1,17},{9,25},{17,1},{25,9},{2,18},{10... | collective-permute-start | bytes 786440 | tf_op jit(solution)/shard_map/ppermute | solution.py:258
  28.5 12.6 %collective-permute-start.10 = (bf16[1,256,512]{2,1,0:T(8,128)(2,1)}, bf16[1,256,512]{2,1,0:T(8,128)(2,1)}, u32[]{:S(2)}, u32[]{:S(2)}) collective-permute-start(bf16[1,256,512]{2,1,0:T(8,128)(2,1)} %get-tuple-element.105), channel_id=1, source_target_pairs={{0,5},{1,4},{2,7},{3,6},{4,1},{5,0},{6,3},{7,2},{8,13},{9,12},{10,... | collective-permute-start | bytes 786440 | tf_op jit(solution)/shard_map/ppermute | solution.py:258
  28.5 13.6 %collective-permute-start.9 = (bf16[1,256,512]{2,1,0:T(8,128)(2,1)}, bf16[1,256,512]{2,1,0:T(8,128)(2,1)}, u32[]{:S(2)}, u32[]{:S(2)}) collective-permute-start(bf16[1,256,512]{2,1,0:T(8,128)(2,1)} %get-tuple-element.104), channel_id=1, source_target_pairs={{0,3},{1,2},{2,1},{3,0},{4,7},{5,6},{6,5},{7,4},{8,11},{9,10},{10,... | collective-permute-start | bytes 786440 | tf_op jit(solution)/shard_map/ppermute | solution.py:258
  34.8 24.5 %collective-permute-start.12 = (bf16[2,256,512]{2,1,0:T(8,128)(2,1)}, bf16[2,256,512]{2,1,0:T(8,128)(2,1)S(1)}, u32[]{:S(2)}, u32[]{:S(2)}) collective-permute-start(bf16[2,256,512]{2,1,0:T(8,128)(2,1)} %get-tuple-element.108.refs_0_), channel_id=1, source_target_pairs={{0,8},{8,0},{16,24},{24,16},{1,9},{9,1},{17,25},{25,17},{2,10},{10... | collective-permute-start | bytes 1572872 | tf_op jit(solution)/shard_map/ppermute | solution.py:258
  35.4 23.9 %collective-permute-start.13 = (bf16[2,256,512]{2,1,0:T(8,128)(2,1)}, bf16[2,256,512]{2,1,0:T(8,128)(2,1)S(1)}, u32[]{:S(2)}, u32[]{:S(2)}) collective-permute-start(bf16[2,256,512]{2,1,0:T(8,128)(2,1)} %get-tuple-element.108.refs_0_), channel_id=1, source_target_pairs={{0,16},{8,24},{16,0},{24,8},{1,17},{9,25},{17,1},{25,9},{2,18},{10... | collective-permute-start | bytes 1572872 | tf_op jit(solution)/shard_map/ppermute | solution.py:258
  43.2 16.7 %collective-permute-start.14 = (bf16[2,256,512]{2,1,0:T(8,128)(2,1)S(1)}, bf16[2,256,512]{2,1,0:T(8,128)(2,1)S(1)}, u32[]{:S(2)}, u32[]{:S(2)}) collective-permute-start(bf16[2,256,512]{2,1,0:T(8,128)(2,1)S(1)} %get-tuple-element.111.refs_0_), channel_id=1, source_target_pairs={{0,8},{8,0},{16,24},{24,16},{1,9},{9,1},{17,25},{25,17},{2,10},{10... | collective-permute-start | bytes 1572872 | tf_op jit(solution)/shard_map/ppermute | solution.py:258
  44.4 15.5 %collective-permute-start.15 = (bf16[2,256,512]{2,1,0:T(8,128)(2,1)S(1)}, bf16[2,256,512]{2,1,0:T(8,128)(2,1)S(1)}, u32[]{:S(2)}, u32[]{:S(2)}) collective-permute-start(bf16[2,256,512]{2,1,0:T(8,128)(2,1)S(1)} %get-tuple-element.111.refs_0_), channel_id=1, source_target_pairs={{0,16},{8,24},{16,0},{24,8},{1,17},{9,25},{17,1},{25,9},{2,18},{10... | collective-permute-start | bytes 1572872 | tf_op jit(solution)/shard_map/ppermute | solution.py:258
  45.9 13.3 %collective-permute-start.11 = (bf16[1,256,512]{2,1,0:T(8,128)(2,1)S(1)}, bf16[1,256,512]{2,1,0:T(8,128)(2,1)S(1)}, u32[]{:S(2)}, u32[]{:S(2)}) collective-permute-start(bf16[1,256,512]{2,1,0:T(8,128)(2,1)S(1)} %get-tuple-element.107), channel_id=1, source_target_pairs={{0,6},{1,7},{2,4},{3,5},{4,2},{5,3},{6,0},{7,1},{8,14},{9,15},{10,... | collective-permute-start | bytes 786440 | tf_op jit(solution)/shard_map/ppermute | solution.py:258
  59.3 16.1 %collective-permute-start.16 = (bf16[2,256,512]{2,1,0:T(8,128)(2,1)S(1)}, bf16[2,256,512]{2,1,0:T(8,128)(2,1)S(1)}, u32[]{:S(2)}, u32[]{:S(2)}) collective-permute-start(bf16[2,256,512]{2,1,0:T(8,128)(2,1)S(1)} %get-tuple-element.113.refs_1_), channel_id=1, source_target_pairs={{0,16},{8,24},{16,0},{24,8},{1,17},{9,25},{17,1},{25,9},{2,18},{10... | collective-permute-start | bytes 1572872 | tf_op jit(solution)/shard_map/ppermute | solution.py:258
  59.9 21.6 %collective-permute-start.18 = (bf16[2,256,512]{2,1,0:T(8,128)(2,1)S(1)}, bf16[2,256,512]{2,1,0:T(8,128)(2,1)S(1)}, u32[]{:S(2)}, u32[]{:S(2)}) collective-permute-start(bf16[2,256,512]{2,1,0:T(8,128)(2,1)S(1)} %get-tuple-element.117.refs_2_), channel_id=1, source_target_pairs={{0,8},{8,0},{16,24},{24,16},{1,9},{9,1},{17,25},{25,17},{2,10},{10... | collective-permute-start | bytes 1572872 | tf_op jit(solution)/shard_map/ppermute | solution.py:258
  61.4 14.1 %collective-permute-start.17 = (bf16[1,256,512]{2,1,0:T(8,128)(2,1)S(1)}, bf16[1,256,512]{2,1,0:T(8,128)(2,1)S(1)}, u32[]{:S(2)}, u32[]{:S(2)}) collective-permute-start(bf16[1,256,512]{2,1,0:T(8,128)(2,1)S(1)} %get-tuple-element.114), channel_id=1, source_target_pairs={{0,7},{1,6},{2,5},{3,4},{4,3},{5,2},{6,1},{7,0},{8,15},{9,14},{10,... | collective-permute-start | bytes 786440 | tf_op jit(solution)/shard_map/ppermute | solution.py:258
  61.4 23.2 %collective-permute-start.19 = (bf16[1,256,512]{2,1,0:T(8,128)(2,1)S(1)}, bf16[1,256,512]{2,1,0:T(8,128)(2,1)S(1)}, u32[]{:S(2)}, u32[]{:S(2)}) collective-permute-start(bf16[1,256,512]{2,1,0:T(8,128)(2,1)S(1)} %get-tuple-element.127.refs_0_), channel_id=1, source_target_pairs={{0,8},{8,0},{16,24},{24,16},{1,9},{9,1},{17,25},{25,17},{2,10},{10... | collective-permute-start | bytes 786440 | tf_op jit(solution)/shard_map/ppermute | solution.py:258
  61.9 22.7 %collective-permute-start.20 = (bf16[1,256,512]{2,1,0:T(8,128)(2,1)S(1)}, bf16[1,256,512]{2,1,0:T(8,128)(2,1)S(1)}, u32[]{:S(2)}, u32[]{:S(2)}) collective-permute-start(bf16[1,256,512]{2,1,0:T(8,128)(2,1)S(1)} %get-tuple-element.127.refs_0_), channel_id=1, source_target_pairs={{0,16},{8,24},{16,0},{24,8},{1,17},{9,25},{17,1},{25,9},{2,18},{10... | collective-permute-start | bytes 786440 | tf_op jit(solution)/shard_map/ppermute | solution.py:258
  75.4 9.7 %collective-permute-start.21 = (bf16[1,256,512]{2,1,0:T(8,128)(2,1)S(1)}, bf16[1,256,512]{2,1,0:T(8,128)(2,1)S(1)}, u32[]{:S(2)}, u32[]{:S(2)}) collective-permute-start(bf16[1,256,512]{2,1,0:T(8,128)(2,1)S(1)} %get-tuple-element.115.refs_0_), channel_id=1, source_target_pairs={{0,8},{8,0},{16,24},{24,16},{1,9},{9,1},{17,25},{25,17},{2,10},{10... | collective-permute-start | bytes 786440 | tf_op jit(solution)/shard_map/ppermute | solution.py:258
  75.8 9.3 %collective-permute-start.22 = (bf16[1,256,512]{2,1,0:T(8,128)(2,1)S(1)}, bf16[1,256,512]{2,1,0:T(8,128)(2,1)S(1)}, u32[]{:S(2)}, u32[]{:S(2)}) collective-permute-start(bf16[1,256,512]{2,1,0:T(8,128)(2,1)S(1)} %get-tuple-element.115.refs_0_), channel_id=1, source_target_pairs={{0,16},{8,24},{16,0},{24,8},{1,17},{9,25},{17,1},{25,9},{2,18},{10... | collective-permute-start | bytes 786440 | tf_op jit(solution)/shard_map/ppermute | solution.py:258
  84.6 8.1 %collective-permute-start.23 = (bf16[1,256,512]{2,1,0:T(8,128)(2,1)S(1)}, bf16[1,256,512]{2,1,0:T(8,128)(2,1)S(1)}, u32[]{:S(2)}, u32[]{:S(2)}) collective-permute-start(bf16[1,256,512]{2,1,0:T(8,128)(2,1)S(1)} %get-tuple-element.131.refs_1_), channel_id=1, source_target_pairs={{0,16},{8,24},{16,0},{24,8},{1,17},{9,25},{17,1},{25,9},{2,18},{10... | collective-permute-start | bytes 786440 | tf_op jit(solution)/shard_map/ppermute | solution.py:258
  85.1 9.6 %collective-permute-start.24 = (bf16[1,256,512]{2,1,0:T(8,128)(2,1)S(1)}, bf16[1,256,512]{2,1,0:T(8,128)(2,1)S(1)}, u32[]{:S(2)}, u32[]{:S(2)}) collective-permute-start(bf16[1,256,512]{2,1,0:T(8,128)(2,1)S(1)} %get-tuple-element.130.refs_2_), channel_id=1, source_target_pairs={{0,8},{8,0},{16,24},{24,16},{1,9},{9,1},{17,25},{25,17},{2,10},{10... | collective-permute-start | bytes 786440 | tf_op jit(solution)/shard_map/ppermute | solution.py:258
  (11 other events, 56.3 us)

commit v14 on v13

--- a/solution.py
+++ b/solution.py
@@ -272,7 +272,7 @@
     ).astype(jnp.int32)
 
     fenced = (replicas, shards) == PLANNED
-    held, made, ready = collections.defaultdict(dict), {}, set()
+    held, made = collections.defaultdict(dict), {}
     state = {"adam": (), "token": (), "out": ()}
 
     def adam(groups, limit=VMEM_LIMIT):
@@ -294,7 +294,6 @@
         made.update(zip(leaving, passed[len(keys) :]))
         for (block, member), array in zip(keys, passed):
             held[block][member] = array
-        ready.update(keys)
 
     def multiply(block):
         ordered = [held[block][member] for member in range(replicas)]
@@ -306,35 +305,32 @@
     if fenced:
         one, two = (2, 4), (3, 5)
         plan = [
-            ([(0, 1), (0, 2), (1, 0)], [(1, 0, 1), (1, 0, 2), (0, 1, 2)], []),
-            ([(2, 0), (4, 0)], [], []),
-            ([(1, 1), (1, 2)], [(1, 2, 1)], []),
-            ([(1, 3)], [], []),
-            (one, [(one, 0, 1), (one, 0, 2)], []),
-            ([(0, 3)], [], [6]),
-            (two, [(two, 0, 1), (two, 0, 2)], []),
-            ([(6, 0), (one, 1), (one, 2)], [(one, 1, 2)], [7]),
-            ([(two, 1), (two, 2)], [(two, 2, 1), (6, 0, 1), (6, 0, 2)], []),
-            ([(one, 3), (7, 0)], [(7, 0, 1), (7, 0, 2)], []),
-            ([(two, 3)], [], []),
-            ([(6, 1), (6, 2)], [(6, 1, 2)], []),
-            ([(7, 1), (7, 2)], [(7, 2, 1)], []),
-            ([(6, 3)], [], []),
-            ([(7, 3)], [], []),
+            ([(0, 1), (0, 2), (1, 0)], [(1, 0, 1), (1, 0, 2), (0, 1, 2)], [], []),
+            ([(2, 0), (4, 0)], [], [], []),
+            ([(1, 1), (1, 2)], [(1, 2, 1)], [], []),
+            ([(1, 3)], [], [], []),
+            (one, [(one, 0, 1), (one, 0, 2)], [], [1]),
+            ([(0, 3)], [], [6], [0]),
+            (two, [(two, 0, 1), (two, 0, 2)], [], []),
+            ([(6, 0), (one, 1), (one, 2)], [(one, 1, 2)], [7], []),
+            ([(two, 1), (two, 2)], [(two, 2, 1), (6, 0, 1), (6, 0, 2)], [], []),
+            ([(one, 3), (7, 0)], [(7, 0, 1), (7, 0, 2)], [], []),
+            ([(two, 3)], [], [], []),
+            ([(6, 1), (6, 2)], [(6, 1, 2)], [], [one]),
+            ([(7, 1), (7, 2)], [(7, 2, 1)], [], [two]),
+            ([(6, 3)], [], [], [6]),
+            ([(7, 3)], [], [], [7]),
         ]
-        waiting = [0, 1, one, two, 6, 7]
         adam(((0,), (1,), (2,), (4,)))
         for block in (0, 1, 2, 4):
             deliver(block)
-        ready.add((0, 0))
         send(0, 0, 1)
         send(0, 0, 2)
-        for step, (keys, sending, leaving) in enumerate(plan):
+        for step, (keys, sending, leaving, finished) in enumerate(plan):
             if isinstance(keys, tuple):
                 pieces = [held[block][0] for block in keys]
                 token, held[keys][0] = join(state["token"][0], pieces, (0, 0))
                 state["token"] = (token,)
-                ready.add((keys, 0))
             else:
                 arrived(keys, leaving)
             for block in leaving:
@@ -345,10 +341,8 @@
                 adam(((3,), (5,), (6,), (7,)), LATER_LIMIT)
                 deliver(5)
                 deliver(3)
-            for block in list(waiting) if step > 3 else []:
-                if all((block, member) in ready for member in range(replicas)):
-                    multiply(block)
-                    waiting.remove(block)
+            for block in finished:
+                multiply(block)
     else:
         for pair in range(0, shards, 2):
             adam(((pair,), (pair + 1,)))

time: 97 us -> 96.1 us (level)
  transfers between devices with their start and end apart: 25 -> 25, of which waited for: 8 -> 10; matrix products, arithmetic and copies ran while one was open for 0% -> 0% of each run, Pallas kernels for 23% -> 23%
where the time goes in v14:
time: 96.1 us; the launch traced here: 95.1 us
  waiting for transfers between devices  36.3 us (38%)
  Pallas kernels  30.6 us (32%)
  starting transfers between devices  25.7 us (27%)
  local copies, waits for them, and re-layouts  1.59 us (2%)
    ppermute x25, waiting for transfers between devices, swap(): return lax.ppermute(value, axis, [(i, i ^ mask) for i in range(size)])  36.3 us
    ppermute x25, starting transfers between devices, swap(): return lax.ppermute(value, axis, [(i, i ^ mask) for i in range(size)])  25.7 us
    pallas_call x6, Pallas kernels, product(): pl.pallas_call(functools.partial(product_kernel, slabs), grid_spec=pltpu....  15.2 us
    pallas_call x2, Pallas kernels, adam_blocks(): pl.pallas_call(functools.partial(adam_kernel, groups, passed), in_specs=[...  13.5 us
  transfers between devices with their start and end apart: 25, of which 10 were waited for; matrix products, arithmetic and copies ran while one was open for 0% of the time, Pallas kernels for 23%

profile of v14, /device:TPU:8, one launch (start us, length us, event | category | flops | bytes accessed | tf_op | source)
XLA Modules:
  0.0 95.1 jit_solution(8702446949274449565)
XLA Ops:
  0.6 6.6 %adam_quantize.2 = (f32[8,256,512]{2,1,0:T(8,128)}, bf16[8,256,512]{2,1,0:T(8,128)(2,1)}, bf16[8,256,512]{2,1,0:T(8,128)(2,1)}, bf16[1,256,512]{2,1,0:T(8,128)(2...) custom-call(s32[8]{0:T(128)} %owner.3, ...), custom_call_target="tpu_custom_call" | custom-call | bytes 65536 | tf_op jit(solution)/shard_map/adam_quantize/pallas_call | solution.py:170
  7.2 1.6 %collective-permute-start = (bf16[1,256,512]{2,1,0:T(8,128)(2,1)}, bf16[1,256,512]{2,1,0:T(8,128)(2,1)S(1)}, u32[]{:S(2)}, u32[]{:S(2)}) collective-permute-start(bf16[1,256,512]{2,1,0:T(8,128)(2,1)} %get-tuple-element.77.refs_0_), channel_id=1, source_target_pairs={{0,8},{8,0},{16,24},{24,16},{1,9},{9,1},{17,25},{25,17},{2,10},{10... | collective-permute-start | bytes 786440 | tf_op jit(solution)/shard_map/ppermute | solution.py:258
  8.8 1.5 %collective-permute-start.1 = (bf16[1,256,512]{2,1,0:T(8,128)(2,1)}, bf16[1,256,512]{2,1,0:T(8,128)(2,1)S(1)}, u32[]{:S(2)}, u32[]{:S(2)}) collective-permute-start(bf16[1,256,512]{2,1,0:T(8,128)(2,1)} %get-tuple-element.77.refs_0_), channel_id=1, source_target_pairs={{0,16},{8,24},{16,0},{24,8},{1,17},{9,25},{17,1},{25,9},{2,18},{10... | collective-permute-start | bytes 786440 | tf_op jit(solution)/shard_map/ppermute | solution.py:258
  10.7 2.6 %collective-permute-start.4 = (bf16[1,256,512]{2,1,0:T(8,128)(2,1)}, bf16[1,256,512]{2,1,0:T(8,128)(2,1)S(1)}, u32[]{:S(2)}, u32[]{:S(2)}) collective-permute-start(bf16[1,256,512]{2,1,0:T(8,128)(2,1)} %get-tuple-element.88), channel_id=1, source_target_pairs={{0,4},{1,5},{2,6},{3,7},{4,0},{5,1},{6,2},{7,3},{8,12},{9,13},{10,... | collective-permute-start | bytes 786440 | tf_op jit(solution)/shard_map/ppermute | solution.py:258
  13.3 2.2 %collective-permute-done.refs_1_ = bf16[1,256,512]{2,1,0:T(8,128)(2,1)S(1)} collective-permute-done((bf16[1,256,512]{2,1,0:T(8,128)(2,1)}, bf16[1,256,512]{2,1,0:T(8,128)(2,1)S(1)}, u32[]{:S(2)}, u32[]{:S(2)}) %collective-permute-start) | collective-permute-done | bytes 262176 | tf_op jit(solution)/shard_map/ppermute | solution.py:258
  17.3 1.5 %collective-permute-start.6 = (bf16[1,256,512]{2,1,0:T(8,128)(2,1)S(1)}, bf16[1,256,512]{2,1,0:T(8,128)(2,1)S(1)}, u32[]{:S(2)}, u32[]{:S(2)}) collective-permute-start(bf16[1,256,512]{2,1,0:T(8,128)(2,1)S(1)} %get-tuple-element.85.refs_0_), channel_id=1, source_target_pairs={{0,16},{8,24},{16,0},{24,8},{1,17},{9,25},{17,1},{25,9},{2,18},{10... | collective-permute-start | bytes 786440 | tf_op jit(solution)/shard_map/ppermute | solution.py:258
  18.8 6.9 %adam_quantize.3 = (f32[8,256,512]{2,1,0:T(8,128)}, bf16[8,256,512]{2,1,0:T(8,128)(2,1)}, bf16[8,256,512]{2,1,0:T(8,128)(2,1)}, bf16[1,256,512]{2,1,0:T(8,128)(2...) custom-call(s32[8]{0:T(128)S(1)} %copy-done.8, ...), custom_call_target="tpu_custom_call", output_to_operand_aliasing={{0}: (5, {}), {1}: (6, {}), {2}: (7, {}), {7}: (8, {})} | custom-call | bytes 65536 | tf_op jit(solution)/shard_map/adam_quantize/pallas_call | solution.py:170
  28.5 2.8 %collective-permute-start.10 = (bf16[1,256,512]{2,1,0:T(8,128)(2,1)}, bf16[1,256,512]{2,1,0:T(8,128)(2,1)}, u32[]{:S(2)}, u32[]{:S(2)}) collective-permute-start(bf16[1,256,512]{2,1,0:T(8,128)(2,1)} %get-tuple-element.105), channel_id=1, source_target_pairs={{0,5},{1,4},{2,7},{3,6},{4,1},{5,0},{6,3},{7,2},{8,13},{9,12},{10,... | collective-permute-start | bytes 786440 | tf_op jit(solution)/shard_map/ppermute | solution.py:258
  31.3 2.7 %collective-permute-done.7.refs_1_ = bf16[1,256,512]{2,1,0:T(8,128)(2,1)S(1)} collective-permute-done((bf16[1,256,512]{2,1,0:T(8,128)(2,1)S(1)}, bf16[1,256,512]{2,1,0:T(8,128)(2,1)S(1)}, u32[]{:S(2)}, u32[]{:S(2)}) %collective-permute-start.7) | collective-permute-done | bytes 262176 | tf_op jit(solution)/shard_map/ppermute | solution.py:258
  37.0 2.0 %expert_product.6 = (f32[135168,128]{1,0:T(8,128)}, bf16[384,4096]{1,0:T(8,128)(2,1)}) custom-call(s32[8]{0:T(128)S(1)} %iota_xor_fusion.1.sources, s32[4]{0:T(128)S(1)} %select_reduce_fusion.places, bf16[384,1024]{1,0:T(8,128)(2,1)S(1)} %bitcast.2, bf16[1,256,512]{2,1,0:T(8,128)(2,1)S(1)} %get-tuple-element.85.refs_0_, ...), custom_call_target="tpu_custom_call", output_to_operand_aliasing={{0}: (7, {})} | custom-call | bytes 65536 | tf_op jit(solution)/shard_map/expert_product/pallas_call | solution.py:238
  39.1 2.0 %expert_product.7 = (f32[135168,128]{1,0:T(8,128)}, bf16[384,4096]{1,0:T(8,128)(2,1)}) custom-call(s32[8]{0:T(128)S(1)} %iota_xor_fusion.1.sources, s32[4]{0:T(128)S(1)} %select_reduce_fusion.places, bf16[384,1024]{1,0:T(8,128)(2,1)S(1)} %bitcast.3, bf16[1,256,512]{2,1,0:T(8,128)(2,1)S(1)} %copy-done.3, ...), custom_call_target="tpu_custom_call", output_to_operand_aliasing={{0}: (7, {}), {1}: (8, {})} | custom-call | bytes 65536 | tf_op jit(solution)/shard_map/expert_product/pallas_call | solution.py:238
  41.1 3.0 %collective-permute-done.10.refs_2_ = bf16[1,256,512]{2,1,0:T(8,128)(2,1)} collective-permute-done((bf16[1,256,512]{2,1,0:T(8,128)(2,1)}, bf16[1,256,512]{2,1,0:T(8,128)(2,1)}, u32[]{:S(2)}, u32[]{:S(2)}) %collective-permute-start.10) | collective-permute-done | bytes 262176 | tf_op jit(solution)/shard_map/ppermute | solution.py:258
  45.7 1.5 %collective-permute-start.15 = (bf16[2,256,512]{2,1,0:T(8,128)(2,1)S(1)}, bf16[2,256,512]{2,1,0:T(8,128)(2,1)S(1)}, u32[]{:S(2)}, u32[]{:S(2)}) collective-permute-start(bf16[2,256,512]{2,1,0:T(8,128)(2,1)S(1)} %get-tuple-element.111.refs_0_), channel_id=1, source_target_pairs={{0,16},{8,24},{16,0},{24,8},{1,17},{9,25},{17,1},{25,9},{2,18},{10... | collective-permute-start | bytes 1572872 | tf_op jit(solution)/shard_map/ppermute | solution.py:258
  47.5 13.1 %collective-permute-done.11.refs_1_ = bf16[1,256,512]{2,1,0:T(8,128)(2,1)S(1)} collective-permute-done((bf16[1,256,512]{2,1,0:T(8,128)(2,1)S(1)}, bf16[1,256,512]{2,1,0:T(8,128)(2,1)S(1)}, u32[]{:S(2)}, u32[]{:S(2)}) %collective-permute-start.11) | collective-permute-done | bytes 262176 | tf_op jit(solution)/shard_map/ppermute | solution.py:258
  61.1 1.5 %collective-permute-start.18 = (bf16[2,256,512]{2,1,0:T(8,128)(2,1)S(1)}, bf16[2,256,512]{2,1,0:T(8,128)(2,1)S(1)}, u32[]{:S(2)}, u32[]{:S(2)}) collective-permute-start(bf16[2,256,512]{2,1,0:T(8,128)(2,1)S(1)} %get-tuple-element.119.refs_2_), channel_id=1, source_target_pairs={{0,8},{8,0},{16,24},{24,16},{1,9},{9,1},{17,25},{25,17},{2,10},{10... | collective-permute-start | bytes 1572872 | tf_op jit(solution)/shard_map/ppermute | solution.py:258
  63.2 1.5 %collective-permute-start.20 = (bf16[1,256,512]{2,1,0:T(8,128)(2,1)S(1)}, bf16[1,256,512]{2,1,0:T(8,128)(2,1)S(1)}, u32[]{:S(2)}, u32[]{:S(2)}) collective-permute-start(bf16[1,256,512]{2,1,0:T(8,128)(2,1)S(1)} %get-tuple-element.121.refs_0_), channel_id=1, source_target_pairs={{0,16},{8,24},{16,0},{24,8},{1,17},{9,25},{17,1},{25,9},{2,18},{10... | collective-permute-start | bytes 786440 | tf_op jit(solution)/shard_map/ppermute | solution.py:258
  64.7 10.2 %collective-permute-done.17.refs_2_ = bf16[1,256,512]{2,1,0:T(8,128)(2,1)S(1)} collective-permute-done((bf16[1,256,512]{2,1,0:T(8,128)(2,1)S(1)}, bf16[1,256,512]{2,1,0:T(8,128)(2,1)S(1)}, u32[]{:S(2)}, u32[]{:S(2)}) %collective-permute-start.17) | collective-permute-done | bytes 262176 | tf_op jit(solution)/shard_map/ppermute | solution.py:258
  77.5 2.8 %collective-permute-done.19.refs_1_ = bf16[1,256,512]{2,1,0:T(8,128)(2,1)S(1)} collective-permute-done((bf16[1,256,512]{2,1,0:T(8,128)(2,1)S(1)}, bf16[1,256,512]{2,1,0:T(8,128)(2,1)S(1)}, u32[]{:S(2)}, u32[]{:S(2)}) %collective-permute-start.19) | collective-permute-done | bytes 262176 | tf_op jit(solution)/shard_map/ppermute | solution.py:258
  80.3 1.5 %collective-permute-start.23 = (bf16[1,256,512]{2,1,0:T(8,128)(2,1)S(1)}, bf16[1,256,512]{2,1,0:T(8,128)(2,1)S(1)}, u32[]{:S(2)}, u32[]{:S(2)}) collective-permute-start(bf16[1,256,512]{2,1,0:T(8,128)(2,1)S(1)} %get-tuple-element.127.refs_1_), channel_id=1, source_target_pairs={{0,16},{8,24},{16,0},{24,8},{1,17},{9,25},{17,1},{25,9},{2,18},{10... | collective-permute-start | bytes 786440 | tf_op jit(solution)/shard_map/ppermute | solution.py:258
  81.8 4.1 %expert_product.8 = (f32[135168,128]{1,0:T(8,128)}, bf16[384,4096]{1,0:T(8,128)(2,1)}) custom-call(s32[8]{0:T(128)S(1)} %iota_xor_fusion.1.sources, s32[4]{0:T(128)S(1)} %select_reduce_fusion.places, bf16[384,1024]{1,0:T(8,128)(2,1)S(1)} %bitcast.4, bf16[2,256,512]{2,1,0:T(8,128)(2,1)} %get-tuple-element.108.refs_0_, ...), custom_call_target="tpu_custom_call", output_to_operand_aliasing={{0}: (7, {}), {1}: (8, {})} | custom-call | bytes 65536 | tf_op jit(solution)/shard_map/expert_product/pallas_call | solution.py:238
  86.2 1.8 %collective-permute-start.24 = (bf16[1,256,512]{2,1,0:T(8,128)(2,1)S(1)}, bf16[1,256,512]{2,1,0:T(8,128)(2,1)S(1)}, u32[]{:S(2)}, u32[]{:S(2)}) collective-permute-start(bf16[1,256,512]{2,1,0:T(8,128)(2,1)S(1)} %get-tuple-element.126.refs_2_), channel_id=1, source_target_pairs={{0,8},{8,0},{16,24},{24,16},{1,9},{9,1},{17,25},{25,17},{2,10},{10... | collective-permute-start | bytes 786440 | tf_op jit(solution)/shard_map/ppermute | solution.py:258
  88.0 3.1 %expert_product.9 = (f32[135168,128]{1,0:T(8,128)}, bf16[384,4096]{1,0:T(8,128)(2,1)}) custom-call(s32[8]{0:T(128)S(1)} %iota_xor_fusion.1.sources, s32[4]{0:T(128)S(1)} %select_reduce_fusion.places, bf16[384,1024]{1,0:T(8,128)(2,1)S(1)} %bitcast.5, ...), custom_call_target="tpu_custom_call", output_to_operand_aliasing={{0}: (7, {}), {1}: (8, {})} | custom-call | bytes 65536 | tf_op jit(solution)/shard_map/expert_product/pallas_call | solution.py:238
  91.1 2.0 %expert_product.10 = (f32[135168,128]{1,0:T(8,128)}, bf16[384,4096]{1,0:T(8,128)(2,1)}) custom-call(s32[8]{0:T(128)S(1)} %iota_xor_fusion.1.sources, s32[4]{0:T(128)S(1)} %select_reduce_fusion.places, bf16[384,1024]{1,0:T(8,128)(2,1)S(1)} %bitcast.6, ...), custom_call_target="tpu_custom_call", output_to_operand_aliasing={{0}: (7, {}), {1}: (8, {})} | custom-call | bytes 65536 | tf_op jit(solution)/shard_map/expert_product/pallas_call | solution.py:238
  93.1 2.0 %expert_product.11 = (f32[135168,128]{1,0:T(8,128)}, bf16[384,4096]{1,0:T(8,128)(2,1)}) custom-call(s32[8]{0:T(128)S(1)} %iota_xor_fusion.1.sources, s32[4]{0:T(128)S(1)} %select_reduce_fusion.places, bf16[384,1024]{1,0:T(8,128)(2,1)S(1)} %bitcast.7, ...), custom_call_target="tpu_custom_call", output_to_operand_aliasing={{0}: (7, {}), {1}: (8, {})} | custom-call | bytes 65536 | tf_op jit(solution)/shard_map/expert_product/pallas_call | solution.py:238
  (72 shorter events, 14.0 us)
Async XLA Ops:
  7.2 8.3 %collective-permute-start = (bf16[1,256,512]{2,1,0:T(8,128)(2,1)}, bf16[1,256,512]{2,1,0:T(8,128)(2,1)S(1)}, u32[]{:S(2)}, u32[]{:S(2)}) collective-permute-start(bf16[1,256,512]{2,1,0:T(8,128)(2,1)} %get-tuple-element.77.refs_0_), channel_id=1, source_target_pairs={{0,8},{8,0},{16,24},{24,16},{1,9},{9,1},{17,25},{25,17},{2,10},{10... | collective-permute-start | bytes 786440 | tf_op jit(solution)/shard_map/ppermute | solution.py:258
  8.8 8.0 %collective-permute-start.1 = (bf16[1,256,512]{2,1,0:T(8,128)(2,1)}, bf16[1,256,512]{2,1,0:T(8,128)(2,1)S(1)}, u32[]{:S(2)}, u32[]{:S(2)}) collective-permute-start(bf16[1,256,512]{2,1,0:T(8,128)(2,1)} %get-tuple-element.77.refs_0_), channel_id=1, source_target_pairs={{0,16},{8,24},{16,0},{24,8},{1,17},{9,25},{17,1},{25,9},{2,18},{10... | collective-permute-start | bytes 786440 | tf_op jit(solution)/shard_map/ppermute | solution.py:258
  10.3 15.5 %collective-permute-start.3 = (bf16[1,256,512]{2,1,0:T(8,128)(2,1)}, bf16[1,256,512]{2,1,0:T(8,128)(2,1)S(1)}, u32[]{:S(2)}, u32[]{:S(2)}) collective-permute-start(bf16[1,256,512]{2,1,0:T(8,128)(2,1)} %get-tuple-element.87), channel_id=1, source_target_pairs={{0,2},{1,3},{2,0},{3,1},{4,6},{5,7},{6,4},{7,5},{8,10},{9,11},{10,... | collective-permute-start | bytes 786440 | tf_op jit(solution)/shard_map/ppermute | solution.py:258
  10.7 15.2 %collective-permute-start.4 = (bf16[1,256,512]{2,1,0:T(8,128)(2,1)}, bf16[1,256,512]{2,1,0:T(8,128)(2,1)S(1)}, u32[]{:S(2)}, u32[]{:S(2)}) collective-permute-start(bf16[1,256,512]{2,1,0:T(8,128)(2,1)} %get-tuple-element.88), channel_id=1, source_target_pairs={{0,4},{1,5},{2,6},{3,7},{4,0},{5,1},{6,2},{7,3},{8,12},{9,13},{10,... | collective-permute-start | bytes 786440 | tf_op jit(solution)/shard_map/ppermute | solution.py:258
  16.8 9.2 %collective-permute-start.5 = (bf16[1,256,512]{2,1,0:T(8,128)(2,1)S(1)}, bf16[1,256,512]{2,1,0:T(8,128)(2,1)S(1)}, u32[]{:S(2)}, u32[]{:S(2)}) collective-permute-start(bf16[1,256,512]{2,1,0:T(8,128)(2,1)S(1)} %get-tuple-element.85.refs_0_), channel_id=1, source_target_pairs={{0,8},{8,0},{16,24},{24,16},{1,9},{9,1},{17,25},{25,17},{2,10},{10... | collective-permute-start | bytes 786440 | tf_op jit(solution)/shard_map/ppermute | solution.py:258
  17.3 8.7 %collective-permute-start.6 = (bf16[1,256,512]{2,1,0:T(8,128)(2,1)S(1)}, bf16[1,256,512]{2,1,0:T(8,128)(2,1)S(1)}, u32[]{:S(2)}, u32[]{:S(2)}) collective-permute-start(bf16[1,256,512]{2,1,0:T(8,128)(2,1)S(1)} %get-tuple-element.85.refs_0_), channel_id=1, source_target_pairs={{0,16},{8,24},{16,0},{24,8},{1,17},{9,25},{17,1},{25,9},{2,18},{10... | collective-permute-start | bytes 786440 | tf_op jit(solution)/shard_map/ppermute | solution.py:258
  26.5 7.4 %collective-permute-start.7 = (bf16[1,256,512]{2,1,0:T(8,128)(2,1)S(1)}, bf16[1,256,512]{2,1,0:T(8,128)(2,1)S(1)}, u32[]{:S(2)}, u32[]{:S(2)}) collective-permute-start(bf16[1,256,512]{2,1,0:T(8,128)(2,1)S(1)} %get-tuple-element.91.refs_2_), channel_id=1, source_target_pairs={{0,8},{8,0},{16,24},{24,16},{1,9},{9,1},{17,25},{25,17},{2,10},{10... | collective-permute-start | bytes 786440 | tf_op jit(solution)/shard_map/ppermute | solution.py:258
  28.0 11.0 %collective-permute-start.8 = (bf16[1,256,512]{2,1,0:T(8,128)(2,1)S(1)}, bf16[1,256,512]{2,1,0:T(8,128)(2,1)S(1)}, u32[]{:S(2)}, u32[]{:S(2)}) collective-permute-start(bf16[1,256,512]{2,1,0:T(8,128)(2,1)S(1)} %get-tuple-element.83.refs_1_), channel_id=1, source_target_pairs={{0,16},{8,24},{16,0},{24,8},{1,17},{9,25},{17,1},{25,9},{2,18},{10... | collective-permute-start | bytes 786440 | tf_op jit(solution)/shard_map/ppermute | solution.py:258
  28.5 12.6 %collective-permute-start.9 = (bf16[1,256,512]{2,1,0:T(8,128)(2,1)}, bf16[1,256,512]{2,1,0:T(8,128)(2,1)}, u32[]{:S(2)}, u32[]{:S(2)}) collective-permute-start(bf16[1,256,512]{2,1,0:T(8,128)(2,1)} %get-tuple-element.104), channel_id=1, source_target_pairs={{0,3},{1,2},{2,1},{3,0},{4,7},{5,6},{6,5},{7,4},{8,11},{9,10},{10,... | collective-permute-start | bytes 786440 | tf_op jit(solution)/shard_map/ppermute | solution.py:258
  28.5 15.5 %collective-permute-start.10 = (bf16[1,256,512]{2,1,0:T(8,128)(2,1)}, bf16[1,256,512]{2,1,0:T(8,128)(2,1)}, u32[]{:S(2)}, u32[]{:S(2)}) collective-permute-start(bf16[1,256,512]{2,1,0:T(8,128)(2,1)} %get-tuple-element.105), channel_id=1, source_target_pairs={{0,5},{1,4},{2,7},{3,6},{4,1},{5,0},{6,3},{7,2},{8,13},{9,12},{10,... | collective-permute-start | bytes 786440 | tf_op jit(solution)/shard_map/ppermute | solution.py:258
  34.8 25.7 %collective-permute-start.12 = (bf16[2,256,512]{2,1,0:T(8,128)(2,1)}, bf16[2,256,512]{2,1,0:T(8,128)(2,1)S(1)}, u32[]{:S(2)}, u32[]{:S(2)}) collective-permute-start(bf16[2,256,512]{2,1,0:T(8,128)(2,1)} %get-tuple-element.108.refs_0_), channel_id=1, source_target_pairs={{0,8},{8,0},{16,24},{24,16},{1,9},{9,1},{17,25},{25,17},{2,10},{10... | collective-permute-start | bytes 1572872 | tf_op jit(solution)/shard_map/ppermute | solution.py:258
  35.4 25.2 %collective-permute-start.13 = (bf16[2,256,512]{2,1,0:T(8,128)(2,1)}, bf16[2,256,512]{2,1,0:T(8,128)(2,1)S(1)}, u32[]{:S(2)}, u32[]{:S(2)}) collective-permute-start(bf16[2,256,512]{2,1,0:T(8,128)(2,1)} %get-tuple-element.108.refs_0_), channel_id=1, source_target_pairs={{0,16},{8,24},{16,0},{24,8},{1,17},{9,25},{17,1},{25,9},{2,18},{10... | collective-permute-start | bytes 1572872 | tf_op jit(solution)/shard_map/ppermute | solution.py:258
  45.1 16.0 %collective-permute-start.14 = (bf16[2,256,512]{2,1,0:T(8,128)(2,1)S(1)}, bf16[2,256,512]{2,1,0:T(8,128)(2,1)S(1)}, u32[]{:S(2)}, u32[]{:S(2)}) collective-permute-start(bf16[2,256,512]{2,1,0:T(8,128)(2,1)S(1)} %get-tuple-element.111.refs_0_), channel_id=1, source_target_pairs={{0,8},{8,0},{16,24},{24,16},{1,9},{9,1},{17,25},{25,17},{2,10},{10... | collective-permute-start | bytes 1572872 | tf_op jit(solution)/shard_map/ppermute | solution.py:258
  45.7 15.5 %collective-permute-start.15 = (bf16[2,256,512]{2,1,0:T(8,128)(2,1)S(1)}, bf16[2,256,512]{2,1,0:T(8,128)(2,1)S(1)}, u32[]{:S(2)}, u32[]{:S(2)}) collective-permute-start(bf16[2,256,512]{2,1,0:T(8,128)(2,1)S(1)} %get-tuple-element.111.refs_0_), channel_id=1, source_target_pairs={{0,16},{8,24},{16,0},{24,8},{1,17},{9,25},{17,1},{25,9},{2,18},{10... | collective-permute-start | bytes 1572872 | tf_op jit(solution)/shard_map/ppermute | solution.py:258
  47.2 13.3 %collective-permute-start.11 = (bf16[1,256,512]{2,1,0:T(8,128)(2,1)S(1)}, bf16[1,256,512]{2,1,0:T(8,128)(2,1)S(1)}, u32[]{:S(2)}, u32[]{:S(2)}) collective-permute-start(bf16[1,256,512]{2,1,0:T(8,128)(2,1)S(1)} %get-tuple-element.107), channel_id=1, source_target_pairs={{0,6},{1,7},{2,4},{3,5},{4,2},{5,3},{6,0},{7,1},{8,14},{9,15},{10,... | collective-permute-start | bytes 786440 | tf_op jit(solution)/shard_map/ppermute | solution.py:258
  60.6 14.9 %collective-permute-start.16 = (bf16[2,256,512]{2,1,0:T(8,128)(2,1)S(1)}, bf16[2,256,512]{2,1,0:T(8,128)(2,1)S(1)}, u32[]{:S(2)}, u32[]{:S(2)}) collective-permute-start(bf16[2,256,512]{2,1,0:T(8,128)(2,1)S(1)} %get-tuple-element.113.refs_1_), channel_id=1, source_target_pairs={{0,16},{8,24},{16,0},{24,8},{1,17},{9,25},{17,1},{25,9},{2,18},{10... | collective-permute-start | bytes 1572872 | tf_op jit(solution)/shard_map/ppermute | solution.py:258
  61.1 16.4 %collective-permute-start.18 = (bf16[2,256,512]{2,1,0:T(8,128)(2,1)S(1)}, bf16[2,256,512]{2,1,0:T(8,128)(2,1)S(1)}, u32[]{:S(2)}, u32[]{:S(2)}) collective-permute-start(bf16[2,256,512]{2,1,0:T(8,128)(2,1)S(1)} %get-tuple-element.119.refs_2_), channel_id=1, source_target_pairs={{0,8},{8,0},{16,24},{24,16},{1,9},{9,1},{17,25},{25,17},{2,10},{10... | collective-permute-start | bytes 1572872 | tf_op jit(solution)/shard_map/ppermute | solution.py:258
  62.6 12.2 %collective-permute-start.17 = (bf16[1,256,512]{2,1,0:T(8,128)(2,1)S(1)}, bf16[1,256,512]{2,1,0:T(8,128)(2,1)S(1)}, u32[]{:S(2)}, u32[]{:S(2)}) collective-permute-start(bf16[1,256,512]{2,1,0:T(8,128)(2,1)S(1)} %get-tuple-element.114), channel_id=1, source_target_pairs={{0,7},{1,6},{2,5},{3,4},{4,3},{5,2},{6,1},{7,0},{8,15},{9,14},{10,... | collective-permute-start | bytes 786440 | tf_op jit(solution)/shard_map/ppermute | solution.py:258
  62.6 17.6 %collective-permute-start.19 = (bf16[1,256,512]{2,1,0:T(8,128)(2,1)S(1)}, bf16[1,256,512]{2,1,0:T(8,128)(2,1)S(1)}, u32[]{:S(2)}, u32[]{:S(2)}) collective-permute-start(bf16[1,256,512]{2,1,0:T(8,128)(2,1)S(1)} %get-tuple-element.121.refs_0_), channel_id=1, source_target_pairs={{0,8},{8,0},{16,24},{24,16},{1,9},{9,1},{17,25},{25,17},{2,10},{10... | collective-permute-start | bytes 786440 | tf_op jit(solution)/shard_map/ppermute | solution.py:258
  63.2 17.1 %collective-permute-start.20 = (bf16[1,256,512]{2,1,0:T(8,128)(2,1)S(1)}, bf16[1,256,512]{2,1,0:T(8,128)(2,1)S(1)}, u32[]{:S(2)}, u32[]{:S(2)}) collective-permute-start(bf16[1,256,512]{2,1,0:T(8,128)(2,1)S(1)} %get-tuple-element.121.refs_0_), channel_id=1, source_target_pairs={{0,16},{8,24},{16,0},{24,8},{1,17},{9,25},{17,1},{25,9},{2,18},{10... | collective-permute-start | bytes 786440 | tf_op jit(solution)/shard_map/ppermute | solution.py:258
  75.5 10.4 %collective-permute-start.21 = (bf16[1,256,512]{2,1,0:T(8,128)(2,1)S(1)}, bf16[1,256,512]{2,1,0:T(8,128)(2,1)S(1)}, u32[]{:S(2)}, u32[]{:S(2)}) collective-permute-start(bf16[1,256,512]{2,1,0:T(8,128)(2,1)S(1)} %get-tuple-element.115.refs_0_), channel_id=1, source_target_pairs={{0,8},{8,0},{16,24},{24,16},{1,9},{9,1},{17,25},{25,17},{2,10},{10... | collective-permute-start | bytes 786440 | tf_op jit(solution)/shard_map/ppermute | solution.py:258
  77.0 9.2 %collective-permute-start.22 = (bf16[1,256,512]{2,1,0:T(8,128)(2,1)S(1)}, bf16[1,256,512]{2,1,0:T(8,128)(2,1)S(1)}, u32[]{:S(2)}, u32[]{:S(2)}) collective-permute-start(bf16[1,256,512]{2,1,0:T(8,128)(2,1)S(1)} %get-tuple-element.115.refs_0_), channel_id=1, source_target_pairs={{0,16},{8,24},{16,0},{24,8},{1,17},{9,25},{17,1},{25,9},{2,18},{10... | collective-permute-start | bytes 786440 | tf_op jit(solution)/shard_map/ppermute | solution.py:258
  80.3 10.8 %collective-permute-start.23 = (bf16[1,256,512]{2,1,0:T(8,128)(2,1)S(1)}, bf16[1,256,512]{2,1,0:T(8,128)(2,1)S(1)}, u32[]{:S(2)}, u32[]{:S(2)}) collective-permute-start(bf16[1,256,512]{2,1,0:T(8,128)(2,1)S(1)} %get-tuple-element.127.refs_1_), channel_id=1, source_target_pairs={{0,16},{8,24},{16,0},{24,8},{1,17},{9,25},{17,1},{25,9},{2,18},{10... | collective-permute-start | bytes 786440 | tf_op jit(solution)/shard_map/ppermute | solution.py:258
  86.2 6.8 %collective-permute-start.24 = (bf16[1,256,512]{2,1,0:T(8,128)(2,1)S(1)}, bf16[1,256,512]{2,1,0:T(8,128)(2,1)S(1)}, u32[]{:S(2)}, u32[]{:S(2)}) collective-permute-start(bf16[1,256,512]{2,1,0:T(8,128)(2,1)S(1)} %get-tuple-element.126.refs_2_), channel_id=1, source_target_pairs={{0,8},{8,0},{16,24},{24,16},{1,9},{9,1},{17,25},{25,17},{2,10},{10... | collective-permute-start | bytes 786440 | tf_op jit(solution)/shard_map/ppermute | solution.py:258
  (11 other events, 57.5 us)

commit v15 on v14

--- a/solution.py
+++ b/solution.py
@@ -314,10 +314,10 @@
             (two, [(two, 0, 1), (two, 0, 2)], [], []),
             ([(6, 0), (one, 1), (one, 2)], [(one, 1, 2)], [7], []),
             ([(two, 1), (two, 2)], [(two, 2, 1), (6, 0, 1), (6, 0, 2)], [], []),
-            ([(one, 3), (7, 0)], [(7, 0, 1), (7, 0, 2)], [], []),
-            ([(two, 3)], [], [], []),
-            ([(6, 1), (6, 2)], [(6, 1, 2)], [], [one]),
-            ([(7, 1), (7, 2)], [(7, 2, 1)], [], [two]),
+            ([(7, 0)], [(7, 0, 1), (7, 0, 2)], [], []),
+            ([(one, 3), (6, 1), (6, 2)], [(6, 1, 2)], [], [one]),
+            ([(7, 1), (7, 2)], [(7, 2, 1)], [], []),
+            ([(two, 3)], [], [], [two]),
             ([(6, 3)], [], [], [6]),
             ([(7, 3)], [], [], [7]),
         ]

time: 96.1 us -> 98.4 us (1.024)
  starting transfers between devices: 25.7 us -> 28.7 us
    ppermute x25, starting transfers between devices: 25.7 us -> 28.7 us  [swap(): return lax.ppermute(value, axis, [(i, i ^ mask) for i in range(size)])]
where the time goes in v15:
time: 98.4 us; the launch traced here: 97.2 us
  waiting for transfers between devices  35.4 us (36%)
  Pallas kernels  30.6 us (31%)
  starting transfers between devices  28.7 us (29%)
  local copies, waits for them, and re-layouts  1.59 us (2%)
    ppermute x25, waiting for transfers between devices, swap(): return lax.ppermute(value, axis, [(i, i ^ mask) for i in range(size)])  35.4 us
    ppermute x25, starting transfers between devices, swap(): return lax.ppermute(value, axis, [(i, i ^ mask) for i in range(size)])  28.7 us
    pallas_call x6, Pallas kernels, product(): pl.pallas_call(functools.partial(product_kernel, slabs), grid_spec=pltpu....  15.2 us
    pallas_call x2, Pallas kernels, adam_blocks(): pl.pallas_call(functools.partial(adam_kernel, groups, passed), in_specs=[...  13.5 us
  transfers between devices with their start and end apart: 25, of which 10 were waited for; matrix products, arithmetic and copies ran while one was open for 0% of the time, Pallas kernels for 23%

profile of v15, /device:TPU:8, one launch (start us, length us, event | category | flops | bytes accessed | tf_op | source)
XLA Modules:
  0.0 97.2 jit_solution(10577097729492622252)
XLA Ops:
  0.6 6.6 %adam_quantize.2 = (f32[8,256,512]{2,1,0:T(8,128)}, bf16[8,256,512]{2,1,0:T(8,128)(2,1)}, bf16[8,256,512]{2,1,0:T(8,128)(2,1)}, bf16[1,256,512]{2,1,0:T(8,128)(2...) custom-call(s32[8]{0:T(128)} %owner.3, ...), custom_call_target="tpu_custom_call" | custom-call | bytes 65536 | tf_op jit(solution)/shard_map/adam_quantize/pallas_call | solution.py:170
  7.2 1.6 %collective-permute-start = (bf16[1,256,512]{2,1,0:T(8,128)(2,1)}, bf16[1,256,512]{2,1,0:T(8,128)(2,1)S(1)}, u32[]{:S(2)}, u32[]{:S(2)}) collective-permute-start(bf16[1,256,512]{2,1,0:T(8,128)(2,1)} %get-tuple-element.77.refs_0_), channel_id=1, source_target_pairs={{0,8},{8,0},{16,24},{24,16},{1,9},{9,1},{17,25},{25,17},{2,10},{10... | collective-permute-start | bytes 786440 | tf_op jit(solution)/shard_map/ppermute | solution.py:258
  8.8 1.5 %collective-permute-start.1 = (bf16[1,256,512]{2,1,0:T(8,128)(2,1)}, bf16[1,256,512]{2,1,0:T(8,128)(2,1)S(1)}, u32[]{:S(2)}, u32[]{:S(2)}) collective-permute-start(bf16[1,256,512]{2,1,0:T(8,128)(2,1)} %get-tuple-element.77.refs_0_), channel_id=1, source_target_pairs={{0,16},{8,24},{16,0},{24,8},{1,17},{9,25},{17,1},{25,9},{2,18},{10... | collective-permute-start | bytes 786440 | tf_op jit(solution)/shard_map/ppermute | solution.py:258
  10.7 2.6 %collective-permute-start.4 = (bf16[1,256,512]{2,1,0:T(8,128)(2,1)}, bf16[1,256,512]{2,1,0:T(8,128)(2,1)S(1)}, u32[]{:S(2)}, u32[]{:S(2)}) collective-permute-start(bf16[1,256,512]{2,1,0:T(8,128)(2,1)} %get-tuple-element.88), channel_id=1, source_target_pairs={{0,4},{1,5},{2,6},{3,7},{4,0},{5,1},{6,2},{7,3},{8,12},{9,13},{10,... | collective-permute-start | bytes 786440 | tf_op jit(solution)/shard_map/ppermute | solution.py:258
  13.3 2.2 %collective-permute-done.refs_1_ = bf16[1,256,512]{2,1,0:T(8,128)(2,1)S(1)} collective-permute-done((bf16[1,256,512]{2,1,0:T(8,128)(2,1)}, bf16[1,256,512]{2,1,0:T(8,128)(2,1)S(1)}, u32[]{:S(2)}, u32[]{:S(2)}) %collective-permute-start) | collective-permute-done | bytes 262176 | tf_op jit(solution)/shard_map/ppermute | solution.py:258
  18.8 6.9 %adam_quantize.3 = (f32[8,256,512]{2,1,0:T(8,128)}, bf16[8,256,512]{2,1,0:T(8,128)(2,1)}, bf16[8,256,512]{2,1,0:T(8,128)(2,1)}, bf16[1,256,512]{2,1,0:T(8,128)(2...) custom-call(s32[8]{0:T(128)S(1)} %copy-done.8, ...), custom_call_target="tpu_custom_call", output_to_operand_aliasing={{0}: (5, {}), {1}: (6, {}), {2}: (7, {}), {7}: (8, {})} | custom-call | bytes 65536 | tf_op jit(solution)/shard_map/adam_quantize/pallas_call | solution.py:170
  28.5 2.8 %collective-permute-start.10 = (bf16[1,256,512]{2,1,0:T(8,128)(2,1)}, bf16[1,256,512]{2,1,0:T(8,128)(2,1)}, u32[]{:S(2)}, u32[]{:S(2)}) collective-permute-start(bf16[1,256,512]{2,1,0:T(8,128)(2,1)} %get-tuple-element.105), channel_id=1, source_target_pairs={{0,5},{1,4},{2,7},{3,6},{4,1},{5,0},{6,3},{7,2},{8,13},{9,12},{10,... | collective-permute-start | bytes 786440 | tf_op jit(solution)/shard_map/ppermute | solution.py:258
  31.3 2.7 %collective-permute-done.7.refs_1_ = bf16[1,256,512]{2,1,0:T(8,128)(2,1)S(1)} collective-permute-done((bf16[1,256,512]{2,1,0:T(8,128)(2,1)S(1)}, bf16[1,256,512]{2,1,0:T(8,128)(2,1)S(1)}, u32[]{:S(2)}, u32[]{:S(2)}) %collective-permute-start.7) | collective-permute-done | bytes 262176 | tf_op jit(solution)/shard_map/ppermute | solution.py:258
  37.0 2.0 %expert_product.6 = (f32[135168,128]{1,0:T(8,128)}, bf16[384,4096]{1,0:T(8,128)(2,1)}) custom-call(s32[8]{0:T(128)S(1)} %iota_xor_fusion.1.sources, s32[4]{0:T(128)S(1)} %select_reduce_fusion.places, bf16[384,1024]{1,0:T(8,128)(2,1)S(1)} %bitcast.2, bf16[1,256,512]{2,1,0:T(8,128)(2,1)S(1)} %get-tuple-element.85.refs_0_, ...), custom_call_target="tpu_custom_call", output_to_operand_aliasing={{0}: (7, {})} | custom-call | bytes 65536 | tf_op jit(solution)/shard_map/expert_product/pallas_call | solution.py:238
  40.5 2.0 %expert_product.7 = (f32[135168,128]{1,0:T(8,128)}, bf16[384,4096]{1,0:T(8,128)(2,1)}) custom-call(s32[8]{0:T(128)S(1)} %iota_xor_fusion.1.sources, s32[4]{0:T(128)S(1)} %select_reduce_fusion.places, bf16[384,1024]{1,0:T(8,128)(2,1)S(1)} %bitcast.3, bf16[1,256,512]{2,1,0:T(8,128)(2,1)S(1)} %copy-done.3, ...), custom_call_target="tpu_custom_call", output_to_operand_aliasing={{0}: (7, {}), {1}: (8, {})} | custom-call | bytes 65536 | tf_op jit(solution)/shard_map/expert_product/pallas_call | solution.py:238
  42.5 7.0 %collective-permute-done.10.refs_2_ = bf16[1,256,512]{2,1,0:T(8,128)(2,1)} collective-permute-done((bf16[1,256,512]{2,1,0:T(8,128)(2,1)}, bf16[1,256,512]{2,1,0:T(8,128)(2,1)}, u32[]{:S(2)}, u32[]{:S(2)}) %collective-permute-start.10) | collective-permute-done | bytes 262176 | tf_op jit(solution)/shard_map/ppermute | solution.py:258
  51.2 1.5 %collective-permute-start.15 = (bf16[2,256,512]{2,1,0:T(8,128)(2,1)S(1)}, bf16[2,256,512]{2,1,0:T(8,128)(2,1)S(1)}, u32[]{:S(2)}, u32[]{:S(2)}) collective-permute-start(bf16[2,256,512]{2,1,0:T(8,128)(2,1)S(1)} %get-tuple-element.111.refs_0_), channel_id=1, source_target_pairs={{0,16},{8,24},{16,0},{24,8},{1,17},{9,25},{17,1},{25,9},{2,18},{10... | collective-permute-start | bytes 1572872 | tf_op jit(solution)/shard_map/ppermute | solution.py:258
  52.7 2.6 %collective-permute-done.11.refs_1_ = bf16[1,256,512]{2,1,0:T(8,128)(2,1)S(1)} collective-permute-done((bf16[1,256,512]{2,1,0:T(8,128)(2,1)S(1)}, bf16[1,256,512]{2,1,0:T(8,128)(2,1)S(1)}, u32[]{:S(2)}, u32[]{:S(2)}) %collective-permute-start.11) | collective-permute-done | bytes 262176 | tf_op jit(solution)/shard_map/ppermute | solution.py:258
  55.4 1.6 %collective-permute-start.17 = (bf16[2,256,512]{2,1,0:T(8,128)(2,1)S(1)}, bf16[2,256,512]{2,1,0:T(8,128)(2,1)S(1)}, u32[]{:S(2)}, u32[]{:S(2)}) collective-permute-start(bf16[2,256,512]{2,1,0:T(8,128)(2,1)S(1)} %get-tuple-element.115.refs_1_), channel_id=1, source_target_pairs={{0,16},{8,24},{16,0},{24,8},{1,17},{9,25},{17,1},{25,9},{2,18},{10... | collective-permute-start | bytes 1572872 | tf_op jit(solution)/shard_map/ppermute | solution.py:258
  57.7 7.5 %collective-permute-done.14.refs_1_ = bf16[2,256,512]{2,1,0:T(8,128)(2,1)S(1)} collective-permute-done((bf16[2,256,512]{2,1,0:T(8,128)(2,1)S(1)}, bf16[2,256,512]{2,1,0:T(8,128)(2,1)S(1)}, u32[]{:S(2)}, u32[]{:S(2)}) %collective-permute-start.14) | collective-permute-done | bytes 524320 | tf_op jit(solution)/shard_map/ppermute | solution.py:258
  65.2 1.9 %collective-permute-start.19 = (bf16[1,256,512]{2,1,0:T(8,128)(2,1)S(1)}, bf16[1,256,512]{2,1,0:T(8,128)(2,1)S(1)}, u32[]{:S(2)}, u32[]{:S(2)}) collective-permute-start(bf16[1,256,512]{2,1,0:T(8,128)(2,1)S(1)} %get-tuple-element.118.refs_0_), channel_id=1, source_target_pairs={{0,16},{8,24},{16,0},{24,8},{1,17},{9,25},{17,1},{25,9},{2,18},{10... | collective-permute-start | bytes 786440 | tf_op jit(solution)/shard_map/ppermute | solution.py:258
  70.8 1.9 %collective-permute-start.21 = (bf16[1,256,512]{2,1,0:T(8,128)(2,1)S(1)}, bf16[1,256,512]{2,1,0:T(8,128)(2,1)S(1)}, u32[]{:S(2)}, u32[]{:S(2)}) collective-permute-start(bf16[1,256,512]{2,1,0:T(8,128)(2,1)S(1)} %get-tuple-element.114.refs_0_), channel_id=1, source_target_pairs={{0,16},{8,24},{16,0},{24,8},{1,17},{9,25},{17,1},{25,9},{2,18},{10... | collective-permute-start | bytes 786440 | tf_op jit(solution)/shard_map/ppermute | solution.py:258
  72.7 10.2 %collective-permute-done.19.refs_3_ = bf16[1,256,512]{2,1,0:T(8,128)(2,1)S(1)} collective-permute-done((bf16[1,256,512]{2,1,0:T(8,128)(2,1)S(1)}, bf16[1,256,512]{2,1,0:T(8,128)(2,1)S(1)}, u32[]{:S(2)}, u32[]{:S(2)}) %collective-permute-start.19) | collective-permute-done | bytes 262176 | tf_op jit(solution)/shard_map/ppermute | solution.py:258
  82.9 1.5 %collective-permute-start.23 = (bf16[1,256,512]{2,1,0:T(8,128)(2,1)S(1)}, bf16[1,256,512]{2,1,0:T(8,128)(2,1)S(1)}, u32[]{:S(2)}, u32[]{:S(2)}) collective-permute-start(bf16[1,256,512]{2,1,0:T(8,128)(2,1)S(1)} %get-tuple-element.125.refs_1_), channel_id=1, source_target_pairs={{0,16},{8,24},{16,0},{24,8},{1,17},{9,25},{17,1},{25,9},{2,18},{10... | collective-permute-start | bytes 786440 | tf_op jit(solution)/shard_map/ppermute | solution.py:258
  84.4 4.1 %expert_product.8 = (f32[135168,128]{1,0:T(8,128)}, bf16[384,4096]{1,0:T(8,128)(2,1)}) custom-call(s32[8]{0:T(128)S(1)} %iota_xor_fusion.1.sources, s32[4]{0:T(128)S(1)} %select_reduce_fusion.places, bf16[384,1024]{1,0:T(8,128)(2,1)S(1)} %bitcast.4, bf16[2,256,512]{2,1,0:T(8,128)(2,1)} %get-tuple-element.108.refs_0_, ...), custom_call_target="tpu_custom_call", output_to_operand_aliasing={{0}: (7, {}), {1}: (8, {})} | custom-call | bytes 65536 | tf_op jit(solution)/shard_map/expert_product/pallas_call | solution.py:238
  88.6 1.6 %collective-permute-start.24 = (bf16[1,256,512]{2,1,0:T(8,128)(2,1)S(1)}, bf16[1,256,512]{2,1,0:T(8,128)(2,1)S(1)}, u32[]{:S(2)}, u32[]{:S(2)}) collective-permute-start(bf16[1,256,512]{2,1,0:T(8,128)(2,1)S(1)} %get-tuple-element.124.refs_2_), channel_id=1, source_target_pairs={{0,8},{8,0},{16,24},{24,16},{1,9},{9,1},{17,25},{25,17},{2,10},{10... | collective-permute-start | bytes 786440 | tf_op jit(solution)/shard_map/ppermute | solution.py:258
  90.1 3.1 %expert_product.9 = (f32[135168,128]{1,0:T(8,128)}, bf16[384,4096]{1,0:T(8,128)(2,1)}) custom-call(s32[8]{0:T(128)S(1)} %iota_xor_fusion.1.sources, s32[4]{0:T(128)S(1)} %select_reduce_fusion.places, bf16[384,1024]{1,0:T(8,128)(2,1)S(1)} %bitcast.5, ...), custom_call_target="tpu_custom_call", output_to_operand_aliasing={{0}: (7, {}), {1}: (8, {})} | custom-call | bytes 65536 | tf_op jit(solution)/shard_map/expert_product/pallas_call | solution.py:238
  93.2 2.0 %expert_product.10 = (f32[135168,128]{1,0:T(8,128)}, bf16[384,4096]{1,0:T(8,128)(2,1)}) custom-call(s32[8]{0:T(128)S(1)} %iota_xor_fusion.1.sources, s32[4]{0:T(128)S(1)} %select_reduce_fusion.places, bf16[384,1024]{1,0:T(8,128)(2,1)S(1)} %bitcast.6, ...), custom_call_target="tpu_custom_call", output_to_operand_aliasing={{0}: (7, {}), {1}: (8, {})} | custom-call | bytes 65536 | tf_op jit(solution)/shard_map/expert_product/pallas_call | solution.py:238
  95.2 2.0 %expert_product.11 = (f32[135168,128]{1,0:T(8,128)}, bf16[384,4096]{1,0:T(8,128)(2,1)}) custom-call(s32[8]{0:T(128)S(1)} %iota_xor_fusion.1.sources, s32[4]{0:T(128)S(1)} %select_reduce_fusion.places, bf16[384,1024]{1,0:T(8,128)(2,1)S(1)} %bitcast.7, ...), custom_call_target="tpu_custom_call", output_to_operand_aliasing={{0}: (7, {}), {1}: (8, {})} | custom-call | bytes 65536 | tf_op jit(solution)/shard_map/expert_product/pallas_call | solution.py:238
  (72 shorter events, 17.2 us)
Async XLA Ops:
  7.2 8.3 %collective-permute-start = (bf16[1,256,512]{2,1,0:T(8,128)(2,1)}, bf16[1,256,512]{2,1,0:T(8,128)(2,1)S(1)}, u32[]{:S(2)}, u32[]{:S(2)}) collective-permute-start(bf16[1,256,512]{2,1,0:T(8,128)(2,1)} %get-tuple-element.77.refs_0_), channel_id=1, source_target_pairs={{0,8},{8,0},{16,24},{24,16},{1,9},{9,1},{17,25},{25,17},{2,10},{10... | collective-permute-start | bytes 786440 | tf_op jit(solution)/shard_map/ppermute | solution.py:258
  8.8 8.0 %collective-permute-start.1 = (bf16[1,256,512]{2,1,0:T(8,128)(2,1)}, bf16[1,256,512]{2,1,0:T(8,128)(2,1)S(1)}, u32[]{:S(2)}, u32[]{:S(2)}) collective-permute-start(bf16[1,256,512]{2,1,0:T(8,128)(2,1)} %get-tuple-element.77.refs_0_), channel_id=1, source_target_pairs={{0,16},{8,24},{16,0},{24,8},{1,17},{9,25},{17,1},{25,9},{2,18},{10... | collective-permute-start | bytes 786440 | tf_op jit(solution)/shard_map/ppermute | solution.py:258
  10.3 15.5 %collective-permute-start.3 = (bf16[1,256,512]{2,1,0:T(8,128)(2,1)}, bf16[1,256,512]{2,1,0:T(8,128)(2,1)S(1)}, u32[]{:S(2)}, u32[]{:S(2)}) collective-permute-start(bf16[1,256,512]{2,1,0:T(8,128)(2,1)} %get-tuple-element.87), channel_id=1, source_target_pairs={{0,2},{1,3},{2,0},{3,1},{4,6},{5,7},{6,4},{7,5},{8,10},{9,11},{10,... | collective-permute-start | bytes 786440 | tf_op jit(solution)/shard_map/ppermute | solution.py:258
  10.7 15.2 %collective-permute-start.4 = (bf16[1,256,512]{2,1,0:T(8,128)(2,1)}, bf16[1,256,512]{2,1,0:T(8,128)(2,1)S(1)}, u32[]{:S(2)}, u32[]{:S(2)}) collective-permute-start(bf16[1,256,512]{2,1,0:T(8,128)(2,1)} %get-tuple-element.88), channel_id=1, source_target_pairs={{0,4},{1,5},{2,6},{3,7},{4,0},{5,1},{6,2},{7,3},{8,12},{9,13},{10,... | collective-permute-start | bytes 786440 | tf_op jit(solution)/shard_map/ppermute | solution.py:258
  16.8 9.2 %collective-permute-start.5 = (bf16[1,256,512]{2,1,0:T(8,128)(2,1)S(1)}, bf16[1,256,512]{2,1,0:T(8,128)(2,1)S(1)}, u32[]{:S(2)}, u32[]{:S(2)}) collective-permute-start(bf16[1,256,512]{2,1,0:T(8,128)(2,1)S(1)} %get-tuple-element.85.refs_0_), channel_id=1, source_target_pairs={{0,8},{8,0},{16,24},{24,16},{1,9},{9,1},{17,25},{25,17},{2,10},{10... | collective-permute-start | bytes 786440 | tf_op jit(solution)/shard_map/ppermute | solution.py:258
  17.3 8.7 %collective-permute-start.6 = (bf16[1,256,512]{2,1,0:T(8,128)(2,1)S(1)}, bf16[1,256,512]{2,1,0:T(8,128)(2,1)S(1)}, u32[]{:S(2)}, u32[]{:S(2)}) collective-permute-start(bf16[1,256,512]{2,1,0:T(8,128)(2,1)S(1)} %get-tuple-element.85.refs_0_), channel_id=1, source_target_pairs={{0,16},{8,24},{16,0},{24,8},{1,17},{9,25},{17,1},{25,9},{2,18},{10... | collective-permute-start | bytes 786440 | tf_op jit(solution)/shard_map/ppermute | solution.py:258
  26.5 7.4 %collective-permute-start.7 = (bf16[1,256,512]{2,1,0:T(8,128)(2,1)S(1)}, bf16[1,256,512]{2,1,0:T(8,128)(2,1)S(1)}, u32[]{:S(2)}, u32[]{:S(2)}) collective-permute-start(bf16[1,256,512]{2,1,0:T(8,128)(2,1)S(1)} %get-tuple-element.91.refs_2_), channel_id=1, source_target_pairs={{0,8},{8,0},{16,24},{24,16},{1,9},{9,1},{17,25},{25,17},{2,10},{10... | collective-permute-start | bytes 786440 | tf_op jit(solution)/shard_map/ppermute | solution.py:258
  28.0 11.0 %collective-permute-start.8 = (bf16[1,256,512]{2,1,0:T(8,128)(2,1)S(1)}, bf16[1,256,512]{2,1,0:T(8,128)(2,1)S(1)}, u32[]{:S(2)}, u32[]{:S(2)}) collective-permute-start(bf16[1,256,512]{2,1,0:T(8,128)(2,1)S(1)} %get-tuple-element.83.refs_1_), channel_id=1, source_target_pairs={{0,16},{8,24},{16,0},{24,8},{1,17},{9,25},{17,1},{25,9},{2,18},{10... | collective-permute-start | bytes 786440 | tf_op jit(solution)/shard_map/ppermute | solution.py:258
  28.5 14.0 %collective-permute-start.9 = (bf16[1,256,512]{2,1,0:T(8,128)(2,1)}, bf16[1,256,512]{2,1,0:T(8,128)(2,1)}, u32[]{:S(2)}, u32[]{:S(2)}) collective-permute-start(bf16[1,256,512]{2,1,0:T(8,128)(2,1)} %get-tuple-element.104), channel_id=1, source_target_pairs={{0,3},{1,2},{2,1},{3,0},{4,7},{5,6},{6,5},{7,4},{8,11},{9,10},{10,... | collective-permute-start | bytes 786440 | tf_op jit(solution)/shard_map/ppermute | solution.py:258
  28.5 21.0 %collective-permute-start.10 = (bf16[1,256,512]{2,1,0:T(8,128)(2,1)}, bf16[1,256,512]{2,1,0:T(8,128)(2,1)}, u32[]{:S(2)}, u32[]{:S(2)}) collective-permute-start(bf16[1,256,512]{2,1,0:T(8,128)(2,1)} %get-tuple-element.105), channel_id=1, source_target_pairs={{0,5},{1,4},{2,7},{3,6},{4,1},{5,0},{6,3},{7,2},{8,13},{9,12},{10,... | collective-permute-start | bytes 786440 | tf_op jit(solution)/shard_map/ppermute | solution.py:258
  34.8 20.5 %collective-permute-start.12 = (bf16[2,256,512]{2,1,0:T(8,128)(2,1)}, bf16[2,256,512]{2,1,0:T(8,128)(2,1)S(1)}, u32[]{:S(2)}, u32[]{:S(2)}) collective-permute-start(bf16[2,256,512]{2,1,0:T(8,128)(2,1)} %get-tuple-element.108.refs_0_), channel_id=1, source_target_pairs={{0,8},{8,0},{16,24},{24,16},{1,9},{9,1},{17,25},{25,17},{2,10},{10... | collective-permute-start | bytes 1572872 | tf_op jit(solution)/shard_map/ppermute | solution.py:258
  35.4 20.0 %collective-permute-start.13 = (bf16[2,256,512]{2,1,0:T(8,128)(2,1)}, bf16[2,256,512]{2,1,0:T(8,128)(2,1)S(1)}, u32[]{:S(2)}, u32[]{:S(2)}) collective-permute-start(bf16[2,256,512]{2,1,0:T(8,128)(2,1)} %get-tuple-element.108.refs_0_), channel_id=1, source_target_pairs={{0,16},{8,24},{16,0},{24,8},{1,17},{9,25},{17,1},{25,9},{2,18},{10... | collective-permute-start | bytes 1572872 | tf_op jit(solution)/shard_map/ppermute | solution.py:258
  39.0 16.3 %collective-permute-start.11 = (bf16[1,256,512]{2,1,0:T(8,128)(2,1)S(1)}, bf16[1,256,512]{2,1,0:T(8,128)(2,1)S(1)}, u32[]{:S(2)}, u32[]{:S(2)}) collective-permute-start(bf16[1,256,512]{2,1,0:T(8,128)(2,1)S(1)} %get-tuple-element.107), channel_id=1, source_target_pairs={{0,6},{1,7},{2,4},{3,5},{4,2},{5,3},{6,0},{7,1},{8,14},{9,15},{10,... | collective-permute-start | bytes 786440 | tf_op jit(solution)/shard_map/ppermute | solution.py:258
  50.6 14.6 %collective-permute-start.14 = (bf16[2,256,512]{2,1,0:T(8,128)(2,1)S(1)}, bf16[2,256,512]{2,1,0:T(8,128)(2,1)S(1)}, u32[]{:S(2)}, u32[]{:S(2)}) collective-permute-start(bf16[2,256,512]{2,1,0:T(8,128)(2,1)S(1)} %get-tuple-element.111.refs_0_), channel_id=1, source_target_pairs={{0,8},{8,0},{16,24},{24,16},{1,9},{9,1},{17,25},{25,17},{2,10},{10... | collective-permute-start | bytes 1572872 | tf_op jit(solution)/shard_map/ppermute | solution.py:258
  51.2 15.8 %collective-permute-start.15 = (bf16[2,256,512]{2,1,0:T(8,128)(2,1)S(1)}, bf16[2,256,512]{2,1,0:T(8,128)(2,1)S(1)}, u32[]{:S(2)}, u32[]{:S(2)}) collective-permute-start(bf16[2,256,512]{2,1,0:T(8,128)(2,1)S(1)} %get-tuple-element.111.refs_0_), channel_id=1, source_target_pairs={{0,16},{8,24},{16,0},{24,8},{1,17},{9,25},{17,1},{25,9},{2,18},{10... | collective-permute-start | bytes 1572872 | tf_op jit(solution)/shard_map/ppermute | solution.py:258
  55.4 27.5 %collective-permute-start.17 = (bf16[2,256,512]{2,1,0:T(8,128)(2,1)S(1)}, bf16[2,256,512]{2,1,0:T(8,128)(2,1)S(1)}, u32[]{:S(2)}, u32[]{:S(2)}) collective-permute-start(bf16[2,256,512]{2,1,0:T(8,128)(2,1)S(1)} %get-tuple-element.115.refs_1_), channel_id=1, source_target_pairs={{0,16},{8,24},{16,0},{24,8},{1,17},{9,25},{17,1},{25,9},{2,18},{10... | collective-permute-start | bytes 1572872 | tf_op jit(solution)/shard_map/ppermute | solution.py:258
  57.0 10.9 %collective-permute-start.16 = (bf16[1,256,512]{2,1,0:T(8,128)(2,1)S(1)}, bf16[1,256,512]{2,1,0:T(8,128)(2,1)S(1)}, u32[]{:S(2)}, u32[]{:S(2)}) collective-permute-start(bf16[1,256,512]{2,1,0:T(8,128)(2,1)S(1)} %get-tuple-element.113), channel_id=1, source_target_pairs={{0,7},{1,6},{2,5},{3,4},{4,3},{5,2},{6,1},{7,0},{8,15},{9,14},{10,... | collective-permute-start | bytes 786440 | tf_op jit(solution)/shard_map/ppermute | solution.py:258
  57.2 13.6 %collective-permute-start.18 = (bf16[1,256,512]{2,1,0:T(8,128)(2,1)S(1)}, bf16[1,256,512]{2,1,0:T(8,128)(2,1)S(1)}, u32[]{:S(2)}, u32[]{:S(2)}) collective-permute-start(bf16[1,256,512]{2,1,0:T(8,128)(2,1)S(1)} %get-tuple-element.118.refs_0_), channel_id=1, source_target_pairs={{0,8},{8,0},{16,24},{24,16},{1,9},{9,1},{17,25},{25,17},{2,10},{10... | collective-permute-start | bytes 786440 | tf_op jit(solution)/shard_map/ppermute | solution.py:258
  65.2 17.7 %collective-permute-start.19 = (bf16[1,256,512]{2,1,0:T(8,128)(2,1)S(1)}, bf16[1,256,512]{2,1,0:T(8,128)(2,1)S(1)}, u32[]{:S(2)}, u32[]{:S(2)}) collective-permute-start(bf16[1,256,512]{2,1,0:T(8,128)(2,1)S(1)} %get-tuple-element.118.refs_0_), channel_id=1, source_target_pairs={{0,16},{8,24},{16,0},{24,8},{1,17},{9,25},{17,1},{25,9},{2,18},{10... | collective-permute-start | bytes 786440 | tf_op jit(solution)/shard_map/ppermute | solution.py:258
  67.0 23.1 %collective-permute-start.22 = (bf16[2,256,512]{2,1,0:T(8,128)(2,1)S(1)}, bf16[2,256,512]{2,1,0:T(8,128)(2,1)S(1)}, u32[]{:S(2)}, u32[]{:S(2)}) collective-permute-start(bf16[2,256,512]{2,1,0:T(8,128)(2,1)S(1)} %get-tuple-element.128.refs_2_), channel_id=1, source_target_pairs={{0,8},{8,0},{16,24},{24,16},{1,9},{9,1},{17,25},{25,17},{2,10},{10... | collective-permute-start | bytes 1572872 | tf_op jit(solution)/shard_map/ppermute | solution.py:258
  67.9 20.7 %collective-permute-start.20 = (bf16[1,256,512]{2,1,0:T(8,128)(2,1)S(1)}, bf16[1,256,512]{2,1,0:T(8,128)(2,1)S(1)}, u32[]{:S(2)}, u32[]{:S(2)}) collective-permute-start(bf16[1,256,512]{2,1,0:T(8,128)(2,1)S(1)} %get-tuple-element.114.refs_0_), channel_id=1, source_target_pairs={{0,8},{8,0},{16,24},{24,16},{1,9},{9,1},{17,25},{25,17},{2,10},{10... | collective-permute-start | bytes 786440 | tf_op jit(solution)/shard_map/ppermute | solution.py:258
  70.8 17.8 %collective-permute-start.21 = (bf16[1,256,512]{2,1,0:T(8,128)(2,1)S(1)}, bf16[1,256,512]{2,1,0:T(8,128)(2,1)S(1)}, u32[]{:S(2)}, u32[]{:S(2)}) collective-permute-start(bf16[1,256,512]{2,1,0:T(8,128)(2,1)S(1)} %get-tuple-element.114.refs_0_), channel_id=1, source_target_pairs={{0,16},{8,24},{16,0},{24,8},{1,17},{9,25},{17,1},{25,9},{2,18},{10... | collective-permute-start | bytes 786440 | tf_op jit(solution)/shard_map/ppermute | solution.py:258
  82.9 10.3 %collective-permute-start.23 = (bf16[1,256,512]{2,1,0:T(8,128)(2,1)S(1)}, bf16[1,256,512]{2,1,0:T(8,128)(2,1)S(1)}, u32[]{:S(2)}, u32[]{:S(2)}) collective-permute-start(bf16[1,256,512]{2,1,0:T(8,128)(2,1)S(1)} %get-tuple-element.125.refs_1_), channel_id=1, source_target_pairs={{0,16},{8,24},{16,0},{24,8},{1,17},{9,25},{17,1},{25,9},{2,18},{10... | collective-permute-start | bytes 786440 | tf_op jit(solution)/shard_map/ppermute | solution.py:258
  88.6 6.6 %collective-permute-start.24 = (bf16[1,256,512]{2,1,0:T(8,128)(2,1)S(1)}, bf16[1,256,512]{2,1,0:T(8,128)(2,1)S(1)}, u32[]{:S(2)}, u32[]{:S(2)}) collective-permute-start(bf16[1,256,512]{2,1,0:T(8,128)(2,1)S(1)} %get-tuple-element.124.refs_2_), channel_id=1, source_target_pairs={{0,8},{8,0},{16,24},{24,16},{1,9},{9,1},{17,25},{25,17},{2,10},{10... | collective-permute-start | bytes 786440 | tf_op jit(solution)/shard_map/ppermute | solution.py:258
  (11 other events, 52.3 us)

commit v16 on v15

--- a/solution.py
+++ b/solution.py
@@ -310,13 +310,14 @@
             ([(1, 1), (1, 2)], [(1, 2, 1)], [], []),
             ([(1, 3)], [], [], []),
             (one, [(one, 0, 1), (one, 0, 2)], [], [1]),
-            ([(0, 3)], [], [6], [0]),
+            ([(0, 3)], [], [], [0]),
+            ([(3, 0), (5, 0)], [], [6], []),
             (two, [(two, 0, 1), (two, 0, 2)], [], []),
             ([(6, 0), (one, 1), (one, 2)], [(one, 1, 2)], [7], []),
             ([(two, 1), (two, 2)], [(two, 2, 1), (6, 0, 1), (6, 0, 2)], [], []),
             ([(7, 0)], [(7, 0, 1), (7, 0, 2)], [], []),
-            ([(one, 3), (6, 1), (6, 2)], [(6, 1, 2)], [], [one]),
-            ([(7, 1), (7, 2)], [(7, 2, 1)], [], []),
+            ([(one, 3), (6, 1), (6, 2)], [(6, 1, 2)], [], []),
+            ([(7, 1), (7, 2)], [(7, 2, 1)], [], [one]),
             ([(two, 3)], [], [], [two]),
             ([(6, 3)], [], [], [6]),
             ([(7, 3)], [], [], [7]),

time: 98.4 us -> 98.7 us (level)
  waiting for transfers between devices: 35.4 us -> 40.4 us
  starting transfers between devices: 28.7 us -> 24.9 us
  local copies, waits for them, and re-layouts: 1.59 us -> 2.66 us
  Pallas kernels: 30.6 us -> 29.6 us
    ppermute x25, waiting for transfers between devices: 35.4 us -> 40.4 us  [swap(): return lax.ppermute(value, axis, [(i, i ^ mask) for i in range(size)])]
    ppermute x25, starting transfers between devices: 28.7 us -> 24.9 us  [swap(): return lax.ppermute(value, axis, [(i, i ^ mask) for i in range(size)])]
    unnamed x20 -> x28, local copies, waits for them, and re-layouts: 1.59 us -> 2.66 us
    pallas_call x2, Pallas kernels: 1.84 us -> 0.84 us  [join(): pl.pallas_call(functools.partial(join_kernel, picks), in_specs=[WHOLE] *...]
  transfers between devices with their start and end apart: 25 -> 25, of which waited for: 10 -> 9; matrix products, arithmetic and copies ran while one was open for 0% -> 0% of each run, Pallas kernels for 23% -> 21%
where the time goes in v16:
time: 98.7 us; the launch traced here: 98.5 us
  waiting for transfers between devices  40.4 us (41%)
  Pallas kernels  29.6 us (30%)
  starting transfers between devices  24.9 us (25%)
  local copies, waits for them, and re-layouts  2.66 us (3%)
    ppermute x25, waiting for transfers between devices, swap(): return lax.ppermute(value, axis, [(i, i ^ mask) for i in range(size)])  40.4 us
    ppermute x25, starting transfers between devices, swap(): return lax.ppermute(value, axis, [(i, i ^ mask) for i in range(size)])  24.9 us
    pallas_call x6, Pallas kernels, product(): pl.pallas_call(functools.partial(product_kernel, slabs), grid_spec=pltpu....  15.2 us
    pallas_call x2, Pallas kernels, adam_blocks(): pl.pallas_call(functools.partial(adam_kernel, groups, passed), in_specs=[...  13.5 us
    unnamed x28, local copies, waits for them, and re-layouts  2.66 us
  transfers between devices with their start and end apart: 25, of which 9 were waited for; matrix products, arithmetic and copies ran while one was open for 0% of the time, Pallas kernels for 21%

profile of v16, /device:TPU:8, one launch (start us, length us, event | category | flops | bytes accessed | tf_op | source)
XLA Modules:
  0.0 98.5 jit_solution(781990706962219865)
XLA Ops:
  0.6 6.6 %adam_quantize.2 = (f32[8,256,512]{2,1,0:T(8,128)}, bf16[8,256,512]{2,1,0:T(8,128)(2,1)}, bf16[8,256,512]{2,1,0:T(8,128)(2,1)}, bf16[1,256,512]{2,1,0:T(8,128)(2...) custom-call(s32[8]{0:T(128)} %owner.3, ...), custom_call_target="tpu_custom_call" | custom-call | bytes 65536 | tf_op jit(solution)/shard_map/adam_quantize/pallas_call | solution.py:170
  7.2 1.6 %collective-permute-start = (bf16[1,256,512]{2,1,0:T(8,128)(2,1)}, bf16[1,256,512]{2,1,0:T(8,128)(2,1)S(1)}, u32[]{:S(2)}, u32[]{:S(2)}) collective-permute-start(bf16[1,256,512]{2,1,0:T(8,128)(2,1)} %get-tuple-element.80.refs_0_), channel_id=1, source_target_pairs={{0,8},{8,0},{16,24},{24,16},{1,9},{9,1},{17,25},{25,17},{2,10},{10... | collective-permute-start | bytes 786440 | tf_op jit(solution)/shard_map/ppermute | solution.py:258
  8.8 1.5 %collective-permute-start.1 = (bf16[1,256,512]{2,1,0:T(8,128)(2,1)}, bf16[1,256,512]{2,1,0:T(8,128)(2,1)S(1)}, u32[]{:S(2)}, u32[]{:S(2)}) collective-permute-start(bf16[1,256,512]{2,1,0:T(8,128)(2,1)} %get-tuple-element.80.refs_0_), channel_id=1, source_target_pairs={{0,16},{8,24},{16,0},{24,8},{1,17},{9,25},{17,1},{25,9},{2,18},{10... | collective-permute-start | bytes 786440 | tf_op jit(solution)/shard_map/ppermute | solution.py:258
  10.7 2.6 %collective-permute-start.4 = (bf16[1,256,512]{2,1,0:T(8,128)(2,1)}, bf16[1,256,512]{2,1,0:T(8,128)(2,1)S(1)}, u32[]{:S(2)}, u32[]{:S(2)}) collective-permute-start(bf16[1,256,512]{2,1,0:T(8,128)(2,1)} %get-tuple-element.91), channel_id=1, source_target_pairs={{0,4},{1,5},{2,6},{3,7},{4,0},{5,1},{6,2},{7,3},{8,12},{9,13},{10,... | collective-permute-start | bytes 786440 | tf_op jit(solution)/shard_map/ppermute | solution.py:258
  13.3 2.2 %collective-permute-done.refs_1_ = bf16[1,256,512]{2,1,0:T(8,128)(2,1)S(1)} collective-permute-done((bf16[1,256,512]{2,1,0:T(8,128)(2,1)}, bf16[1,256,512]{2,1,0:T(8,128)(2,1)S(1)}, u32[]{:S(2)}, u32[]{:S(2)}) %collective-permute-start) | collective-permute-done | bytes 262176 | tf_op jit(solution)/shard_map/ppermute | solution.py:258
  17.4 1.5 %collective-permute-start.6 = (bf16[1,256,512]{2,1,0:T(8,128)(2,1)S(1)}, bf16[1,256,512]{2,1,0:T(8,128)(2,1)S(1)}, u32[]{:S(2)}, u32[]{:S(2)}) collective-permute-start(bf16[1,256,512]{2,1,0:T(8,128)(2,1)S(1)} %get-tuple-element.88.refs_0_), channel_id=1, source_target_pairs={{0,16},{8,24},{16,0},{24,8},{1,17},{9,25},{17,1},{25,9},{2,18},{10... | collective-permute-start | bytes 786440 | tf_op jit(solution)/shard_map/ppermute | solution.py:258
  18.9 6.9 %adam_quantize.3 = (f32[8,256,512]{2,1,0:T(8,128)}, bf16[8,256,512]{2,1,0:T(8,128)(2,1)}, bf16[8,256,512]{2,1,0:T(8,128)(2,1)}, bf16[1,256,512]{2,1,0:T(8,128)(2...) custom-call(s32[8]{0:T(128)S(1)} %copy-done.12, ...), custom_call_target="tpu_custom_call", output_to_operand_aliasing={{0}: (5, {}), {1}: (6, {}), {2}: (7, {}), {7}: (8, {})} | custom-call | bytes 65536 | tf_op jit(solution)/shard_map/adam_quantize/pallas_call | solution.py:170
  28.6 2.8 %collective-permute-start.10 = (bf16[1,256,512]{2,1,0:T(8,128)(2,1)}, bf16[1,256,512]{2,1,0:T(8,128)(2,1)S(1)}, u32[]{:S(2)}, u32[]{:S(2)}) collective-permute-start(bf16[1,256,512]{2,1,0:T(8,128)(2,1)} %get-tuple-element.107), channel_id=1, source_target_pairs={{0,5},{1,4},{2,7},{3,6},{4,1},{5,0},{6,3},{7,2},{8,13},{9,12},{10,... | collective-permute-start | bytes 786440 | tf_op jit(solution)/shard_map/ppermute | solution.py:258
  31.4 2.6 %collective-permute-done.7.refs_1_ = bf16[1,256,512]{2,1,0:T(8,128)(2,1)S(1)} collective-permute-done((bf16[1,256,512]{2,1,0:T(8,128)(2,1)S(1)}, bf16[1,256,512]{2,1,0:T(8,128)(2,1)S(1)}, u32[]{:S(2)}, u32[]{:S(2)}) %collective-permute-start.7) | collective-permute-done | bytes 262176 | tf_op jit(solution)/shard_map/ppermute | solution.py:258
  38.0 2.0 %expert_product.6 = (f32[135168,128]{1,0:T(8,128)}, bf16[384,4096]{1,0:T(8,128)(2,1)}) custom-call(s32[8]{0:T(128)S(1)} %iota_xor_fusion.1.sources, s32[4]{0:T(128)S(1)} %select_reduce_fusion.places, bf16[384,1024]{1,0:T(8,128)(2,1)S(1)} %bitcast.2, bf16[1,256,512]{2,1,0:T(8,128)(2,1)S(1)} %copy-done.4, ...), custom_call_target="tpu_custom_call", output_to_operand_aliasing={{0}: (7, {})} | custom-call | bytes 65536 | tf_op jit(solution)/shard_map/expert_product/pallas_call | solution.py:238
  40.0 2.0 %expert_product.7 = (f32[135168,128]{1,0:T(8,128)}, bf16[384,4096]{1,0:T(8,128)(2,1)}) custom-call(s32[8]{0:T(128)S(1)} %iota_xor_fusion.1.sources, s32[4]{0:T(128)S(1)} %select_reduce_fusion.places, bf16[384,1024]{1,0:T(8,128)(2,1)S(1)} %bitcast.3, bf16[1,256,512]{2,1,0:T(8,128)(2,1)S(1)} %copy-done.9, ...), custom_call_target="tpu_custom_call", output_to_operand_aliasing={{0}: (7, {}), {1}: (8, {})} | custom-call | bytes 65536 | tf_op jit(solution)/shard_map/expert_product/pallas_call | solution.py:238
  42.0 2.0 %collective-permute-done.10.refs_2_ = bf16[1,256,512]{2,1,0:T(8,128)(2,1)S(1)} collective-permute-done((bf16[1,256,512]{2,1,0:T(8,128)(2,1)}, bf16[1,256,512]{2,1,0:T(8,128)(2,1)S(1)}, u32[]{:S(2)}, u32[]{:S(2)}) %collective-permute-start.10) | collective-permute-done | bytes 262176 | tf_op jit(solution)/shard_map/ppermute | solution.py:258
  44.7 1.5 %collective-permute-start.15 = (bf16[2,256,512]{2,1,0:T(8,128)(2,1)S(1)}, bf16[2,256,512]{2,1,0:T(8,128)(2,1)S(1)}, u32[]{:S(2)}, u32[]{:S(2)}) collective-permute-start(bf16[2,256,512]{2,1,0:T(8,128)(2,1)S(1)} %get-tuple-element.117.refs_0_), channel_id=1, source_target_pairs={{0,16},{8,24},{16,0},{24,8},{1,17},{9,25},{17,1},{25,9},{2,18},{10... | collective-permute-start | bytes 1572872 | tf_op jit(solution)/shard_map/ppermute | solution.py:258
  46.4 13.2 %collective-permute-done.11.refs_1_ = bf16[1,256,512]{2,1,0:T(8,128)(2,1)S(1)} collective-permute-done((bf16[1,256,512]{2,1,0:T(8,128)(2,1)S(1)}, bf16[1,256,512]{2,1,0:T(8,128)(2,1)S(1)}, u32[]{:S(2)}, u32[]{:S(2)}) %collective-permute-start.11) | collective-permute-done | bytes 262176 | tf_op jit(solution)/shard_map/ppermute | solution.py:258
  62.2 1.5 %collective-permute-start.19 = (bf16[1,256,512]{2,1,0:T(8,128)(2,1)S(1)}, bf16[1,256,512]{2,1,0:T(8,128)(2,1)S(1)}, u32[]{:S(2)}, u32[]{:S(2)}) collective-permute-start(bf16[1,256,512]{2,1,0:T(8,128)(2,1)S(1)} %get-tuple-element.123.refs_0_), channel_id=1, source_target_pairs={{0,16},{8,24},{16,0},{24,8},{1,17},{9,25},{17,1},{25,9},{2,18},{10... | collective-permute-start | bytes 786440 | tf_op jit(solution)/shard_map/ppermute | solution.py:258
  63.7 8.0 %collective-permute-done.16.refs_1_ = bf16[1,256,512]{2,1,0:T(8,128)(2,1)S(1)} collective-permute-done((bf16[1,256,512]{2,1,0:T(8,128)(2,1)S(1)}, bf16[1,256,512]{2,1,0:T(8,128)(2,1)S(1)}, u32[]{:S(2)}, u32[]{:S(2)}) %collective-permute-start.16) | collective-permute-done | bytes 262176 | tf_op jit(solution)/shard_map/ppermute | solution.py:258
  73.1 1.5 %collective-permute-start.21 = (bf16[1,256,512]{2,1,0:T(8,128)(2,1)S(1)}, bf16[1,256,512]{2,1,0:T(8,128)(2,1)S(1)}, u32[]{:S(2)}, u32[]{:S(2)}) collective-permute-start(bf16[1,256,512]{2,1,0:T(8,128)(2,1)S(1)} %get-tuple-element.120.refs_0_), channel_id=1, source_target_pairs={{0,16},{8,24},{16,0},{24,8},{1,17},{9,25},{17,1},{25,9},{2,18},{10... | collective-permute-start | bytes 786440 | tf_op jit(solution)/shard_map/ppermute | solution.py:258
  74.6 5.3 %collective-permute-done.19.refs_3_ = bf16[1,256,512]{2,1,0:T(8,128)(2,1)S(1)} collective-permute-done((bf16[1,256,512]{2,1,0:T(8,128)(2,1)S(1)}, bf16[1,256,512]{2,1,0:T(8,128)(2,1)S(1)}, u32[]{:S(2)}, u32[]{:S(2)}) %collective-permute-start.19) | collective-permute-done | bytes 262176 | tf_op jit(solution)/shard_map/ppermute | solution.py:258
  79.9 5.7 %collective-permute-done.20.refs_1_ = bf16[1,256,512]{2,1,0:T(8,128)(2,1)S(1)} collective-permute-done((bf16[1,256,512]{2,1,0:T(8,128)(2,1)S(1)}, bf16[1,256,512]{2,1,0:T(8,128)(2,1)S(1)}, u32[]{:S(2)}, u32[]{:S(2)}) %collective-permute-start.20) | collective-permute-done | bytes 262176 | tf_op jit(solution)/shard_map/ppermute | solution.py:258
  85.7 1.6 %collective-permute-start.24 = (bf16[1,256,512]{2,1,0:T(8,128)(2,1)S(1)}, bf16[1,256,512]{2,1,0:T(8,128)(2,1)S(1)}, u32[]{:S(2)}, u32[]{:S(2)}) collective-permute-start(bf16[1,256,512]{2,1,0:T(8,128)(2,1)S(1)} %get-tuple-element.126.refs_2_), channel_id=1, source_target_pairs={{0,8},{8,0},{16,24},{24,16},{1,9},{9,1},{17,25},{25,17},{2,10},{10... | collective-permute-start | bytes 786440 | tf_op jit(solution)/shard_map/ppermute | solution.py:258
  87.2 4.1 %expert_product.8 = (f32[135168,128]{1,0:T(8,128)}, bf16[384,4096]{1,0:T(8,128)(2,1)}) custom-call(s32[8]{0:T(128)S(1)} %iota_xor_fusion.1.sources, s32[4]{0:T(128)S(1)} %select_reduce_fusion.places, bf16[384,1024]{1,0:T(8,128)(2,1)S(1)} %bitcast.4, bf16[2,256,512]{2,1,0:T(8,128)(2,1)} %get-tuple-element.114.refs_0_, ...), custom_call_target="tpu_custom_call", output_to_operand_aliasing={{0}: (7, {}), {1}: (8, {})} | custom-call | bytes 65536 | tf_op jit(solution)/shard_map/expert_product/pallas_call | solution.py:238
  91.4 3.1 %expert_product.9 = (f32[135168,128]{1,0:T(8,128)}, bf16[384,4096]{1,0:T(8,128)(2,1)}) custom-call(s32[8]{0:T(128)S(1)} %iota_xor_fusion.1.sources, s32[4]{0:T(128)S(1)} %select_reduce_fusion.places, bf16[384,1024]{1,0:T(8,128)(2,1)S(1)} %bitcast.5, ...), custom_call_target="tpu_custom_call", output_to_operand_aliasing={{0}: (7, {}), {1}: (8, {})} | custom-call | bytes 65536 | tf_op jit(solution)/shard_map/expert_product/pallas_call | solution.py:238
  94.4 2.0 %expert_product.10 = (f32[135168,128]{1,0:T(8,128)}, bf16[384,4096]{1,0:T(8,128)(2,1)}) custom-call(s32[8]{0:T(128)S(1)} %iota_xor_fusion.1.sources, s32[4]{0:T(128)S(1)} %select_reduce_fusion.places, bf16[384,1024]{1,0:T(8,128)(2,1)S(1)} %bitcast.6, ...), custom_call_target="tpu_custom_call", output_to_operand_aliasing={{0}: (7, {}), {1}: (8, {})} | custom-call | bytes 65536 | tf_op jit(solution)/shard_map/expert_product/pallas_call | solution.py:238
  96.5 2.0 %expert_product.11 = (f32[135168,128]{1,0:T(8,128)}, bf16[384,4096]{1,0:T(8,128)(2,1)}) custom-call(s32[8]{0:T(128)S(1)} %iota_xor_fusion.1.sources, s32[4]{0:T(128)S(1)} %select_reduce_fusion.places, bf16[384,1024]{1,0:T(8,128)(2,1)S(1)} %bitcast.7, ...), custom_call_target="tpu_custom_call", output_to_operand_aliasing={{0}: (7, {}), {1}: (8, {})} | custom-call | bytes 65536 | tf_op jit(solution)/shard_map/expert_product/pallas_call | solution.py:238
  (81 shorter events, 13.9 us)
Async XLA Ops:
  7.2 8.3 %collective-permute-start = (bf16[1,256,512]{2,1,0:T(8,128)(2,1)}, bf16[1,256,512]{2,1,0:T(8,128)(2,1)S(1)}, u32[]{:S(2)}, u32[]{:S(2)}) collective-permute-start(bf16[1,256,512]{2,1,0:T(8,128)(2,1)} %get-tuple-element.80.refs_0_), channel_id=1, source_target_pairs={{0,8},{8,0},{16,24},{24,16},{1,9},{9,1},{17,25},{25,17},{2,10},{10... | collective-permute-start | bytes 786440 | tf_op jit(solution)/shard_map/ppermute | solution.py:258
  8.8 8.0 %collective-permute-start.1 = (bf16[1,256,512]{2,1,0:T(8,128)(2,1)}, bf16[1,256,512]{2,1,0:T(8,128)(2,1)S(1)}, u32[]{:S(2)}, u32[]{:S(2)}) collective-permute-start(bf16[1,256,512]{2,1,0:T(8,128)(2,1)} %get-tuple-element.80.refs_0_), channel_id=1, source_target_pairs={{0,16},{8,24},{16,0},{24,8},{1,17},{9,25},{17,1},{25,9},{2,18},{10... | collective-permute-start | bytes 786440 | tf_op jit(solution)/shard_map/ppermute | solution.py:258
  10.3 15.5 %collective-permute-start.3 = (bf16[1,256,512]{2,1,0:T(8,128)(2,1)}, bf16[1,256,512]{2,1,0:T(8,128)(2,1)S(1)}, u32[]{:S(2)}, u32[]{:S(2)}) collective-permute-start(bf16[1,256,512]{2,1,0:T(8,128)(2,1)} %get-tuple-element.90), channel_id=1, source_target_pairs={{0,2},{1,3},{2,0},{3,1},{4,6},{5,7},{6,4},{7,5},{8,10},{9,11},{10,... | collective-permute-start | bytes 786440 | tf_op jit(solution)/shard_map/ppermute | solution.py:258
  10.7 15.2 %collective-permute-start.4 = (bf16[1,256,512]{2,1,0:T(8,128)(2,1)}, bf16[1,256,512]{2,1,0:T(8,128)(2,1)S(1)}, u32[]{:S(2)}, u32[]{:S(2)}) collective-permute-start(bf16[1,256,512]{2,1,0:T(8,128)(2,1)} %get-tuple-element.91), channel_id=1, source_target_pairs={{0,4},{1,5},{2,6},{3,7},{4,0},{5,1},{6,2},{7,3},{8,12},{9,13},{10,... | collective-permute-start | bytes 786440 | tf_op jit(solution)/shard_map/ppermute | solution.py:258
  16.8 9.2 %collective-permute-start.5 = (bf16[1,256,512]{2,1,0:T(8,128)(2,1)S(1)}, bf16[1,256,512]{2,1,0:T(8,128)(2,1)S(1)}, u32[]{:S(2)}, u32[]{:S(2)}) collective-permute-start(bf16[1,256,512]{2,1,0:T(8,128)(2,1)S(1)} %get-tuple-element.88.refs_0_), channel_id=1, source_target_pairs={{0,8},{8,0},{16,24},{24,16},{1,9},{9,1},{17,25},{25,17},{2,10},{10... | collective-permute-start | bytes 786440 | tf_op jit(solution)/shard_map/ppermute | solution.py:258
  17.4 8.6 %collective-permute-start.6 = (bf16[1,256,512]{2,1,0:T(8,128)(2,1)S(1)}, bf16[1,256,512]{2,1,0:T(8,128)(2,1)S(1)}, u32[]{:S(2)}, u32[]{:S(2)}) collective-permute-start(bf16[1,256,512]{2,1,0:T(8,128)(2,1)S(1)} %get-tuple-element.88.refs_0_), channel_id=1, source_target_pairs={{0,16},{8,24},{16,0},{24,8},{1,17},{9,25},{17,1},{25,9},{2,18},{10... | collective-permute-start | bytes 786440 | tf_op jit(solution)/shard_map/ppermute | solution.py:258
  26.6 7.3 %collective-permute-start.7 = (bf16[1,256,512]{2,1,0:T(8,128)(2,1)S(1)}, bf16[1,256,512]{2,1,0:T(8,128)(2,1)S(1)}, u32[]{:S(2)}, u32[]{:S(2)}) collective-permute-start(bf16[1,256,512]{2,1,0:T(8,128)(2,1)S(1)} %get-tuple-element.94.refs_2_), channel_id=1, source_target_pairs={{0,8},{8,0},{16,24},{24,16},{1,9},{9,1},{17,25},{25,17},{2,10},{10... | collective-permute-start | bytes 786440 | tf_op jit(solution)/shard_map/ppermute | solution.py:258
  28.1 11.9 %collective-permute-start.8 = (bf16[1,256,512]{2,1,0:T(8,128)(2,1)S(1)}, bf16[1,256,512]{2,1,0:T(8,128)(2,1)S(1)}, u32[]{:S(2)}, u32[]{:S(2)}) collective-permute-start(bf16[1,256,512]{2,1,0:T(8,128)(2,1)S(1)} %get-tuple-element.86.refs_1_), channel_id=1, source_target_pairs={{0,16},{8,24},{16,0},{24,8},{1,17},{9,25},{17,1},{25,9},{2,18},{10... | collective-permute-start | bytes 786440 | tf_op jit(solution)/shard_map/ppermute | solution.py:258
  28.6 13.4 %collective-permute-start.9 = (bf16[1,256,512]{2,1,0:T(8,128)(2,1)}, bf16[1,256,512]{2,1,0:T(8,128)(2,1)S(1)}, u32[]{:S(2)}, u32[]{:S(2)}) collective-permute-start(bf16[1,256,512]{2,1,0:T(8,128)(2,1)} %get-tuple-element.106), channel_id=1, source_target_pairs={{0,3},{1,2},{2,1},{3,0},{4,7},{5,6},{6,5},{7,4},{8,11},{9,10},{10,... | collective-permute-start | bytes 786440 | tf_op jit(solution)/shard_map/ppermute | solution.py:258
  28.6 15.4 %collective-permute-start.10 = (bf16[1,256,512]{2,1,0:T(8,128)(2,1)}, bf16[1,256,512]{2,1,0:T(8,128)(2,1)S(1)}, u32[]{:S(2)}, u32[]{:S(2)}) collective-permute-start(bf16[1,256,512]{2,1,0:T(8,128)(2,1)} %get-tuple-element.107), channel_id=1, source_target_pairs={{0,5},{1,4},{2,7},{3,6},{4,1},{5,0},{6,3},{7,2},{8,13},{9,12},{10,... | collective-permute-start | bytes 786440 | tf_op jit(solution)/shard_map/ppermute | solution.py:258
  34.8 24.7 %collective-permute-start.12 = (bf16[2,256,512]{2,1,0:T(8,128)(2,1)}, bf16[2,256,512]{2,1,0:T(8,128)(2,1)S(1)}, u32[]{:S(2)}, u32[]{:S(2)}) collective-permute-start(bf16[2,256,512]{2,1,0:T(8,128)(2,1)} %get-tuple-element.114.refs_0_), channel_id=1, source_target_pairs={{0,8},{8,0},{16,24},{24,16},{1,9},{9,1},{17,25},{25,17},{2,10},{10... | collective-permute-start | bytes 1572872 | tf_op jit(solution)/shard_map/ppermute | solution.py:258
  35.4 24.2 %collective-permute-start.13 = (bf16[2,256,512]{2,1,0:T(8,128)(2,1)}, bf16[2,256,512]{2,1,0:T(8,128)(2,1)S(1)}, u32[]{:S(2)}, u32[]{:S(2)}) collective-permute-start(bf16[2,256,512]{2,1,0:T(8,128)(2,1)} %get-tuple-element.114.refs_0_), channel_id=1, source_target_pairs={{0,16},{8,24},{16,0},{24,8},{1,17},{9,25},{17,1},{25,9},{2,18},{10... | collective-permute-start | bytes 1572872 | tf_op jit(solution)/shard_map/ppermute | solution.py:258
  44.1 17.5 %collective-permute-start.14 = (bf16[2,256,512]{2,1,0:T(8,128)(2,1)S(1)}, bf16[2,256,512]{2,1,0:T(8,128)(2,1)S(1)}, u32[]{:S(2)}, u32[]{:S(2)}) collective-permute-start(bf16[2,256,512]{2,1,0:T(8,128)(2,1)S(1)} %get-tuple-element.117.refs_0_), channel_id=1, source_target_pairs={{0,8},{8,0},{16,24},{24,16},{1,9},{9,1},{17,25},{25,17},{2,10},{10... | collective-permute-start | bytes 1572872 | tf_op jit(solution)/shard_map/ppermute | solution.py:258
  44.7 16.9 %collective-permute-start.15 = (bf16[2,256,512]{2,1,0:T(8,128)(2,1)S(1)}, bf16[2,256,512]{2,1,0:T(8,128)(2,1)S(1)}, u32[]{:S(2)}, u32[]{:S(2)}) collective-permute-start(bf16[2,256,512]{2,1,0:T(8,128)(2,1)S(1)} %get-tuple-element.117.refs_0_), channel_id=1, source_target_pairs={{0,16},{8,24},{16,0},{24,8},{1,17},{9,25},{17,1},{25,9},{2,18},{10... | collective-permute-start | bytes 1572872 | tf_op jit(solution)/shard_map/ppermute | solution.py:258
  46.2 13.3 %collective-permute-start.11 = (bf16[1,256,512]{2,1,0:T(8,128)(2,1)S(1)}, bf16[1,256,512]{2,1,0:T(8,128)(2,1)S(1)}, u32[]{:S(2)}, u32[]{:S(2)}) collective-permute-start(bf16[1,256,512]{2,1,0:T(8,128)(2,1)S(1)} %get-tuple-element.113), channel_id=1, source_target_pairs={{0,6},{1,7},{2,4},{3,5},{4,2},{5,3},{6,0},{7,1},{8,14},{9,15},{10,... | collective-permute-start | bytes 786440 | tf_op jit(solution)/shard_map/ppermute | solution.py:258
  59.6 20.3 %collective-permute-start.17 = (bf16[2,256,512]{2,1,0:T(8,128)(2,1)S(1)}, bf16[2,256,512]{2,1,0:T(8,128)(2,1)S(1)}, u32[]{:S(2)}, u32[]{:S(2)}) collective-permute-start(bf16[2,256,512]{2,1,0:T(8,128)(2,1)S(1)} %get-tuple-element.122.refs_1_), channel_id=1, source_target_pairs={{0,16},{8,24},{16,0},{24,8},{1,17},{9,25},{17,1},{25,9},{2,18},{10... | collective-permute-start | bytes 1572872 | tf_op jit(solution)/shard_map/ppermute | solution.py:258
  60.2 11.6 %collective-permute-start.16 = (bf16[1,256,512]{2,1,0:T(8,128)(2,1)S(1)}, bf16[1,256,512]{2,1,0:T(8,128)(2,1)S(1)}, u32[]{:S(2)}, u32[]{:S(2)}) collective-permute-start(bf16[1,256,512]{2,1,0:T(8,128)(2,1)S(1)} %get-tuple-element.119), channel_id=1, source_target_pairs={{0,7},{1,6},{2,5},{3,4},{4,3},{5,2},{6,1},{7,0},{8,15},{9,14},{10,... | collective-permute-start | bytes 786440 | tf_op jit(solution)/shard_map/ppermute | solution.py:258
  60.2 12.9 %collective-permute-start.18 = (bf16[1,256,512]{2,1,0:T(8,128)(2,1)S(1)}, bf16[1,256,512]{2,1,0:T(8,128)(2,1)S(1)}, u32[]{:S(2)}, u32[]{:S(2)}) collective-permute-start(bf16[1,256,512]{2,1,0:T(8,128)(2,1)S(1)} %get-tuple-element.123.refs_0_), channel_id=1, source_target_pairs={{0,8},{8,0},{16,24},{24,16},{1,9},{9,1},{17,25},{25,17},{2,10},{10... | collective-permute-start | bytes 786440 | tf_op jit(solution)/shard_map/ppermute | solution.py:258
  61.7 29.7 %collective-permute-start.22 = (bf16[2,256,512]{2,1,0:T(8,128)(2,1)S(1)}, bf16[2,256,512]{2,1,0:T(8,128)(2,1)S(1)}, u32[]{:S(2)}, u32[]{:S(2)}) collective-permute-start(bf16[2,256,512]{2,1,0:T(8,128)(2,1)S(1)} %get-tuple-element.130.refs_2_), channel_id=1, source_target_pairs={{0,8},{8,0},{16,24},{24,16},{1,9},{9,1},{17,25},{25,17},{2,10},{10... | collective-permute-start | bytes 1572872 | tf_op jit(solution)/shard_map/ppermute | solution.py:258
  62.2 17.7 %collective-permute-start.19 = (bf16[1,256,512]{2,1,0:T(8,128)(2,1)S(1)}, bf16[1,256,512]{2,1,0:T(8,128)(2,1)S(1)}, u32[]{:S(2)}, u32[]{:S(2)}) collective-permute-start(bf16[1,256,512]{2,1,0:T(8,128)(2,1)S(1)} %get-tuple-element.123.refs_0_), channel_id=1, source_target_pairs={{0,16},{8,24},{16,0},{24,8},{1,17},{9,25},{17,1},{25,9},{2,18},{10... | collective-permute-start | bytes 786440 | tf_op jit(solution)/shard_map/ppermute | solution.py:258
  71.7 13.9 %collective-permute-start.20 = (bf16[1,256,512]{2,1,0:T(8,128)(2,1)S(1)}, bf16[1,256,512]{2,1,0:T(8,128)(2,1)S(1)}, u32[]{:S(2)}, u32[]{:S(2)}) collective-permute-start(bf16[1,256,512]{2,1,0:T(8,128)(2,1)S(1)} %get-tuple-element.120.refs_0_), channel_id=1, source_target_pairs={{0,8},{8,0},{16,24},{24,16},{1,9},{9,1},{17,25},{25,17},{2,10},{10... | collective-permute-start | bytes 786440 | tf_op jit(solution)/shard_map/ppermute | solution.py:258
  73.1 12.6 %collective-permute-start.21 = (bf16[1,256,512]{2,1,0:T(8,128)(2,1)S(1)}, bf16[1,256,512]{2,1,0:T(8,128)(2,1)S(1)}, u32[]{:S(2)}, u32[]{:S(2)}) collective-permute-start(bf16[1,256,512]{2,1,0:T(8,128)(2,1)S(1)} %get-tuple-element.120.refs_0_), channel_id=1, source_target_pairs={{0,16},{8,24},{16,0},{24,8},{1,17},{9,25},{17,1},{25,9},{2,18},{10... | collective-permute-start | bytes 786440 | tf_op jit(solution)/shard_map/ppermute | solution.py:258
  79.9 14.5 %collective-permute-start.23 = (bf16[1,256,512]{2,1,0:T(8,128)(2,1)S(1)}, bf16[1,256,512]{2,1,0:T(8,128)(2,1)S(1)}, u32[]{:S(2)}, u32[]{:S(2)}) collective-permute-start(bf16[1,256,512]{2,1,0:T(8,128)(2,1)S(1)} %get-tuple-element.127.refs_1_), channel_id=1, source_target_pairs={{0,16},{8,24},{16,0},{24,8},{1,17},{9,25},{17,1},{25,9},{2,18},{10... | collective-permute-start | bytes 786440 | tf_op jit(solution)/shard_map/ppermute | solution.py:258
  85.7 10.8 %collective-permute-start.24 = (bf16[1,256,512]{2,1,0:T(8,128)(2,1)S(1)}, bf16[1,256,512]{2,1,0:T(8,128)(2,1)S(1)}, u32[]{:S(2)}, u32[]{:S(2)}) collective-permute-start(bf16[1,256,512]{2,1,0:T(8,128)(2,1)S(1)} %get-tuple-element.126.refs_2_), channel_id=1, source_target_pairs={{0,8},{8,0},{16,24},{24,16},{1,9},{9,1},{17,25},{25,17},{2,10},{10... | collective-permute-start | bytes 786440 | tf_op jit(solution)/shard_map/ppermute | solution.py:258
  (15 other events, 75.1 us)
